TPU v7x, 32 devices: a whole 2x2x4 slice. The times are simulated.
32 devices in a mesh: dp: 2 (over y), expert: 16 (over z, x, core).
Axes of the slice: x: 2, y: 2, z: 4, core: 2. Of those that a mesh axis runs over, the one named last changes fastest.
Arguments:
- layer_input: bfloat16 [2, 2, 1024, 2048], P(None, 'dp', 'expert'), may hold values from -6 to 6
- out_cotangent: bfloat16 [2, 2, 1024, 2048], P(None, 'dp', 'expert'), may hold values from -6 to 6
- lengths: int32 [2, 2], P(None, 'dp'), may hold values from 256 to 1024, as said below
- routes: int32 [2, 2, 1024, 6], P(None, 'dp', 'expert'), may hold values from 0 to 15, all different within a row; in each aligned block of 64 rows (0 to 63, 64 to 127, ..., all dimensions but the last counted through in order) at most 30 rows name the same one
- attn_gain: bfloat16 [2048], P(('dp', 'expert')), may hold values from 0.5 to 1.5
- query_weight: bfloat16 [2048, 3072], P(('dp', 'expert')), may hold values from -0.125 to 0.125
- latent_weight: bfloat16 [2048, 576], P(('dp', 'expert')), may hold values from -0.125 to 0.125
- latent_gain: bfloat16 [512], P(('dp', 'expert')), may hold values from 0.5 to 1.5
- expand_weight: bfloat16 [512, 4096], P(('dp', 'expert')), may hold values from -0.25 to 0.25
- output_weight: bfloat16 [2048, 2048], P(('dp', 'expert')), may hold values from -2 to 2
- mixer_gain: bfloat16 [2048], P(('dp', 'expert')), may hold values from 0.5 to 1.5
- router_weight: bfloat16 [2048, 16], P(('dp', 'expert')), may hold values from -0.0625 to 0.0625
- gate_weight: bfloat16 [16, 2048, 1408], P('expert', 'dp'), may hold values from -0.125 to 0.125
- up_weight: bfloat16 [16, 2048, 1408], P('expert', 'dp'), may hold values from -0.125 to 0.125
- down_weight: bfloat16 [16, 1408, 2048], P('expert', 'dp'), may hold values from -0.15625 to 0.15625
- shared_gate: bfloat16 [2048, 2816], P('dp', 'expert'), may hold values from -0.125 to 0.125
- shared_up: bfloat16 [2048, 2816], P('dp', 'expert'), may hold values from -0.125 to 0.125
- shared_down: bfloat16 [2816, 2048], P('expert', 'dp'), may hold values from -0.109375 to 0.109375
Outputs:
- layer_output: float32 [2, 2, 1024, 2048], P(None, 'dp', 'expert')
- grad_input: float32 [2, 2, 1024, 2048], P(None, 'dp', 'expert')
- grad_attn_gain: float32 [2048], P(('dp', 'expert'))
- grad_query_weight: float32 [2048, 3072], P(('dp', 'expert'))
- grad_latent_weight: float32 [2048, 576], P(('dp', 'expert'))
- grad_latent_gain: float32 [512], P(('dp', 'expert'))
- grad_expand_weight: float32 [512, 4096], P(('dp', 'expert'))
- grad_output_weight: float32 [2048, 2048], P(('dp', 'expert'))
- grad_mixer_gain: float32 [2048], P(('dp', 'expert'))
- grad_router_weight: float32 [2048, 16], P(('dp', 'expert'))
- grad_gate_weight: float32 [16, 2048, 1408], P('expert', 'dp')
- grad_up_weight: float32 [16, 2048, 1408], P('expert', 'dp')
- grad_down_weight: float32 [16, 1408, 2048], P('expert', 'dp')
- grad_shared_gate: float32 [2048, 2816], P('dp', 'expert')
- grad_shared_up: float32 [2048, 2816], P('dp', 'expert')
- grad_shared_down: float32 [2816, 2048], P('expert', 'dp')
Inputs may be any that keep to these rules, and one draw needn't show every extreme that they name: `lengths`: for every index of dp, one of the 2 micro-batches holds a sequence of full length 1024. `routes`: in each micro-batch the 64 positions of one device name any one expert at most 30 times, a bound that some block reaches.
All inputs are finite; a program needn't handle non-finite values.
Results may differ from a plain program's by a relative error of at most 0.019.
Values may be sent and summed in bfloat16 or wider, within the bound.
A program may use at most 320 MiB of HBM per device.

v0:
```python
import jax
import jax.numpy as jnp
from jax import lax
from jax.sharding import PartitionSpec as P

H = 16
QK_NOPE = 128
ROPE = 64
V_DIM = 128
KV_RANK = 512
TOP = 6
EXP_DEV = 1


EPSILON = 1e-06
ROTARY_BASE = 10000.0


def product(left_side, right_side):
    return jnp.dot(left_side, right_side, preferred_element_type=jnp.float32)


def product_lead(left_side, right_side):
    return lax.dot_general(
        left_side, right_side, (((0,), (0,)), ((), ())), preferred_element_type=jnp.float32
    )


def product_trail(left_side, right_side):
    return lax.dot_general(
        left_side, right_side, (((1,), (1,)), ((), ())), preferred_element_type=jnp.float32
    )


def precise_lead(left_side, right_side):
    return lax.dot_general(
        left_side,
        right_side,
        (((0,), (0,)), ((), ())),
        precision=lax.Precision.HIGHEST,
        preferred_element_type=jnp.float32,
    )


def precise_trail(left_side, right_side):
    return lax.dot_general(
        left_side,
        right_side,
        (((1,), (1,)), ((), ())),
        precision=lax.Precision.HIGHEST,
        preferred_element_type=jnp.float32,
    )


def rotary_tables(positions, rotary_width):
    half_width = rotary_width // 2
    frequency = ROTARY_BASE ** (-jnp.arange(half_width, dtype=jnp.float32) * 2.0 / rotary_width)
    angles = positions[:, None] * frequency[None, :]
    return (jnp.cos(angles), jnp.sin(angles))


def rotate(values, cosine, sine_table):
    half_width = values.shape[-1] // 2
    first_half = values[..., :half_width]
    second_half = values[..., half_width:]
    return jnp.concatenate(
        [
            first_half * cosine - second_half * sine_table,
            second_half * cosine + first_half * sine_table,
        ],
        axis=-1,
    )


def unrotate(gradient, cosine, sine_table):
    half_width = gradient.shape[-1] // 2
    first_half = gradient[..., :half_width]
    second_half = gradient[..., half_width:]
    return jnp.concatenate(
        [
            first_half * cosine + second_half * sine_table,
            second_half * cosine - first_half * sine_table,
        ],
        axis=-1,
    )


def norm_forward(values, gains):
    factor = lax.rsqrt(jnp.mean(values * values, axis=-1, keepdims=True) + EPSILON)
    normed = values * factor
    return (normed * gains, normed, factor)


def norm_backward(gradient, normed, factor, gains):
    gain_grad = jnp.sum(gradient * normed, axis=0)
    scaled = gradient * gains
    return (
        factor * (scaled - normed * jnp.mean(scaled * normed, axis=-1, keepdims=True)),
        gain_grad,
    )


def silu_pair(gate_in):
    sigmoid = jax.nn.sigmoid(gate_in)
    return (gate_in * sigmoid, sigmoid * (1.0 + gate_in * (1.0 - sigmoid)))


def slot_index(route_rows, experts_total, capacity):
    flat_routes = route_rows.reshape(-1)
    onehot = (flat_routes[:, None] == jnp.arange(experts_total, dtype=jnp.int32)[None, :]).astype(
        jnp.int32
    )
    earlier = jnp.cumsum(onehot, axis=0) - onehot
    position = jnp.sum(earlier * onehot, axis=1)
    return (flat_routes * capacity + position).reshape(route_rows.shape)


def compute_scores(query_nope, query_rope, key_nope, key_rope, allowed, scale_factor):
    raw_scores = jnp.einsum(
        "thd,shd->hts", query_nope, key_nope, preferred_element_type=jnp.float32
    )
    raw_scores = raw_scores + jnp.einsum(
        "thd,sd->hts", query_rope, key_rope, preferred_element_type=jnp.float32
    )
    return jnp.where(allowed[None, :, :], raw_scores * scale_factor, -1e30)


def expert_hidden(stacked, gate_mats, up_mats):
    gate_in = jnp.einsum("erd,edf->erf", stacked, gate_mats, preferred_element_type=jnp.float32)
    up_in = jnp.einsum("erd,edf->erf", stacked, up_mats, preferred_element_type=jnp.float32)
    activated, slope = silu_pair(gate_in)
    return (gate_in, up_in, activated, slope, (activated * up_in).astype(jnp.bfloat16))


def per_device(
    layer_input,
    out_cotangent,
    lengths,
    routes,
    attn_gain,
    query_weight,
    latent_weight,
    latent_gain,
    expand_weight,
    output_weight,
    mixer_gain,
    router_weight,
    gate_weight,
    up_weight,
    down_weight,
    shared_gate,
    shared_up,
    shared_down,
):
    dense = (
        lax.all_gather(attn_gain, ("dp", "expert"), axis=0, tiled=True),
        lax.all_gather(latent_gain, ("dp", "expert"), axis=0, tiled=True),
        lax.all_gather(mixer_gain, ("dp", "expert"), axis=0, tiled=True),
        lax.all_gather(query_weight, ("dp", "expert"), axis=0, tiled=True),
        lax.all_gather(latent_weight, ("dp", "expert"), axis=0, tiled=True),
        lax.all_gather(expand_weight, ("dp", "expert"), axis=0, tiled=True),
        lax.all_gather(output_weight, ("dp", "expert"), axis=0, tiled=True),
        lax.all_gather(router_weight, ("dp", "expert"), axis=0, tiled=True),
    )
    gain_attn = dense[0].astype(jnp.float32)
    gain_latent = dense[1].astype(jnp.float32)
    gain_mixer = dense[2].astype(jnp.float32)
    query_full, latent_full, expand_full, output_full, router_full = (
        dense[3],
        dense[4],
        dense[5],
        dense[6],
        dense[7],
    )
    expand_wide = expand_full.astype(jnp.float32)
    owned = (
        lax.all_gather(gate_weight, "dp", axis=1, tiled=True),
        lax.all_gather(up_weight, "dp", axis=1, tiled=True),
        lax.all_gather(down_weight, "dp", axis=1, tiled=True),
        lax.all_gather(shared_gate, "dp", axis=0, tiled=True),
        lax.all_gather(shared_up, "dp", axis=0, tiled=True),
        lax.all_gather(shared_down, "dp", axis=1, tiled=True),
    )
    gate_full, up_full, down_full, share_gate, share_up, share_down = owned
    batches = layer_input.shape[0]
    tokens_here = layer_input.shape[2]
    width = layer_input.shape[3]
    groups = lax.axis_size("expert")
    group_index = lax.axis_index("expert")
    seq_total = tokens_here * groups
    experts_total = EXP_DEV * groups
    capacity = max(2, (tokens_here * TOP + experts_total - 1) // experts_total * 5 // 4)
    scale_factor = float(QK_NOPE + ROPE) ** (-0.5)
    positions = group_index * tokens_here + jnp.arange(tokens_here, dtype=jnp.int32)
    key_positions = jnp.arange(seq_total, dtype=jnp.int32)
    cosine, sine_table = rotary_tables(positions.astype(jnp.float32), ROPE)
    dense_local = tuple((jnp.zeros(item.shape, jnp.float32) for item in dense))
    owned_local = tuple((jnp.zeros(item.shape, jnp.float32) for item in owned))
    dense_total = None
    owned_total = None
    outputs = []
    input_grads = []
    for batch_index in range(batches):
        inputs = layer_input[batch_index, 0].astype(jnp.float32)
        seq_length = lengths[batch_index, 0]
        valid = (positions < seq_length).astype(jnp.float32)
        normed_attn, unit_attn, factor_attn = norm_forward(inputs, gain_attn)
        hidden_attn = normed_attn.astype(jnp.bfloat16)
        query_raw = product(hidden_attn, query_full).reshape(tokens_here, H, QK_NOPE + ROPE)
        query_nope = query_raw[..., :QK_NOPE].astype(jnp.bfloat16)
        query_rope = rotate(
            query_raw[..., QK_NOPE:], cosine[:, None, :], sine_table[:, None, :]
        ).astype(jnp.bfloat16)
        latent_raw = product(hidden_attn, latent_full)
        normed_latent, unit_latent, factor_latent = norm_forward(
            latent_raw[:, :KV_RANK], gain_latent
        )
        latent = normed_latent.astype(jnp.bfloat16)
        key_rope = rotate(latent_raw[:, KV_RANK:], cosine, sine_table).astype(jnp.bfloat16)
        outgoing = (product(latent, expand_full).astype(jnp.bfloat16), key_rope)
        incoming = (
            lax.all_gather(outgoing[0], "expert", axis=0, tiled=True),
            lax.all_gather(outgoing[1], "expert", axis=0, tiled=True),
        )
        expanded = incoming[0]
        all_rope = incoming[1]
        expanded = expanded.reshape(seq_total, H, QK_NOPE + V_DIM)
        key_nope = expanded[..., :QK_NOPE]
        key_values = expanded[..., QK_NOPE:]
        allowed = (key_positions[None, :] <= positions[:, None]) & (
            key_positions[None, :] < seq_length
        )
        scores = compute_scores(query_nope, query_rope, key_nope, all_rope, allowed, scale_factor)
        peak = jnp.max(scores, axis=-1, keepdims=True)
        log_total = peak + jnp.log(jnp.sum(jnp.exp(scores - peak), axis=-1, keepdims=True))
        probs_low = jnp.exp(scores - log_total).astype(jnp.bfloat16)
        attended = jnp.einsum(
            "hts,shd->thd", probs_low, key_values, preferred_element_type=jnp.float32
        ).astype(jnp.bfloat16)
        attended_flat = attended.reshape(tokens_here, H * V_DIM)
        middle = inputs + product(attended_flat, output_full)
        normed_mix, unit_mix, factor_mix = norm_forward(middle, gain_mixer)
        hidden_mix = normed_mix.astype(jnp.bfloat16)
        logits = product(hidden_mix, router_full)
        route_rows = routes[batch_index, 0]
        picker = (route_rows[..., None] == jnp.arange(experts_total, dtype=jnp.int32)).astype(
            jnp.float32
        )
        chosen = jnp.sum(picker * logits[:, None, :], axis=-1)
        softened = jax.nn.softmax(chosen, axis=-1)
        gates = softened * valid[:, None]
        gathered_rows = lax.all_gather(hidden_mix, "expert", axis=0, tiled=True)
        shared_gate_in = product(gathered_rows, share_gate)
        shared_up_in = product(gathered_rows, share_up)
        shared_act, shared_slope = silu_pair(shared_gate_in)
        shared_hidden = (shared_act * shared_up_in).astype(jnp.bfloat16)
        shared_out = lax.psum_scatter(
            product(shared_hidden, share_down).astype(jnp.bfloat16),
            "expert",
            scatter_dimension=0,
            tiled=True,
        ).astype(jnp.float32)
        flat_slots = slot_index(route_rows, experts_total, capacity)
        slot_list = flat_slots.reshape(-1)
        masked = hidden_mix * valid[:, None].astype(jnp.bfloat16)
        outgoing_rows = (
            jnp.zeros((experts_total * capacity, width), jnp.bfloat16)
            .at[slot_list]
            .set(jnp.repeat(masked, TOP, axis=0))
        )
        outgoing_rows = outgoing_rows.reshape(experts_total, 1, capacity, width)
        received = lax.all_to_all(outgoing_rows, "expert", split_axis=0, concat_axis=1, tiled=True)
        slots_here = received.shape[2]
        stacked_rows = received.reshape(EXP_DEV, groups * slots_here, width)
        hidden_part = expert_hidden(stacked_rows, gate_full, up_full)[4]
        result_rows = jnp.einsum(
            "erf,efd->erd", hidden_part, down_full, preferred_element_type=jnp.float32
        ).astype(jnp.bfloat16)
        result_rows = result_rows.reshape(EXP_DEV, groups, slots_here, width)
        returned = lax.all_to_all(result_rows, "expert", split_axis=1, concat_axis=0, tiled=True)
        picked = returned.reshape(experts_total * capacity, width)[flat_slots].astype(jnp.float32)
        routed_out = jnp.sum(gates[..., None] * picked, axis=1)
        outputs.append(valid[:, None] * (middle + shared_out + routed_out))
        grad_out = out_cotangent[batch_index, 0].astype(jnp.float32) * valid[:, None]
        grad_low = grad_out.astype(jnp.bfloat16)
        grad_rows = lax.all_gather(grad_low, "expert", axis=0, tiled=True)
        grad_shared_down = product_lead(shared_hidden, grad_rows)
        grad_shared_hidden = product_trail(grad_rows, share_down)
        grad_shared_gate_in = (grad_shared_hidden * shared_up_in * shared_slope).astype(
            jnp.bfloat16
        )
        grad_shared_up_in = (grad_shared_hidden * shared_act).astype(jnp.bfloat16)
        grad_shared_gate = product_lead(gathered_rows, grad_shared_gate_in)
        grad_shared_up = product_lead(gathered_rows, grad_shared_up_in)
        shared_input_part = product_trail(grad_shared_gate_in, share_gate) + product_trail(
            grad_shared_up_in, share_up
        )
        grad_mix = lax.psum_scatter(
            shared_input_part.astype(jnp.bfloat16), "expert", scatter_dimension=0, tiled=True
        ).astype(jnp.float32)
        grad_gates = jnp.sum(grad_out[:, None, :] * picked, axis=-1)
        grad_picked = (gates[..., None] * grad_out[:, None, :]).astype(jnp.bfloat16)
        grad_outgoing = (
            jnp.zeros((experts_total * capacity, width), jnp.bfloat16)
            .at[slot_list]
            .set(grad_picked.reshape(tokens_here * TOP, width))
        )
        grad_outgoing = grad_outgoing.reshape(experts_total, 1, capacity, width)
        grad_received = lax.all_to_all(
            grad_outgoing, "expert", split_axis=0, concat_axis=1, tiled=True
        )
        stacked_rows = received.reshape(EXP_DEV, groups * capacity, width)
        grad_stacked = grad_received.reshape(EXP_DEV, groups * capacity, width)
        gate_in, up_in, activated, slope, hidden_part = expert_hidden(
            stacked_rows, gate_full, up_full
        )
        grad_down_w = jnp.einsum(
            "erf,erd->efd", hidden_part, grad_stacked, preferred_element_type=jnp.float32
        )
        grad_hidden = jnp.einsum(
            "erd,efd->erf", grad_stacked, down_full, preferred_element_type=jnp.float32
        )
        grad_gate_in = (grad_hidden * up_in * slope).astype(jnp.bfloat16)
        grad_up_in = (grad_hidden * activated).astype(jnp.bfloat16)
        grad_gate_w = jnp.einsum(
            "erd,erf->edf", stacked_rows, grad_gate_in, preferred_element_type=jnp.float32
        )
        grad_up_w = jnp.einsum(
            "erd,erf->edf", stacked_rows, grad_up_in, preferred_element_type=jnp.float32
        )
        grad_back = jnp.einsum(
            "erf,edf->erd", grad_gate_in, gate_full, preferred_element_type=jnp.float32
        )
        grad_back = grad_back + jnp.einsum(
            "erf,edf->erd", grad_up_in, up_full, preferred_element_type=jnp.float32
        )
        grad_back = grad_back.astype(jnp.bfloat16).reshape(EXP_DEV, groups, capacity, width)
        grad_returned = lax.all_to_all(grad_back, "expert", split_axis=1, concat_axis=0, tiled=True)
        grad_copies = grad_returned.reshape(experts_total * capacity, width)[flat_slots].astype(
            jnp.float32
        )
        grad_mix = grad_mix + jnp.sum(grad_copies, axis=1) * valid[:, None]
        masked_grad = grad_gates * valid[:, None]
        grad_chosen = softened * (
            masked_grad - jnp.sum(masked_grad * softened, axis=-1, keepdims=True)
        )
        grad_logits = jnp.sum(picker * grad_chosen[..., None], axis=1).astype(jnp.bfloat16)
        grad_mix = grad_mix + product_trail(grad_logits, router_full)
        grad_router = product_lead(hidden_mix, grad_logits)
        grad_middle_norm, grad_gain_mixer = norm_backward(
            grad_mix, unit_mix, factor_mix, gain_mixer
        )
        grad_middle = grad_out + grad_middle_norm
        grad_attn_out = grad_middle.astype(jnp.bfloat16)
        grad_output_w = product_lead(attended_flat, grad_attn_out)
        grad_attended = (
            product_trail(grad_attn_out, output_full)
            .astype(jnp.bfloat16)
            .reshape(tokens_here, H, V_DIM)
        )
        scores = compute_scores(query_nope, query_rope, key_nope, all_rope, allowed, scale_factor)
        probs = jnp.exp(scores - log_total)
        probs_low = probs.astype(jnp.bfloat16)
        grad_probs = jnp.einsum(
            "thd,shd->hts", grad_attended, key_values, preferred_element_type=jnp.float32
        )
        inner_sum = jnp.sum(grad_probs * probs, axis=-1, keepdims=True)
        grad_scores = (probs * (grad_probs - inner_sum)).astype(jnp.bfloat16)
        grad_query_nope = (
            jnp.einsum("hts,shd->thd", grad_scores, key_nope, preferred_element_type=jnp.float32)
            * scale_factor
        )
        grad_query_rope = (
            jnp.einsum("hts,sd->thd", grad_scores, all_rope, preferred_element_type=jnp.float32)
            * scale_factor
        )
        grad_key_nope = (
            jnp.einsum("hts,thd->shd", grad_scores, query_nope, preferred_element_type=jnp.float32)
            * scale_factor
        )
        grad_key_rope = (
            jnp.einsum("hts,thd->sd", grad_scores, query_rope, preferred_element_type=jnp.float32)
            * scale_factor
        )
        grad_values = jnp.einsum(
            "hts,thd->shd", probs_low, grad_attended, preferred_element_type=jnp.float32
        )
        grad_expanded_part = jnp.concatenate([grad_key_nope, grad_values], axis=-1).reshape(
            seq_total, H * (QK_NOPE + V_DIM)
        )
        grad_expanded, grad_rope_own = (
            lax.psum_scatter(
                grad_expanded_part.astype(jnp.bfloat16), "expert", scatter_dimension=0, tiled=True
            ).astype(jnp.float32),
            lax.psum_scatter(
                grad_key_rope.astype(jnp.bfloat16), "expert", scatter_dimension=0, tiled=True
            ).astype(jnp.float32),
        )
        grad_expand_w = precise_lead(latent.astype(jnp.float32), grad_expanded)
        grad_latent = precise_trail(grad_expanded, expand_wide)
        grad_latent_in, grad_gain_latent = norm_backward(
            grad_latent, unit_latent, factor_latent, gain_latent
        )
        grad_latent_raw = jnp.concatenate(
            [grad_latent_in, unrotate(grad_rope_own, cosine, sine_table)], axis=-1
        ).astype(jnp.bfloat16)
        grad_query_raw = jnp.concatenate(
            [
                grad_query_nope,
                unrotate(grad_query_rope, cosine[:, None, :], sine_table[:, None, :]),
            ],
            axis=-1,
        )
        grad_query_raw = grad_query_raw.reshape(tokens_here, H * (QK_NOPE + ROPE)).astype(
            jnp.bfloat16
        )
        grad_query_w = product_lead(hidden_attn, grad_query_raw)
        grad_latent_w = product_lead(hidden_attn, grad_latent_raw)
        grad_hidden_attn = product_trail(grad_query_raw, query_full) + product_trail(
            grad_latent_raw, latent_full
        )
        grad_input_norm, grad_gain_attn = norm_backward(
            grad_hidden_attn, unit_attn, factor_attn, gain_attn
        )
        input_grads.append(grad_middle + grad_input_norm)
        dense_fresh = (
            grad_gain_attn,
            grad_gain_latent,
            grad_gain_mixer,
            grad_query_w,
            grad_latent_w,
            grad_expand_w,
            grad_output_w,
            grad_router,
        )
        owned_fresh = (
            grad_gate_w,
            grad_up_w,
            grad_down_w,
            grad_shared_gate,
            grad_shared_up,
            grad_shared_down,
        )
        dense_local = tuple((running + fresh for running, fresh in zip(dense_local, dense_fresh)))
        owned_local = tuple((running + fresh for running, fresh in zip(owned_local, owned_fresh)))
        flush = batch_index == batches - 1
        if flush:
            dense_part = lax.psum_scatter(
                dense_local, ("dp", "expert"), scatter_dimension=0, tiled=True
            )
            owned_part = (
                lax.psum_scatter(
                    owned_local[0].astype(jnp.bfloat16), "dp", scatter_dimension=1, tiled=True
                ).astype(jnp.float32),
                lax.psum_scatter(
                    owned_local[1].astype(jnp.bfloat16), "dp", scatter_dimension=1, tiled=True
                ).astype(jnp.float32),
                lax.psum_scatter(
                    owned_local[2].astype(jnp.bfloat16), "dp", scatter_dimension=1, tiled=True
                ).astype(jnp.float32),
                lax.psum_scatter(
                    owned_local[3].astype(jnp.bfloat16), "dp", scatter_dimension=0, tiled=True
                ).astype(jnp.float32),
                lax.psum_scatter(
                    owned_local[4].astype(jnp.bfloat16), "dp", scatter_dimension=0, tiled=True
                ).astype(jnp.float32),
                lax.psum_scatter(
                    owned_local[5].astype(jnp.bfloat16), "dp", scatter_dimension=1, tiled=True
                ).astype(jnp.float32),
            )
            dense_total = dense_part
            owned_total = owned_part
            dense_local = tuple((jnp.zeros_like(running) for running in dense_local))
            owned_local = tuple((jnp.zeros_like(running) for running in owned_local))
    result_out = jnp.stack(outputs)[:, None]
    result_grad = jnp.stack(input_grads)[:, None]
    return (
        result_out,
        result_grad,
        dense_total[0],
        dense_total[3],
        dense_total[4],
        dense_total[1],
        dense_total[5],
        dense_total[6],
        dense_total[2],
        dense_total[7],
        owned_total[0],
        owned_total[1],
        owned_total[2],
        owned_total[3],
        owned_total[4],
        owned_total[5],
    )


def solution(mesh):
    return jax.shard_map(
        per_device,
        mesh=mesh,
        in_specs=(
            P(None, "dp", "expert", None),
            P(None, "dp", "expert", None),
            P(None, "dp"),
            P(None, "dp", "expert", None),
            P(("dp", "expert")),
            P(("dp", "expert"), None),
            P(("dp", "expert"), None),
            P(("dp", "expert")),
            P(("dp", "expert"), None),
            P(("dp", "expert"), None),
            P(("dp", "expert")),
            P(("dp", "expert"), None),
            P("expert", "dp", None),
            P("expert", "dp", None),
            P("expert", "dp", None),
            P("dp", "expert"),
            P("dp", "expert"),
            P("expert", "dp"),
        ),
        out_specs=(
            P(None, "dp", "expert", None),
            P(None, "dp", "expert", None),
            P(("dp", "expert")),
            P(("dp", "expert"), None),
            P(("dp", "expert"), None),
            P(("dp", "expert")),
            P(("dp", "expert"), None),
            P(("dp", "expert"), None),
            P(("dp", "expert")),
            P(("dp", "expert"), None),
            P("expert", "dp", None),
            P("expert", "dp", None),
            P("expert", "dp", None),
            P("dp", "expert"),
            P("dp", "expert"),
            P("expert", "dp"),
        ),
        check_vma=False,
    )
```

profile of v0, /device:TPU:0, one launch (start us, length us, event | category | flops | bytes accessed | tf_op | source)
XLA Modules:
  0.0 2852.9 jit_solution(9623149417888088339)
XLA Ops:
  11.3 42.2 %all-reduce.7 = (bf16[2048]{0:T(1024)(128)(2,1)S(1)}, bf16[512]{0:T(512)(128)(2,1)S(1)}, bf16[2048]{0:T(1024)(128)(2,1)S(1)}) all-reduce(bf16[2048]{0:T(1024)(128)(2,1)S(1)} %dynamic-update-slice, bf16[512]{0:T(512)(128)(2,1)S(1)} %dynamic-update-slice.1, ...), channel_id=1, replica_groups=mesh['dp'=2,'expert'=16] {'dp','expert'}, use_global_device_ids=true, to_apply=%add | all-reduce | flops 4608 | bytes 18432
  74.5 61.2 %all-gather.17.cloned.1.call-done = bf16[512,4096]{1,0:T(8,128)(2,1)} async-done(((bf16[16,4096]{1,0:T(8,128)(2,1)}), bf16[512,4096]{1,0:T(8,128)(2,1)}) %all-gather.17.cloned.1.call-update) | async-done | bytes 4194320 | tf_op jit(solution)/shard_map/all_gather | solution.py:161
  226.3 66.4 %all-gather.33.cloned.1.call-done = bf16[1024,4096]{1,0:T(8,128)(2,1)} async-done(((bf16[64,4096]{1,0:T(8,128)(2,1)}), bf16[1024,4096]{1,0:T(8,128)(2,1)}) %all-gather.33.cloned.1.call-update) | async-done | bytes 8388624 | tf_op jit(solution)/shard_map/all_gather | solution.py:222
  315.4 74.3 %all-gather.21.cloned.1.call-done = bf16[2048,3072]{1,0:T(8,128)(2,1)} async-done(((bf16[64,3072]{1,0:T(8,128)(2,1)}), bf16[2048,3072]{1,0:T(8,128)(2,1)}) %all-gather.21.cloned.1.call-update) | async-done | bytes 12582928 | tf_op jit(solution)/shard_map/all_gather | solution.py:159
  436.2 31.9 %all-gather.23.cloned.1.call-done = bf16[2048,2048]{1,0:T(8,128)(2,1)} async-done(((bf16[64,2048]{1,0:T(8,128)(2,1)}), bf16[2048,2048]{1,0:T(8,128)(2,1)}) %all-gather.23.cloned.1.call-update) | async-done | bytes 8388624 | tf_op jit(solution)/shard_map/all_gather | solution.py:162
  492.4 40.2 %all-gather = bf16[32,64,16]{1,2,0:T(8,128)(2,1)S(1)} all-gather(bf16[1,64,16]{1,2,0:T(8,128)(2,1)S(1)} %bitcast.486), channel_id=1, replica_groups=mesh['dp'=2,'expert'=16] {'dp','expert'}, dimensions={0}, use_global_device_ids=true | all-gather | bytes 67584 | tf_op jit(solution)/shard_map/all_gather | solution.py:163
  698.9 56.7 %all-gather.25.cloned.1.call-done = bf16[1024,2048]{1,0:T(8,128)(2,1)} async-done(((bf16[64,2048]{1,0:T(8,128)(2,1)}), bf16[1024,2048]{1,0:T(8,128)(2,1)}) %all-gather.25.cloned.1.call-update) | async-done | bytes 4194320 | tf_op jit(solution)/shard_map/all_gather | solution.py:252
  761.1 45.8 %all-gather.37.cloned.1.call-done = bf16[1024,2048]{1,0:T(8,128)(2,1)} async-done(((bf16[64,2048]{1,0:T(8,128)(2,1)}), bf16[1024,2048]{1,0:T(8,128)(2,1)}) %all-gather.37.cloned.1.call-update) | async-done | bytes 4194320 | tf_op jit(solution)/shard_map/all_gather | solution.py:286
  821.5 59.8 %all-gather.31.cloned.1.call-done = bf16[1,1408,2048]{2,1,0:T(8,128)(2,1)} async-done(((bf16[1,704,2048]{2,1,0:T(8,128)(2,1)}), bf16[1,1408,2048]{2,1,0:T(8,128)(2,1)}) %all-gather.31.cloned.1.call-update) | async-done | bytes 5767184 | tf_op jit(solution)/shard_map/all_gather | solution.py:179
  889.2 68.0 %all-gather.27.cloned.1.call-done = bf16[1,2048,1408]{2,1,0:T(8,128)(2,1)} async-done(((bf16[1,1024,1408]{2,1,0:T(8,128)(2,1)}), bf16[1,2048,1408]{2,1,0:T(8,128)(2,1)}) %all-gather.27.cloned.1.call-update) | async-done | bytes 5767184 | tf_op jit(solution)/shard_map/all_gather | solution.py:177
  1098.7 27.2 all-to-all-start.7
  1214.3 29.5 %all-to-all-done.5 = bf16[1,16,30,2048]{3,2,0,1:T(8,128)(2,1)} async-done(((bf16[1,16,30,2048]{3,2,0,1:T(8,128)(2,1)}), bf16[1,16,30,2048]{3,2,0,1:T(8,128)(2,1)}, u32[]{:S(2)}, u32[]{:S(2)}) %all-to-all-start.5) | async-done | bytes 1966112 | tf_op jit(solution)/shard_map/all_to_all | solution.py:338
  1266.1 70.8 %reduce-scatter.26.cloned.1.call-done = bf16[64,2048]{1,0:T(8,128)(2,1)} async-done(((bf16[1024,2048]{1,0:T(8,128)(2,1)}), bf16[64,2048]{1,0:T(8,128)(2,1)}) %reduce-scatter.26.cloned.1.call-update) | async-done | bytes 262160 | tf_op jit(solution)/shard_map/reduce_scatter | solution.py:257
  1485.0 106.7 %reduce-scatter.58.cloned.1.call-done = bf16[64,4096]{1,0:T(8,128)(2,1)} async-done(((bf16[1024,4096]{1,0:T(8,128)(2,1)}), bf16[64,4096]{1,0:T(8,128)(2,1)}) %reduce-scatter.58.cloned.1.call-update) | async-done | bytes 524304
  1596.1 104.2 %reduce-scatter.60.cloned.1.call-done = bf16[64,4096]{1,0:T(8,128)(2,1)} async-done(((bf16[1024,4096]{1,0:T(8,128)(2,1)}), bf16[64,4096]{1,0:T(8,128)(2,1)}) %reduce-scatter.60.cloned.1.call-update) | async-done | bytes 524304
  1771.4 66.2 %reduce-scatter.62.cloned.1.call-done = f32[64,16]{1,0:T(8,128)} async-done(((f32[2048,16]{1,0:T(8,128)}), f32[64,16]{1,0:T(8,128)}) %reduce-scatter.62.cloned.1.call-update) | async-done | bytes 4112
  1896.3 70.6 %reduce-scatter.50.cloned.1.call-done = bf16[1,704,2048]{2,1,0:T(8,128)(2,1)} async-done(((bf16[1,1408,2048]{2,1,0:T(8,128)(2,1)}), bf16[1,704,2048]{2,1,0:T(8,128)(2,1)}) %reduce-scatter.50.cloned.1.call-update) | async-done | bytes 2883600 | tf_op jit(solution)/shard_map/reduce_scatter | solution.py:458
  1972.0 69.1 %reduce-scatter.46.cloned.1.call-done = bf16[1,1024,1408]{2,1,0:T(8,128)(2,1)} async-done(((bf16[1,2048,1408]{2,1,0:T(8,128)(2,1)}), bf16[1,1024,1408]{2,1,0:T(8,128)(2,1)}) %reduce-scatter.46.cloned.1.call-update) | async-done | bytes 2883600 | tf_op jit(solution)/shard_map/reduce_scatter | solution.py:452
  2045.9 69.0 %reduce-scatter.48.cloned.1.call-done = bf16[1,1024,1408]{2,1,0:T(8,128)(2,1)} async-done(((bf16[1,2048,1408]{2,1,0:T(8,128)(2,1)}), bf16[1,1024,1408]{2,1,0:T(8,128)(2,1)}) %reduce-scatter.48.cloned.1.call-update) | async-done | bytes 2883600 | tf_op jit(solution)/shard_map/reduce_scatter | solution.py:455
  2139.0 40.7 %all-reduce.6 = (f32[2048]{0:T(1024)S(1)}, f32[512]{0:T(512)S(1)}, f32[2048]{0:T(1024)S(1)}) all-reduce(f32[2048]{0:T(1024)S(1)} %add.442, f32[512]{0:T(512)S(1)} %copy-done.174, f32[2048]{0:T(1024)S(1)} %copy-done.156), channel_id=10, replica_groups=mesh['dp'=2,'expert'=16] {'dp','expert'}, use_global_device_ids=true, to_apply=%region_54.55.clone | all-reduce | flops 4608 | bytes 36864
  2184.1 77.1 %reduce-scatter.40.cloned.1.call-done = f32[64,576]{1,0:T(8,128)} async-done(((f32[2048,576]{1,0:T(8,128)}), f32[64,576]{1,0:T(8,128)}) %reduce-scatter.40.cloned.1.call-update) | async-done | bytes 147472 | tf_op jit(solution)/shard_map/reduce_scatter | solution.py:448
  2261.3 147.6 %reduce-scatter.42.cloned.1.call-done = f32[16,4096]{1,0:T(8,128)} async-done(((f32[512,4096]{1,0:T(8,128)}), f32[16,4096]{1,0:T(8,128)}) %reduce-scatter.42.cloned.1.call-update) | async-done | bytes 262160 | tf_op jit(solution)/shard_map/reduce_scatter | solution.py:448
  2408.8 180.4 %reduce-scatter.44.cloned.1.call-done = f32[64,2048]{1,0:T(8,128)} async-done(((f32[2048,2048]{1,0:T(8,128)}), f32[64,2048]{1,0:T(8,128)}) %reduce-scatter.44.cloned.1.call-update) | async-done | bytes 524304 | tf_op jit(solution)/shard_map/reduce_scatter | solution.py:448
  2589.2 256.9 %reduce-scatter.38.cloned.1.call-done = f32[64,3072]{1,0:T(8,128)} async-done(((f32[2048,3072]{1,0:T(8,128)}), f32[64,3072]{1,0:T(8,128)}) %reduce-scatter.38.cloned.1.call-update) | async-done | bytes 786448 | tf_op jit(solution)/shard_map/reduce_scatter | solution.py:448
  (780 shorter events, 973.1 us)
Async XLA Ops:
  144.4 245.3 %all-gather.21.cloned.1.call-start = ((), (), s32[]{:S(2)}) async-start(), calls=%async_computation.30 | async-start | bytes 12976128 | tf_op jit(solution)/shard_map/all_gather | solution.py:159
  145.0 323.2 %all-gather.23.cloned.1.call-start = ((), (), s32[]{:S(2)}) async-start(), calls=%async_computation.31 | async-start | bytes 8650752 | tf_op jit(solution)/shard_map/all_gather | solution.py:162
  145.5 479.2 %all-gather.35.cloned.1.call-start = ((), (), s32[]{:S(2)}) async-start(), calls=%async_computation.38 | async-start | bytes 4456448 | tf_op jit(solution)/shard_map/all_gather | solution.py:252
  488.7 266.8 %all-gather.25.cloned.1.call-start = ((), (), s32[]{:S(2)}) async-start(), calls=%async_computation.32 | async-start | bytes 4456448 | tf_op jit(solution)/shard_map/all_gather | solution.py:252
  489.3 317.5 %all-gather.37.cloned.1.call-start = ((), (), s32[]{:S(2)}) async-start(), calls=%async_computation.40 | async-start | bytes 4456448 | tf_op jit(solution)/shard_map/all_gather | solution.py:286
  490.1 391.2 %all-gather.31.cloned.1.call-start = ((), (), s32[]{:S(2)}) async-start(), calls=%async_computation.36 | async-start | bytes 8650752 | tf_op jit(solution)/shard_map/all_gather | solution.py:179
  551.6 405.6 %all-gather.27.cloned.1.call-start = ((), (), s32[]{:S(2)}) async-start(), calls=%async_computation.34 | async-start | bytes 8650752 | tf_op jit(solution)/shard_map/all_gather | solution.py:177
  624.4 638.3 %reduce-scatter.34.cloned.1.call-start = ((), (), s32[]{:S(2)}) async-start(), calls=%async_computation.44 | async-start | bytes 4456448 | tf_op jit(solution)/shard_map/reduce_scatter | solution.py:298
  815.5 448.6 %reduce-scatter.30.cloned.1.call-start = ((), (), s32[]{:S(2)}) async-start(), calls=%async_computation.41 | async-start | bytes 4456448 | tf_op jit(solution)/shard_map/reduce_scatter | solution.py:298
  1125.9 211.0 %reduce-scatter.26.cloned.1.call-start = ((), (), s32[]{:S(2)}) async-start(), calls=%async_computation.33 | async-start | bytes 4456448 | tf_op jit(solution)/shard_map/reduce_scatter | solution.py:257
  1185.9 292.5 %reduce-scatter.32.cloned.1.call-start = ((), (), s32[]{:S(2)}) async-start(), calls=%async_computation.42 | async-start | bytes 278528 | tf_op jit(solution)/shard_map/reduce_scatter | solution.py:395
  1377.1 214.6 %reduce-scatter.58.cloned.1.call-start = ((), (), s32[]{:S(2)}) async-start(), calls=%async_computation.56 | async-start | bytes 8912896
  1396.8 303.5 %reduce-scatter.60.cloned.1.call-start = ((), (), s32[]{:S(2)}) async-start(), calls=%async_computation.57 | async-start | bytes 8912896
  1424.6 413.0 %reduce-scatter.62.cloned.1.call-start = ((), (), s32[]{:S(2)}) async-start(), calls=%async_computation.58 | async-start | bytes 1081344
  1427.2 426.4 %reduce-scatter.56.cloned.1.call-start = ((), (), s32[]{:S(2)}) async-start(), calls=%async_computation.55 | async-start | bytes 1081344 | tf_op jit(solution)/shard_map/reduce_scatter | solution.py:467
  1432.6 440.5 %reduce-scatter.52.cloned.1.call-start = ((), (), s32[]{:S(2)}) async-start(), calls=%async_computation.53 | async-start | bytes 1081344 | tf_op jit(solution)/shard_map/reduce_scatter | solution.py:461
  1438.0 454.7 %reduce-scatter.54.cloned.1.call-start = ((), (), s32[]{:S(2)}) async-start(), calls=%async_computation.54 | async-start | bytes 1081344 | tf_op jit(solution)/shard_map/reduce_scatter | solution.py:464
  1443.5 523.4 %reduce-scatter.50.cloned.1.call-start = ((), (), s32[]{:S(2)}) async-start(), calls=%async_computation.52 | async-start | bytes 8650752 | tf_op jit(solution)/shard_map/reduce_scatter | solution.py:458
  1454.1 587.1 %reduce-scatter.46.cloned.1.call-start = ((), (), s32[]{:S(2)}) async-start(), calls=%async_computation.50 | async-start | bytes 8650752 | tf_op jit(solution)/shard_map/reduce_scatter | solution.py:452
  1466.2 648.7 %reduce-scatter.48.cloned.1.call-start = ((), (), s32[]{:S(2)}) async-start(), calls=%async_computation.51 | async-start | bytes 8650752 | tf_op jit(solution)/shard_map/reduce_scatter | solution.py:455
  1478.3 783.0 %reduce-scatter.40.cloned.1.call-start = ((), (), s32[]{:S(2)}) async-start(), calls=%async_computation.47 | async-start | bytes 5406720 | tf_op jit(solution)/shard_map/reduce_scatter | solution.py:448
  1709.0 699.8 %reduce-scatter.42.cloned.1.call-start = ((), (), s32[]{:S(2)}) async-start(), calls=%async_computation.48 | async-start | bytes 8650752 | tf_op jit(solution)/shard_map/reduce_scatter | solution.py:448
  1716.1 873.1 %reduce-scatter.44.cloned.1.call-start = ((), (), s32[]{:S(2)}) async-start(), calls=%async_computation.49 | async-start | bytes 17301504 | tf_op jit(solution)/shard_map/reduce_scatter | solution.py:448
  1727.9 1118.2 %reduce-scatter.38.cloned.1.call-start = ((), (), s32[]{:S(2)}) async-start(), calls=%async_computation.46 | async-start | bytes 25952256 | tf_op jit(solution)/shard_map/reduce_scatter | solution.py:448
  (227 other events, 9405.9 us)
Sparse Core Ops, SparseCore 0:
  74.6 61.0 all-gather.16
  139.7 76.6 all-gather.18
  219.0 73.5 all-gather.32
  295.4 94.2 all-gather.20
  392.4 75.7 all-gather.22
  538.8 75.6 all-gather.38
  616.1 75.4 all-gather.28
  693.6 61.9 all-gather.24
  808.2 72.9 all-gather.30
  882.8 74.4 all-gather.26
  961.0 99.3 reduce-scatter.33
  1064.6 89.0 reduce-scatter.29
  1157.4 104.2 reduce-scatter.27
  1265.9 70.9 reduce-scatter.25
  1487.9 103.7 reduce-scatter.57
  1595.8 104.4 reduce-scatter.59
  1703.1 134.5 reduce-scatter.61
  1895.5 71.3 reduce-scatter.49
  1969.7 71.3 reduce-scatter.45
  2043.4 71.3 reduce-scatter.47
  2117.8 143.4 reduce-scatter.39
  2264.1 144.6 reduce-scatter.41
  2411.8 177.3 reduce-scatter.43
  2597.4 248.6 reduce-scatter.37
  (8 shorter events, 314.3 us)
where the time goes:
time: 2860 us; the launch traced here: 2850 us
  waiting for transfers between devices  1910 us (67%)
  matrix products  345 us (12%)
  blocking collectives  199 us (7%)
  local copies, waits for them, and re-layouts  191 us (7%)
  other arithmetic  94 us (3%)
  starting transfers between devices  93.7 us (3%)
    reduce_scatter x4, waiting for transfers between devices, per_device(): lax.psum_scatter(dense_local, ('dp', 'expert'), scatter_dimension=0, tile...  662 us
    unnamed x35, waiting for transfers between devices  283 us
    all_gather x2, waiting for transfers between devices, per_device(): lax.all_gather(outgoing[0], 'expert', axis=0, tiled=True)  88.3 us
    unnamed x2, blocking collectives  83 us
    unnamed x440, local copies, waits for them, and re-layouts  75.6 us
    all_gather x1, waiting for transfers between devices, per_device(): lax.all_gather(query_weight, ('dp', 'expert'), axis=0, tiled=True)  74.3 us
    reduce_scatter x2, waiting for transfers between devices, per_device(): lax.psum_scatter(product(shared_hidden, share_down).astype(jnp.bfloat16),...  70.8 us
    reduce_scatter x1, waiting for transfers between devices, per_device(): lax.psum_scatter(owned_local[2].astype(jnp.bfloat16), 'dp', scatter_dimen...  70.6 us
  transfers between devices with their start and end apart: 40, of which 32 were waited for; matrix products, arithmetic and copies ran while one was open for 19% of the time, Pallas kernels for 0%

commit v1 on v0

v1 whole, which is shorter than its diff:
```python
import functools
import jax
import jax.numpy as jnp
from jax import lax
from jax.experimental import pallas as pl
from jax.experimental.pallas import tpu as pltpu
from jax.sharding import PartitionSpec as P

MESH = pl.DeviceIdType.MESH
NZ = 4


def place():
    me = lax.axis_index("expert")
    z = me // 4
    x = (me // 2) % 2
    c = me % 2
    return me, z, x, c, me + 1 - 2 * c, me + 2 - 4 * x


def enter(me, z, core, side):
    barrier = pltpu.get_barrier_semaphore()
    for other in (core, side):
        pl.semaphore_signal(barrier, inc=1, device_id={"expert": other}, device_id_type=MESH)

    @pl.when(z < NZ - 1)
    def _():
        pl.semaphore_signal(barrier, inc=1, device_id={"expert": me + 4}, device_id_type=MESH)

    @pl.when(z > 0)
    def _():
        pl.semaphore_signal(barrier, inc=1, device_id={"expert": me - 4}, device_id_type=MESH)

    pl.semaphore_wait(barrier, 2 + (z < NZ - 1).astype(jnp.int32) + (z > 0).astype(jnp.int32))


def gather_kernel(chunks, x_ref, o_ref, own_sem, up_s, up_r, dn_s, dn_r, xs, xr, cs, cr):
    me, z, x, c, core, side = place()
    rows = x_ref.shape[0] // chunks

    def part(ref, k):
        return ref.at[pl.ds(k * rows, rows)]

    def copy(block, k, src, send, recv, to):
        return pltpu.make_async_remote_copy(
            src_ref=part(x_ref if src is None else o_ref.at[src], k),
            dst_ref=part(o_ref.at[block], k),
            send_sem=send, recv_sem=recv,
            device_id={"expert": to}, device_id_type=MESH,
        )

    def up(k, s, src=None):
        b = me - 4 * s
        return copy(b, k, src, up_s.at[s, k], up_r.at[s, k], me + 4)

    def down(k, s, src=None):
        b = me + 4 * s
        return copy(b, k, src, dn_s.at[s, k], dn_r.at[s, k], me - 4)

    def across(k, slot, block, src=None):
        return copy(block, k, src, xs.at[slot, k], xr.at[slot, k], side)

    def over(k, slot, block, src=None):
        return copy(block, k, src, cs.at[slot, k], cr.at[slot, k], core)

    enter(me, z, core, side)
    own = pltpu.make_async_copy(x_ref, o_ref.at[me], own_sem)
    own.start()
    for k in range(chunks):
        across(k, 0, me).start()

        @pl.when(z < NZ - 1)
        def _():
            up(k, 0).start()

        @pl.when(z > 0)
        def _():
            down(k, 0).start()

        over(k, 0, me).start()

    def line(k, s):
        @pl.when(z >= s)
        def _():
            b = me - 4 * s
            up_in(k, s).wait_recv()
            across(k, s, b, b).start()

            @pl.when(z < NZ - 1)
            def _():
                up(k, s, b).start()

            over(k, s, b, b).start()

        @pl.when(z + s <= NZ - 1)
        def _():
            b = me + 4 * s
            dn_in(k, s).wait_recv()
            across(k, 3 + s, b, b).start()

            @pl.when(z > 0)
            def _():
                down(k, s, b).start()

            over(k, 3 + s, b, b).start()

    def up_in(k, s):
        b = me - 4 * s
        return copy(b, k, b, up_s.at[s - 1, k], up_r.at[s - 1, k], side)

    def dn_in(k, s):
        b = me + 4 * s
        return copy(b, k, b, dn_s.at[s - 1, k], dn_r.at[s - 1, k], side)

    def side_block(slot):
        return side - 4 * slot if slot <= 3 else side + 4 * (slot - 3)

    def core_block(slot):
        if slot < 7:
            return core - 4 * slot if slot <= 3 else core + 4 * (slot - 3)
        other = core + 2 - 4 * x
        slot = slot - 7
        return other - 4 * slot if slot <= 3 else other + 4 * (slot - 3)

    def has(slot):
        slot = slot % 7
        if slot == 0:
            return z >= 0
        return z >= slot if slot <= 3 else z + (slot - 3) <= NZ - 1

    def from_side(k, slot):
        @pl.when(has(slot))
        def _():
            b = side_block(slot)
            across(k, slot, b, b).wait_recv()
            over(k, 7 + slot, b, b).start()

    for s in range(1, NZ):
        for k in range(chunks):
            line(k, s)
        for k in range(chunks):
            for slot in ((0,) if s == 1 else (s - 1, s + 2)):
                from_side(k, slot)
    for k in range(chunks):
        for slot in (NZ - 1, NZ + 2):
            from_side(k, slot)
    own.wait()
    for k in range(chunks):
        for slot in range(14):
            @pl.when(has(slot))
            def _():
                b = core_block(slot)
                over(k, slot, b, b).wait_recv()
                over(k, slot, b, b).wait_send()
        for slot in range(7):
            @pl.when(has(slot))
            def _():
                across(k, slot, me).wait_send()
        for s in range(NZ - 1):
            @pl.when((z >= s) & (z < NZ - 1))
            def _():
                up(k, s).wait_send()

            @pl.when((z + s <= NZ - 1) & (z > 0))
            def _():
                down(k, s).wait_send()


def gather16(v, cid, chunks=2):
    rows, width = v.shape
    dma = pltpu.SemaphoreType.DMA
    return pl.pallas_call(
        functools.partial(gather_kernel, chunks),
        out_shape=jax.ShapeDtypeStruct((16, rows, width), v.dtype),
        in_specs=[pl.BlockSpec(memory_space=pl.ANY)],
        out_specs=pl.BlockSpec(memory_space=pl.ANY),
        scratch_shapes=[
            dma, dma((4, chunks)), dma((4, chunks)), dma((4, chunks)), dma((4, chunks)),
            dma((7, chunks)), dma((7, chunks)), dma((14, chunks)), dma((14, chunks)),
        ],
        compiler_params=pltpu.CompilerParams(collective_id=cid, has_side_effects=True),
        cost_estimate=pl.CostEstimate(flops=0, bytes_accessed=150_000_000, transcendentals=0),
        name="gather16",
    )(v)


def order(z, i):
    a, b = (3, 2, 1, 0)[i], (3, 2, 0, 1)[i]
    return jnp.where(z == 0, a, jnp.where(z == 1, b, jnp.where(z == 2, 3 - b, 3 - a)))


def scatter_kernel(chunks, p_ref, o_ref, cbuf, own, xbuf, ubuf, dbuf,
                   ld, cs, cr, xs, xr, us, ur, ds_, dr):
    me, z, x, c, core, side = place()
    rows = o_ref.shape[0] // chunks
    f32 = jnp.float32

    def rng(k):
        return pl.ds(k * rows, rows)

    def over(i, j, k):
        b = 4 * order(z, i) + 2 * jnp.where(j == 0, 1 - x, x)
        return pltpu.make_async_remote_copy(
            src_ref=p_ref.at[b + 1 - c, rng(k)], dst_ref=cbuf.at[2 * i + j, rng(k)],
            send_sem=cs.at[2 * i + j, k], recv_sem=cr.at[2 * i + j, k],
            device_id={"expert": core}, device_id_type=MESH)

    def load(i, j):
        b = 4 * order(z, i) + 2 * jnp.where(j == 0, 1 - x, x)
        return pltpu.make_async_copy(p_ref.at[b + c], own.at[2 * i + j], ld.at[2 * i + j])

    def across(i, k):
        return pltpu.make_async_remote_copy(
            src_ref=own.at[2 * i, rng(k)], dst_ref=xbuf.at[i, rng(k)],
            send_sem=xs.at[i, k], recv_sem=xr.at[i, k],
            device_id={"expert": side}, device_id_type=MESH)

    def up(t, i, k):
        return pltpu.make_async_remote_copy(
            src_ref=own.at[2 * i + 1, rng(k)], dst_ref=ubuf.at[t, rng(k)],
            send_sem=us.at[t, k], recv_sem=ur.at[t, k],
            device_id={"expert": me + 4}, device_id_type=MESH)

    def down(t, i, k):
        return pltpu.make_async_remote_copy(
            src_ref=own.at[2 * i + 1, rng(k)], dst_ref=dbuf.at[t, rng(k)],
            send_sem=ds_.at[t, k], recv_sem=dr.at[t, k],
            device_id={"expert": me - 4}, device_id_type=MESH)

    enter(me, z, core, side)
    for i in range(NZ):
        for j in range(2):
            load(i, j).start()
            for k in range(chunks):
                over(i, j, k).start()

    def first(i):
        load(i, 0).wait()
        for k in range(chunks):
            over(i, 0, k).wait_recv()
            s = rng(k)
            own[2 * i, s] = (own[2 * i, s].astype(f32) + cbuf[2 * i, s].astype(f32)).astype(own.dtype)
            across(i, k).start()

    def second(i):
        t = order(z, i)
        load(i, 1).wait()
        for k in range(chunks):
            s = rng(k)
            over(i, 1, k).wait_recv()
            across(i, k).wait_recv()

            def base():
                return (own[2 * i + 1, s].astype(f32) + cbuf[2 * i + 1, s].astype(f32)
                        + xbuf[i, s].astype(f32))

            if i < NZ - 1:
                @pl.when(t > z)
                def _():
                    @pl.when(z > 0)
                    def _():
                        up(t, i, k).wait_recv()
                        own[2 * i + 1, s] = (base() + ubuf[t, s].astype(f32)).astype(own.dtype)

                    @pl.when(z == 0)
                    def _():
                        own[2 * i + 1, s] = base().astype(own.dtype)

                    up(t, i, k).start()

                @pl.when(t < z)
                def _():
                    @pl.when(z < NZ - 1)
                    def _():
                        down(t, i, k).wait_recv()
                        own[2 * i + 1, s] = (base() + dbuf[t, s].astype(f32)).astype(own.dtype)

                    @pl.when(z == NZ - 1)
                    def _():
                        own[2 * i + 1, s] = base().astype(own.dtype)

                    down(t, i, k).start()
            else:
                @pl.when(z > 0)
                def _():
                    up(t, i, k).wait_recv()

                @pl.when(z < NZ - 1)
                def _():
                    down(t, i, k).wait_recv()

                @pl.when((z > 0) & (z < NZ - 1))
                def _():
                    o_ref[s] = (base() + ubuf[t, s].astype(f32) + dbuf[t, s].astype(f32)).astype(o_ref.dtype)

                @pl.when(z == 0)
                def _():
                    o_ref[s] = (base() + dbuf[t, s].astype(f32)).astype(o_ref.dtype)

                @pl.when(z == NZ - 1)
                def _():
                    o_ref[s] = (base() + ubuf[t, s].astype(f32)).astype(o_ref.dtype)

    first(0)
    for i in range(NZ):
        if i + 1 < NZ:
            first(i + 1)
        second(i)

    for k in range(chunks):
        for i in range(NZ):
            across(i, k).wait_send()
            for j in range(2):
                over(i, j, k).wait_send()
            if i < NZ - 1:
                t = order(z, i)

                @pl.when(t > z)
                def _():
                    up(t, i, k).wait_send()

                @pl.when(t < z)
                def _():
                    down(t, i, k).wait_send()


def scatter16(p, cid, chunks=2, out_dtype=jnp.float32):
    _, rows, width = p.shape
    dma = pltpu.SemaphoreType.DMA
    bf = p.dtype
    return pl.pallas_call(
        functools.partial(scatter_kernel, chunks),
        out_shape=jax.ShapeDtypeStruct((rows, width), out_dtype),
        in_specs=[pl.BlockSpec(memory_space=pl.ANY)],
        out_specs=pl.BlockSpec(memory_space=pltpu.VMEM),
        scratch_shapes=[
            pltpu.VMEM((8, rows, width), bf), pltpu.VMEM((8, rows, width), bf),
            pltpu.VMEM((4, rows, width), bf), pltpu.VMEM((4, rows, width), bf), pltpu.VMEM((4, rows, width), bf),
            dma((8,)), dma((8, chunks)), dma((8, chunks)), dma((4, chunks)), dma((4, chunks)),
            dma((4, chunks)), dma((4, chunks)), dma((4, chunks)), dma((4, chunks)),
        ],
        compiler_params=pltpu.CompilerParams(collective_id=cid, has_side_effects=True,
                                             vmem_limit_bytes=32 * 1024 * 1024),
        cost_estimate=pl.CostEstimate(flops=0, bytes_accessed=150_000_000, transcendentals=0),
        name="scatter16",
    )(p)


H = 16
QK_NOPE = 128
ROPE = 64
V_DIM = 128
KV_RANK = 512
GROUPS = 16
EPSILON = 1e-06
ROTARY_BASE = 10000.0
BF = jnp.bfloat16
F32 = jnp.float32


def product(left_side, right_side):
    return jnp.dot(left_side, right_side, preferred_element_type=F32)


def product_lead(left_side, right_side):
    return lax.dot_general(
        left_side, right_side, (((0,), (0,)), ((), ())), preferred_element_type=F32
    )


def product_trail(left_side, right_side):
    return lax.dot_general(
        left_side, right_side, (((1,), (1,)), ((), ())), preferred_element_type=F32
    )


def rotary_tables(positions):
    half_width = ROPE // 2
    frequency = ROTARY_BASE ** (-jnp.arange(half_width, dtype=F32) * 2.0 / ROPE)
    angles = positions[:, None] * frequency[None, :]
    return (jnp.cos(angles), jnp.sin(angles))


def rotate(values, cosine, sine_table):
    first_half, second_half = jnp.split(values, 2, axis=-1)
    return jnp.concatenate(
        [
            first_half * cosine - second_half * sine_table,
            second_half * cosine + first_half * sine_table,
        ],
        axis=-1,
    )


def norm_forward(values, gains):
    factor = lax.rsqrt(jnp.mean(values * values, axis=-1, keepdims=True) + EPSILON)
    normed = values * factor
    return (normed * gains, normed, factor)


def norm_backward(gradient, normed, factor, gains):
    gain_grad = jnp.sum(gradient * normed, axis=0)
    scaled = gradient * gains
    return (
        factor * (scaled - normed * jnp.mean(scaled * normed, axis=-1, keepdims=True)),
        gain_grad,
    )


def silu_pair(gate_in):
    sigmoid = jax.nn.sigmoid(gate_in)
    return (gate_in * sigmoid, sigmoid * (1.0 + gate_in * (1.0 - sigmoid)))


def selected_experts(routes):
    chosen = routes[:, :, None] == jnp.arange(GROUPS, dtype=routes.dtype)
    return jnp.any(chosen, axis=1)


def masked_softmax(logits, mask):
    held = jnp.where(mask, logits, -1e30)
    peak = jnp.max(held, axis=-1, keepdims=True)
    raised = jnp.where(mask, jnp.exp(held - peak), 0.0)
    return raised / jnp.sum(raised, axis=-1, keepdims=True)


def head_blocks(dp):
    rounds = []
    for i in range(dp):
        sources, blocks = [], []
        for head in range(H):
            j = (i + head * dp // GROUPS) % dp
            blocks.append((dp * head + j) // GROUPS)
            sources.append((dp * head + j) % GROUPS)
        rounds.append((sources, blocks))
    return rounds


def per_device(
    layer_input,
    out_cotangent,
    lengths,
    routes,
    attn_gain,
    query_weight,
    latent_weight,
    latent_gain,
    expand_weight,
    output_weight,
    mixer_gain,
    router_weight,
    gate_weight,
    up_weight,
    down_weight,
    shared_gate,
    shared_up,
    shared_down,
):
    dp = lax.axis_size("dp")
    me = lax.axis_index("expert")
    plane = lax.axis_index("dp")
    batches, _, here, width = layer_input.shape
    own = batches * here
    total = own * GROUPS
    seq_total = here * GROUPS
    rows_w = query_weight.shape[0]
    rows_l = expand_weight.shape[0]
    scale_factor = float(QK_NOPE + ROPE) ** (-0.5)

    x_own = layer_input.reshape(own, width)
    x_all = gather16(x_own, 1).reshape(total, width)

    latent_column = jnp.zeros((rows_w,), BF).at[:rows_l].set(latent_gain)
    small = jnp.concatenate(
        [
            latent_weight,
            router_weight,
            attn_gain[:, None],
            mixer_gain[:, None],
            latent_column[:, None],
            jnp.zeros((rows_w, 640 - 595), BF),
        ],
        axis=1,
    )
    small = lax.all_gather(small, ("dp", "expert"), axis=0, tiled=True)
    latent_full = small[:, :576]
    router_full = small[:, 576:592]
    gain_attn = small[:, 592].astype(F32)
    gain_mixer = small[:, 593].astype(F32)
    gain_latent = small[:, 594].reshape(dp * GROUPS, rows_w)[:, :rows_l].reshape(-1).astype(F32)

    query_parts = query_weight.reshape(rows_w, H, QK_NOPE + ROPE).transpose(1, 0, 2)
    expand_parts = expand_weight.reshape(rows_l, H, QK_NOPE + V_DIM).transpose(1, 0, 2)
    query_head = lax.all_to_all(query_parts, "expert", 0, 0, tiled=True)
    expand_head = lax.all_to_all(expand_parts, "expert", 0, 0, tiled=True)
    query_head = lax.all_gather(query_head, "dp", axis=0, tiled=True).reshape(width, QK_NOPE + ROPE)
    expand_head = lax.all_gather(expand_head, "dp", axis=0, tiled=True).reshape(KV_RANK, QK_NOPE + V_DIM)
    output_rows = lax.all_gather(output_weight, "dp", axis=0)
    received = []
    shift = (me * dp) // GROUPS
    for sources, blocks in head_blocks(dp):
        table = [0] * GROUPS
        for source, block in zip(sources, blocks):
            table[source] = block
        block = lax.dynamic_index_in_dim(output_rows, jnp.array(table, jnp.int32)[me], 0, False)
        received.append(lax.ppermute(block, "expert", [(s, h) for h, s in enumerate(sources)]))
    received = jnp.stack(received)
    output_head = jnp.stack(
        [lax.dynamic_index_in_dim(received, (j - shift) % dp, 0, False) for j in range(dp)]
    ).reshape(V_DIM, width)

    gate_full = lax.all_gather(gate_weight[0], "dp", axis=0, tiled=True)
    up_full = lax.all_gather(up_weight[0], "dp", axis=0, tiled=True)
    down_full = lax.all_gather(down_weight[0], "dp", axis=0, tiled=True)
    share_gate = lax.all_gather(shared_gate, "dp", axis=0, tiled=True)
    share_up = lax.all_gather(shared_up, "dp", axis=0, tiled=True)
    share_down = lax.all_gather(shared_down, "dp", axis=1, tiled=True)

    seq_lengths = lengths.reshape(batches)
    own_positions = me * here + jnp.arange(here, dtype=jnp.int32)
    valid_own = (own_positions[None, :] < seq_lengths[:, None]).reshape(own).astype(F32)
    all_positions = jnp.arange(seq_total, dtype=jnp.int32).reshape(GROUPS, 1, here)
    valid_all = jnp.broadcast_to(
        all_positions < seq_lengths[None, :, None], (GROUPS, batches, here)
    ).reshape(total)
    key_positions = jnp.arange(seq_total, dtype=jnp.int32)
    cosine, sine_table = rotary_tables(key_positions.astype(F32))
    cosine_own = lax.dynamic_slice_in_dim(cosine, me * here, here)
    sine_own = lax.dynamic_slice_in_dim(sine_table, me * here, here)

    def by_sequence(v):
        return v.reshape(GROUPS, batches, here, v.shape[-1]).swapaxes(0, 1).reshape(batches, seq_total, -1)

    def by_device(v):
        return v.reshape(batches, GROUPS, here, v.shape[-1]).swapaxes(0, 1).reshape(total, -1)

    grad_own = out_cotangent.reshape(own, width) * valid_own[:, None].astype(BF)
    routes_own = routes.reshape(own, -1)
    packed = jnp.concatenate(
        [grad_own, routes_own.astype(BF), jnp.zeros((own, 128 - routes_own.shape[1]), BF)], axis=1
    )
    packed = lax.all_gather(packed, "expert", axis=0, tiled=True)
    grad_all = packed[:, :width]
    routes_all = packed[:, width : width + routes_own.shape[1]].astype(jnp.int32)

    hidden_all = norm_forward(x_all.astype(F32), gain_attn)[0].astype(BF)
    raw = product(hidden_all, jnp.concatenate([query_head, latent_full], axis=1))
    raw = by_sequence(raw)
    query_nope = raw[..., :QK_NOPE].astype(BF)
    query_rope = rotate(raw[..., QK_NOPE : QK_NOPE + ROPE], cosine, sine_table).astype(BF)
    query = jnp.concatenate([query_nope, query_rope], axis=-1)
    latent_raw = raw[..., QK_NOPE + ROPE :]
    latent = norm_forward(latent_raw[..., :KV_RANK], gain_latent)[0].astype(BF)
    key_rope = rotate(latent_raw[..., KV_RANK:], cosine, sine_table).astype(BF)
    expanded = product(latent, expand_head).astype(BF)
    key = jnp.concatenate([expanded[..., :QK_NOPE], key_rope], axis=-1)
    values = expanded[..., QK_NOPE:]
    allowed = (key_positions[None, None, :] <= key_positions[None, :, None]) & (
        key_positions[None, None, :] < seq_lengths[:, None, None]
    )

    def score(query, key):
        raw_scores = jnp.einsum("btd,bsd->bts", query, key, preferred_element_type=F32)
        return jnp.where(allowed, raw_scores * scale_factor, -1e30)

    scores = score(query, key)
    peak = jnp.max(scores, axis=-1, keepdims=True)
    log_total = peak + jnp.log(jnp.sum(jnp.exp(scores - peak), axis=-1, keepdims=True))
    probs_low = jnp.exp(scores - log_total).astype(BF)
    attended = jnp.einsum("bts,bsd->btd", probs_low, values, preferred_element_type=F32).astype(BF)
    attended_rows = by_device(attended)
    attn_part = product(attended_rows, output_head).astype(BF).reshape(GROUPS, own, width)
    attn_out = scatter16(attn_part, 2)

    x_wide = x_own.astype(F32)
    middle = x_wide + attn_out
    normed_mix, unit_mix, factor_mix = norm_forward(middle, gain_mixer)
    hidden_mix = normed_mix.astype(BF)
    mix_all = gather16(hidden_mix, 3).reshape(total, width)

    shared_width = share_gate.shape[1]
    fan = jnp.concatenate(
        [share_gate, router_full, jnp.zeros((width, 256 - shared_width - GROUPS), BF),
         share_up, jnp.zeros((width, 256 - shared_width), BF)], axis=1)
    fanned = product(mix_all, fan)
    shared_gate_in = fanned[:, :shared_width]
    logits_all = fanned[:, shared_width : shared_width + GROUPS]
    shared_up_in = fanned[:, 256 : 256 + shared_width]
    shared_act, shared_slope = silu_pair(shared_gate_in)
    shared_hidden = (shared_act * shared_up_in).astype(BF)

    blocks = GROUPS * batches
    mask_all = selected_experts(routes_all)
    gates_all = masked_softmax(logits_all, mask_all)
    mine = jnp.arange(GROUPS) == me
    taken = (jnp.any(mask_all & mine, axis=1) & valid_all).reshape(blocks, here)
    gates_mine = jnp.sum(jnp.where(mine, gates_all, 0.0), axis=1).reshape(blocks, here)
    place_in = jnp.cumsum(taken.astype(jnp.int32), axis=1) - 1
    slots = 32
    spread = (place_in[:, None, :] == jnp.arange(slots)[None, :, None]) & taken[:, None, :]
    spread_low = spread.astype(BF)
    gates_rows = jnp.sum(jnp.where(spread, gates_mine[:, None, :], 0.0), axis=2).reshape(blocks * slots, 1)

    def to_slots(v):
        return jnp.einsum(
            "bst,btd->bsd", spread_low, v.reshape(blocks, here, width), preferred_element_type=F32
        ).astype(BF).reshape(blocks * slots, width)

    def to_tokens(v):
        return jnp.einsum(
            "bst,bsd->btd", spread_low, v.reshape(blocks, slots, width), preferred_element_type=F32
        ).reshape(total, width)

    rows = to_slots(mix_all)
    grad_rows = to_slots(grad_all)
    gate_in = product(rows, gate_full)
    up_in = product(rows, up_full)
    activated, slope = silu_pair(gate_in)
    hidden = (activated * up_in).astype(BF)
    result = product(hidden, down_full).astype(BF)
    out_part = product(shared_hidden, share_down) + gates_mine.reshape(total, 1) * to_tokens(result)
    out_part = out_part.astype(BF).reshape(GROUPS, own, width)
    mixed = scatter16(out_part, 4)
    layer_output = valid_own[:, None] * (middle + mixed)

    grad_wide = grad_rows.astype(F32)
    grad_gates = jnp.sum(grad_wide * result.astype(F32), axis=1).reshape(blocks, slots)
    grad_gates = jnp.sum(jnp.where(spread, grad_gates[:, :, None], 0.0), axis=1).reshape(total, 1)
    grad_result = (gates_rows * grad_wide).astype(BF)
    grad_down = product_lead(hidden, grad_result).astype(BF)
    grad_hidden = product_trail(grad_result, down_full)
    grad_gate_in = (grad_hidden * up_in * slope).astype(BF)
    grad_up_in = (grad_hidden * activated).astype(BF)
    grad_gate = product_lead(rows, grad_gate_in).astype(BF)
    grad_up = product_lead(rows, grad_up_in).astype(BF)
    grad_taken = (product_trail(grad_gate_in, gate_full) + product_trail(grad_up_in, up_full)).astype(BF)

    grad_shared_down = product_lead(shared_hidden, grad_all).astype(BF)
    grad_shared_hidden = product_trail(grad_all, share_down)
    grad_shared_gate_in = (grad_shared_hidden * shared_up_in * shared_slope).astype(BF)
    grad_shared_up_in = (grad_shared_hidden * shared_act).astype(BF)
    grad_shared_gate = product_lead(mix_all, grad_shared_gate_in).astype(BF)
    grad_shared_up = product_lead(mix_all, grad_shared_up_in).astype(BF)
    mix_part = (
        product_trail(grad_shared_gate_in, share_gate)
        + product_trail(grad_shared_up_in, share_up)
        + to_tokens(grad_taken)
    ).astype(BF)
    gates_high = grad_gates.astype(BF)
    gates_low = (grad_gates - gates_high.astype(F32)).astype(BF)
    lane = jnp.arange(128)
    gates_part = jnp.where(lane == me, gates_high, jnp.where(lane == me + GROUPS, gates_low, 0))
    mix_part = jnp.concatenate([mix_part, gates_part], axis=1).reshape(GROUPS, own, width + 128)
    mix_part, grad_gate, grad_up, grad_down = lax.optimization_barrier(
        (mix_part, grad_gate, grad_up, grad_down))
    mix_sum = scatter16(mix_part, 5)

    out_gate = lax.psum_scatter(grad_gate, "dp", scatter_dimension=0, tiled=True)
    out_up = lax.psum_scatter(grad_up, "dp", scatter_dimension=0, tiled=True)
    out_down = lax.psum_scatter(grad_down, "dp", scatter_dimension=0, tiled=True)
    out_shared_gate = lax.psum_scatter(grad_shared_gate, "dp", scatter_dimension=0, tiled=True)
    out_shared_up = lax.psum_scatter(grad_shared_up, "dp", scatter_dimension=0, tiled=True)
    out_shared_down = lax.psum_scatter(grad_shared_down, "dp", scatter_dimension=1, tiled=True)

    mask_own = selected_experts(routes_own)
    soft_own = masked_softmax(product(hidden_mix, router_full), mask_own)
    grad_masked = (mix_sum[:, width : width + GROUPS] + mix_sum[:, width + GROUPS : width + 2 * GROUPS])
    grad_masked = grad_masked * valid_own[:, None]
    grad_logits = soft_own * (grad_masked - jnp.sum(grad_masked * soft_own, axis=1, keepdims=True))
    grad_logits = grad_logits.astype(BF)
    grad_mix = mix_sum[:, :width] + product_trail(grad_logits, router_full)
    grad_middle_norm, grad_gain_mixer = norm_backward(grad_mix, unit_mix, factor_mix, gain_mixer)
    grad_middle = grad_own.astype(F32) + grad_middle_norm

    grad_attn_all = gather16(grad_middle.astype(BF), 6).reshape(total, width)
    grad_output = product_lead(attended_rows, grad_attn_all)
    grad_attended = by_sequence(product_trail(grad_attn_all, output_head).astype(BF))
    probs = jnp.exp(score(query, key) - log_total)
    probs_low = probs.astype(BF)
    grad_probs = jnp.einsum("btd,bsd->bts", grad_attended, values, preferred_element_type=F32)
    inner_sum = jnp.sum(grad_probs * probs, axis=-1, keepdims=True)
    grad_scores = (probs * (grad_probs - inner_sum)).astype(BF)
    grad_query = jnp.einsum("bts,bsd->btd", grad_scores, key, preferred_element_type=F32) * scale_factor
    grad_key = jnp.einsum("bts,btd->bsd", grad_scores, query, preferred_element_type=F32) * scale_factor
    grad_values = jnp.einsum("bts,btd->bsd", probs_low, grad_attended, preferred_element_type=F32)
    grad_expanded = jnp.concatenate([grad_key[..., :QK_NOPE], grad_values], axis=-1).astype(BF)
    grad_expanded = grad_expanded.reshape(total, -1)
    grad_expand = product_lead(latent.reshape(total, -1), grad_expanded)
    grad_latent = product_trail(grad_expanded, expand_head)
    grad_query = jnp.concatenate(
        [grad_query[..., :QK_NOPE], rotate(grad_query[..., QK_NOPE:], cosine, -sine_table)], axis=-1
    ).astype(BF)
    grad_query = by_device(grad_query)
    grad_query_w = product_lead(hidden_all, grad_query)
    back_part = product_trail(grad_query, query_head).astype(BF)
    latent_part = jnp.concatenate(
        [grad_latent.astype(BF).reshape(batches, seq_total, -1), grad_key[..., QK_NOPE:].astype(BF),
         jnp.zeros((batches, seq_total, 64), BF)], axis=-1)
    back_part = jnp.concatenate([back_part, by_device(latent_part)], axis=1)
    back_sum = scatter16(back_part.reshape(GROUPS, own, back_part.shape[1]), 7)

    x_normed, unit_attn, factor_attn = norm_forward(x_wide, gain_attn)
    hidden_own = x_normed.astype(BF)
    latent_own = product(hidden_own, latent_full)
    _, unit_latent, factor_latent = norm_forward(latent_own[:, :KV_RANK], gain_latent)
    grad_latent_in, grad_gain_latent = norm_backward(
        back_sum[:, width : width + KV_RANK], unit_latent, factor_latent, gain_latent
    )
    grad_rope = back_sum[:, width + KV_RANK : width + KV_RANK + ROPE].reshape(batches, here, ROPE)
    grad_rope = rotate(grad_rope, cosine_own, -sine_own).reshape(own, ROPE)
    grad_latent_raw = jnp.concatenate([grad_latent_in, grad_rope], axis=1).astype(BF)
    grad_hidden_attn = back_sum[:, :width] + product_trail(grad_latent_raw, latent_full)
    grad_input_norm, grad_gain_attn = norm_backward(grad_hidden_attn, unit_attn, factor_attn, gain_attn)
    grad_input = grad_middle + grad_input_norm

    latent_rows = grad_gain_latent.reshape(dp * GROUPS, rows_l)
    latent_rows = jnp.pad(latent_rows, ((0, 0), (0, rows_w - rows_l))).reshape(width, 1)
    tokens_side = jnp.concatenate([hidden_own, hidden_mix], axis=0)
    grads_side = jnp.concatenate(
        [jnp.pad(grad_latent_raw, ((0, 0), (0, 64))), jnp.pad(grad_logits, ((0, 0), (576, 640 - 592)))], axis=0)
    lane = jnp.arange(640)[None, :]
    small_grad = product_lead(tokens_side, grads_side)
    small_grad = small_grad + jnp.where(lane == 592, grad_gain_attn[:, None], 0.0)
    small_grad = small_grad + jnp.where(lane == 593, grad_gain_mixer[:, None], 0.0)
    small_grad = (small_grad + jnp.where(lane == 594, latent_rows, 0.0)).astype(BF)
    small_sum = lax.psum_scatter(small_grad, ("dp", "expert"), scatter_dimension=0, tiled=True).astype(F32)

    def home(v, rows):
        v = v.reshape(dp, GROUPS, rows, v.shape[-1])
        v = lax.psum_scatter(v.astype(BF), "dp", scatter_dimension=0, tiled=False)
        v = lax.all_to_all(v, "expert", 0, 0, tiled=True)
        return v.transpose(1, 0, 2).reshape(rows, -1).astype(F32)

    out_query = home(grad_query_w, rows_w)
    out_expand = home(grad_expand, rows_l)
    grad_output = lax.psum(grad_output, "dp").reshape(dp, rows_w, width)
    out_output = jnp.zeros((rows_w, width), F32)
    for i, (sources, blocks) in enumerate(head_blocks(dp)):
        block = lax.dynamic_index_in_dim(grad_output, (i + shift) % dp, 0, False)
        block = lax.ppermute(block, "expert", [(h, s) for h, s in enumerate(sources)])
        table = [0] * GROUPS
        for source, at in zip(sources, blocks):
            table[source] = at
        out_output = jnp.where(jnp.array(table, jnp.int32)[me] == plane, block, out_output)

    def as_input(v):
        return v.reshape(batches, 1, here, width)

    return (
        as_input(layer_output),
        as_input(grad_input),
        small_sum[:, 592],
        out_query,
        small_sum[:, :576],
        small_sum[:rows_l, 594],
        out_expand,
        out_output,
        small_sum[:, 593],
        small_sum[:, 576:592],
        out_gate.astype(F32)[None],
        out_up.astype(F32)[None],
        out_down.astype(F32)[None],
        out_shared_gate.astype(F32),
        out_shared_up.astype(F32),
        out_shared_down.astype(F32),
    )


def solution(mesh):
    split = P(("dp", "expert"), None)
    line = P(("dp", "expert"))
    tokens = P(None, "dp", "expert", None)
    expert = P("expert", "dp", None)
    return jax.shard_map(
        per_device,
        mesh=mesh,
        in_specs=(
            tokens, tokens, P(None, "dp"), tokens, line, split, split, line, split, split, line, split,
            expert, expert, expert, P("dp", "expert"), P("dp", "expert"), P("expert", "dp"),
        ),
        out_specs=(
            tokens, tokens, line, split, split, line, split, split, line, split,
            expert, expert, expert, P("dp", "expert"), P("dp", "expert"), P("expert", "dp"),
        ),
        check_vma=False,
    )
```

time: 2860 us -> 1280 us (0.45)
  waiting for transfers between devices: 1910 us -> 242 us
  Pallas kernels: 0 us -> 409 us
  blocking collectives: 199 us -> 71 us
  local copies, waits for them, and re-layouts: 191 us -> 114 us
  matrix products: 345 us -> 277 us
  starting transfers between devices: 93.7 us -> 36 us
    reduce_scatter x16 -> x9, waiting for transfers between devices: 996 us -> 221 us  [the longest x1 69.4 us: per_device(): lax.psum_scatter(grad_gate, 'dp', scatter_dimension=0, tiled=True)]
    all_gather x13 -> x5, waiting for transfers between devices: 505 us -> 0.01 us  [the longest x1 0.01 us: per_device(): small = lax.all_gather(small, ('dp', 'expert'), axis=0, tiled=True)]
    pallas_call x0 -> x7, Pallas kernels: none -> 409 us  [the longest x4 231 us: scatter16(): pl.pallas_call(functools.partial(scatter_kernel, chunks), out_shape=jax.S...]
    unnamed x35 -> x15, waiting for transfers between devices: 283 us -> 2.95 us
    all_to_all x8 -> x4, waiting for transfers between devices: 129 us -> 9.91 us  [the longest x2 9.91 us: home(): v = lax.all_to_all(v, 'expert', 0, 0, tiled=True)]
    dot_general x56 -> x20, matrix products: 234 us -> 121 us  [the longest x10 71.8 us: product(): return jnp.dot(left_side, right_side, preferred_element_type=F32)]
    unnamed x2 -> x0, blocking collectives: 83 us -> none
    all_to_all x8 -> x4, starting transfers between devices: 91.1 us -> 23.5 us  [the longest x2 12.6 us: home(): v = lax.all_to_all(v, 'expert', 0, 0, tiled=True)]
  transfers between devices with their start and end apart: 40 -> 23, of which waited for: 32 -> 7; matrix products, arithmetic and copies ran while one was open for 19% -> 22% of each run, Pallas kernels for 0% -> 24%
where the time goes in v1:
time: 1280 us; the launch traced here: 1270 us
  Pallas kernels  409 us (32%)
  matrix products  277 us (22%)
  waiting for transfers between devices  242 us (19%)
  local copies, waits for them, and re-layouts  114 us (9%)
  other arithmetic  96.8 us (8%)
  blocking collectives  71 us (6%)
  starting transfers between devices  36 us (3%)
  between operations  20.9 us (2%)
    pallas_call x4, Pallas kernels, scatter16(): pl.pallas_call(functools.partial(scatter_kernel, chunks), out_shape=jax.S...  231 us
    pallas_call x3, Pallas kernels, gather16(): pl.pallas_call(functools.partial(gather_kernel, chunks), out_shape=jax.Sh...  178 us
    dot_general x11, matrix products, product_trail(): lax.dot_general(left_side, right_side, (((1,), (1,)), ((), ())), preferre...  88.1 us
    dot_general x10, matrix products, product(): return jnp.dot(left_side, right_side, preferred_element_type=F32)  71.8 us
    reduce_scatter x1, waiting for transfers between devices, per_device(): lax.psum_scatter(grad_gate, 'dp', scatter_dimension=0, tiled=True)  69.4 us
    reduce_scatter x1, waiting for transfers between devices, per_device(): out_up = lax.psum_scatter(grad_up, 'dp', scatter_dimension=0, tiled=True)  69.1 us
    dot_general x10, matrix products, product_lead(): lax.dot_general(left_side, right_side, (((0,), (0,)), ((), ())), preferre...  68.2 us
    reduce_scatter x1, waiting for transfers between devices, per_device(): lax.psum_scatter(grad_down, 'dp', scatter_dimension=0, tiled=True)  64.6 us
  transfers between devices with their start and end apart: 23, of which 7 were waited for; matrix products, arithmetic and copies ran while one was open for 22% of the time, Pallas kernels for 24%

profile of v1, /device:TPU:0, one launch (start us, length us, event | category | flops | bytes accessed | tf_op | source)
XLA Modules:
  0.0 1267.0 jit_solution(579008463000711547)
XLA Ops:
  60.6 14.6 %all_gather.42 = bf16[2048,176]{0,1:T(8,128)(2,1)S(1)} all-gather(bf16[1024,176]{0,1:T(8,128)(2,1)S(1)} %copy-done.44), channel_id=1, replica_groups=mesh['dp'=2,'expert'=16] {'dp'}, dimensions={0}, use_global_device_ids=true | all-gather | bytes 1081344 | tf_op jit(solution)/shard_map/all_gather | solution.py:516
  75.2 76.8 %gather16.3 = bf16[16,128,2048]{2,1,0:T(8,128)(2,1)} custom-call(bf16[128,2048]{1,0:T(8,128)(2,1)} %bitcast.250), custom_call_target="tpu_custom_call" | custom-call | bytes 150000000 | tf_op jit(solution)/shard_map/gather16/pallas_call | solution.py:172
  167.2 11.6 all_gather.43
  186.7 18.9 %all_gather.37 = bf16[32,64,192]{2,1,0:T(8,128)(2,1)S(1)} all-gather(bf16[16,64,192]{2,1,0:T(8,128)(2,1)S(1)} %all-to-all-done), channel_id=1, replica_groups=mesh['dp'=2,'expert'=16] {'dp'}, dimensions={0}, use_global_device_ids=true | all-gather | bytes 1179648 | tf_op jit(solution)/shard_map/all_gather | solution.py:496
  208.5 11.1 fusion.30
  241.9 12.5 copy.357
  282.2 50.2 %scatter16.4 = f32[128,2048]{1,0:T(8,128)S(1)} custom-call(bf16[16,128,2048]{2,1,0:T(8,128)(2,1)S(1)} %bitcast.223), custom_call_target="tpu_custom_call" | custom-call | bytes 150000000 | tf_op jit(solution)/shard_map/scatter16/pallas_call | solution.py:331
  335.5 51.1 %gather16.4 = bf16[16,128,2048]{2,1,0:T(8,128)(2,1)} custom-call(bf16[128,2048]{1,0:T(8,128)(2,1)} %multiply_convert_fusion.13.x_ref), custom_call_target="tpu_custom_call" | custom-call | bytes 150000000 | tf_op jit(solution)/shard_map/gather16/pallas_call | solution.py:172
  426.0 11.7 fusion.20
  437.7 13.1 %multiply_convert_fusion.5 = (bf16[1024,1408]{1,0:T(8,128)(2,1)}, f32[1024,1408]{1,0:T(8,128)}) fusion(f32[1024,1408]{1,0:T(8,128)} %fusion.20, bf16[1024,2048]{1,0:T(8,128)(2,1)} %bitcast.257, bf16[1,2048,1408]{2,1,0:T(8,128)(2,1)} %all-gather.16.cloned.1.call-done), kind=kOutput, calls=%fused_computation.44 | convolution fusion | flops 5914230784 | bytes 24379392 | tf_op jit(solution)/shard_map/dot_general | solution.py:362
  450.8 11.8 fusion.5
  478.2 15.5 %multiply_convert_fusion.4 = (bf16[1024,1408]{1,0:T(8,128)(2,1)S(1)}, bf16[1024,1408]{1,0:T(8,128)(2,1)}) fusion(f32[1024,1408]{1,0:T(8,128)} %fusion.20, f32[1024,1408]{1,0:T(8,128)} %get-tuple-element.218, bf16[1024,2048]{1,0:T(8,128)(2,1)} %copy-done.19, bf16[1,1408,2048]{2,1,0:T(8,128)(2,1)} %all-gather.18.cloned.1.call-done), kind=kOutput, calls=%fused_computation.43 | convolution fusion | flops 5924323328 | bytes 27262976 | tf_op jit(solution)/shard_map/dot_general | solution.py:372
  504.0 11.0 convolution_convert_fusion.2
  542.2 17.7 %copy.338 = f32[2048,2048]{0,1:T(8,128)} copy(f32[2048,2048]{1,0:T(8,128)} %bitcast.228) | data formatting | bytes 33554432 | tf_op jit(solution)/shard_map/reshape | solution.py:612
  576.5 15.5 %add_convert_fusion = bf16[2048,2048]{0,1:T(8,128)(2,1)} fusion(f32[2048,2048]{0,1:T(8,128)} %copy.338, f32[2048,2048]{0,1:T(8,128)} %fusion.109, bf16[2048,176]{0,1:T(8,128)(2,1)S(1)} %get-tuple-element.188, bf16[2048,176]{0,1:T(8,128)(2,1)S(1)} %copy-done.14), kind=kOutput, calls=%fused_computation.6 | convolution fusion | flops 1488977920 | bytes 43384832 | tf_op jit(solution)/shard_map/dot_general | solution.py:372
  599.5 11.7 copy.339
  614.8 54.5 %scatter16.6 = f32[128,2176]{1,0:T(8,128)S(1)} custom-call(bf16[16,128,2176]{2,1,0:T(8,128)(2,1)S(1)} %bitcast.224), custom_call_target="tpu_custom_call" | custom-call | bytes 150000000 | tf_op jit(solution)/shard_map/scatter16/pallas_call | solution.py:331
  673.7 50.3 %gather16.5 = bf16[16,128,2048]{2,1,0:T(8,128)(2,1)} custom-call(bf16[128,2048]{1,0:T(8,128)(2,1)} %fusion.99.x_ref), custom_call_target="tpu_custom_call" | custom-call | bytes 150000000 | tf_op jit(solution)/shard_map/gather16/pallas_call | solution.py:172
  803.6 65.2 %scatter16.7 = f32[128,2688]{1,0:T(8,128)S(1)} custom-call(bf16[16,128,2688]{2,1,0:T(8,128)(2,1)S(1)} %pad_maximum_fusion.p_ref), custom_call_target="tpu_custom_call" | custom-call | bytes 150000000 | tf_op jit(solution)/shard_map/scatter16/pallas_call | solution.py:331
  904.7 61.0 %scatter16.5 = f32[128,2048]{1,0:T(8,128)S(1)} custom-call(bf16[16,128,2048]{2,1,0:T(8,128)(2,1)S(1)} %bitcast.225), custom_call_target="tpu_custom_call" | custom-call | bytes 150000000 | tf_op jit(solution)/shard_map/scatter16/pallas_call | solution.py:331
  1019.6 17.6 %reduce-scatter.10.cloned.1.call-done = bf16[64,640]{1,0:T(8,128)(2,1)} async-done(((bf16[2048,640]{1,0:T(8,128)(2,1)}), bf16[64,640]{1,0:T(8,128)(2,1)}) %reduce-scatter.10.cloned.1.call-update) | async-done | bytes 81936 | tf_op jit(solution)/shard_map/reduce_scatter | solution.py:726
  1042.5 64.6 %reduce-scatter.20.cloned.1.call-done = bf16[704,2048]{1,0:T(8,128)(2,1)} async-done(((bf16[1408,2048]{1,0:T(8,128)(2,1)}), bf16[704,2048]{1,0:T(8,128)(2,1)}) %reduce-scatter.20.cloned.1.call-update) | async-done | bytes 2883600 | tf_op jit(solution)/shard_map/reduce_scatter | solution.py:660
  1112.2 69.1 %reduce-scatter.18.cloned.1.call-done = bf16[1024,1408]{1,0:T(8,128)(2,1)} async-done(((bf16[2048,1408]{1,0:T(8,128)(2,1)}), bf16[1024,1408]{1,0:T(8,128)(2,1)}) %reduce-scatter.18.cloned.1.call-update) | async-done | bytes 2883600 | tf_op jit(solution)/shard_map/reduce_scatter | solution.py:659
  1186.1 69.4 %reduce-scatter.16.cloned.1.call-done = bf16[1024,1408]{1,0:T(8,128)(2,1)} async-done(((bf16[2048,1408]{1,0:T(8,128)(2,1)}), bf16[1024,1408]{1,0:T(8,128)(2,1)}) %reduce-scatter.16.cloned.1.call-update) | async-done | bytes 2883600 | tf_op jit(solution)/shard_map/reduce_scatter | solution.py:658
  (441 shorter events, 439.6 us)
Async XLA Ops:
  7.2 198.3 %all-gather.10.cloned.1.call-start = ((), (), s32[]{:S(2)}) async-start(), calls=%async_computation.13 | async-start | bytes 2703360 | tf_op jit(solution)/shard_map/all_gather | solution.py:485
  12.0 387.3 %all-gather.12.cloned.1.call-start = ((), (), s32[]{:S(2)}) async-start(), calls=%async_computation.14 | async-start | bytes 9469952 | tf_op jit(solution)/shard_map/all_gather | solution.py:542
  15.9 410.1 %all-gather.14.cloned.1.call-start = ((), (), s32[]{:S(2)}) async-start(), calls=%async_computation.25 | async-start | bytes 8650752 | tf_op jit(solution)/shard_map/all_gather | solution.py:512
  16.7 421.0 %all-gather.16.cloned.1.call-start = ((), (), s32[]{:S(2)}) async-start(), calls=%async_computation.26 | async-start | bytes 8650752 | tf_op jit(solution)/shard_map/all_gather | solution.py:513
  18.0 143.6 %all-to-all-start.1 = ((bf16[16,16,256]{2,1,0:T(8,128)(2,1)}), bf16[16,16,256]{2,1,0:T(8,128)(2,1)S(1)}, u32[]{:S(2)}, u32[]{:S(2)}) async-start(bf16[16,16,256]{2,1,0:T(8,128)(2,1)} %copy.328), calls=%async_computation.1 | async-start | bytes 262144 | tf_op jit(solution)/shard_map/all_to_all | solution.py:495
  25.4 425.5 %all-gather.18.cloned.1.call-start = ((), (), s32[]{:S(2)}) async-start(), calls=%async_computation.27 | async-start | bytes 8650752 | tf_op jit(solution)/shard_map/all_gather | solution.py:514
  40.7 143.8 %collective-permute-start.1 = (bf16[64,2048]{1,0:T(8,128)(2,1)}, bf16[64,2048]{1,0:T(8,128)(2,1)}, u32[]{:S(2)}, u32[]{:S(2)}) collective-permute-start(bf16[64,2048]{1,0:T(8,128)(2,1)} %get-tuple-element.204), channel_id=1, source_target_pairs={{1,0},{3,1},{5,2},{7,3},{9,4},{11,5},{13,6},{15,7},{0,8},{2,9},{4,... | collective-permute-start | bytes 786440 | tf_op jit(solution)/shard_map/ppermute | solution.py:506
  43.2 141.3 %collective-permute-start = (bf16[64,2048]{1,0:T(8,128)(2,1)}, bf16[64,2048]{1,0:T(8,128)(2,1)}, u32[]{:S(2)}, u32[]{:S(2)}) collective-permute-start(bf16[64,2048]{1,0:T(8,128)(2,1)} %get-tuple-element.205), channel_id=1, source_target_pairs={{0,0},{2,1},{4,2},{6,3},{8,4},{10,5},{12,6},{14,7},{1,8},{3,9},{5,... | collective-permute-start | bytes 786440 | tf_op jit(solution)/shard_map/ppermute | solution.py:506
  161.6 25.1 %all-to-all-start = ((bf16[16,64,192]{2,1,0:T(8,128)(2,1)}), bf16[16,64,192]{2,1,0:T(8,128)(2,1)S(1)}, u32[]{:S(2)}, u32[]{:S(2)}) async-start(bf16[16,64,192]{2,1,0:T(8,128)(2,1)} %copy.323), calls=%async_computation | async-start | bytes 1048576 | tf_op jit(solution)/shard_map/all_to_all | solution.py:494
  165.1 800.6 %reduce-scatter.14.cloned.1.call-start = ((), (), s32[]{:S(2)}) async-start(), calls=%async_computation.17 | async-start | bytes 393216 | tf_op jit(solution)/shard_map/reduce_scatter | solution.py:730
  167.1 221.0 %copy-start.49 = (pred[128,16]{1,0:T(32,128)(4,1)}, pred[128,16]{1,0:T(32,128)(4,1)S(1)}, u32[]{:S(2)}) copy-start(pred[128,16]{1,0:T(32,128)(4,1)S(1)} %copy.343) | copy-start | bytes 6148
  750.4 222.0 %all-reduce.6.cloned.1.call-start = ((), (), s32[]{:S(2)}) async-start(), calls=%async_computation.18 | async-start | bytes 2097152 | tf_op jit(solution)/shard_map/psum | solution.py:736
  756.2 224.3 %reduce-scatter.12.cloned.1.call-start = ((), (), s32[]{:S(2)}) async-start(), calls=%async_computation.16 | async-start | bytes 1572864 | tf_op jit(solution)/shard_map/reduce_scatter | solution.py:730
  765.4 225.5 %reduce-scatter.24.cloned.1.call-start = ((), (), s32[]{:S(2)}) async-start(), calls=%async_computation.23 | async-start | bytes 1081344 | tf_op jit(solution)/shard_map/reduce_scatter | solution.py:662
  775.2 217.6 %reduce-scatter.22.cloned.1.call-start = ((), (), s32[]{:S(2)}) async-start(), calls=%async_computation.22 | async-start | bytes 1081344 | tf_op jit(solution)/shard_map/reduce_scatter | solution.py:661
  794.4 200.3 %reduce-scatter.26.cloned.1.call-start = ((), (), s32[]{:S(2)}) async-start(), calls=%async_computation.24 | async-start | bytes 1081344 | tf_op jit(solution)/shard_map/reduce_scatter | solution.py:663
  875.4 161.8 %reduce-scatter.10.cloned.1.call-start = ((), (), s32[]{:S(2)}) async-start(), calls=%async_computation.15 | async-start | bytes 2703360 | tf_op jit(solution)/shard_map/reduce_scatter | solution.py:726
  883.5 223.6 %reduce-scatter.20.cloned.1.call-start = ((), (), s32[]{:S(2)}) async-start(), calls=%async_computation.21 | async-start | bytes 8650752 | tf_op jit(solution)/shard_map/reduce_scatter | solution.py:660
  884.2 297.1 %reduce-scatter.18.cloned.1.call-start = ((), (), s32[]{:S(2)}) async-start(), calls=%async_computation.20 | async-start | bytes 8650752 | tf_op jit(solution)/shard_map/reduce_scatter | solution.py:659
  884.8 370.7 %reduce-scatter.16.cloned.1.call-start = ((), (), s32[]{:S(2)}) async-start(), calls=%async_computation.19 | async-start | bytes 8650752 | tf_op jit(solution)/shard_map/reduce_scatter | solution.py:658
  965.7 14.7 %all-to-all-start.3 = ((bf16[16,16,256]{2,1,0:T(8,128)(2,1)}), bf16[16,16,256]{2,1,0:T(8,128)(2,1)S(1)}, u32[]{:S(2)}, u32[]{:S(2)}) async-start(bf16[16,16,256]{2,1,0:T(8,128)(2,1)} %bitcast.290), calls=%async_computation.6 | async-start | bytes 262144 | tf_op jit(solution)/shard_map/all_to_all | solution.py:731
  974.7 21.9 %collective-permute-start.3 = (f32[64,2048]{1,0:T(8,128)}, f32[64,2048]{1,0:T(8,128)}, u32[]{:S(2)}, u32[]{:S(2)}) collective-permute-start(f32[64,2048]{1,0:T(8,128)} %get-tuple-element.193), channel_id=1, source_target_pairs={{0,0},{1,2},{2,4},{3,6},{4,8},{5,10},{6,12},{7,14},{8,1},{9,3},{10... | collective-permute-start | bytes 1572872 | tf_op jit(solution)/shard_map/ppermute | solution.py:740
  980.1 25.0 %collective-permute-start.2 = (f32[64,2048]{1,0:T(8,128)}, f32[64,2048]{1,0:T(8,128)}, u32[]{:S(2)}, u32[]{:S(2)}) collective-permute-start(f32[64,2048]{1,0:T(8,128)} %get-tuple-element.194), channel_id=1, source_target_pairs={{0,1},{1,3},{2,5},{3,7},{4,9},{5,11},{6,13},{7,15},{8,0},{9,2},{10... | collective-permute-start | bytes 1572872 | tf_op jit(solution)/shard_map/ppermute | solution.py:740
  980.4 36.1 %all-to-all-start.2 = ((bf16[16,64,192]{2,1,0:T(8,128)(2,1)}), bf16[16,64,192]{2,1,0:T(8,128)(2,1)}, u32[]{:S(2)}, u32[]{:S(2)}) async-start(bf16[16,64,192]{2,1,0:T(8,128)(2,1)} %bitcast.283), calls=%async_computation.4 | async-start | bytes 1048576 | tf_op jit(solution)/shard_map/all_to_all | solution.py:731
  (93 other events, 2112.6 us)
Sparse Core Ops, SparseCore 0:
  12.2 68.3 all-gather.9
  83.4 99.3 all-gather.11
  184.4 78.0 all-gather.13
  263.9 75.4 all-gather.15
  340.8 74.4 all-gather.17
  750.5 11.8 reduce-scatter.13
  764.8 40.0 all-reduce.5
  807.6 20.3 reduce-scatter.11
  830.9 16.6 reduce-scatter.23
  850.3 16.7 reduce-scatter.21
  875.5 16.7 reduce-scatter.25
  895.1 142.0 reduce-scatter.9
  1039.5 67.5 reduce-scatter.19
  1109.9 71.3 reduce-scatter.17
  1184.1 71.3 reduce-scatter.15

commit v2 on v1

v2 whole, which is shorter than its diff:
```python
import functools
import jax
import jax.numpy as jnp
from jax import lax
from jax.experimental import pallas as pl
from jax.experimental.pallas import tpu as pltpu
from jax.sharding import PartitionSpec as P

MESH = pl.DeviceIdType.MESH
NZ = 4
NE = 16


def place():
    me = lax.axis_index("expert")
    z = me // 4
    x = (me // 2) % 2
    c = me % 2
    return me, z, x, c, me + 1 - 2 * c, me + 2 - 4 * x


def enter(me, z, core, side):
    barrier = pltpu.get_barrier_semaphore()
    for other in (core, side):
        pl.semaphore_signal(barrier, inc=1, device_id={"expert": other}, device_id_type=MESH)

    @pl.when(z < NZ - 1)
    def _():
        pl.semaphore_signal(barrier, inc=1, device_id={"expert": me + 4}, device_id_type=MESH)

    @pl.when(z > 0)
    def _():
        pl.semaphore_signal(barrier, inc=1, device_id={"expert": me - 4}, device_id_type=MESH)

    pl.semaphore_wait(barrier, 2 + (z < NZ - 1).astype(jnp.int32) + (z > 0).astype(jnp.int32))


def enter_all(me, plane, dp):
    barrier = pltpu.get_barrier_semaphore()
    for r in range(1, NE):
        pl.semaphore_signal(
            barrier, inc=1, device_id={"expert": (me + r) % NE}, device_id_type=MESH)
    for r in range(1, dp):
        pl.semaphore_signal(
            barrier, inc=1, device_id={"dp": (plane + r) % dp}, device_id_type=MESH)
    pl.semaphore_wait(barrier, NE - 1 + dp - 1)


class Gather:
    def __init__(self, src, out, chunks, sems):
        self.src, self.out, self.chunks = src, out, chunks
        self.rows = src.shape[0] // chunks
        self.own_sem, self.us, self.ur, self.ds, self.dr, self.xs, self.xr, self.cs, self.cr = sems
        self.me, self.z, self.x, self.c, self.core, self.side = place()

    @staticmethod
    def scratch(chunks):
        dma = pltpu.SemaphoreType.DMA
        return [dma] + [dma((4, chunks))] * 4 + [dma((7, chunks))] * 2 + [dma((14, chunks))] * 2

    def copy(self, block, k, src, send, recv, to):
        part = pl.ds(k * self.rows, self.rows)
        return pltpu.make_async_remote_copy(
            src_ref=(self.src if src is None else self.out.at[src]).at[part],
            dst_ref=self.out.at[block].at[part],
            send_sem=send, recv_sem=recv,
            device_id={"expert": to}, device_id_type=MESH,
        )

    def up(self, k, s, src=None):
        return self.copy(self.me - 4 * s, k, src, self.us.at[s, k], self.ur.at[s, k], self.me + 4)

    def down(self, k, s, src=None):
        return self.copy(self.me + 4 * s, k, src, self.ds.at[s, k], self.dr.at[s, k], self.me - 4)

    def across(self, k, slot, block, src=None):
        return self.copy(block, k, src, self.xs.at[slot, k], self.xr.at[slot, k], self.side)

    def over(self, k, slot, block, src=None):
        return self.copy(block, k, src, self.cs.at[slot, k], self.cr.at[slot, k], self.core)

    def up_in(self, k, s):
        b = self.me - 4 * s
        return self.copy(b, k, b, self.us.at[s - 1, k], self.ur.at[s - 1, k], self.side)

    def dn_in(self, k, s):
        b = self.me + 4 * s
        return self.copy(b, k, b, self.ds.at[s - 1, k], self.dr.at[s - 1, k], self.side)

    def shift(self, base, slot):
        return base - 4 * slot if slot <= 3 else base + 4 * (slot - 3)

    def core_block(self, slot):
        if slot < 7:
            return self.shift(self.core, slot)
        return self.shift(self.core + 2 - 4 * self.x, slot - 7)

    def has(self, slot):
        slot = slot % 7
        if slot == 0:
            return self.z >= 0
        return self.z >= slot if slot <= 3 else self.z + (slot - 3) <= NZ - 1

    def start(self):
        z, me = self.z, self.me
        self.own = pltpu.make_async_copy(self.src, self.out.at[me], self.own_sem)
        self.own.start()
        for k in range(self.chunks):
            self.across(k, 0, me).start()

            @pl.when(z < NZ - 1)
            def _():
                self.up(k, 0).start()

            @pl.when(z > 0)
            def _():
                self.down(k, 0).start()

            self.over(k, 0, me).start()

    def line(self, k, s):
        z, me = self.z, self.me

        @pl.when(z >= s)
        def _():
            b = me - 4 * s
            self.up_in(k, s).wait_recv()
            self.across(k, s, b, b).start()

            @pl.when(z < NZ - 1)
            def _():
                self.up(k, s, b).start()

            self.over(k, s, b, b).start()

        @pl.when(z + s <= NZ - 1)
        def _():
            b = me + 4 * s
            self.dn_in(k, s).wait_recv()
            self.across(k, 3 + s, b, b).start()

            @pl.when(z > 0)
            def _():
                self.down(k, s, b).start()

            self.over(k, 3 + s, b, b).start()

    def from_side(self, k, slot):
        @pl.when(self.has(slot))
        def _():
            b = self.shift(self.side, slot)
            self.across(k, slot, b, b).wait_recv()
            self.over(k, 7 + slot, b, b).start()

    def round(self, s):
        if s < NZ:
            for k in range(self.chunks):
                self.line(k, s)
        for k in range(self.chunks):
            for slot in ((0,) if s == 1 else (s - 1, s + 2)):
                self.from_side(k, slot)

    def finish(self):
        z = self.z
        self.own.wait()
        for k in range(self.chunks):
            for slot in range(14):
                @pl.when(self.has(slot))
                def _():
                    b = self.core_block(slot)
                    self.over(k, slot, b, b).wait_recv()
                    self.over(k, slot, b, b).wait_send()
            for slot in range(7):
                @pl.when(self.has(slot))
                def _():
                    self.across(k, slot, self.me).wait_send()
            for s in range(NZ - 1):
                @pl.when((z >= s) & (z < NZ - 1))
                def _():
                    self.up(k, s).wait_send()

                @pl.when((z + s <= NZ - 1) & (z > 0))
                def _():
                    self.down(k, s).wait_send()


def gather_kernel(chunks, x_ref, o_ref, *sems):
    g = Gather(x_ref, o_ref, chunks, sems)
    enter(g.me, g.z, g.core, g.side)
    g.start()
    for s in range(1, NZ + 1):
        g.round(s)
    g.finish()


COST = pl.CostEstimate(flops=0, bytes_accessed=4_000_000, transcendentals=0)
ANY = pl.BlockSpec(memory_space=pl.ANY)


def gather16(v, cid, chunks=4):
    rows, width = v.shape
    return pl.pallas_call(
        functools.partial(gather_kernel, chunks),
        out_shape=jax.ShapeDtypeStruct((NE, rows, width), v.dtype),
        in_specs=[ANY],
        out_specs=ANY,
        scratch_shapes=Gather.scratch(chunks),
        compiler_params=pltpu.CompilerParams(collective_id=cid, has_side_effects=True),
        cost_estimate=COST,
        name="gather16",
    )(v)


def opening_kernel(dp, chunks, x_ref, small_ref, parts_ref, out_ref,
                   x_all, small_all, parts_head, out_head, small_dp, parts_dp, out_dp, *sems):
    ng = 9
    gx = Gather(x_ref, x_all, chunks, sems[:ng])
    gs = Gather(small_dp, small_all, 1, sems[ng:2 * ng])
    loc, ys, yr, ps, pr, os_, or_, pl_sem, ol_sem = sems[2 * ng:]
    me = gx.me
    plane = lax.axis_index("dp")
    rows = parts_ref.shape[1]
    enter_all(me, plane, dp)
    pairs = ((small_ref, small_dp.at[pl.ds(plane * rows, rows)]), (parts_ref, parts_dp.at[plane]),
             (out_ref, out_dp.at[plane]))

    def lift(i, r):
        src, dst = pairs[i]
        return pltpu.make_async_remote_copy(
            src_ref=src, dst_ref=dst, send_sem=ys.at[i, r], recv_sem=yr.at[i, r],
            device_id={"dp": (plane + r) % dp}, device_id_type=MESH)

    def landed(i, r):
        p = (plane - r + dp) % dp
        dst = (small_dp.at[pl.ds(p * rows, rows)], parts_dp.at[p], out_dp.at[p])[i]
        return pltpu.make_async_remote_copy(
            src_ref=dst, dst_ref=dst, send_sem=ys.at[i, r], recv_sem=yr.at[i, r],
            device_id={"dp": p}, device_id_type=MESH)

    def kept(i):
        src, dst = pairs[i]
        return pltpu.make_async_copy(src, dst, loc.at[i])

    for i in range(3):
        for r in range(1, dp):
            lift(i, r).start()
        kept(i).start()
    gx.start()
    gx.round(1)

    kept(0).wait()
    for r in range(1, dp):
        landed(0, r).wait_recv()
    gs.start()

    def part(r):
        h = (me + r) % NE
        return pltpu.make_async_remote_copy(
            src_ref=parts_dp.at[:, h], dst_ref=parts_head.at[:, me],
            send_sem=ps.at[r], recv_sem=pr.at[r],
            device_id={"expert": h}, device_id_type=MESH)

    def part_in(r):
        e = (me - r + NE) % NE
        return pltpu.make_async_remote_copy(
            src_ref=parts_head.at[:, e], dst_ref=parts_head.at[:, e],
            send_sem=ps.at[r], recv_sem=pr.at[r],
            device_id={"expert": e}, device_id_type=MESH)

    def part_kept():
        return pltpu.make_async_copy(parts_dp.at[:, me], parts_head.at[:, me], pl_sem)

    kept(1).wait()
    for r in range(1, dp):
        landed(1, r).wait_recv()
    for r in range(1, NE):
        part(r).start()
    part_kept().start()
    gx.round(2)

    def row(d):
        b = NE * d + me
        return pltpu.make_async_remote_copy(
            src_ref=out_dp.at[d], dst_ref=out_head.at[b % dp],
            send_sem=os_.at[d], recv_sem=or_.at[b % dp],
            device_id={"expert": b // dp}, device_id_type=MESH)

    def row_kept(d):
        b = NE * d + me
        return pltpu.make_async_copy(out_dp.at[d], out_head.at[b % dp], ol_sem.at[d])

    kept(2).wait()
    for r in range(1, dp):
        landed(2, r).wait_recv()
    for d in range(dp):
        home = (NE * d + me) // dp

        @pl.when(home != me)
        def _():
            row(d).start()

        @pl.when(home == me)
        def _():
            row_kept(d).start()

    gs.round(1)
    gx.round(3)
    gs.round(2)
    gx.round(4)
    gs.round(3)
    gs.round(4)

    def row_in(j):
        return pltpu.make_async_remote_copy(
            src_ref=out_head.at[j], dst_ref=out_head.at[j], send_sem=os_.at[j], recv_sem=or_.at[j],
            device_id={"expert": gx.core}, device_id_type=MESH)

    for r in range(1, NE):
        part_in(r).wait_recv()
        part(r).wait_send()
    part_kept().wait()
    for j in range(dp):
        @pl.when((dp * me + j) % NE != me)
        def _():
            row_in(j).wait_recv()
    for d in range(dp):
        home = (NE * d + me) // dp

        @pl.when(home != me)
        def _():
            row(d).wait_send()

        @pl.when(home == me)
        def _():
            row_kept(d).wait()
    for i in range(3):
        for r in range(1, dp):
            lift(i, r).wait_send()
    gx.finish()
    gs.finish()


def opening(dp, x, small, parts, out, cid, chunks=4):
    dma = pltpu.SemaphoreType.DMA
    rows, ws = small.shape
    bf = x.dtype
    wo = out.shape[1]
    shape = jax.ShapeDtypeStruct
    res = pl.pallas_call(
        functools.partial(opening_kernel, dp, chunks),
        out_shape=(
            shape((NE,) + x.shape, bf), shape((NE, dp * rows, ws), bf), shape((dp, NE) + parts.shape[1:], bf),
            shape((dp, rows, wo), bf),
            shape((dp * rows, ws), bf), shape((dp,) + parts.shape, bf), shape((dp, rows, wo), bf),
        ),
        in_specs=[ANY] * 4,
        out_specs=[ANY] * 7,
        scratch_shapes=Gather.scratch(chunks) + Gather.scratch(1) + [
            dma((3,)), dma((3, dp)), dma((3, dp)), dma((NE,)), dma((NE,)), dma((dp,)), dma((dp,)), dma, dma((dp,))],
        compiler_params=pltpu.CompilerParams(collective_id=cid, has_side_effects=True),
        cost_estimate=COST,
        name="opening",
    )(x, small, parts, out)
    return res[:4]


def order(z, i):
    a, b = (3, 2, 1, 0)[i], (3, 2, 0, 1)[i]
    return jnp.where(z == 0, a, jnp.where(z == 1, b, jnp.where(z == 2, 3 - b, 3 - a)))


class Scatter:
    def __init__(self, p_ref, o_ref, chunks, scratch):
        self.p, self.o, self.chunks = p_ref, o_ref, chunks
        (self.cbuf, self.own, self.xbuf, self.ubuf, self.dbuf, self.ld, self.cs, self.cr, self.xs, self.xr,
         self.us, self.ur, self.ds, self.dr) = scratch
        self.rows = o_ref.shape[0] // chunks
        self.me, self.z, self.x, self.c, self.core, self.side = place()

    @staticmethod
    def scratch(rows, width, chunks, bf):
        dma = pltpu.SemaphoreType.DMA
        return [pltpu.VMEM((n, rows, width), bf) for n in (8, 8, 4, 4, 4)] + [
            dma((8,)), dma((8, chunks)), dma((8, chunks))] + [dma((4, chunks))] * 6

    def rng(self, k):
        return pl.ds(k * self.rows, self.rows)

    def column(self, i, j):
        return 4 * order(self.z, i) + 2 * jnp.where(j == 0, 1 - self.x, self.x)

    def remote(self, src, dst, send, recv, to):
        return pltpu.make_async_remote_copy(
            src_ref=src, dst_ref=dst, send_sem=send, recv_sem=recv,
            device_id={"expert": to}, device_id_type=MESH)

    def over(self, i, j, k):
        n = 2 * i + j
        return self.remote(
            self.p.at[self.column(i, j) + 1 - self.c, self.rng(k)], self.cbuf.at[n, self.rng(k)],
            self.cs.at[n, k], self.cr.at[n, k], self.core)

    def load(self, i, j):
        n = 2 * i + j
        return pltpu.make_async_copy(self.p.at[self.column(i, j) + self.c], self.own.at[n], self.ld.at[n])

    def across(self, i, k):
        return self.remote(self.own.at[2 * i, self.rng(k)], self.xbuf.at[i, self.rng(k)],
                           self.xs.at[i, k], self.xr.at[i, k], self.side)

    def up(self, t, i, k):
        return self.remote(self.own.at[2 * i + 1, self.rng(k)], self.ubuf.at[t, self.rng(k)],
                           self.us.at[t, k], self.ur.at[t, k], self.me + 4)

    def down(self, t, i, k):
        return self.remote(self.own.at[2 * i + 1, self.rng(k)], self.dbuf.at[t, self.rng(k)],
                           self.ds.at[t, k], self.dr.at[t, k], self.me - 4)

    def start(self):
        for i in range(NZ):
            for j in range(2):
                self.load(i, j).start()
                for k in range(self.chunks):
                    self.over(i, j, k).start()

    def first(self, i):
        f32 = jnp.float32
        self.load(i, 0).wait()
        for k in range(self.chunks):
            self.over(i, 0, k).wait_recv()
            s = self.rng(k)
            self.own[2 * i, s] = (
                self.own[2 * i, s].astype(f32) + self.cbuf[2 * i, s].astype(f32)).astype(self.own.dtype)
            self.across(i, k).start()

    def second(self, i):
        f32 = jnp.float32
        z, own, o = self.z, self.own, self.o
        t = order(z, i)
        self.load(i, 1).wait()
        for k in range(self.chunks):
            s = self.rng(k)
            self.over(i, 1, k).wait_recv()
            self.across(i, k).wait_recv()

            def base():
                return (own[2 * i + 1, s].astype(f32) + self.cbuf[2 * i + 1, s].astype(f32)
                        + self.xbuf[i, s].astype(f32))

            if i < NZ - 1:
                @pl.when(t > z)
                def _():
                    @pl.when(z > 0)
                    def _():
                        self.up(t, i, k).wait_recv()
                        own[2 * i + 1, s] = (base() + self.ubuf[t, s].astype(f32)).astype(own.dtype)

                    @pl.when(z == 0)
                    def _():
                        own[2 * i + 1, s] = base().astype(own.dtype)

                    self.up(t, i, k).start()

                @pl.when(t < z)
                def _():
                    @pl.when(z < NZ - 1)
                    def _():
                        self.down(t, i, k).wait_recv()
                        own[2 * i + 1, s] = (base() + self.dbuf[t, s].astype(f32)).astype(own.dtype)

                    @pl.when(z == NZ - 1)
                    def _():
                        own[2 * i + 1, s] = base().astype(own.dtype)

                    self.down(t, i, k).start()
            else:
                @pl.when(z > 0)
                def _():
                    self.up(t, i, k).wait_recv()

                @pl.when(z < NZ - 1)
                def _():
                    self.down(t, i, k).wait_recv()

                @pl.when((z > 0) & (z < NZ - 1))
                def _():
                    o[s] = (base() + self.ubuf[t, s].astype(f32) + self.dbuf[t, s].astype(f32)).astype(o.dtype)

                @pl.when(z == 0)
                def _():
                    o[s] = (base() + self.dbuf[t, s].astype(f32)).astype(o.dtype)

                @pl.when(z == NZ - 1)
                def _():
                    o[s] = (base() + self.ubuf[t, s].astype(f32)).astype(o.dtype)

    def run(self):
        self.first(0)
        for i in range(NZ):
            if i + 1 < NZ:
                self.first(i + 1)
            self.second(i)

    def finish(self):
        z = self.z
        for k in range(self.chunks):
            for i in range(NZ):
                self.across(i, k).wait_send()
                for j in range(2):
                    self.over(i, j, k).wait_send()
                if i < NZ - 1:
                    t = order(z, i)

                    @pl.when(t > z)
                    def _():
                        self.up(t, i, k).wait_send()

                    @pl.when(t < z)
                    def _():
                        self.down(t, i, k).wait_send()


def scatter_kernel(chunks, p_ref, o_ref, *scratch):
    s = Scatter(p_ref, o_ref, chunks, scratch)
    enter(s.me, s.z, s.core, s.side)
    s.start()
    s.run()
    s.finish()


VMEM = pl.BlockSpec(memory_space=pltpu.VMEM)


def scatter16(p, cid, chunks=2, out_dtype=jnp.float32):
    _, rows, width = p.shape
    return pl.pallas_call(
        functools.partial(scatter_kernel, chunks),
        out_shape=jax.ShapeDtypeStruct((rows, width), out_dtype),
        in_specs=[ANY],
        out_specs=VMEM,
        scratch_shapes=Scatter.scratch(rows, width, chunks, p.dtype),
        compiler_params=pltpu.CompilerParams(
            collective_id=cid, has_side_effects=True, vmem_limit_bytes=32 * 1024 * 1024),
        cost_estimate=COST,
        name="scatter16",
    )(p)


def return_kernel(dp, chunks, p_ref, parts_ref, rows_ref, o_ref, parts_in, rows_in, parts_far, rows_far, *scratch):
    ns = 14
    s = Scatter(p_ref, o_ref, chunks, scratch[:ns])
    ps, pr, os_, or_, pl_sem, ol_sem, ys, yr = scratch[ns:]
    me = s.me
    plane = lax.axis_index("dp")
    enter_all(me, plane, dp)

    def part(r):
        e = (me + r) % NE
        return pltpu.make_async_remote_copy(
            src_ref=parts_ref.at[:, e], dst_ref=parts_in.at[:, me],
            send_sem=ps.at[r], recv_sem=pr.at[r],
            device_id={"expert": e}, device_id_type=MESH)

    def part_in(r):
        h = (me - r + NE) % NE
        return pltpu.make_async_remote_copy(
            src_ref=parts_in.at[:, h], dst_ref=parts_in.at[:, h],
            send_sem=ps.at[r], recv_sem=pr.at[r],
            device_id={"expert": h}, device_id_type=MESH)

    def part_kept():
        return pltpu.make_async_copy(parts_ref.at[:, me], parts_in.at[:, me], pl_sem)

    def row(j):
        b = dp * me + j
        return pltpu.make_async_remote_copy(
            src_ref=rows_ref.at[j], dst_ref=rows_in.at[b // NE],
            send_sem=os_.at[j], recv_sem=or_.at[b // NE],
            device_id={"expert": b % NE}, device_id_type=MESH)

    def row_kept(j):
        b = dp * me + j
        return pltpu.make_async_copy(rows_ref.at[j], rows_in.at[b // NE], ol_sem.at[j])

    def row_in(d):
        return pltpu.make_async_remote_copy(
            src_ref=rows_in.at[d], dst_ref=rows_in.at[d], send_sem=os_.at[d], recv_sem=or_.at[d],
            device_id={"expert": s.core}, device_id_type=MESH)

    def lift(i, r):
        to = (plane + r) % dp
        src, dst = ((parts_in.at[to], parts_far.at[r - 1]), (rows_in.at[to], rows_far.at[r - 1]))[i]
        return pltpu.make_async_remote_copy(
            src_ref=src, dst_ref=dst, send_sem=ys.at[i, r], recv_sem=yr.at[i, r],
            device_id={"dp": to}, device_id_type=MESH)

    s.start()
    for r in range(1, NE):
        part(r).start()
    part_kept().start()
    for j in range(dp):
        @pl.when((dp * me + j) % NE != me)
        def _():
            row(j).start()

        @pl.when((dp * me + j) % NE == me)
        def _():
            row_kept(j).start()
    s.first(0)
    s.first(1)
    s.second(0)
    for r in range(1, NE):
        part_in(r).wait_recv()
    part_kept().wait()
    for j in range(dp):
        @pl.when((dp * me + j) % NE == me)
        def _():
            row_kept(j).wait()
    for d in range(dp):
        @pl.when((NE * d + me) // dp != me)
        def _():
            row_in(d).wait_recv()
    for i in range(2):
        for r in range(1, dp):
            lift(i, r).start()
    s.first(2)
    s.second(1)
    s.first(3)
    s.second(2)
    s.second(3)
    for i in range(2):
        for r in range(1, dp):
            lift(i, r).wait_recv()
            lift(i, r).wait_send()
    for r in range(1, NE):
        part(r).wait_send()
    for j in range(dp):
        @pl.when((dp * me + j) % NE != me)
        def _():
            row(j).wait_send()
    s.finish()


def returning(dp, p, parts, rows, cid, chunks=2):
    dma = pltpu.SemaphoreType.DMA
    _, n, width = p.shape
    shape = jax.ShapeDtypeStruct
    out, parts_in, rows_in, parts_far, rows_far = pl.pallas_call(
        functools.partial(return_kernel, dp, chunks),
        out_shape=(
            shape((n, width), jnp.float32), shape(parts.shape, parts.dtype), shape(rows.shape, rows.dtype),
            shape((dp - 1,) + parts.shape[1:], parts.dtype), shape((dp - 1,) + rows.shape[1:], rows.dtype)),
        in_specs=[ANY] * 3,
        out_specs=[VMEM] + [ANY] * 4,
        scratch_shapes=Scatter.scratch(n, width, chunks, p.dtype) + [
            dma((NE,)), dma((NE,)), dma((dp,)), dma((dp,)), dma, dma((dp,)), dma((2, dp)), dma((2, dp))],
        compiler_params=pltpu.CompilerParams(
            collective_id=cid, has_side_effects=True, vmem_limit_bytes=48 * 1024 * 1024),
        cost_estimate=COST,
        name="returning",
    )(p, parts, rows)
    plane = lax.axis_index("dp")

    def total(near, far):
        own = lax.dynamic_index_in_dim(near, plane, 0, False).astype(jnp.float32)
        return own + jnp.sum(far.astype(jnp.float32), axis=0)

    return out, total(parts_in, parts_far), total(rows_in, rows_far)


def closing_kernel(dp, chunks, p_ref, o_ref, far_ref, *scratch):
    ns = 14
    s = Scatter(p_ref, o_ref, chunks, scratch[:ns])
    ys, yr = scratch[ns:]
    plane = lax.axis_index("dp")
    rows = o_ref.shape[0] // dp
    barrier = pltpu.get_barrier_semaphore()
    for r in range(1, dp):
        pl.semaphore_signal(barrier, inc=1, device_id={"dp": (plane + r) % dp}, device_id_type=MESH)
    z = s.z
    for other in (s.core, s.side):
        pl.semaphore_signal(barrier, inc=1, device_id={"expert": other}, device_id_type=MESH)

    @pl.when(z < NZ - 1)
    def _():
        pl.semaphore_signal(barrier, inc=1, device_id={"expert": s.me + 4}, device_id_type=MESH)

    @pl.when(z > 0)
    def _():
        pl.semaphore_signal(barrier, inc=1, device_id={"expert": s.me - 4}, device_id_type=MESH)

    pl.semaphore_wait(barrier, dp + 1 + (z < NZ - 1).astype(jnp.int32) + (z > 0).astype(jnp.int32))

    def lift(r):
        to = (plane + r) % dp
        return pltpu.make_async_remote_copy(
            src_ref=o_ref.at[pl.ds(pl.multiple_of(to * rows, 16), rows)], dst_ref=far_ref.at[r - 1],
            send_sem=ys.at[r], recv_sem=yr.at[r],
            device_id={"dp": to}, device_id_type=MESH)

    s.start()
    s.run()
    for r in range(1, dp):
        lift(r).start()
    s.finish()
    for r in range(1, dp):
        lift(r).wait_recv()
        lift(r).wait_send()


def closing(dp, p, cid):
    dma = pltpu.SemaphoreType.DMA
    _, n, width = p.shape
    shape = jax.ShapeDtypeStruct
    near, far = pl.pallas_call(
        functools.partial(closing_kernel, dp, 1),
        out_shape=(shape((n, width), p.dtype), shape((dp - 1, n // dp, width), p.dtype)),
        in_specs=[ANY],
        out_specs=[VMEM, VMEM],
        scratch_shapes=Scatter.scratch(n, width, 1, p.dtype) + [dma((dp,)), dma((dp,))],
        compiler_params=pltpu.CompilerParams(
            collective_id=cid, has_side_effects=True, vmem_limit_bytes=32 * 1024 * 1024),
        cost_estimate=COST,
        name="closing",
    )(p)
    own = lax.dynamic_slice_in_dim(near, lax.axis_index("dp") * (n // dp), n // dp).astype(jnp.float32)
    return own + jnp.sum(far.astype(jnp.float32), axis=0)
BF = jnp.bfloat16
F32 = jnp.float32


def mm(a, b):
    return jnp.dot(a, b, preferred_element_type=F32)


def mm_t(a, b):
    return lax.dot_general(a, b, (((1,), (1,)), ((), ())), preferred_element_type=F32)


def silu_pair(gate_in):
    sigmoid = 1.0 / (1.0 + jnp.exp(-gate_in))
    return (gate_in * sigmoid, sigmoid * (1.0 + gate_in * (1.0 - sigmoid)))


TILE = 256
WIDE = 512
SHARE = 176


def mixture_kernel(pick_ref, mix_ref, dy_ref, slot_row, slot_col, valid_ref, gu_ref, wd_ref, fan_ref, sd_ref,
                   out_ref, dh_ref, rows_ref, deo_ref, hid_ref, dgu_ref, sh_ref, ds_ref,
                   act_buf, slo_buf):
    tokens, width = mix_ref.shape
    groups = tokens // 256
    slots = 128
    ff = hid_ref.shape[1]

    def lanes(j):
        return pl.ds(pl.multiple_of(j * WIDE, WIDE), WIDE)

    mix = mix_ref[...]
    fanned = mm_t(mix, fan_ref[:TILE, :])
    s_up = mm_t(mix, fan_ref[TILE:, :])
    s_act, s_slope = silu_pair(fanned)
    s_hidden = (s_act * s_up).astype(BF)
    sh_ref[...] = s_hidden
    logits = fanned[:, SHARE:SHARE + 16]
    lane16 = lax.broadcasted_iota(jnp.int32, (tokens, 16), 1).astype(F32)
    routes = dy_ref[:, width:width + 16].astype(F32)
    mask = lane16 < 0
    for k in range(6):
        mask = mask | (lane16 == routes[:, k:k + 1])
    held = jnp.where(mask, logits, -1e30)
    raised = jnp.where(mask, jnp.exp(held - jnp.max(held, axis=1, keepdims=True)), 0.0)
    soft = raised / jnp.sum(raised, axis=1, keepdims=True)
    gate = jnp.sum(soft * pick_ref[:, :16], axis=1, keepdims=True) * valid_ref[...]
    dy = dy_ref[:, :width]
    d_sh = mm_t(dy, sd_ref[...])
    ds_ref[:, :TILE] = (d_sh * s_up * s_slope).astype(BF)
    ds_ref[:, TILE:] = (d_sh * s_act).astype(BF)

    to_slot, to_token = [], []
    for g in range(groups):
        row = slot_row[:, g * 256:(g + 1) * 256]
        col = slot_col[g * 256:(g + 1) * 256, :]
        to_slot.append((lax.broadcasted_iota(jnp.int32, (slots, 256), 0) == row).astype(BF))
        to_token.append((lax.broadcasted_iota(jnp.int32, (256, slots), 1) == col).astype(BF))

    def dispatch(j, _):
        for g in range(groups):
            t = pl.ds(g * 256, 256)
            s = pl.ds(g * slots, slots)
            rows_ref[s, lanes(j)] = mm(to_slot[g], mix_ref[t, lanes(j)]).astype(BF)
            gated = (gate[g * 256:(g + 1) * 256] * dy_ref[t, lanes(j)].astype(F32)).astype(BF)
            deo_ref[s, lanes(j)] = mm(to_slot[g], gated).astype(BF)
        return 0

    lax.fori_loop(0, width // WIDE, dispatch, 0)

    def fan_in(start, size):
        both = mm(rows_ref[...], gu_ref[:, pl.ds(start, size)])
        for i in range(size // TILE):
            gate_in, up_in = both[:, i * TILE:i * TILE + 128], both[:, i * TILE + 128:(i + 1) * TILE]
            act, slope = silu_pair(gate_in)
            half = pl.ds(pl.multiple_of(start // 2 + i * 128, 128), 128)
            hid_ref[:, half] = (act * up_in).astype(BF)
            act_buf[:, half] = act
            slo_buf[:, half] = up_in * slope

    def fan_loop(j, _):
        fan_in(pl.multiple_of(j * WIDE, WIDE), WIDE)
        return 0

    lax.fori_loop(0, 2 * ff // WIDE, fan_loop, 0)
    if 2 * ff % WIDE:
        fan_in(2 * ff // WIDE * WIDE, 2 * ff % WIDE)

    def fan_out(j, d_gates):
        eo = mm(hid_ref[...], wd_ref[:, lanes(j)]).astype(BF)
        shared = mm(s_hidden, sd_ref[:, lanes(j)])
        picked = jnp.concatenate(
            [mm(to_token[g], eo[g * slots:(g + 1) * slots]) for g in range(groups)], axis=0)
        out_ref[:, lanes(j)] = (shared + gate * picked).astype(BF)
        return d_gates + jnp.sum(dy_ref[:, lanes(j)].astype(F32) * picked, axis=1, keepdims=True)

    d_gates = lax.fori_loop(0, width // WIDE, fan_out, jnp.zeros((tokens, 1), F32))

    def back_out(start, size):
        cols = pl.ds(start, size)
        d_eh = mm_t(deo_ref[...], wd_ref[cols, :])
        dg = (d_eh * slo_buf[:, cols]).astype(BF)
        du = (d_eh * act_buf[:, cols]).astype(BF)
        for i in range(size // 128):
            at = pl.multiple_of(2 * start + i * TILE, TILE)
            dgu_ref[:, pl.ds(at, 128)] = dg[:, i * 128:(i + 1) * 128]
            dgu_ref[:, pl.ds(at + 128, 128)] = du[:, i * 128:(i + 1) * 128]

    def back_loop(j, _):
        back_out(pl.multiple_of(j * WIDE, WIDE), WIDE)
        return 0

    lax.fori_loop(0, ff // WIDE, back_loop, 0)
    if ff % WIDE:
        back_out(ff // WIDE * WIDE, ff % WIDE)

    d_s = ds_ref[...]

    def back_in(j, _):
        d_rows = mm_t(dgu_ref[...], gu_ref[lanes(j), :]).astype(BF)
        shared = mm(d_s, fan_ref[:, lanes(j)])
        taken = jnp.concatenate(
            [mm(to_token[g], d_rows[g * slots:(g + 1) * slots]) for g in range(groups)], axis=0)
        dh_ref[:, lanes(j)] = (shared + taken).astype(BF)
        return 0

    lax.fori_loop(0, width // WIDE, back_in, 0)
    high = d_gates.astype(BF).astype(F32)
    tail = high * pick_ref[:, :128] + (d_gates - high) * pick_ref[:, 128:]
    dh_ref[:, width:] = tail.astype(BF)


def mixture(pick, mix, packed, slot_row, slot_col, valid, gu, wd, fan, sd, step=512):
    total, width = mix.shape
    steps = total // step
    ff = wd.shape[0]
    rows = total // 2
    shape = jax.ShapeDtypeStruct
    once = pl.Buffered(buffer_count=1)

    def whole(v):
        return pl.BlockSpec(v.shape, lambda i: (0, 0), pipeline_mode=once)

    def tokens(w):
        return pl.BlockSpec((step, w), lambda i: (i, 0))

    def slots(w):
        return pl.BlockSpec((step // 2, w), lambda i: (i, 0))

    return pl.pallas_call(
        mixture_kernel,
        grid=(steps,),
        out_shape=(
            shape((total, width), BF), shape((total, width + 128), BF), shape((rows, width), BF),
            shape((rows, width), BF), shape((rows, ff), BF), shape((rows, 2 * ff), BF),
            shape((total, TILE), BF), shape((total, 2 * TILE), BF)),
        in_specs=[whole(pick), tokens(width), tokens(width + 128), pl.BlockSpec((1, step), lambda i: (0, i)),
                  tokens(1), tokens(1), whole(gu), whole(wd), whole(fan), whole(sd)],
        out_specs=[tokens(width), tokens(width + 128), slots(width), slots(width), slots(ff), slots(2 * ff),
                   tokens(TILE), tokens(2 * TILE)],
        scratch_shapes=[pltpu.VMEM((step // 2, ff), F32), pltpu.VMEM((step // 2, ff), F32)],
        compiler_params=pltpu.CompilerParams(vmem_limit_bytes=60 * 1024 * 1024),
        cost_estimate=pl.CostEstimate(flops=60_000_000_000, bytes_accessed=60_000_000, transcendentals=0),
        name="mixture",
    )(pick, mix, packed, slot_row, slot_col, valid, gu, wd, fan, sd)


H = 16
QK_NOPE = 128
ROPE = 64
V_DIM = 128
KV_RANK = 512
GROUPS = 16
EPSILON = 1e-06
ROTARY_BASE = 10000.0


def product(left_side, right_side):
    return jnp.dot(left_side, right_side, preferred_element_type=F32)


def product_lead(left_side, right_side):
    return lax.dot_general(
        left_side, right_side, (((0,), (0,)), ((), ())), preferred_element_type=F32
    )


def product_trail(left_side, right_side):
    return lax.dot_general(
        left_side, right_side, (((1,), (1,)), ((), ())), preferred_element_type=F32
    )


def rotary_tables(positions):
    half_width = ROPE // 2
    frequency = ROTARY_BASE ** (-jnp.arange(half_width, dtype=F32) * 2.0 / ROPE)
    angles = positions[:, None] * frequency[None, :]
    return (jnp.cos(angles), jnp.sin(angles))


def rotate(values, cosine, sine_table):
    first_half, second_half = jnp.split(values, 2, axis=-1)
    return jnp.concatenate(
        [
            first_half * cosine - second_half * sine_table,
            second_half * cosine + first_half * sine_table,
        ],
        axis=-1,
    )


def norm_forward(values, gains):
    factor = lax.rsqrt(jnp.mean(values * values, axis=-1, keepdims=True) + EPSILON)
    normed = values * factor
    return (normed * gains, normed, factor)


def norm_backward(gradient, normed, factor, gains):
    gain_grad = jnp.sum(gradient * normed, axis=0)
    scaled = gradient * gains
    return (
        factor * (scaled - normed * jnp.mean(scaled * normed, axis=-1, keepdims=True)),
        gain_grad,
    )


def selected_experts(routes):
    chosen = routes[:, :, None] == jnp.arange(GROUPS, dtype=routes.dtype)
    return jnp.any(chosen, axis=1)


def masked_softmax(logits, mask):
    held = jnp.where(mask, logits, -1e30)
    peak = jnp.max(held, axis=-1, keepdims=True)
    raised = jnp.where(mask, jnp.exp(held - peak), 0.0)
    return raised / jnp.sum(raised, axis=-1, keepdims=True)


def per_device(
    layer_input,
    out_cotangent,
    lengths,
    routes,
    attn_gain,
    query_weight,
    latent_weight,
    latent_gain,
    expand_weight,
    output_weight,
    mixer_gain,
    router_weight,
    gate_weight,
    up_weight,
    down_weight,
    shared_gate,
    shared_up,
    shared_down,
):
    dp = lax.axis_size("dp")
    me = lax.axis_index("expert")
    plane = lax.axis_index("dp")
    batches, _, here, width = layer_input.shape
    own = batches * here
    total = own * GROUPS
    seq_total = here * GROUPS
    rows_w = query_weight.shape[0]
    rows_l = expand_weight.shape[0]
    scale_factor = float(QK_NOPE + ROPE) ** (-0.5)

    x_own = layer_input.reshape(own, width)
    latent_column = jnp.zeros((rows_w,), BF).at[:rows_l].set(latent_gain)
    small = jnp.concatenate(
        [
            latent_weight,
            router_weight,
            attn_gain[:, None],
            mixer_gain[:, None],
            latent_column[:, None],
            jnp.zeros((rows_w, 640 - 595), BF),
        ],
        axis=1,
    )
    query_parts = query_weight.reshape(rows_w, H, QK_NOPE + ROPE).transpose(1, 0, 2)
    expand_parts = expand_weight.reshape(rows_l, H, QK_NOPE + V_DIM).transpose(1, 0, 2)
    parts = jnp.concatenate([query_parts, expand_parts.reshape(H, rows_w, ROPE)], axis=2)
    x_all, small, parts_head, output_head = opening(dp, x_own, small, parts, output_weight, 1)
    x_all = x_all.reshape(total, width)
    small = small.reshape(GROUPS, dp, rows_w, 640).swapaxes(0, 1).reshape(width, 640)
    latent_full = small[:, :576]
    router_full = small[:, 576:592]
    gain_attn = small[:, 592].astype(F32)
    gain_mixer = small[:, 593].astype(F32)
    gain_latent = small[:, 594].reshape(dp * GROUPS, rows_w)[:, :rows_l].reshape(-1).astype(F32)
    query_head = parts_head[..., : QK_NOPE + ROPE].reshape(width, QK_NOPE + ROPE)
    expand_head = parts_head[..., QK_NOPE + ROPE :].reshape(KV_RANK, QK_NOPE + V_DIM)
    output_head = output_head.reshape(V_DIM, width)

    ff = gate_weight.shape[2]
    fan_own = jnp.stack(
        [gate_weight[0].reshape(-1, ff // 128, 128), up_weight[0].reshape(-1, ff // 128, 128)], axis=2
    ).reshape(-1, 2 * ff)
    share_own = jnp.concatenate([shared_gate.T, shared_up.T, shared_down], axis=0)
    share_width = shared_down.shape[0]
    fan_full = lax.all_gather(fan_own, "dp", axis=0, tiled=True)
    down_full = lax.all_gather(down_weight[0], "dp", axis=0, tiled=True)
    share_full = lax.all_gather(share_own, "dp", axis=0)
    share_full = share_full.transpose(1, 0, 2).reshape(3 * share_width, width)

    seq_lengths = lengths.reshape(batches)
    own_positions = me * here + jnp.arange(here, dtype=jnp.int32)
    valid_own = (own_positions[None, :] < seq_lengths[:, None]).reshape(own).astype(F32)
    all_positions = jnp.arange(seq_total, dtype=jnp.int32).reshape(GROUPS, 1, here)
    valid_all = jnp.broadcast_to(
        all_positions < seq_lengths[None, :, None], (GROUPS, batches, here)
    ).reshape(total)
    key_positions = jnp.arange(seq_total, dtype=jnp.int32)
    cosine, sine_table = rotary_tables(key_positions.astype(F32))
    cosine_own = lax.dynamic_slice_in_dim(cosine, me * here, here)
    sine_own = lax.dynamic_slice_in_dim(sine_table, me * here, here)

    def by_sequence(v):
        return v.reshape(GROUPS, batches, here, v.shape[-1]).swapaxes(0, 1).reshape(batches, seq_total, -1)

    def by_device(v):
        return v.reshape(batches, GROUPS, here, v.shape[-1]).swapaxes(0, 1).reshape(total, -1)

    grad_own = out_cotangent.reshape(own, width) * valid_own[:, None].astype(BF)
    routes_own = routes.reshape(own, -1)
    packed = jnp.concatenate(
        [grad_own, routes_own.astype(BF), jnp.zeros((own, 128 - routes_own.shape[1]), BF)], axis=1
    )
    packed = lax.all_gather(packed, "expert", axis=0, tiled=True)
    routes_all = packed[:, width : width + routes_own.shape[1]].astype(jnp.int32)
    taken = jnp.any(routes_all == me, axis=1) & valid_all
    places = jnp.cumsum(taken.reshape(-1, here).astype(jnp.int32), axis=1) - 1
    places = places + 32 * (jnp.arange(places.shape[0], dtype=jnp.int32) % 4)[:, None]
    slot = jnp.where(taken, places.reshape(total), -1)

    hidden_all = norm_forward(x_all.astype(F32), gain_attn)[0].astype(BF)
    raw = product(hidden_all, jnp.concatenate([query_head, latent_full], axis=1))
    raw = by_sequence(raw)
    query_nope = raw[..., :QK_NOPE].astype(BF)
    query_rope = rotate(raw[..., QK_NOPE : QK_NOPE + ROPE], cosine, sine_table).astype(BF)
    query = jnp.concatenate([query_nope, query_rope], axis=-1)
    latent_raw = raw[..., QK_NOPE + ROPE :]
    latent = norm_forward(latent_raw[..., :KV_RANK], gain_latent)[0].astype(BF)
    key_rope = rotate(latent_raw[..., KV_RANK:], cosine, sine_table).astype(BF)
    expanded = product(latent, expand_head).astype(BF)
    key = jnp.concatenate([expanded[..., :QK_NOPE], key_rope], axis=-1)
    values = expanded[..., QK_NOPE:]
    allowed = (key_positions[None, None, :] <= key_positions[None, :, None]) & (
        key_positions[None, None, :] < seq_lengths[:, None, None]
    )

    def score(query, key):
        raw_scores = jnp.einsum("btd,bsd->bts", query, key, preferred_element_type=F32)
        return jnp.where(allowed, raw_scores * scale_factor, -1e30)

    scores = score(query, key)
    peak = jnp.max(scores, axis=-1, keepdims=True)
    log_total = peak + jnp.log(jnp.sum(jnp.exp(scores - peak), axis=-1, keepdims=True))
    probs_low = jnp.exp(scores - log_total).astype(BF)
    attended = jnp.einsum("bts,bsd->btd", probs_low, values, preferred_element_type=F32).astype(BF)
    attended_rows = by_device(attended)
    attn_part = product(attended_rows, output_head).astype(BF).reshape(GROUPS, own, width)
    attn_out = scatter16(attn_part, 2)

    x_wide = x_own.astype(F32)
    middle = x_wide + attn_out
    normed_mix, unit_mix, factor_mix = norm_forward(middle, gain_mixer)
    hidden_mix = normed_mix.astype(BF)
    mix_all = gather16(hidden_mix, 3).reshape(total, width)

    pad = TILE - share_width
    fan_share = jnp.concatenate(
        [share_full[:share_width], router_full.T, jnp.zeros((pad - GROUPS, width), BF),
         share_full[share_width : 2 * share_width], jnp.zeros((pad, width), BF)], axis=0)
    down_share = jnp.concatenate([share_full[2 * share_width :], jnp.zeros((pad, width), BF)], axis=0)
    lane = jnp.arange(128)[None, :]
    pick = jnp.concatenate([lane == me, lane == me + GROUPS], axis=1).astype(F32)
    out_part, mix_part, rows, grad_result, hidden, grad_fan_in, share_hidden, grad_share_in = mixture(
        pick, mix_all, packed, slot[None, :], slot[:, None], valid_all.astype(F32)[:, None],
        fan_full, down_full, fan_share, down_share)
    grad_down = product_lead(hidden, grad_result).astype(BF)
    grad_fan = product_lead(rows, grad_fan_in).astype(BF)
    grad_share_fan = product_lead(grad_share_in, mix_all).astype(BF)
    grad_share_down = product_lead(share_hidden, packed[:, :width]).astype(BF)
    mix_part, grad_down, grad_fan = lax.optimization_barrier((mix_part, grad_down, grad_fan))
    mix_sum = scatter16(mix_part.reshape(GROUPS, own, width + 128), 5)
    mixed = scatter16(out_part.reshape(GROUPS, own, width), 4)
    layer_output = valid_own[:, None] * (middle + mixed)

    out_down = lax.psum_scatter(grad_down, "dp", scatter_dimension=0, tiled=True)
    out_fan = lax.psum_scatter(grad_fan, "dp", scatter_dimension=0, tiled=True)
    out_fan = out_fan.reshape(-1, ff // 128, 2, 128)
    grad_share = jnp.concatenate(
        [grad_share_fan[:share_width], grad_share_fan[TILE : TILE + share_width], grad_share_down[:share_width]],
        axis=0)
    grad_share = grad_share.reshape(3 * share_width, dp, width // dp).swapaxes(0, 1)
    out_share = lax.psum_scatter(grad_share, "dp", scatter_dimension=0, tiled=False).astype(F32)

    mask_own = selected_experts(routes_own)
    soft_own = masked_softmax(product(hidden_mix, router_full), mask_own)
    grad_masked = (mix_sum[:, width : width + GROUPS] + mix_sum[:, width + GROUPS : width + 2 * GROUPS])
    grad_masked = grad_masked * valid_own[:, None]
    grad_logits = soft_own * (grad_masked - jnp.sum(grad_masked * soft_own, axis=1, keepdims=True))
    grad_logits = grad_logits.astype(BF)
    grad_mix = mix_sum[:, :width] + product_trail(grad_logits, router_full)
    grad_middle_norm, grad_gain_mixer = norm_backward(grad_mix, unit_mix, factor_mix, gain_mixer)
    grad_middle = grad_own.astype(F32) + grad_middle_norm

    grad_attn_all = gather16(grad_middle.astype(BF), 6).reshape(total, width)
    grad_output = product_lead(attended_rows, grad_attn_all)
    grad_attended = by_sequence(product_trail(grad_attn_all, output_head).astype(BF))
    probs = jnp.exp(score(query, key) - log_total)
    probs_low = probs.astype(BF)
    grad_probs = jnp.einsum("btd,bsd->bts", grad_attended, values, preferred_element_type=F32)
    inner_sum = jnp.sum(grad_probs * probs, axis=-1, keepdims=True)
    grad_scores = (probs * (grad_probs - inner_sum)).astype(BF)
    grad_query = jnp.einsum("bts,bsd->btd", grad_scores, key, preferred_element_type=F32) * scale_factor
    grad_key = jnp.einsum("bts,btd->bsd", grad_scores, query, preferred_element_type=F32) * scale_factor
    grad_values = jnp.einsum("bts,btd->bsd", probs_low, grad_attended, preferred_element_type=F32)
    grad_expanded = jnp.concatenate([grad_key[..., :QK_NOPE], grad_values], axis=-1).astype(BF)
    grad_expanded = grad_expanded.reshape(total, -1)
    grad_expand = product_lead(latent.reshape(total, -1), grad_expanded)
    grad_latent = product_trail(grad_expanded, expand_head)
    grad_query = jnp.concatenate(
        [grad_query[..., :QK_NOPE], rotate(grad_query[..., QK_NOPE:], cosine, -sine_table)], axis=-1
    ).astype(BF)
    grad_query = by_device(grad_query)
    grad_query_w = product_lead(hidden_all, grad_query)
    back_part = product_trail(grad_query, query_head).astype(BF)
    latent_part = jnp.concatenate(
        [grad_latent.astype(BF).reshape(batches, seq_total, -1), grad_key[..., QK_NOPE:].astype(BF),
         jnp.zeros((batches, seq_total, 64), BF)], axis=-1)
    back_part = jnp.concatenate([back_part, by_device(latent_part)], axis=1)
    parts_grad = jnp.concatenate(
        [grad_query_w.astype(BF), grad_expand.astype(BF).reshape(width, ROPE)], axis=1)
    back_sum, out_parts, out_output = returning(
        dp, back_part.reshape(GROUPS, own, back_part.shape[1]),
        parts_grad.reshape(dp, GROUPS, rows_w, TILE), grad_output.astype(BF).reshape(dp, rows_w, width), 7)
    out_query = out_parts[..., : QK_NOPE + ROPE].transpose(1, 0, 2).reshape(rows_w, -1)
    out_expand = out_parts[..., QK_NOPE + ROPE :].reshape(H, rows_l, QK_NOPE + V_DIM)
    out_expand = out_expand.transpose(1, 0, 2).reshape(rows_l, -1)

    x_normed, unit_attn, factor_attn = norm_forward(x_wide, gain_attn)
    hidden_own = x_normed.astype(BF)
    latent_own = product(hidden_own, latent_full)
    _, unit_latent, factor_latent = norm_forward(latent_own[:, :KV_RANK], gain_latent)
    grad_latent_in, grad_gain_latent = norm_backward(
        back_sum[:, width : width + KV_RANK], unit_latent, factor_latent, gain_latent
    )
    grad_rope = back_sum[:, width + KV_RANK : width + KV_RANK + ROPE].reshape(batches, here, ROPE)
    grad_rope = rotate(grad_rope, cosine_own, -sine_own).reshape(own, ROPE)
    grad_latent_raw = jnp.concatenate([grad_latent_in, grad_rope], axis=1).astype(BF)
    grad_hidden_attn = back_sum[:, :width] + product_trail(grad_latent_raw, latent_full)
    grad_input_norm, grad_gain_attn = norm_backward(grad_hidden_attn, unit_attn, factor_attn, gain_attn)
    grad_input = grad_middle + grad_input_norm

    latent_rows = grad_gain_latent.reshape(dp * GROUPS, rows_l)
    latent_rows = jnp.pad(latent_rows, ((0, 0), (0, rows_w - rows_l))).reshape(width, 1)
    tokens_side = jnp.concatenate([hidden_own, hidden_mix], axis=0)
    grads_side = jnp.concatenate(
        [jnp.pad(grad_latent_raw, ((0, 0), (0, 64))), jnp.pad(grad_logits, ((0, 0), (576, 640 - 592)))], axis=0)
    lane = jnp.arange(640)[None, :]
    small_grad = product_lead(tokens_side, grads_side)
    small_grad = small_grad + jnp.where(lane == 592, grad_gain_attn[:, None], 0.0)
    small_grad = small_grad + jnp.where(lane == 593, grad_gain_mixer[:, None], 0.0)
    small_grad = (small_grad + jnp.where(lane == 594, latent_rows, 0.0)).astype(BF)
    small_grad = small_grad.reshape(dp, GROUPS, rows_w, 640).swapaxes(0, 1).reshape(GROUPS, dp * rows_w, 640)
    small_sum = closing(dp, small_grad, 9)

    def as_input(v):
        return v.reshape(batches, 1, here, width)

    return (
        as_input(layer_output),
        as_input(grad_input),
        small_sum[:, 592],
        out_query,
        small_sum[:, :576],
        small_sum[:rows_l, 594],
        out_expand,
        out_output,
        small_sum[:, 593],
        small_sum[:, 576:592],
        out_fan[:, :, 0].reshape(-1, ff).astype(F32)[None],
        out_fan[:, :, 1].reshape(-1, ff).astype(F32)[None],
        out_down.astype(F32)[None],
        out_share[:share_width].T,
        out_share[share_width : 2 * share_width].T,
        out_share[2 * share_width :],
    )


def solution(mesh):
    split = P(("dp", "expert"), None)
    line = P(("dp", "expert"))
    tokens = P(None, "dp", "expert", None)
    expert = P("expert", "dp", None)
    return jax.shard_map(
        per_device,
        mesh=mesh,
        in_specs=(
            tokens, tokens, P(None, "dp"), tokens, line, split, split, line, split, split, line, split,
            expert, expert, expert, P("dp", "expert"), P("dp", "expert"), P("expert", "dp"),
        ),
        out_specs=(
            tokens, tokens, line, split, split, line, split, split, line, split,
            expert, expert, expert, P("dp", "expert"), P("dp", "expert"), P("expert", "dp"),
        ),
        check_vma=False,
    )
```

time: 1280 us -> 1020 us (0.80)
  waiting for transfers between devices: 242 us -> 18.2 us
  Pallas kernels: 409 us -> 600 us
  matrix products: 277 us -> 114 us
  blocking collectives: 71 us -> 0 us
  local copies, waits for them, and re-layouts: 114 us -> 157 us
  starting transfers between devices: 36 us -> 0.71 us
  other arithmetic: 96.8 us -> 110 us
    pallas_call x0 -> x4, Pallas kernels: none -> 343 us  [the longest x1 134 us: opening(): pl.pallas_call(functools.partial(opening_kernel, dp, chunks), out_shape=(...]
    reduce_scatter x8 -> x2, waiting for transfers between devices: 156 us -> 0.01 us  [the longest x1 0.01 us: per_device(): lax.psum_scatter(grad_share, 'dp', scatter_dimension=0, tiled=False)]
    pallas_call x4 -> x3, Pallas kernels: 231 us -> 154 us  [scatter16(): pl.pallas_call(functools.partial(scatter_kernel, chunks), out_shape=jax.S...]
    pallas_call x3 -> x2, Pallas kernels: 178 us -> 103 us  [gather16(): pl.pallas_call(functools.partial(gather_kernel, chunks), out_shape=jax.Sh...]
    all_gather x6 -> x0, blocking collectives: 71 us -> none  [the longest x1 18.9 us: per_device(): lax.all_gather(query_head, 'dp', axis=0, tiled=True)]
    dot_general x11 -> x5, matrix products: 88.1 us -> 18.1 us  [product_trail(): lax.dot_general(left_side, right_side, (((1,), (1,)), ((), ())), preferre...]
    reduce_scatter x1, waiting for transfers between devices: 64.6 us -> 0.01 us  [per_device(): lax.psum_scatter(grad_down, 'dp', scatter_dimension=0, tiled=True)]
    dot_general x10 -> x5, matrix products: 71.8 us -> 21.4 us  [product(): return jnp.dot(left_side, right_side, preferred_element_type=F32)]
  transfers between devices with their start and end apart: 23 -> 7, of which waited for: 7 -> 1; matrix products, arithmetic and copies ran while one was open for 22% -> 28% of each run, Pallas kernels for 24% -> 50%
where the time goes in v2:
time: 1020 us
  Pallas kernels  600 us (59%)
  local copies, waits for them, and re-layouts  157 us (15%)
  matrix products  114 us (11%)
  other arithmetic  110 us (11%)
  waiting for transfers between devices  18.2 us (2%)
  between operations  16.1 us (2%)
    pallas_call x3, Pallas kernels, scatter16(): pl.pallas_call(functools.partial(scatter_kernel, chunks), out_shape=jax.S...  154 us
    pallas_call x1, Pallas kernels, opening(): pl.pallas_call(functools.partial(opening_kernel, dp, chunks), out_shape=(...  134 us
    pallas_call x2, Pallas kernels, gather16(): pl.pallas_call(functools.partial(gather_kernel, chunks), out_shape=jax.Sh...  103 us
    pallas_call x1, Pallas kernels, mixture(): pl.pallas_call(mixture_kernel, grid=(steps,), out_shape=(shape((total, wi...  93.9 us
    pallas_call x1, Pallas kernels, returning(): pl.pallas_call(functools.partial(return_kernel, dp, chunks), out_shape=(s...  81.9 us
    dot_general x8, matrix products, product_lead(): lax.dot_general(left_side, right_side, (((0,), (0,)), ((), ())), preferre...  55.1 us
    convert_element_type x1, other arithmetic, per_device(): out_fan[:, :, 1].reshape(-1, ff).astype(F32)[None]  39.3 us
    unnamed x201, local copies, waits for them, and re-layouts  39.2 us
  transfers between devices with their start and end apart: 7, of which 1 were waited for; matrix products, arithmetic and copies ran while one was open for 28% of the time, Pallas kernels for 50%

profile of v2, /device:TPU:0, one launch (start us, length us, event | category | flops | bytes accessed | tf_op | source)
XLA Modules:
  0.0 1015.2 jit_solution(10250294403698173990)
XLA Ops:
  27.9 14.9 %copy.253 = bf16[1024,11,2,128]{3,2,1,0:T(2,128)(2,1)} copy(bf16[1024,11,2,128]{0,3,1,2:T(8,128)(2,1)} %pad_maximum_fusion.1) | data formatting | bytes 11534336 | tf_op jit(solution)/shard_map/stack | solution.py:1028
  42.9 13.4 %reshape.765 = bf16[1024,2816]{1,0:T(8,128)(2,1)} reshape(bf16[1024,11,2,128]{3,2,1,0:T(2,128)(2,1)} %copy.253) | data formatting | bytes 11534336 | tf_op jit(solution)/shard_map/reshape | solution.py:1030
  60.4 133.9 %opening.1 = (bf16[16,128,2048]{2,1,0:T(8,128)(2,1)}, bf16[16,128,640]{2,1,0:T(8,128)(2,1)}, bf16[2,16,64,256]{3,2,1,0:T(8,128)(2,1)}, bf16[2,64,2048]{2,1,0:T(8...) custom-call(bf16[128,2048]{1,0:T(8,128)(2,1)} %bitcast.219, ...), custom_call_target="tpu_custom_call" | custom-call | bytes 4000000 | tf_op jit(solution)/shard_map/opening/pallas_call | solution.py:349
  196.6 6.0 multiply_reduce_fusion
  209.0 11.0 %fusion.10 = f32[2,16,64,768]{3,2,0,1:T(8,128)S(1)} fusion(bf16[2048,576]{1,0:T(8,128)(2,1)S(1)} %bitcast.203, bf16[2048,192]{1,0:T(8,128)(2,1)} %bitcast.233, f32[2048]{0:T(1024)S(1)} %get-tuple-element.155, f32[16,2,64]{2,1,0:T(2,128)S(1)} %rsqrt.48, bf16[16,2,64,2048]{3,2,1,0:T(8,128)(2,1)} %bitcast.198), kind=kOutput, calls=%fused_computation.34 | convolution fusion | flops 6465519616 | bytes 17842176 | tf_op jit(solution)/shard_map/dot_general | solution.py:908
  259.1 50.5 %scatter16.3 = f32[128,2048]{1,0:T(8,128)S(1)} custom-call(bf16[16,128,2048]{2,1,0:T(8,128)(2,1)S(1)} %bitcast.181), custom_call_target="tpu_custom_call" | custom-call | bytes 4000000 | tf_op jit(solution)/shard_map/scatter16/pallas_call | solution.py:536
  312.0 51.3 %gather16.2 = bf16[16,128,2048]{2,1,0:T(8,128)(2,1)} custom-call(bf16[128,2048]{1,0:T(8,128)(2,1)} %multiply_convert_fusion.7.x_ref), custom_call_target="tpu_custom_call" | custom-call | bytes 4000000 | tf_op jit(solution)/shard_map/gather16/pallas_call | solution.py:202
  381.6 17.0 %all-gather.9.cloned.1.call-done.gu_ref = bf16[2048,2816]{1,0:T(8,128)(2,1)} async-done(((bf16[1024,2816]{1,0:T(8,128)(2,1)}), bf16[2048,2816]{1,0:T(8,128)(2,1)}) %all-gather.9.cloned.1.call-update) | async-done | bytes 11534352 | tf_op jit(solution)/shard_map/all_gather | solution.py:1033
  398.6 93.9 %mixture.1 = (bf16[2048,2048]{1,0:T(8,128)(2,1)}, bf16[2048,2176]{1,0:T(8,128)(2,1)}, bf16[1024,2048]{1,0:T(8,128)(2,1)}, bf16[1024,2048]{1,0:T(8,128)(2,1)}, bf...) custom-call(f32[1,256]{1,0:T(1,128)} %add_convert_fusion.5.pick_ref,, ...), custom_call_target="tpu_custom_call" | custom-call | flops 60000002048 | bytes 60000000 | tf_op jit(solution)/shard_map/mixture/pallas_call | solution.py:879
  492.5 8.7 convolution_convert_fusion.5
  505.6 10.6 %convolution_convert_fusion.2 = bf16[1408,2048]{1,0:T(8,128)(2,1)} fusion(bf16[1024,1408]{1,0:T(8,128)(2,1)} %get-tuple-element.56, bf16[1024,2048]{1,0:T(8,128)(2,1)} %get-tuple-element.57), kind=kOutput, calls=%fused_computation.16 | convolution fusion | flops 5908463616 | bytes 12845056 | tf_op jit(solution)/shard_map/dot_general | solution.py:912
  516.3 18.2 %convolution_convert_fusion = bf16[2048,2816]{1,0:T(8,128)(2,1)} fusion(bf16[1024,2048]{1,0:T(8,128)(2,1)} %get-tuple-element.58, bf16[1024,2816]{1,0:T(8,128)(2,1)} %get-tuple-element.59), kind=kOutput, calls=%fused_computation.3 | convolution fusion | flops 11816927232 | bytes 21495808 | tf_op jit(solution)/shard_map/dot_general | solution.py:912
  542.6 8.7 multiply_convert_fusion
  554.9 53.8 %scatter16.5 = f32[128,2176]{1,0:T(8,128)S(1)} custom-call(bf16[16,128,2176]{2,1,0:T(8,128)(2,1)S(1)} %bitcast.183), custom_call_target="tpu_custom_call" | custom-call | bytes 4000000 | tf_op jit(solution)/shard_map/scatter16/pallas_call | solution.py:536
  613.5 51.8 %gather16.3 = bf16[16,128,2048]{2,1,0:T(8,128)(2,1)} custom-call(bf16[128,2048]{1,0:T(8,128)(2,1)} %fusion.67.x_ref), custom_call_target="tpu_custom_call" | custom-call | bytes 4000000 | tf_op jit(solution)/shard_map/gather16/pallas_call | solution.py:202
  691.1 6.2 convolution_convert_fusion.6
  728.2 7.0 pad_maximum_fusion.p_ref
  735.2 81.9 %returning.1 = (f32[128,2688]{1,0:T(8,128)S(1)}, bf16[2,16,64,256]{3,2,1,0:T(8,128)(2,1)S(1)}, bf16[2,64,2048]{2,1,0:T(8,128)(2,1)S(1)}, bf16[1,16,64,256]{3,2,1,0:T(8,128)(2,1)S(1)}, bf16[1,64,2048]{2,1,0:T(8,128)(2,1)S(1)}) custom-call(bf16[16,128,2688]{2,1,0:T(8,128)(2,1)} %pad_maximum_fusion.p_ref, ...), custom_call_target="tpu_custom_call" | custom-call | bytes 4000000 | tf_op jit(solution)/shard_map/returning/pallas_call | solution.py:648
  840.2 33.1 %closing.1 = (bf16[128,640]{1,0:T(8,128)(2,1)S(1)}, bf16[1,64,640]{2,1,0:T(8,128)(2,1)S(1)}) custom-call(bf16[16,128,640]{2,1,0:T(8,128)(2,1)S(1)} %bitcast.182), custom_call_target="tpu_custom_call" | custom-call | bytes 4000000 | tf_op jit(solution)/shard_map/closing/pallas_call | solution.py:715
  877.6 50.1 %scatter16.4 = f32[128,2048]{1,0:T(8,128)S(1)} custom-call(bf16[16,128,2048]{2,1,0:T(8,128)(2,1)S(1)} %bitcast.184), custom_call_target="tpu_custom_call" | custom-call | bytes 4000000 | tf_op jit(solution)/shard_map/scatter16/pallas_call | solution.py:536
  940.0 11.7 %reshape.783 = bf16[1024,11,2,128]{3,2,1,0:T(2,128)(2,1)} reshape(bf16[1024,2816]{1,0:T(8,128)(2,1)} %reduce-scatter.4.cloned.1.call-done) | data formatting | bytes 11534336 | tf_op jit(solution)/shard_map/reshape | solution.py:1124
  951.7 39.3 %fusion.6 = (f32[1024,11,128]{2,1,0:T(8,128)}, f32[1024,11,128]{2,1,0:T(8,128)}) fusion(bf16[1024,11,2,128]{3,2,1,0:T(2,128)(2,1)} %reshape.783), kind=kLoop, calls=%fused_computation.20 | loop fusion | flops 2883584 | bytes 17301504 | tf_op jit(solution)/shard_map/convert_element_type | solution.py:1217
  991.0 8.5 reshape.791
  999.5 8.5 reshape.792
  (387 shorter events, 209.1 us)
Async XLA Ops:
  7.2 358.3 %all-gather.13.cloned.1.call-start = ((), (), s32[]{:S(2)}) async-start(), calls=%async_computation.9 | async-start | bytes 3244032 | tf_op jit(solution)/shard_map/all_gather | solution.py:1035
  9.5 367.2 %all-gather.7.cloned.1.call-start = ((), (), s32[]{:S(2)}) async-start(), calls=%async_computation.3 | async-start | bytes 9469952 | tf_op jit(solution)/shard_map/all_gather | solution.py:1061
  14.5 367.1 %all-gather.11.cloned.1.call-start = ((), (), s32[]{:S(2)}) async-start(), calls=%async_computation.8 | async-start | bytes 8650752 | tf_op jit(solution)/shard_map/all_gather | solution.py:1034
  15.3 383.3 %all-gather.9.cloned.1.call-start = ((), (), s32[]{:S(2)}) async-start(), calls=%async_computation.4 | async-start | bytes 17301504 | tf_op jit(solution)/shard_map/all_gather | solution.py:1033
  56.3 875.7 %reduce-scatter.8.cloned.1.call-start = ((), (), s32[]{:S(2)}) async-start(), calls=%async_computation.7 | async-start | bytes 3244032 | tf_op jit(solution)/shard_map/reduce_scatter | solution.py:1129
  57.3 145.3 %copy-start.54 = (s32[16,64]{1,0:T(8,128)}, s32[16,64]{1,0:T(8,128)S(1)}, u32[]{:S(2)}) copy-start(s32[16,64]{1,0:T(8,128)S(1)} %multiply_add_fusion.1) | copy-start | bytes 12292
  311.0 300.3 %copy-start.64 = (f32[128]{0:T(128)}, f32[128]{0:T(128)S(1)}, u32[]{:S(2)}) copy-start(f32[128]{0:T(128)S(1)} %add_rsqrt_fusion.4) | copy-start | bytes 1540
  505.6 429.3 %reduce-scatter.6.cloned.1.call-start = ((), (), s32[]{:S(2)}) async-start(), calls=%async_computation.6 | async-start | bytes 8650752 | tf_op jit(solution)/shard_map/reduce_scatter | solution.py:1122
  534.5 405.5 %reduce-scatter.4.cloned.1.call-start = ((), (), s32[]{:S(2)}) async-start(), calls=%async_computation.5 | async-start | bytes 17301504 | tf_op jit(solution)/shard_map/reduce_scatter | solution.py:1123
  554.9 53.8 %copy-start.70 = (f32[128]{0:T(128)S(1)}, f32[128]{0:T(128)}, u32[]{:S(2)}) copy-start(f32[128]{0:T(128)} %copy-done.69) | copy-start | bytes 1540
  554.9 57.4 %copy-start.73 = (bf16[128]{0:T(256)(128)(2,1)S(1)}, bf16[128]{0:T(256)(128)(2,1)}, u32[]{:S(2)}) copy-start(bf16[128]{0:T(256)(128)(2,1)} %copy-done.72) | copy-start | bytes 772
  609.1 56.2 %copy-start.40 = (bf16[128,16]{1,0:T(8,128)(2,1)}, bf16[128,16]{1,0:T(8,128)(2,1)S(1)}, u32[]{:S(2)}) copy-start(bf16[128,16]{1,0:T(8,128)(2,1)S(1)} %multiply_convert_fusion.11) | copy-start | bytes 12292
  611.3 54.0 %copy-start.78 = (f32[128]{0:T(128)}, f32[128]{0:T(128)S(1)}, u32[]{:S(2)}) copy-start(f32[128]{0:T(128)S(1)} %broadcast_multiply_fusion.2) | copy-start | bytes 1540
  613.5 51.8 %copy-start.37 = (bf16[2,64,2048]{2,1,0:T(8,128)(2,1)S(1)}, bf16[2,64,2048]{2,1,0:T(8,128)(2,1)}, u32[]{:S(2)}) copy-start(bf16[2,64,2048]{2,1,0:T(8,128)(2,1)} %get-tuple-element.53) | copy-start | bytes 1572868
  873.4 55.0 %copy-start.38 = (f32[64,640]{1,0:T(8,128)}, f32[64,640]{1,0:T(8,128)S(1)}, u32[]{:S(2)}) copy-start(f32[64,640]{1,0:T(8,128)S(1)} %convert_add_fusion.1) | copy-start | bytes 491524
  877.5 52.4 %copy-start.8 = (f32[128,2048]{1,0:T(8,128)S(1)}, f32[128,2048]{1,0:T(8,128)}, u32[]{:S(2)}) copy-start(f32[128,2048]{1,0:T(8,128)} %copy-done.7) | copy-start | bytes 3145732
  877.5 52.4 %copy-start.10 = (bf16[2,1,64,2048]{3,2,1,0:T(8,128)(2,1)S(1)}, bf16[2,1,64,2048]{3,2,1,0:T(8,128)(2,1)}, u32[]{:S(2)}) copy-start(bf16[2,1,64,2048]{3,2,1,0:T(8,128)(2,1)} %param.20) | copy-start | bytes 1572868
  877.5 52.4 %copy-start.15 = (bf16[2,1,64,2048]{3,2,1,0:T(8,128)(2,1)S(1)}, bf16[2,1,64,2048]{3,2,1,0:T(8,128)(2,1)}, u32[]{:S(2)}) copy-start(bf16[2,1,64,2048]{3,2,1,0:T(8,128)(2,1)} %param.21) | copy-start | bytes 1572868
  877.5 52.4 %copy-start.26 = (f32[128,2048]{1,0:T(8,128)S(1)}, f32[128,2048]{1,0:T(8,128)}, u32[]{:S(2)}) copy-start(f32[128,2048]{1,0:T(8,128)} %get-tuple-element.203) | copy-start | bytes 3145732
  877.5 52.4 %copy-start.65 = (f32[128]{0:T(128)S(1)}, f32[128]{0:T(128)}, u32[]{:S(2)}) copy-start(f32[128]{0:T(128)} %copy-done.64) | copy-start | bytes 1540
  877.5 52.4 %copy-start.71 = (f32[128]{0:T(128)S(1)}, f32[128]{0:T(128)}, u32[]{:S(2)}) copy-start(f32[128]{0:T(128)} %copy-done.69) | copy-start | bytes 1540
  877.5 52.4 %copy-start.74 = (bf16[128]{0:T(256)(128)(2,1)S(1)}, bf16[128]{0:T(256)(128)(2,1)}, u32[]{:S(2)}) copy-start(bf16[128]{0:T(256)(128)(2,1)} %copy-done.72) | copy-start | bytes 772
  877.5 52.4 %copy-start.77 = (f32[128]{0:T(128)S(1)}, f32[128]{0:T(128)}, u32[]{:S(2)}) copy-start(f32[128]{0:T(128)} %copy-done.76) | copy-start | bytes 1540
  877.6 52.4 %copy-start.79 = (f32[128]{0:T(128)S(1)}, f32[128]{0:T(128)}, u32[]{:S(2)}) copy-start(f32[128]{0:T(128)} %copy-done.78) | copy-start | bytes 1540
  (74 other events, 577.0 us)
Sparse Core Ops, SparseCore 0:
  10.1 36.5 all-gather.12
  49.6 130.9 all-gather.6
  182.1 73.4 all-gather.10
  257.5 141.0 all-gather.8
  505.7 32.5 reduce-scatter.7
  541.1 71.4 reduce-scatter.5
  614.9 133.1 reduce-scatter.3

commit v3 on v2

--- a/solution.py
+++ b/solution.py
@@ -47,8 +47,8 @@
 
 
 class Gather:
-    def __init__(self, src, out, chunks, sems):
-        self.src, self.out, self.chunks = src, out, chunks
+    def __init__(self, src, out, chunks, sems, view=lambda ref, b: ref.at[b]):
+        self.src, self.out, self.chunks, self.view = src, out, chunks, view
         self.rows = src.shape[0] // chunks
         self.own_sem, self.us, self.ur, self.ds, self.dr, self.xs, self.xr, self.cs, self.cr = sems
         self.me, self.z, self.x, self.c, self.core, self.side = place()
@@ -59,10 +59,14 @@
         return [dma] + [dma((4, chunks))] * 4 + [dma((7, chunks))] * 2 + [dma((14, chunks))] * 2
 
     def copy(self, block, k, src, send, recv, to):
-        part = pl.ds(k * self.rows, self.rows)
+        src_ref = self.src if src is None else self.view(self.out, src)
+        dst_ref = self.view(self.out, block)
+        if self.chunks > 1:
+            part = pl.ds(k * self.rows, self.rows)
+            src_ref, dst_ref = src_ref.at[part], dst_ref.at[part]
         return pltpu.make_async_remote_copy(
-            src_ref=(self.src if src is None else self.out.at[src]).at[part],
-            dst_ref=self.out.at[block].at[part],
+            src_ref=src_ref,
+            dst_ref=dst_ref,
             send_sem=send, recv_sem=recv,
             device_id={"expert": to}, device_id_type=MESH,
         )
@@ -103,7 +107,7 @@
 
     def start(self):
         z, me = self.z, self.me
-        self.own = pltpu.make_async_copy(self.src, self.out.at[me], self.own_sem)
+        self.own = pltpu.make_async_copy(self.src, self.view(self.out, me), self.own_sem)
         self.own.start()
         for k in range(self.chunks):
             self.across(k, 0, me).start()
@@ -215,13 +219,12 @@
                    x_all, small_all, parts_head, out_head, small_dp, parts_dp, out_dp, *sems):
     ng = 9
     gx = Gather(x_ref, x_all, chunks, sems[:ng])
-    gs = Gather(small_dp, small_all, 1, sems[ng:2 * ng])
+    gs = Gather(small_dp, small_all, 1, sems[ng:2 * ng], lambda ref, b: ref.at[:, b])
     loc, ys, yr, ps, pr, os_, or_, pl_sem, ol_sem = sems[2 * ng:]
     me = gx.me
     plane = lax.axis_index("dp")
-    rows = parts_ref.shape[1]
     enter_all(me, plane, dp)
-    pairs = ((small_ref, small_dp.at[pl.ds(plane * rows, rows)]), (parts_ref, parts_dp.at[plane]),
+    pairs = ((small_ref, small_dp.at[plane]), (parts_ref, parts_dp.at[plane]),
              (out_ref, out_dp.at[plane]))
 
     def lift(i, r):
@@ -232,7 +235,7 @@
 
     def landed(i, r):
         p = (plane - r + dp) % dp
-        dst = (small_dp.at[pl.ds(p * rows, rows)], parts_dp.at[p], out_dp.at[p])[i]
+        dst = (small_dp.at[p], parts_dp.at[p], out_dp.at[p])[i]
         return pltpu.make_async_remote_copy(
             src_ref=dst, dst_ref=dst, send_sem=ys.at[i, r], recv_sem=yr.at[i, r],
             device_id={"dp": p}, device_id_type=MESH)
@@ -349,9 +352,9 @@
     res = pl.pallas_call(
         functools.partial(opening_kernel, dp, chunks),
         out_shape=(
-            shape((NE,) + x.shape, bf), shape((NE, dp * rows, ws), bf), shape((dp, NE) + parts.shape[1:], bf),
+            shape((NE,) + x.shape, bf), shape((dp, NE, rows, ws), bf), shape((dp, NE) + parts.shape[1:], bf),
             shape((dp, rows, wo), bf),
-            shape((dp * rows, ws), bf), shape((dp,) + parts.shape, bf), shape((dp, rows, wo), bf),
+            shape((dp, rows, ws), bf), shape((dp,) + parts.shape, bf), shape((dp, rows, wo), bf),
         ),
         in_specs=[ANY] * 4,
         out_specs=[ANY] * 7,
@@ -747,8 +750,8 @@
 SHARE = 176
 
 
-def mixture_kernel(pick_ref, mix_ref, dy_ref, slot_row, slot_col, valid_ref, gu_ref, wd_ref, fan_ref, sd_ref,
-                   out_ref, dh_ref, rows_ref, deo_ref, hid_ref, dgu_ref, sh_ref, ds_ref,
+def mixture_kernel(pick_ref, mix_ref, dy_ref, slot_row, slot_col, valid_ref, wg_ref, wu_ref, wd_ref, fan_ref, sd_ref,
+                   out_ref, dh_ref, rows_ref, deo_ref, hid_ref, dg_ref, du_ref, sh_ref, ds_ref,
                    act_buf, slo_buf):
     tokens, width = mix_ref.shape
     groups = tokens // 256
@@ -798,22 +801,21 @@
     lax.fori_loop(0, width // WIDE, dispatch, 0)
 
     def fan_in(start, size):
-        both = mm(rows_ref[...], gu_ref[:, pl.ds(start, size)])
-        for i in range(size // TILE):
-            gate_in, up_in = both[:, i * TILE:i * TILE + 128], both[:, i * TILE + 128:(i + 1) * TILE]
-            act, slope = silu_pair(gate_in)
-            half = pl.ds(pl.multiple_of(start // 2 + i * 128, 128), 128)
-            hid_ref[:, half] = (act * up_in).astype(BF)
-            act_buf[:, half] = act
-            slo_buf[:, half] = up_in * slope
+        cols = pl.ds(start, size)
+        gate_in = mm(rows_ref[...], wg_ref[:, cols])
+        up_in = mm(rows_ref[...], wu_ref[:, cols])
+        act, slope = silu_pair(gate_in)
+        hid_ref[:, cols] = (act * up_in).astype(BF)
+        act_buf[:, cols] = act
+        slo_buf[:, cols] = up_in * slope
 
     def fan_loop(j, _):
         fan_in(pl.multiple_of(j * WIDE, WIDE), WIDE)
         return 0
 
-    lax.fori_loop(0, 2 * ff // WIDE, fan_loop, 0)
-    if 2 * ff % WIDE:
-        fan_in(2 * ff // WIDE * WIDE, 2 * ff % WIDE)
+    lax.fori_loop(0, ff // WIDE, fan_loop, 0)
+    if ff % WIDE:
+        fan_in(ff // WIDE * WIDE, ff % WIDE)
 
     def fan_out(j, d_gates):
         eo = mm(hid_ref[...], wd_ref[:, lanes(j)]).astype(BF)
@@ -828,12 +830,8 @@
     def back_out(start, size):
         cols = pl.ds(start, size)
         d_eh = mm_t(deo_ref[...], wd_ref[cols, :])
-        dg = (d_eh * slo_buf[:, cols]).astype(BF)
-        du = (d_eh * act_buf[:, cols]).astype(BF)
-        for i in range(size // 128):
-            at = pl.multiple_of(2 * start + i * TILE, TILE)
-            dgu_ref[:, pl.ds(at, 128)] = dg[:, i * 128:(i + 1) * 128]
-            dgu_ref[:, pl.ds(at + 128, 128)] = du[:, i * 128:(i + 1) * 128]
+        dg_ref[:, cols] = (d_eh * slo_buf[:, cols]).astype(BF)
+        du_ref[:, cols] = (d_eh * act_buf[:, cols]).astype(BF)
 
     def back_loop(j, _):
         back_out(pl.multiple_of(j * WIDE, WIDE), WIDE)
@@ -846,7 +844,7 @@
     d_s = ds_ref[...]
 
     def back_in(j, _):
-        d_rows = mm_t(dgu_ref[...], gu_ref[lanes(j), :]).astype(BF)
+        d_rows = (mm_t(dg_ref[...], wg_ref[lanes(j), :]) + mm_t(du_ref[...], wu_ref[lanes(j), :])).astype(BF)
         shared = mm(d_s, fan_ref[:, lanes(j)])
         taken = jnp.concatenate(
             [mm(to_token[g], d_rows[g * slots:(g + 1) * slots]) for g in range(groups)], axis=0)
@@ -859,7 +857,7 @@
     dh_ref[:, width:] = tail.astype(BF)
 
 
-def mixture(pick, mix, packed, slot_row, slot_col, valid, gu, wd, fan, sd, step=512):
+def mixture(pick, mix, packed, slot_row, slot_col, valid, wg, wu, wd, fan, sd, step=512):
     total, width = mix.shape
     steps = total // step
     ff = wd.shape[0]
@@ -881,17 +879,223 @@
         grid=(steps,),
         out_shape=(
             shape((total, width), BF), shape((total, width + 128), BF), shape((rows, width), BF),
-            shape((rows, width), BF), shape((rows, ff), BF), shape((rows, 2 * ff), BF),
+            shape((rows, width), BF), shape((rows, ff), BF), shape((rows, ff), BF), shape((rows, ff), BF),
             shape((total, TILE), BF), shape((total, 2 * TILE), BF)),
         in_specs=[whole(pick), tokens(width), tokens(width + 128), pl.BlockSpec((1, step), lambda i: (0, i)),
-                  tokens(1), tokens(1), whole(gu), whole(wd), whole(fan), whole(sd)],
-        out_specs=[tokens(width), tokens(width + 128), slots(width), slots(width), slots(ff), slots(2 * ff),
+                  tokens(1), tokens(1), whole(wg), whole(wu), whole(wd), whole(fan), whole(sd)],
+        out_specs=[tokens(width), tokens(width + 128), slots(width), slots(width), slots(ff), slots(ff), slots(ff),
                    tokens(TILE), tokens(2 * TILE)],
         scratch_shapes=[pltpu.VMEM((step // 2, ff), F32), pltpu.VMEM((step // 2, ff), F32)],
         compiler_params=pltpu.CompilerParams(vmem_limit_bytes=60 * 1024 * 1024),
         cost_estimate=pl.CostEstimate(flops=60_000_000_000, bytes_accessed=60_000_000, transcendentals=0),
         name="mixture",
-    )(pick, mix, packed, slot_row, slot_col, valid, gu, wd, fan, sd)
+    )(pick, mix, packed, slot_row, slot_col, valid, wg, wu, wd, fan, sd)
+
+
+def mm_lead(a, b):
+    return lax.dot_general(a, b, (((0,), (0,)), ((), ())), preferred_element_type=F32)
+
+
+def turn(v, cosine, sine):
+    half = v.shape[1] // 2
+    a, b = v[:, :half], v[:, half:]
+    return jnp.concatenate([a * cosine - b * sine, b * cosine + a * sine], axis=1)
+
+
+def project_kernel(x_ref, gain_ref, lgain_ref, wq_ref, wl_ref, we_ref, cos_ref, sin_ref,
+                   h_ref, q_ref, k_ref, v_ref, lat_ref):
+    blocks = x_ref.shape[0]
+    batches, rows, _ = q_ref.shape
+    here = rows // blocks
+    x = x_ref[...].reshape(blocks * batches * here, x_ref.shape[2]).astype(F32)
+    h = x * lax.rsqrt(jnp.mean(x * x, axis=1, keepdims=True) + 1e-6) * gain_ref[...]
+    h = h.astype(BF)
+    h_ref[...] = h
+    raw = mm(h, wq_ref[...])
+    raw_lat = mm(h, wl_ref[...])
+    cosine, sine = cos_ref[...], sin_ref[...]
+    zeros = jnp.zeros((raw.shape[0], 64), BF)
+    q = jnp.concatenate([raw[:, :128].astype(BF), turn(raw[:, 128:192], cosine, sine).astype(BF), zeros], axis=1)
+    k_rope = turn(raw_lat[:, 512:576], cosine, sine).astype(BF)
+    lat = raw_lat[:, :512]
+    lat = (lat * lax.rsqrt(jnp.mean(lat * lat, axis=1, keepdims=True) + 1e-6) * lgain_ref[...]).astype(BF)
+    expanded = mm(lat, we_ref[...]).astype(BF)
+    k = jnp.concatenate([expanded[:, :128], k_rope, zeros], axis=1)
+    for e in range(blocks):
+        for m in range(batches):
+            src = slice((e * batches + m) * here, (e * batches + m + 1) * here)
+            dst = slice(e * here, (e + 1) * here)
+            q_ref[m, dst] = q[src]
+            k_ref[m, dst] = k[src]
+            v_ref[m, dst] = expanded[src, 128:]
+            lat_ref[m, dst] = lat[src]
+
+
+def project(x_all, gain, lgain, wq, wl, we, cosine, sine, batches):
+    groups, rows, width = x_all.shape
+    here = rows // batches
+    per = 4
+    seq = groups * here
+    shape = jax.ShapeDtypeStruct
+
+    def whole(v):
+        return pl.BlockSpec(v.shape, lambda i: (0, 0))
+
+    def by_seq(w):
+        return pl.BlockSpec((batches, per * here, w), lambda i: (0, i, 0))
+
+    table = pl.BlockSpec((per * rows, 32), lambda i: (i, 0))
+    return pl.pallas_call(
+        project_kernel,
+        grid=(groups // per,),
+        out_shape=(shape((groups * rows, width), BF), shape((batches, seq, 256), BF), shape((batches, seq, 256), BF),
+                   shape((batches, seq, 128), BF), shape((batches, seq, 512), BF)),
+        in_specs=[pl.BlockSpec((per, rows, width), lambda i: (i, 0, 0)), whole(gain), whole(lgain), whole(wq), whole(wl), whole(we),
+                  table, table],
+        out_specs=[pl.BlockSpec((per * rows, width), lambda i: (i, 0)), by_seq(256), by_seq(256), by_seq(128), by_seq(512)],
+        compiler_params=pltpu.CompilerParams(vmem_limit_bytes=48 * 1024 * 1024),
+        cost_estimate=pl.CostEstimate(flops=7_000_000_000, bytes_accessed=20_000_000, transcendentals=0),
+        name="project",
+    )(x_all, gain, lgain, wq, wl, we, cosine, sine)
+
+
+ROWS = 256
+SCALE = 192.0 ** -0.5
+
+
+def held_scores(q, k, first, length):
+    s = mm_t(q, k) * SCALE
+    t = lax.broadcasted_iota(jnp.int32, s.shape, 0) + first
+    u = lax.broadcasted_iota(jnp.int32, s.shape, 1)
+    return jnp.where((u <= t) & (u < length), s, -1e30)
+
+
+def attend_kernel(len_ref, q_ref, k_ref, v_ref, wo_ref, part_ref, att_ref, lse_ref):
+    length = len_ref[pl.program_id(0)]
+    seq = q_ref.shape[1]
+    groups, _, here, width = part_ref.shape
+    for i in range(seq // ROWS):
+        tile = slice(i * ROWS, (i + 1) * ROWS)
+        ext = (i + 1) * ROWS
+        s = held_scores(q_ref[0, tile], k_ref[0, :ext], i * ROWS, length)
+        peak = jnp.max(s, axis=1, keepdims=True)
+        raised = jnp.exp(s - peak)
+        total = jnp.sum(raised, axis=1, keepdims=True)
+        lse_ref[0, tile] = peak + jnp.log(total)
+        p = (raised / total).astype(BF)
+        att = mm(p, v_ref[0, :ext]).astype(BF)
+        per = ROWS // here
+        att_ref[i * per:(i + 1) * per, 0] = att.reshape(per, here, att.shape[1])
+        for j in range(width // 512):
+            cols = slice(j * 512, (j + 1) * 512)
+            part_ref[i * per:(i + 1) * per, 0, :, cols] = mm(att, wo_ref[:, cols]).astype(BF).reshape(per, here, 512)
+
+
+def attend(lengths, q, k, v, wo, groups):
+    batches, seq, _ = q.shape
+    here = seq // groups
+    width = wo.shape[1]
+    shape = jax.ShapeDtypeStruct
+
+    def by_seq(w):
+        return pl.BlockSpec((1, seq, w), lambda m: (m, 0, 0))
+
+    def by_dev(w):
+        return pl.BlockSpec((groups, 1, here, w), lambda m: (0, m, 0, 0))
+
+    return pl.pallas_call(
+        attend_kernel,
+        grid=(batches,),
+        out_shape=(shape((groups, batches, here, width), BF), shape((groups, batches, here, 128), BF),
+                   shape((batches, seq, 1), F32)),
+        in_specs=[pl.BlockSpec(memory_space=pltpu.SMEM), by_seq(256), by_seq(256), by_seq(128),
+                  pl.BlockSpec(wo.shape, lambda m: (0, 0))],
+        out_specs=[by_dev(width), by_dev(128), by_seq(1)],
+        compiler_params=pltpu.CompilerParams(vmem_limit_bytes=48 * 1024 * 1024),
+        cost_estimate=pl.CostEstimate(flops=4_000_000_000, bytes_accessed=15_000_000, transcendentals=2_000_000),
+        name="attend",
+    )(lengths, q, k, v, wo)
+
+
+def attend_back_kernel(len_ref, dout_ref, q_ref, k_ref, v_ref, lat_ref, att_ref, lse_ref, wo_ref, wq_ref, we_ref,
+                       cos_ref, sin_ref, part_ref, dq_ref, gwo_ref, gwe_ref, dk, dv, datt):
+    m = pl.program_id(0)
+    length = len_ref[m]
+    seq = q_ref.shape[1]
+    groups, _, here, width = dout_ref.shape
+    per = ROWS // here
+
+    @pl.when(m == 0)
+    def _():
+        gwo_ref[...] = jnp.zeros_like(gwo_ref)
+        gwe_ref[...] = jnp.zeros_like(gwe_ref)
+
+    for j in range(4):
+        blocks = slice(j * groups // 4, (j + 1) * groups // 4)
+        dout = dout_ref[blocks].reshape(seq // 4, width)
+        rows = slice(j * seq // 4, (j + 1) * seq // 4)
+        datt[rows] = mm_t(dout, wo_ref[...]).astype(BF)
+        gwo_ref[...] += mm_lead(att_ref[blocks].reshape(seq // 4, 128), dout)
+    dk[...] = jnp.zeros_like(dk)
+    dv[...] = jnp.zeros_like(dv)
+    for i in range(seq // ROWS):
+        tile = slice(i * ROWS, (i + 1) * ROWS)
+        ext = (i + 1) * ROWS
+        q = q_ref[0, tile]
+        p = jnp.exp(held_scores(q, k_ref[0, :ext], i * ROWS, length) - lse_ref[0, tile])
+        da = datt[tile]
+        dp = mm_t(da, v_ref[0, :ext])
+        inner = jnp.sum(dp * p, axis=1, keepdims=True)
+        ds = (p * (dp - inner)).astype(BF)
+        dq = mm(ds, k_ref[0, :ext]) * SCALE
+        dk[:ext] += mm_lead(ds, q)
+        dv[:ext] += mm_lead(p.astype(BF), da)
+        rope = turn(dq[:, 128:192], cos_ref[tile], -sin_ref[tile])
+        dq = jnp.concatenate([dq[:, :128].astype(BF), rope.astype(BF), jnp.zeros((ROWS, 64), BF)], axis=1)
+        dq_ref[i * per:(i + 1) * per, 0] = dq.reshape(per, here, 256)
+        for j in range(width // 512):
+            cols = slice(j * 512, (j + 1) * 512)
+            part_ref[i * per:(i + 1) * per, 0, :, cols] = mm_t(dq, wq_ref[cols]).astype(BF).reshape(per, here, 512)
+    for i in range(seq // ROWS):
+        tile = slice(i * ROWS, (i + 1) * ROWS)
+        d_k = dk[tile] * SCALE
+        d_exp = jnp.concatenate([d_k[:, :128].astype(BF), dv[tile].astype(BF)], axis=1)
+        gwe_ref[...] += mm_lead(lat_ref[0, tile], d_exp)
+        d_lat = mm_t(d_exp, we_ref[...]).astype(BF)
+        tail = jnp.concatenate([d_lat, d_k[:, 128:].astype(BF)], axis=1)
+        pad = part_ref.shape[3] - width - tail.shape[1]
+        if pad > 0:
+            tail = jnp.concatenate([tail, jnp.zeros((ROWS, pad), BF)], axis=1)
+        part_ref[i * per:(i + 1) * per, 0, :, width:] = tail[:, :part_ref.shape[3] - width].reshape(per, here, -1)
+
+
+def attend_back(lengths, dout, q, k, v, lat, att, lse, wo, wq, we, cosine, sine, tail):
+    groups, batches, here, width = dout.shape
+    seq = groups * here
+    shape = jax.ShapeDtypeStruct
+
+    def by_seq(w):
+        return pl.BlockSpec((1, seq, w), lambda m: (m, 0, 0))
+
+    def by_dev(w):
+        return pl.BlockSpec((groups, 1, here, w), lambda m: (0, m, 0, 0))
+
+    def whole(v):
+        return pl.BlockSpec(v.shape, lambda m: (0, 0))
+
+    return pl.pallas_call(
+        attend_back_kernel,
+        grid=(batches,),
+        out_shape=(shape((groups, batches, here, width + tail), BF), shape((groups, batches, here, 256), BF),
+                   shape(wo.shape, F32), shape(we.shape, F32)),
+        in_specs=[pl.BlockSpec(memory_space=pltpu.SMEM), by_dev(width), by_seq(256), by_seq(256), by_seq(128),
+                  by_seq(512), by_dev(128), by_seq(1), whole(wo), whole(wq), whole(we), whole(cosine), whole(sine)],
+        out_specs=[by_dev(width + tail), by_dev(256), whole(wo), whole(we)],
+        scratch_shapes=[pltpu.VMEM((seq, 256), F32), pltpu.VMEM((seq, 128), F32), pltpu.VMEM((seq, 128), BF)],
+        compiler_params=pltpu.CompilerParams(vmem_limit_bytes=56 * 1024 * 1024),
+        cost_estimate=pl.CostEstimate(flops=14_000_000_000, bytes_accessed=25_000_000, transcendentals=2_000_000),
+        name="attend_back",
+    )(lengths, dout, q, k, v, lat, att, lse, wo, wq, we, cosine, sine)
 
 
 H = 16
@@ -994,7 +1198,6 @@
     seq_total = here * GROUPS
     rows_w = query_weight.shape[0]
     rows_l = expand_weight.shape[0]
-    scale_factor = float(QK_NOPE + ROPE) ** (-0.5)
 
     x_own = layer_input.reshape(own, width)
     latent_column = jnp.zeros((rows_w,), BF).at[:rows_l].set(latent_gain)
@@ -1014,23 +1217,20 @@
     parts = jnp.concatenate([query_parts, expand_parts.reshape(H, rows_w, ROPE)], axis=2)
     x_all, small, parts_head, output_head = opening(dp, x_own, small, parts, output_weight, 1)
     x_all = x_all.reshape(total, width)
-    small = small.reshape(GROUPS, dp, rows_w, 640).swapaxes(0, 1).reshape(width, 640)
+    small = small.reshape(width, 640)
+    parts_head = parts_head.reshape(width, TILE)
     latent_full = small[:, :576]
     router_full = small[:, 576:592]
     gain_attn = small[:, 592].astype(F32)
     gain_mixer = small[:, 593].astype(F32)
     gain_latent = small[:, 594].reshape(dp * GROUPS, rows_w)[:, :rows_l].reshape(-1).astype(F32)
-    query_head = parts_head[..., : QK_NOPE + ROPE].reshape(width, QK_NOPE + ROPE)
-    expand_head = parts_head[..., QK_NOPE + ROPE :].reshape(KV_RANK, QK_NOPE + V_DIM)
+    expand_head = parts_head[:, QK_NOPE + ROPE :].reshape(KV_RANK, QK_NOPE + V_DIM)
     output_head = output_head.reshape(V_DIM, width)
 
-    ff = gate_weight.shape[2]
-    fan_own = jnp.stack(
-        [gate_weight[0].reshape(-1, ff // 128, 128), up_weight[0].reshape(-1, ff // 128, 128)], axis=2
-    ).reshape(-1, 2 * ff)
     share_own = jnp.concatenate([shared_gate.T, shared_up.T, shared_down], axis=0)
     share_width = shared_down.shape[0]
-    fan_full = lax.all_gather(fan_own, "dp", axis=0, tiled=True)
+    gate_full = lax.all_gather(gate_weight[0], "dp", axis=0, tiled=True)
+    up_full = lax.all_gather(up_weight[0], "dp", axis=0, tiled=True)
     down_full = lax.all_gather(down_weight[0], "dp", axis=0, tiled=True)
     share_full = lax.all_gather(share_own, "dp", axis=0)
     share_full = share_full.transpose(1, 0, 2).reshape(3 * share_width, width)
@@ -1058,6 +1258,7 @@
     packed = jnp.concatenate(
         [grad_own, routes_own.astype(BF), jnp.zeros((own, 128 - routes_own.shape[1]), BF)], axis=1
     )
+    packed, x_all = lax.optimization_barrier((packed, x_all))
     packed = lax.all_gather(packed, "expert", axis=0, tiled=True)
     routes_all = packed[:, width : width + routes_own.shape[1]].astype(jnp.int32)
     taken = jnp.any(routes_all == me, axis=1) & valid_all
@@ -1065,33 +1266,15 @@
     places = places + 32 * (jnp.arange(places.shape[0], dtype=jnp.int32) % 4)[:, None]
     slot = jnp.where(taken, places.reshape(total), -1)
 
-    hidden_all = norm_forward(x_all.astype(F32), gain_attn)[0].astype(BF)
-    raw = product(hidden_all, jnp.concatenate([query_head, latent_full], axis=1))
-    raw = by_sequence(raw)
-    query_nope = raw[..., :QK_NOPE].astype(BF)
-    query_rope = rotate(raw[..., QK_NOPE : QK_NOPE + ROPE], cosine, sine_table).astype(BF)
-    query = jnp.concatenate([query_nope, query_rope], axis=-1)
-    latent_raw = raw[..., QK_NOPE + ROPE :]
-    latent = norm_forward(latent_raw[..., :KV_RANK], gain_latent)[0].astype(BF)
-    key_rope = rotate(latent_raw[..., KV_RANK:], cosine, sine_table).astype(BF)
-    expanded = product(latent, expand_head).astype(BF)
-    key = jnp.concatenate([expanded[..., :QK_NOPE], key_rope], axis=-1)
-    values = expanded[..., QK_NOPE:]
-    allowed = (key_positions[None, None, :] <= key_positions[None, :, None]) & (
-        key_positions[None, None, :] < seq_lengths[:, None, None]
-    )
-
-    def score(query, key):
-        raw_scores = jnp.einsum("btd,bsd->bts", query, key, preferred_element_type=F32)
-        return jnp.where(allowed, raw_scores * scale_factor, -1e30)
-
-    scores = score(query, key)
-    peak = jnp.max(scores, axis=-1, keepdims=True)
-    log_total = peak + jnp.log(jnp.sum(jnp.exp(scores - peak), axis=-1, keepdims=True))
-    probs_low = jnp.exp(scores - log_total).astype(BF)
-    attended = jnp.einsum("bts,bsd->btd", probs_low, values, preferred_element_type=F32).astype(BF)
-    attended_rows = by_device(attended)
-    attn_part = product(attended_rows, output_head).astype(BF).reshape(GROUPS, own, width)
+    def by_token(table):
+        return jnp.broadcast_to(
+            table.reshape(GROUPS, 1, here, -1), (GROUPS, batches, here, table.shape[1])).reshape(total, -1)
+
+    hidden_all, query, key, values, latent = project(
+        x_all.reshape(GROUPS, own, width), gain_attn[None], gain_latent[None], parts_head, small, expand_head,
+        by_token(cosine), by_token(sine_table), batches)
+    attn_part, attended, log_total = attend(seq_lengths, query, key, values, output_head, GROUPS)
+    attn_part = attn_part.reshape(GROUPS, own, width)
     attn_out = scatter16(attn_part, 2)
 
     x_wide = x_own.astype(F32)
@@ -1107,21 +1290,22 @@
     down_share = jnp.concatenate([share_full[2 * share_width :], jnp.zeros((pad, width), BF)], axis=0)
     lane = jnp.arange(128)[None, :]
     pick = jnp.concatenate([lane == me, lane == me + GROUPS], axis=1).astype(F32)
-    out_part, mix_part, rows, grad_result, hidden, grad_fan_in, share_hidden, grad_share_in = mixture(
+    out_part, mix_part, rows, grad_result, hidden, grad_gate_in, grad_up_in, share_hidden, grad_share_in = mixture(
         pick, mix_all, packed, slot[None, :], slot[:, None], valid_all.astype(F32)[:, None],
-        fan_full, down_full, fan_share, down_share)
+        gate_full, up_full, down_full, fan_share, down_share)
     grad_down = product_lead(hidden, grad_result).astype(BF)
-    grad_fan = product_lead(rows, grad_fan_in).astype(BF)
+    grad_gate = product_lead(rows, grad_gate_in).astype(BF)
+    grad_up = product_lead(rows, grad_up_in).astype(BF)
     grad_share_fan = product_lead(grad_share_in, mix_all).astype(BF)
     grad_share_down = product_lead(share_hidden, packed[:, :width]).astype(BF)
-    mix_part, grad_down, grad_fan = lax.optimization_barrier((mix_part, grad_down, grad_fan))
+    mix_part, grad_down, grad_gate, grad_up = lax.optimization_barrier((mix_part, grad_down, grad_gate, grad_up))
     mix_sum = scatter16(mix_part.reshape(GROUPS, own, width + 128), 5)
     mixed = scatter16(out_part.reshape(GROUPS, own, width), 4)
     layer_output = valid_own[:, None] * (middle + mixed)
 
     out_down = lax.psum_scatter(grad_down, "dp", scatter_dimension=0, tiled=True)
-    out_fan = lax.psum_scatter(grad_fan, "dp", scatter_dimension=0, tiled=True)
-    out_fan = out_fan.reshape(-1, ff // 128, 2, 128)
+    out_gate = lax.psum_scatter(grad_gate, "dp", scatter_dimension=0, tiled=True)
+    out_up = lax.psum_scatter(grad_up, "dp", scatter_dimension=0, tiled=True)
     grad_share = jnp.concatenate(
         [grad_share_fan[:share_width], grad_share_fan[TILE : TILE + share_width], grad_share_down[:share_width]],
         axis=0)
@@ -1138,35 +1322,15 @@
     grad_middle_norm, grad_gain_mixer = norm_backward(grad_mix, unit_mix, factor_mix, gain_mixer)
     grad_middle = grad_own.astype(F32) + grad_middle_norm
 
-    grad_attn_all = gather16(grad_middle.astype(BF), 6).reshape(total, width)
-    grad_output = product_lead(attended_rows, grad_attn_all)
-    grad_attended = by_sequence(product_trail(grad_attn_all, output_head).astype(BF))
-    probs = jnp.exp(score(query, key) - log_total)
-    probs_low = probs.astype(BF)
-    grad_probs = jnp.einsum("btd,bsd->bts", grad_attended, values, preferred_element_type=F32)
-    inner_sum = jnp.sum(grad_probs * probs, axis=-1, keepdims=True)
-    grad_scores = (probs * (grad_probs - inner_sum)).astype(BF)
-    grad_query = jnp.einsum("bts,bsd->btd", grad_scores, key, preferred_element_type=F32) * scale_factor
-    grad_key = jnp.einsum("bts,btd->bsd", grad_scores, query, preferred_element_type=F32) * scale_factor
-    grad_values = jnp.einsum("bts,btd->bsd", probs_low, grad_attended, preferred_element_type=F32)
-    grad_expanded = jnp.concatenate([grad_key[..., :QK_NOPE], grad_values], axis=-1).astype(BF)
-    grad_expanded = grad_expanded.reshape(total, -1)
-    grad_expand = product_lead(latent.reshape(total, -1), grad_expanded)
-    grad_latent = product_trail(grad_expanded, expand_head)
-    grad_query = jnp.concatenate(
-        [grad_query[..., :QK_NOPE], rotate(grad_query[..., QK_NOPE:], cosine, -sine_table)], axis=-1
-    ).astype(BF)
-    grad_query = by_device(grad_query)
-    grad_query_w = product_lead(hidden_all, grad_query)
-    back_part = product_trail(grad_query, query_head).astype(BF)
-    latent_part = jnp.concatenate(
-        [grad_latent.astype(BF).reshape(batches, seq_total, -1), grad_key[..., QK_NOPE:].astype(BF),
-         jnp.zeros((batches, seq_total, 64), BF)], axis=-1)
-    back_part = jnp.concatenate([back_part, by_device(latent_part)], axis=1)
+    grad_attn_all = gather16(grad_middle.astype(BF), 6).reshape(GROUPS, batches, here, width)
+    back_part, grad_query, grad_output, grad_expand = attend_back(
+        seq_lengths, grad_attn_all, query, key, values, latent, attended, log_total, output_head, parts_head,
+        expand_head, cosine, sine_table, 640)
+    grad_query_w = product_lead(hidden_all, grad_query.reshape(total, TILE)).astype(BF)
     parts_grad = jnp.concatenate(
-        [grad_query_w.astype(BF), grad_expand.astype(BF).reshape(width, ROPE)], axis=1)
+        [grad_query_w[:, : QK_NOPE + ROPE], grad_expand.astype(BF).reshape(width, ROPE)], axis=1)
     back_sum, out_parts, out_output = returning(
-        dp, back_part.reshape(GROUPS, own, back_part.shape[1]),
+        dp, back_part.reshape(GROUPS, own, back_part.shape[3]),
         parts_grad.reshape(dp, GROUPS, rows_w, TILE), grad_output.astype(BF).reshape(dp, rows_w, width), 7)
     out_query = out_parts[..., : QK_NOPE + ROPE].transpose(1, 0, 2).reshape(rows_w, -1)
     out_expand = out_parts[..., QK_NOPE + ROPE :].reshape(H, rows_l, QK_NOPE + V_DIM)
@@ -1213,8 +1377,8 @@
         out_output,
         small_sum[:, 593],
         small_sum[:, 576:592],
-        out_fan[:, :, 0].reshape(-1, ff).astype(F32)[None],
-        out_fan[:, :, 1].reshape(-1, ff).astype(F32)[None],
+        out_gate.astype(F32)[None],
+        out_up.astype(F32)[None],
         out_down.astype(F32)[None],
         out_share[:share_width].T,
         out_share[share_width : 2 * share_width].T,

time: 1020 us -> 951 us (0.932)
  waiting for transfers between devices: 18.2 us -> 144 us
  local copies, waits for them, and re-layouts: 157 us -> 56.8 us
  other arithmetic: 110 us -> 45 us
  matrix products: 114 us -> 62.9 us
  Pallas kernels: 600 us -> 621 us
    all_gather x1, waiting for transfers between devices: 0.01 us -> 75.9 us  [per_device(): down_full = lax.all_gather(down_weight[0], 'dp', axis=0, tiled=True)]
    convert_element_type x4 -> x3, other arithmetic: 51.7 us -> 2.51 us  [the longest x1 1.29 us: per_device(): grad_output.astype(BF).reshape(dp, rows_w, width)]
    all_gather x1 -> x2, waiting for transfers between devices: 17 us -> 65.2 us  [the longest x1 65.2 us: per_device(): up_full = lax.all_gather(up_weight[0], 'dp', axis=0, tiled=True)]
    pallas_call x0 -> x3, Pallas kernels: none -> 46.8 us  [the longest x1 20.4 us: attend_back(): pl.pallas_call(attend_back_kernel, grid=(batches,), out_shape=(shape((gro...]
    pallas_call x1, Pallas kernels: 134 us -> 88.2 us  [opening(): pl.pallas_call(functools.partial(opening_kernel, dp, chunks), out_shape=(...]
    reshape x5 -> x1, local copies, waits for them, and re-layouts: 28.8 us -> 0.33 us  [per_device(): parts_head[:, QK_NOPE + ROPE:].reshape(KV_RANK, QK_NOPE + V_DIM)]
    pallas_call x3, Pallas kernels: 154 us -> 176 us  [scatter16(): pl.pallas_call(functools.partial(scatter_kernel, chunks), out_shape=jax.S...]
    dot_general x6 -> x0, matrix products: 19.4 us -> none  [the longest x1 6 us: per_device(): jnp.einsum('bts,btd->bsd', probs_low, grad_attended, preferred_element_ty...]
  transfers between devices with their start and end apart: 7 -> 9, of which waited for: 1 -> 2; matrix products, arithmetic and copies ran while one was open for 28% -> 14% of each run, Pallas kernels for 50% -> 56%
where the time goes in v3:
time: 951 us; the launch traced here: 946 us
  Pallas kernels  621 us (65%)
  waiting for transfers between devices  144 us (15%)
  matrix products  62.9 us (7%)
  local copies, waits for them, and re-layouts  56.8 us (6%)
  other arithmetic  45 us (5%)
  between operations  15.4 us (2%)
    pallas_call x3, Pallas kernels, scatter16(): pl.pallas_call(functools.partial(scatter_kernel, chunks), out_shape=jax.S...  176 us
    pallas_call x2, Pallas kernels, gather16(): pl.pallas_call(functools.partial(gather_kernel, chunks), out_shape=jax.Sh...  103 us
    pallas_call x1, Pallas kernels, mixture(): pl.pallas_call(mixture_kernel, grid=(steps,), out_shape=(shape((total, wi...  91.7 us
    pallas_call x1, Pallas kernels, opening(): pl.pallas_call(functools.partial(opening_kernel, dp, chunks), out_shape=(...  88.2 us
    pallas_call x1, Pallas kernels, returning(): pl.pallas_call(functools.partial(return_kernel, dp, chunks), out_shape=(s...  81.5 us
    all_gather x1, waiting for transfers between devices, per_device(): down_full = lax.all_gather(down_weight[0], 'dp', axis=0, tiled=True)  75.9 us
    all_gather x1, waiting for transfers between devices, per_device(): up_full = lax.all_gather(up_weight[0], 'dp', axis=0, tiled=True)  65.2 us
    dot_general x7, matrix products, product_lead(): lax.dot_general(left_side, right_side, (((0,), (0,)), ((), ())), preferre...  51.7 us
  transfers between devices with their start and end apart: 9, of which 2 were waited for; matrix products, arithmetic and copies ran while one was open for 14% of the time, Pallas kernels for 56%

profile of v3, /device:TPU:0, one launch (start us, length us, event | category | flops | bytes accessed | tf_op | source)
XLA Modules:
  0.0 945.7 jit_solution(2369145243045613086)
XLA Ops:
  14.8 88.2 %opening.1 = (bf16[16,128,2048]{2,1,0:T(8,128)(2,1)}, bf16[2,16,64,640]{3,2,1,0:T(8,128)(2,1)}, bf16[2,16,64,256]{3,2,1,0:T(8,128)(2,1)}, bf16[2,64,2048]{2,1,0:...) custom-call(bf16[128,2048]{1,0:T(8,128)(2,1)} %bitcast.158, ...), custom_call_target="tpu_custom_call" | custom-call | bytes 4000000 | tf_op jit(solution)/shard_map/opening/pallas_call | solution.py:352
  114.4 16.6 %project.1 = (bf16[2048,2048]{1,0:T(8,128)(2,1)}, bf16[2,1024,256]{2,1,0:T(8,128)(2,1)S(1)}, bf16[2,1024,256]{2,1,0:T(8,128)(2,1)S(1)}, bf16[2,1024,128]{2,1,0:T(8,128)(2,1)S(1)}, bf16[2,1024,512]{2,1,0:T(8,128)(2,1)}) custom-call(bf16[16,128,2048]{2,1,0:T(8,128)(2,1)} %get-tuple-element.66, f32[1,2048]{1,0:T(1,128)S(1)} %bitcast.143, ...), custom_call_target="tpu_custom_call" | custom-call | flops 7000000000 | bytes 20000000 | tf_op jit(solution)/shard_map/project/pallas_call | solution.py:948
  131.0 9.9 %attend.1 = (bf16[16,2,64,2048]{3,2,1,0:T(8,128)(2,1)}, bf16[16,2,64,128]{3,2,1,0:T(8,128)(2,1)S(1)}, f32[2,1024,1]{2,1,0:T(8,128)S(1)}) custom-call(s32[2]{0:T(128)S(1)} %bitcast.147, bf16[2,1024,256]{2,1,0:T(8,128)(2,1)S(1)} %get-tuple-element.70.q_ref, bf16[2,1024,256]{2,1,0:T(8,128)(2,1)S(1)} %get-tuple-element.71.k_ref, ...), custom_call_target="tpu_custom_call" | custom-call | flops 4000000000 | bytes 15000000 | tf_op jit(solution)/shard_map/attend/pallas_call | solution.py:1006
  140.9 4.0 copy-done.2
  145.0 72.6 %scatter16.3 = f32[128,2048]{1,0:T(8,128)S(1)} custom-call(bf16[16,128,2048]{2,1,0:T(8,128)(2,1)S(1)} %bitcast.136), custom_call_target="tpu_custom_call" | custom-call | bytes 4000000 | tf_op jit(solution)/shard_map/scatter16/pallas_call | solution.py:539
  220.0 51.0 %gather16.2 = bf16[16,128,2048]{2,1,0:T(8,128)(2,1)} custom-call(bf16[128,2048]{1,0:T(8,128)(2,1)} %multiply_convert_fusion.x_ref), custom_call_target="tpu_custom_call" | custom-call | bytes 4000000 | tf_op jit(solution)/shard_map/gather16/pallas_call | solution.py:206
  289.5 65.2 %all-gather.14.cloned.1.call-done = bf16[1,2048,1408]{2,1,0:T(8,128)(2,1)} async-done(((bf16[1,1024,1408]{2,1,0:T(8,128)(2,1)}), bf16[1,2048,1408]{2,1,0:T(8,128)(2,1)}) %all-gather.14.cloned.1.call-update) | async-done | bytes 5767184 | tf_op jit(solution)/shard_map/all_gather | solution.py:1233
  354.7 75.9 %all-gather.16.cloned.1.call-done = bf16[1,1408,2048]{2,1,0:T(8,128)(2,1)} async-done(((bf16[1,704,2048]{2,1,0:T(8,128)(2,1)}), bf16[1,1408,2048]{2,1,0:T(8,128)(2,1)}) %all-gather.16.cloned.1.call-update) | async-done | bytes 5767184 | tf_op jit(solution)/shard_map/all_gather | solution.py:1234
  430.6 91.7 %mixture.1 = (bf16[2048,2048]{1,0:T(8,128)(2,1)}, bf16[2048,2176]{1,0:T(8,128)(2,1)}, bf16[1024,2048]{1,0:T(8,128)(2,1)}, bf16[1024,2048]{1,0:T(8,128)(2,1)}, bf...) custom-call(f32[1,256]{1,0:T(1,128)} %add_convert_fusion.2.pick_ref,, ...), custom_call_target="tpu_custom_call" | custom-call | flops 60000002048 | bytes 60000000 | tf_op jit(solution)/shard_map/mixture/pallas_call | solution.py:877
  522.3 8.7 convolution_convert_fusion.3
  536.5 10.7 %convolution_convert_fusion.2 = bf16[1408,2048]{1,0:T(8,128)(2,1)} fusion(bf16[1024,1408]{1,0:T(8,128)(2,1)} %get-tuple-element.78, bf16[1024,2048]{1,0:T(8,128)(2,1)} %get-tuple-element.79), kind=kOutput, calls=%fused_computation.4 | convolution fusion | flops 5908463616 | bytes 12845056 | tf_op jit(solution)/shard_map/dot_general | solution.py:1116
  547.2 11.0 %convolution_convert_fusion = bf16[2048,1408]{1,0:T(8,128)(2,1)} fusion(bf16[1024,2048]{1,0:T(8,128)(2,1)} %get-tuple-element.80, bf16[1024,1408]{1,0:T(8,128)(2,1)} %get-tuple-element.82), kind=kOutput, calls=%fused_computation.2 | convolution fusion | flops 5908463616 | bytes 12845056 | tf_op jit(solution)/shard_map/dot_general | solution.py:1116
  558.1 11.0 %convolution_convert_fusion.1 = bf16[2048,1408]{1,0:T(8,128)(2,1)} fusion(bf16[1024,2048]{1,0:T(8,128)(2,1)} %get-tuple-element.80, bf16[1024,1408]{1,0:T(8,128)(2,1)} %get-tuple-element.81), kind=kOutput, calls=%fused_computation.3 | convolution fusion | flops 5908463616 | bytes 12845056 | tf_op jit(solution)/shard_map/dot_general | solution.py:1116
  584.6 53.4 %scatter16.5 = f32[128,2176]{1,0:T(8,128)S(1)} custom-call(bf16[16,128,2176]{2,1,0:T(8,128)(2,1)S(1)} %bitcast.134), custom_call_target="tpu_custom_call" | custom-call | bytes 4000000 | tf_op jit(solution)/shard_map/scatter16/pallas_call | solution.py:539
  643.0 51.8 %gather16.3 = bf16[16,128,2048]{2,1,0:T(8,128)(2,1)} custom-call(bf16[128,2048]{1,0:T(8,128)(2,1)} %fusion.43.x_ref), custom_call_target="tpu_custom_call" | custom-call | bytes 4000000 | tf_op jit(solution)/shard_map/gather16/pallas_call | solution.py:206
  694.8 20.4 %attend_back.1 = (bf16[16,2,64,2688]{3,2,1,0:T(8,128)(2,1)}, bf16[16,2,64,256]{3,2,1,0:T(8,128)(2,1)}, f32[128,2048]{1,0:T(8,128)}, f32[512,256]{1,0:T(8,128)}) custom-call(s32[2]{0:T(128)} %bitcast.144, bf16[16,2,64,2048]{3,2,1,0:T(8,128)(2,1)} %bitcast.157, bf16[2,1024,256]{2,1,0:T(8,128)(2,1)} %copy-done.9, bf16[2,1024,256]{2,1,0:T(8,128)(2,1)} %copy-done.10, ...), custom_call_target="tpu_custom_call" | custom-call | flops 14000000000 | bytes 25000000 | tf_op jit(solution)/shard_map/attend_back/pallas_call | solution.py:1086
  715.1 6.1 fusion.47
  724.2 81.5 %returning.1 = (f32[128,2688]{1,0:T(8,128)S(1)}, bf16[2,16,64,256]{3,2,1,0:T(8,128)(2,1)S(1)}, bf16[2,64,2048]{2,1,0:T(8,128)(2,1)S(1)}, bf16[1,16,64,256]{3,2,1,0:T(8,128)(2,1)S(1)}, bf16[1,64,2048]{2,1,0:T(8,128)(2,1)S(1)}) custom-call(bf16[16,128,2688]{2,1,0:T(8,128)(2,1)} %bitcast.151, bf16[2,16,64,256]{3,2,1,0:T(8,128)(2,1)S(1)} %pad_maximum_fusion.2.parts_ref, ...), custom_call_target="tpu_custom_call" | custom-call | bytes 4000000 | tf_op jit(solution)/shard_map/returning/pallas_call | solution.py:651
  822.8 3.9 fusion.18
  828.9 33.3 %closing.1 = (bf16[128,640]{1,0:T(8,128)(2,1)S(1)}, bf16[1,64,640]{2,1,0:T(8,128)(2,1)S(1)}) custom-call(bf16[16,128,640]{2,1,0:T(8,128)(2,1)S(1)} %bitcast.133), custom_call_target="tpu_custom_call" | custom-call | bytes 4000000 | tf_op jit(solution)/shard_map/closing/pallas_call | solution.py:718
  866.5 50.5 %scatter16.4 = f32[128,2048]{1,0:T(8,128)S(1)} custom-call(bf16[16,128,2048]{2,1,0:T(8,128)(2,1)S(1)} %bitcast.135), custom_call_target="tpu_custom_call" | custom-call | bytes 4000000 | tf_op jit(solution)/shard_map/scatter16/pallas_call | solution.py:539
  924.2 5.1 bitcast_convert_fusion
  929.3 4.7 bitcast_convert_fusion.1
  934.0 4.7 bitcast_convert_fusion.2
  (281 shorter events, 98.5 us)
Async XLA Ops:
  7.2 266.0 %all-gather.18.cloned.1.call-start = ((), (), s32[]{:S(2)}) async-start(), calls=%async_computation.12 | async-start | bytes 3244032 | tf_op jit(solution)/shard_map/all_gather | solution.py:1235
  9.8 274.8 %all-gather.10.cloned.1.call-start = ((), (), s32[]{:S(2)}) async-start(), calls=%async_computation.4 | async-start | bytes 9469952 | tf_op jit(solution)/shard_map/all_gather | solution.py:1262
  103.0 186.5 %all-gather.12.cloned.1.call-start = ((), (), s32[]{:S(2)}) async-start(), calls=%async_computation.9 | async-start | bytes 8650752 | tf_op jit(solution)/shard_map/all_gather | solution.py:1232
  103.7 251.0 %all-gather.14.cloned.1.call-start = ((), (), s32[]{:S(2)}) async-start(), calls=%async_computation.10 | async-start | bytes 8650752 | tf_op jit(solution)/shard_map/all_gather | solution.py:1233
  104.3 326.3 %all-gather.16.cloned.1.call-start = ((), (), s32[]{:S(2)}) async-start(), calls=%async_computation.11 | async-start | bytes 8650752 | tf_op jit(solution)/shard_map/all_gather | solution.py:1234
  104.9 816.4 %reduce-scatter.11.cloned.1.call-start = ((), (), s32[]{:S(2)}) async-start(), calls=%async_computation.8 | async-start | bytes 3244032 | tf_op jit(solution)/shard_map/reduce_scatter | solution.py:1313
  107.2 110.7 %copy-start.5 = (f32[2048]{0:T(1024)}, f32[2048]{0:T(1024)S(1)}, u32[]{:S(2)}) copy-start(f32[2048]{0:T(1024)S(1)} %get-tuple-element.185) | copy-start | bytes 24580
  140.9 76.7 %copy-start.11 = (f32[2,1024,1]{2,1,0:T(8,128)}, f32[2,1024,1]{2,1,0:T(8,128)S(1)}, u32[]{:S(2)}) copy-start(f32[2,1024,1]{2,1,0:T(8,128)S(1)} %get-tuple-element.86.lse_ref) | copy-start | bytes 24580
  140.9 76.7 %copy-start.13 = (bf16[16,2,64,128]{3,2,1,0:T(8,128)(2,1)}, bf16[16,2,64,128]{3,2,1,0:T(8,128)(2,1)S(1)}, u32[]{:S(2)}) copy-start(bf16[16,2,64,128]{3,2,1,0:T(8,128)(2,1)S(1)} %get-tuple-element.85.att_ref) | copy-start | bytes 1572868
  145.0 72.6 %copy-start.16 = (bf16[2,1,64,2048]{3,2,1,0:T(8,128)(2,1)S(1)}, bf16[2,1,64,2048]{3,2,1,0:T(8,128)(2,1)}, u32[]{:S(2)}) copy-start(bf16[2,1,64,2048]{3,2,1,0:T(8,128)(2,1)} %param.20) | copy-start | bytes 1572868
  536.4 387.7 %reduce-scatter.9.cloned.1.call-start = ((), (), s32[]{:S(2)}) async-start(), calls=%async_computation.7 | async-start | bytes 8650752 | tf_op jit(solution)/shard_map/reduce_scatter | solution.py:1306
  569.1 360.1 %reduce-scatter.7.cloned.1.call-start = ((), (), s32[]{:S(2)}) async-start(), calls=%async_computation.6 | async-start | bytes 8650752 | tf_op jit(solution)/shard_map/reduce_scatter | solution.py:1308
  569.9 364.1 %reduce-scatter.5.cloned.1.call-start = ((), (), s32[]{:S(2)}) async-start(), calls=%async_computation.5 | async-start | bytes 8650752 | tf_op jit(solution)/shard_map/reduce_scatter | solution.py:1307
  574.6 63.5 %copy-start.25 = (f32[1024,32]{1,0:T(8,128)}, f32[1024,32]{1,0:T(8,128)S(1)}, u32[]{:S(2)}) copy-start(f32[1024,32]{1,0:T(8,128)S(1)} %get-tuple-element.211.sin_ref) | copy-start | bytes 393220
  574.6 63.5 %copy-start.26 = (f32[1024,32]{1,0:T(8,128)}, f32[1024,32]{1,0:T(8,128)S(1)}, u32[]{:S(2)}) copy-start(f32[1024,32]{1,0:T(8,128)S(1)} %get-tuple-element.212.cos_ref) | copy-start | bytes 393220
  584.6 53.5 %copy-start.43 = (f32[128]{0:T(128)S(1)}, f32[128]{0:T(128)}, u32[]{:S(2)}) copy-start(f32[128]{0:T(128)} %copy-done.42) | copy-start | bytes 1540
  584.6 53.9 %copy-start.38 = (f32[128]{0:T(128)S(1)}, f32[128]{0:T(128)}, u32[]{:S(2)}) copy-start(f32[128]{0:T(128)} %copy-done.37) | copy-start | bytes 1540
  640.7 54.0 %copy-start.53 = (f32[128]{0:T(128)}, f32[128]{0:T(128)S(1)}, u32[]{:S(2)}) copy-start(f32[128]{0:T(128)S(1)} %broadcast_multiply_fusion.2) | copy-start | bytes 1540
  862.3 55.4 %copy-start.29 = (f32[64,640]{1,0:T(8,128)}, f32[64,640]{1,0:T(8,128)S(1)}, u32[]{:S(2)}) copy-start(f32[64,640]{1,0:T(8,128)S(1)} %convert_add_fusion.1) | copy-start | bytes 491524
  866.4 52.8 %copy-start.39 = (f32[128]{0:T(128)S(1)}, f32[128]{0:T(128)}, u32[]{:S(2)}) copy-start(f32[128]{0:T(128)} %copy-done.37) | copy-start | bytes 1540
  866.4 52.8 %copy-start.44 = (f32[128]{0:T(128)S(1)}, f32[128]{0:T(128)}, u32[]{:S(2)}) copy-start(f32[128]{0:T(128)} %copy-done.42) | copy-start | bytes 1540
  866.4 52.8 %copy-start.47 = (bf16[128]{0:T(256)(128)(2,1)S(1)}, bf16[128]{0:T(256)(128)(2,1)}, u32[]{:S(2)}) copy-start(bf16[128]{0:T(256)(128)(2,1)} %copy-done.45) | copy-start | bytes 772
  866.4 52.8 %copy-start.50 = (f32[128]{0:T(128)S(1)}, f32[128]{0:T(128)}, u32[]{:S(2)}) copy-start(f32[128]{0:T(128)} %copy-done.49) | copy-start | bytes 1540
  866.5 52.8 %copy-start.54 = (f32[128]{0:T(128)S(1)}, f32[128]{0:T(128)}, u32[]{:S(2)}) copy-start(f32[128]{0:T(128)} %copy-done.53) | copy-start | bytes 1540
  (47 other events, 527.6 us)
Sparse Core Ops, SparseCore 0:
  10.2 55.1 all-gather.17
  103.1 96.0 all-gather.9
  200.7 78.0 all-gather.11
  280.2 74.4 all-gather.13
  356.1 74.4 all-gather.15
  536.6 32.5 reduce-scatter.10
  572.1 71.3 reduce-scatter.8
  646.4 71.3 reduce-scatter.6
  720.8 88.2 reduce-scatter.4

commit v4 on v3

--- a/solution.py
+++ b/solution.py
@@ -750,16 +750,44 @@
 SHARE = 176
 
 
-def mixture_kernel(pick_ref, mix_ref, dy_ref, slot_row, slot_col, valid_ref, wg_ref, wu_ref, wd_ref, fan_ref, sd_ref,
-                   out_ref, dh_ref, rows_ref, deo_ref, hid_ref, dg_ref, du_ref, sh_ref, ds_ref,
-                   act_buf, slo_buf):
+def one_hots(slot_row, slot_col, groups, slots):
+    to_slot, to_token = [], []
+    for g in range(groups):
+        row = slot_row[:, g * 256:(g + 1) * 256]
+        col = slot_col[g * 256:(g + 1) * 256, :]
+        to_slot.append((lax.broadcasted_iota(jnp.int32, (slots, 256), 0) == row).astype(BF))
+        to_token.append((lax.broadcasted_iota(jnp.int32, (256, slots), 1) == col).astype(BF))
+    return to_slot, to_token
+
+
+def lanes(j):
+    return pl.ds(pl.multiple_of(j * WIDE, WIDE), WIDE)
+
+
+def over_columns(total, body):
+    def step(j, _):
+        body(pl.multiple_of(j * WIDE, WIDE), WIDE)
+        return 0
+
+    lax.fori_loop(0, total // WIDE, step, 0)
+    if total % WIDE:
+        body(total // WIDE * WIDE, total % WIDE)
+
+
+def forward_kernel(chunks, pick_ref, mix_ref, routes_ref, slot_row, slot_col, valid_ref, wg_ref, wu_ref, wd_ref,
+                   fan_ref, sd_ref, dy_ref,
+                   out_ref, rows_ref, hid_ref, act_ref, slo_ref, eo_ref, sh_ref, sact_ref, sslo_ref, gate_ref,
+                   dy_all, *sems):
+    step = pl.program_id(0)
     tokens, width = mix_ref.shape
-    groups = tokens // 256
-    slots = 128
+    groups, slots = tokens // 256, 128
     ff = hid_ref.shape[1]
-
-    def lanes(j):
-        return pl.ds(pl.multiple_of(j * WIDE, WIDE), WIDE)
+    g = Gather(dy_ref, dy_all, chunks, sems)
+
+    @pl.when(step == 0)
+    def _():
+        enter(g.me, g.z, g.core, g.side)
+        g.start()
 
     mix = mix_ref[...]
     fanned = mm_t(mix, fan_ref[:TILE, :])
@@ -767,35 +795,24 @@
     s_act, s_slope = silu_pair(fanned)
     s_hidden = (s_act * s_up).astype(BF)
     sh_ref[...] = s_hidden
+    sact_ref[...] = s_act.astype(BF)
+    sslo_ref[...] = (s_up * s_slope).astype(BF)
     logits = fanned[:, SHARE:SHARE + 16]
-    lane16 = lax.broadcasted_iota(jnp.int32, (tokens, 16), 1).astype(F32)
-    routes = dy_ref[:, width:width + 16].astype(F32)
+    lane16 = lax.broadcasted_iota(jnp.int32, (tokens, 16), 1)
     mask = lane16 < 0
-    for k in range(6):
-        mask = mask | (lane16 == routes[:, k:k + 1])
+    for k in range(routes_ref.shape[1]):
+        mask = mask | (lane16 == routes_ref[:, k:k + 1])
     held = jnp.where(mask, logits, -1e30)
     raised = jnp.where(mask, jnp.exp(held - jnp.max(held, axis=1, keepdims=True)), 0.0)
     soft = raised / jnp.sum(raised, axis=1, keepdims=True)
     gate = jnp.sum(soft * pick_ref[:, :16], axis=1, keepdims=True) * valid_ref[...]
-    dy = dy_ref[:, :width]
-    d_sh = mm_t(dy, sd_ref[...])
-    ds_ref[:, :TILE] = (d_sh * s_up * s_slope).astype(BF)
-    ds_ref[:, TILE:] = (d_sh * s_act).astype(BF)
-
-    to_slot, to_token = [], []
-    for g in range(groups):
-        row = slot_row[:, g * 256:(g + 1) * 256]
-        col = slot_col[g * 256:(g + 1) * 256, :]
-        to_slot.append((lax.broadcasted_iota(jnp.int32, (slots, 256), 0) == row).astype(BF))
-        to_token.append((lax.broadcasted_iota(jnp.int32, (256, slots), 1) == col).astype(BF))
+    gate_ref[...] = gate
+    to_slot, to_token = one_hots(slot_row, slot_col, groups, slots)
 
     def dispatch(j, _):
-        for g in range(groups):
-            t = pl.ds(g * 256, 256)
-            s = pl.ds(g * slots, slots)
-            rows_ref[s, lanes(j)] = mm(to_slot[g], mix_ref[t, lanes(j)]).astype(BF)
-            gated = (gate[g * 256:(g + 1) * 256] * dy_ref[t, lanes(j)].astype(F32)).astype(BF)
-            deo_ref[s, lanes(j)] = mm(to_slot[g], gated).astype(BF)
+        for n in range(groups):
+            rows_ref[n * slots:(n + 1) * slots, lanes(j)] = mm(
+                to_slot[n], mix_ref[n * 256:(n + 1) * 256, lanes(j)]).astype(BF)
         return 0
 
     lax.fori_loop(0, width // WIDE, dispatch, 0)
@@ -806,40 +823,89 @@
         up_in = mm(rows_ref[...], wu_ref[:, cols])
         act, slope = silu_pair(gate_in)
         hid_ref[:, cols] = (act * up_in).astype(BF)
-        act_buf[:, cols] = act
-        slo_buf[:, cols] = up_in * slope
-
-    def fan_loop(j, _):
-        fan_in(pl.multiple_of(j * WIDE, WIDE), WIDE)
-        return 0
-
-    lax.fori_loop(0, ff // WIDE, fan_loop, 0)
-    if ff % WIDE:
-        fan_in(ff // WIDE * WIDE, ff % WIDE)
-
-    def fan_out(j, d_gates):
+        act_ref[:, cols] = act.astype(BF)
+        slo_ref[:, cols] = (up_in * slope).astype(BF)
+
+    over_columns(ff, fan_in)
+
+    def fan_out(j, _):
         eo = mm(hid_ref[...], wd_ref[:, lanes(j)]).astype(BF)
+        eo_ref[:, lanes(j)] = eo
         shared = mm(s_hidden, sd_ref[:, lanes(j)])
         picked = jnp.concatenate(
-            [mm(to_token[g], eo[g * slots:(g + 1) * slots]) for g in range(groups)], axis=0)
+            [mm(to_token[n], eo[n * slots:(n + 1) * slots]) for n in range(groups)], axis=0)
         out_ref[:, lanes(j)] = (shared + gate * picked).astype(BF)
-        return d_gates + jnp.sum(dy_ref[:, lanes(j)].astype(F32) * picked, axis=1, keepdims=True)
-
-    d_gates = lax.fori_loop(0, width // WIDE, fan_out, jnp.zeros((tokens, 1), F32))
+        return 0
+
+    lax.fori_loop(0, width // WIDE, fan_out, 0)
+    steps = pl.num_programs(0)
+    for r in range(1, NZ + 1):
+        @pl.when(step == r - 1)
+        def _():
+            g.round(r)
+
+    @pl.when(step == steps - 1)
+    def _():
+        g.finish()
+
+
+def backward_kernel(chunks, pick_ref, dy_ref, slot_row, slot_col, wg_ref, wu_ref, wd_ref, fan_ref, sd_ref,
+                    act_ref, slo_ref, eo_ref, sact_ref, sslo_ref, gate_ref, part_ref,
+                    dh_ref, deo_ref, dg_ref, du_ref, ds_ref, sum_ref, *scratch):
+    step = pl.program_id(0)
+    tokens, width = dy_ref.shape
+    groups, slots = tokens // 256, 128
+    ff = dg_ref.shape[1]
+    sc = Scatter(part_ref, sum_ref, chunks, scratch)
+
+    @pl.when(step == 0)
+    def _():
+        enter(sc.me, sc.z, sc.core, sc.side)
+        sc.start()
+
+    d_sh = mm_t(dy_ref[...], sd_ref[...])
+    ds_ref[:, :TILE] = (d_sh * sslo_ref[...].astype(F32)).astype(BF)
+    ds_ref[:, TILE:] = (d_sh * sact_ref[...].astype(F32)).astype(BF)
+    to_slot, to_token = one_hots(slot_row, slot_col, groups, slots)
+    gate = gate_ref[...]
+
+    def dispatch(j, total):
+        dy = dy_ref[:, lanes(j)].astype(F32)
+        gated = (gate * dy).astype(BF)
+        for n in range(groups):
+            deo_ref[n * slots:(n + 1) * slots, lanes(j)] = mm(to_slot[n], gated[n * 256:(n + 1) * 256]).astype(BF)
+        picked = jnp.concatenate(
+            [mm(to_token[n], eo_ref[n * slots:(n + 1) * slots, lanes(j)]) for n in range(groups)], axis=0)
+        return total + jnp.sum(dy * picked, axis=1, keepdims=True)
+
+    d_gates = lax.fori_loop(0, width // WIDE, dispatch, jnp.zeros((tokens, 1), F32))
+
+    @pl.when(step == 0)
+    def _():
+        sc.first(0)
+        sc.first(1)
 
     def back_out(start, size):
         cols = pl.ds(start, size)
         d_eh = mm_t(deo_ref[...], wd_ref[cols, :])
-        dg_ref[:, cols] = (d_eh * slo_buf[:, cols]).astype(BF)
-        du_ref[:, cols] = (d_eh * act_buf[:, cols]).astype(BF)
-
-    def back_loop(j, _):
-        back_out(pl.multiple_of(j * WIDE, WIDE), WIDE)
-        return 0
-
-    lax.fori_loop(0, ff // WIDE, back_loop, 0)
-    if ff % WIDE:
-        back_out(ff // WIDE * WIDE, ff % WIDE)
+        dg_ref[:, cols] = (d_eh * slo_ref[:, cols].astype(F32)).astype(BF)
+        du_ref[:, cols] = (d_eh * act_ref[:, cols].astype(F32)).astype(BF)
+
+    over_columns(ff, back_out)
+
+    @pl.when(step == 1)
+    def _():
+        sc.second(0)
+        sc.first(2)
+
+    @pl.when(step == 2)
+    def _():
+        sc.second(1)
+        sc.first(3)
+
+    @pl.when(step == 3)
+    def _():
+        sc.second(2)
 
     d_s = ds_ref[...]
 
@@ -847,49 +913,78 @@
         d_rows = (mm_t(dg_ref[...], wg_ref[lanes(j), :]) + mm_t(du_ref[...], wu_ref[lanes(j), :])).astype(BF)
         shared = mm(d_s, fan_ref[:, lanes(j)])
         taken = jnp.concatenate(
-            [mm(to_token[g], d_rows[g * slots:(g + 1) * slots]) for g in range(groups)], axis=0)
+            [mm(to_token[n], d_rows[n * slots:(n + 1) * slots]) for n in range(groups)], axis=0)
         dh_ref[:, lanes(j)] = (shared + taken).astype(BF)
         return 0
 
     lax.fori_loop(0, width // WIDE, back_in, 0)
     high = d_gates.astype(BF).astype(F32)
-    tail = high * pick_ref[:, :128] + (d_gates - high) * pick_ref[:, 128:]
-    dh_ref[:, width:] = tail.astype(BF)
-
-
-def mixture(pick, mix, packed, slot_row, slot_col, valid, wg, wu, wd, fan, sd, step=512):
+    dh_ref[:, width:] = (high * pick_ref[:, :128] + (d_gates - high) * pick_ref[:, 128:]).astype(BF)
+
+    @pl.when(step == 3)
+    def _():
+        sc.second(3)
+        sc.finish()
+
+
+def whole(v):
+    return pl.BlockSpec(v.shape, lambda i: (0, 0), pipeline_mode=pl.Buffered(buffer_count=1))
+
+
+def tiles(rows, w):
+    return pl.BlockSpec((rows, w), lambda i: (i, 0))
+
+
+def mixture_forward(pick, mix, routes, slot, valid, wg, wu, wd, fan, sd, dy, cid, chunks=2):
     total, width = mix.shape
-    steps = total // step
+    step, half = total // 4, total // 8
     ff = wd.shape[0]
+    shape = jax.ShapeDtypeStruct
     rows = total // 2
+    return pl.pallas_call(
+        functools.partial(forward_kernel, chunks),
+        grid=(4,),
+        out_shape=(
+            shape((total, width), BF), shape((rows, width), BF), shape((rows, ff), BF), shape((rows, ff), BF),
+            shape((rows, ff), BF), shape((rows, width), BF), shape((total, TILE), BF), shape((total, TILE), BF),
+            shape((total, TILE), BF), shape((total, 1), F32), shape((NE,) + dy.shape, BF)),
+        in_specs=[whole(pick), tiles(step, width), tiles(step, routes.shape[1]), pl.BlockSpec((1, step), lambda i: (0, i)),
+                  tiles(step, 1), tiles(step, 1), whole(wg), whole(wu), whole(wd), whole(fan), whole(sd), ANY],
+        out_specs=[tiles(step, width), tiles(half, width), tiles(half, ff), tiles(half, ff), tiles(half, ff),
+                   tiles(half, width), tiles(step, TILE), tiles(step, TILE), tiles(step, TILE), tiles(step, 1), ANY],
+        scratch_shapes=Gather.scratch(chunks),
+        compiler_params=pltpu.CompilerParams(
+            collective_id=cid, has_side_effects=True, vmem_limit_bytes=60 * 1024 * 1024),
+        cost_estimate=COST,
+        name="mixture_forward",
+    )(pick, mix, routes, slot[None, :], slot[:, None], valid, wg, wu, wd, fan, sd, dy)
+
+
+def mixture_backward(pick, dy, slot, wg, wu, wd, fan, sd, act, slo, eo, sact, sslo, gate, part, cid, chunks=2):
+    total, width = dy.shape
+    step, half = total // 4, total // 8
+    ff = wd.shape[0]
     shape = jax.ShapeDtypeStruct
-    once = pl.Buffered(buffer_count=1)
-
-    def whole(v):
-        return pl.BlockSpec(v.shape, lambda i: (0, 0), pipeline_mode=once)
-
-    def tokens(w):
-        return pl.BlockSpec((step, w), lambda i: (i, 0))
-
-    def slots(w):
-        return pl.BlockSpec((step // 2, w), lambda i: (i, 0))
-
+    rows = total // 2
+    _, own, _ = part.shape
     return pl.pallas_call(
-        mixture_kernel,
-        grid=(steps,),
+        functools.partial(backward_kernel, chunks),
+        grid=(4,),
         out_shape=(
-            shape((total, width), BF), shape((total, width + 128), BF), shape((rows, width), BF),
-            shape((rows, width), BF), shape((rows, ff), BF), shape((rows, ff), BF), shape((rows, ff), BF),
-            shape((total, TILE), BF), shape((total, 2 * TILE), BF)),
-        in_specs=[whole(pick), tokens(width), tokens(width + 128), pl.BlockSpec((1, step), lambda i: (0, i)),
-                  tokens(1), tokens(1), whole(wg), whole(wu), whole(wd), whole(fan), whole(sd)],
-        out_specs=[tokens(width), tokens(width + 128), slots(width), slots(width), slots(ff), slots(ff), slots(ff),
-                   tokens(TILE), tokens(2 * TILE)],
-        scratch_shapes=[pltpu.VMEM((step // 2, ff), F32), pltpu.VMEM((step // 2, ff), F32)],
-        compiler_params=pltpu.CompilerParams(vmem_limit_bytes=60 * 1024 * 1024),
-        cost_estimate=pl.CostEstimate(flops=60_000_000_000, bytes_accessed=60_000_000, transcendentals=0),
-        name="mixture",
-    )(pick, mix, packed, slot_row, slot_col, valid, wg, wu, wd, fan, sd)
+            shape((total, width + 128), BF), shape((rows, width), BF), shape((rows, ff), BF), shape((rows, ff), BF),
+            shape((total, 2 * TILE), BF), shape((own, width), F32)),
+        in_specs=[whole(pick), tiles(step, width), pl.BlockSpec((1, step), lambda i: (0, i)), tiles(step, 1),
+                  whole(wg), whole(wu), whole(wd), whole(fan), whole(sd),
+                  tiles(half, ff), tiles(half, ff), tiles(half, width), tiles(step, TILE), tiles(step, TILE),
+                  tiles(step, 1), ANY],
+        out_specs=[tiles(step, width + 128), tiles(half, width), tiles(half, ff), tiles(half, ff),
+                   tiles(step, 2 * TILE), pl.BlockSpec((own, width), lambda i: (0, 0))],
+        scratch_shapes=Scatter.scratch(own, width, chunks, BF),
+        compiler_params=pltpu.CompilerParams(
+            collective_id=cid, has_side_effects=True, vmem_limit_bytes=60 * 1024 * 1024),
+        cost_estimate=COST,
+        name="mixture_backward",
+    )(pick, dy, slot[None, :], slot[:, None], wg, wu, wd, fan, sd, act, slo, eo, sact, sslo, gate, part)
 
 
 def mm_lead(a, b):
@@ -1200,6 +1295,10 @@
     rows_l = expand_weight.shape[0]
 
     x_own = layer_input.reshape(own, width)
+    routes_own = routes.reshape(own, -1)
+    choices = routes_own.shape[1]
+    route_columns = routes_own.astype(BF).reshape(rows_w, -1)
+    small_width = -(-(595 + route_columns.shape[1]) // 128) * 128
     latent_column = jnp.zeros((rows_w,), BF).at[:rows_l].set(latent_gain)
     small = jnp.concatenate(
         [
@@ -1208,7 +1307,8 @@
             attn_gain[:, None],
             mixer_gain[:, None],
             latent_column[:, None],
-            jnp.zeros((rows_w, 640 - 595), BF),
+            route_columns,
+            jnp.zeros((rows_w, small_width - 595 - route_columns.shape[1]), BF),
         ],
         axis=1,
     )
@@ -1217,7 +1317,9 @@
     parts = jnp.concatenate([query_parts, expand_parts.reshape(H, rows_w, ROPE)], axis=2)
     x_all, small, parts_head, output_head = opening(dp, x_own, small, parts, output_weight, 1)
     x_all = x_all.reshape(total, width)
-    small = small.reshape(width, 640)
+    routes_all = lax.dynamic_index_in_dim(small, plane, 0, False)[..., 595 : 595 + route_columns.shape[1]]
+    routes_all = routes_all.reshape(total, choices).astype(jnp.int32)
+    small = small.reshape(width, small_width)
     parts_head = parts_head.reshape(width, TILE)
     latent_full = small[:, :576]
     router_full = small[:, 576:592]
@@ -1254,13 +1356,6 @@
         return v.reshape(batches, GROUPS, here, v.shape[-1]).swapaxes(0, 1).reshape(total, -1)
 
     grad_own = out_cotangent.reshape(own, width) * valid_own[:, None].astype(BF)
-    routes_own = routes.reshape(own, -1)
-    packed = jnp.concatenate(
-        [grad_own, routes_own.astype(BF), jnp.zeros((own, 128 - routes_own.shape[1]), BF)], axis=1
-    )
-    packed, x_all = lax.optimization_barrier((packed, x_all))
-    packed = lax.all_gather(packed, "expert", axis=0, tiled=True)
-    routes_all = packed[:, width : width + routes_own.shape[1]].astype(jnp.int32)
     taken = jnp.any(routes_all == me, axis=1) & valid_all
     places = jnp.cumsum(taken.reshape(-1, here).astype(jnp.int32), axis=1) - 1
     places = places + 32 * (jnp.arange(places.shape[0], dtype=jnp.int32) % 4)[:, None]
@@ -1290,17 +1385,20 @@
     down_share = jnp.concatenate([share_full[2 * share_width :], jnp.zeros((pad, width), BF)], axis=0)
     lane = jnp.arange(128)[None, :]
     pick = jnp.concatenate([lane == me, lane == me + GROUPS], axis=1).astype(F32)
-    out_part, mix_part, rows, grad_result, hidden, grad_gate_in, grad_up_in, share_hidden, grad_share_in = mixture(
-        pick, mix_all, packed, slot[None, :], slot[:, None], valid_all.astype(F32)[:, None],
-        gate_full, up_full, down_full, fan_share, down_share)
+    out_part, rows, hidden, act, slope, result, share_hidden, share_act, share_slope, gates, grad_all = mixture_forward(
+        pick, mix_all, routes_all, slot, valid_all.astype(F32)[:, None],
+        gate_full, up_full, down_full, fan_share, down_share, grad_own, 4)
+    grad_all = grad_all.reshape(total, width)
+    mix_part, grad_result, grad_gate_in, grad_up_in, grad_share_in, mixed = mixture_backward(
+        pick, grad_all, slot, gate_full, up_full, down_full, fan_share, down_share, act, slope, result,
+        share_act, share_slope, gates, out_part.reshape(GROUPS, own, width), 8)
     grad_down = product_lead(hidden, grad_result).astype(BF)
     grad_gate = product_lead(rows, grad_gate_in).astype(BF)
     grad_up = product_lead(rows, grad_up_in).astype(BF)
     grad_share_fan = product_lead(grad_share_in, mix_all).astype(BF)
-    grad_share_down = product_lead(share_hidden, packed[:, :width]).astype(BF)
+    grad_share_down = product_lead(share_hidden, grad_all).astype(BF)
     mix_part, grad_down, grad_gate, grad_up = lax.optimization_barrier((mix_part, grad_down, grad_gate, grad_up))
     mix_sum = scatter16(mix_part.reshape(GROUPS, own, width + 128), 5)
-    mixed = scatter16(out_part.reshape(GROUPS, own, width), 4)
     layer_output = valid_own[:, None] * (middle + mixed)
 
     out_down = lax.psum_scatter(grad_down, "dp", scatter_dimension=0, tiled=True)

time: 951 us -> 830 us (0.87)
  waiting for transfers between devices: 144 us -> 21.3 us
    pallas_call x3 -> x2, Pallas kernels: 176 us -> 104 us  [scatter16(): pl.pallas_call(functools.partial(scatter_kernel, chunks), out_shape=jax.S...]
    all_gather x1, waiting for transfers between devices: 65.2 us -> 0.02 us  [per_device(): up_full = lax.all_gather(up_weight[0], 'dp', axis=0, tiled=True)]
    pallas_call x1 -> x2, Pallas kernels: 91.7 us -> 155 us  [the longest x1 91.1 us: mixture_backward(): pl.pallas_call(functools.partial(backward_kernel, chunks), grid=(4,), out...]
    all_gather x1, waiting for transfers between devices: 75.9 us -> 18.3 us  [per_device(): down_full = lax.all_gather(down_weight[0], 'dp', axis=0, tiled=True)]
    unnamed x136 -> x132, local copies, waits for them, and re-layouts: 20.9 us -> 17.3 us
  transfers between devices with their start and end apart: 9 -> 8, of which waited for: 2 -> 1; matrix products, arithmetic and copies ran while one was open for 14% -> 16% of each run, Pallas kernels for 56% -> 56%
where the time goes in v4:
time: 830 us; the launch traced here: 822 us
  Pallas kernels  614 us (74%)
  matrix products  65.4 us (8%)
  local copies, waits for them, and re-layouts  57.5 us (7%)
  other arithmetic  47.6 us (6%)
  waiting for transfers between devices  21.3 us (3%)
  between operations  15.6 us (2%)
    pallas_call x2, Pallas kernels, scatter16(): pl.pallas_call(functools.partial(scatter_kernel, chunks), out_shape=jax.S...  104 us
    pallas_call x2, Pallas kernels, gather16(): pl.pallas_call(functools.partial(gather_kernel, chunks), out_shape=jax.Sh...  103 us
    pallas_call x1, Pallas kernels, mixture_backward(): pl.pallas_call(functools.partial(backward_kernel, chunks), grid=(4,), out...  91.1 us
    pallas_call x1, Pallas kernels, opening(): pl.pallas_call(functools.partial(opening_kernel, dp, chunks), out_shape=(...  88.3 us
    pallas_call x1, Pallas kernels, returning(): pl.pallas_call(functools.partial(return_kernel, dp, chunks), out_shape=(s...  82.8 us
    pallas_call x1, Pallas kernels, mixture_forward(): pl.pallas_call(functools.partial(forward_kernel, chunks), grid=(4,), out_...  63.8 us
    dot_general x7, matrix products, product_lead(): lax.dot_general(left_side, right_side, (((0,), (0,)), ((), ())), preferre...  55.4 us
    pallas_call x1, Pallas kernels, closing(): pl.pallas_call(functools.partial(closing_kernel, dp, 1), out_shape=(shape...  32.8 us
  transfers between devices with their start and end apart: 8, of which 1 were waited for; matrix products, arithmetic and copies ran while one was open for 16% of the time, Pallas kernels for 56%

profile of v4, /device:TPU:0, one launch (start us, length us, event | category | flops | bytes accessed | tf_op | source)
XLA Modules:
  0.0 822.1 jit_solution(2335134067410764717)
XLA Ops:
  15.1 88.3 %opening.1 = (bf16[16,128,2048]{2,1,0:T(8,128)(2,1)}, bf16[2,16,64,640]{3,2,1,0:T(8,128)(2,1)}, bf16[2,16,64,256]{3,2,1,0:T(8,128)(2,1)}, bf16[2,64,2048]{2,1,0:...) custom-call(bf16[128,2048]{1,0:T(8,128)(2,1)} %bitcast.171, ...), custom_call_target="tpu_custom_call" | custom-call | bytes 4000000 | tf_op jit(solution)/shard_map/opening/pallas_call | solution.py:352
  113.7 16.9 %project.1 = (bf16[2048,2048]{1,0:T(8,128)(2,1)}, bf16[2,1024,256]{2,1,0:T(8,128)(2,1)S(1)}, bf16[2,1024,256]{2,1,0:T(8,128)(2,1)S(1)}, bf16[2,1024,128]{2,1,0:T(8,128)(2,1)S(1)}, bf16[2,1024,512]{2,1,0:T(8,128)(2,1)}) custom-call(bf16[16,128,2048]{2,1,0:T(8,128)(2,1)} %get-tuple-element.72.x_ref, f32[1,2048]{1,0:T(1,128)S(1)} %bitcast.148, ...), custom_call_target="tpu_custom_call" | custom-call | flops 7000000000 | bytes 20000000 | tf_op jit(solution)/shard_map/project/pallas_call | solution.py:1043
  139.2 10.1 %attend.1 = (bf16[16,2,64,2048]{3,2,1,0:T(8,128)(2,1)}, bf16[16,2,64,128]{3,2,1,0:T(8,128)(2,1)S(1)}, f32[2,1024,1]{2,1,0:T(8,128)S(1)}) custom-call(s32[2]{0:T(128)S(1)} %bitcast.152, bf16[2,1024,256]{2,1,0:T(8,128)(2,1)S(1)} %copy-done.7, bf16[2,1024,256]{2,1,0:T(8,128)(2,1)S(1)} %copy-done.9, bf16[2,1024,128]{2,1,0:T(8,128)(2,1)S(1)} %get-tuple-element.77.v_ref, ...), custom_call_target="tpu_custom_call" | custom-call | flops 4000000000 | bytes 15000000 | tf_op jit(solution)/shard_map/attend/pallas_call | solution.py:1101
  149.3 4.6 copy-done.1
  153.9 51.6 %scatter16.2 = f32[128,2048]{1,0:T(8,128)S(1)} custom-call(bf16[16,128,2048]{2,1,0:T(8,128)(2,1)S(1)} %bitcast.141), custom_call_target="tpu_custom_call" | custom-call | bytes 4000000 | tf_op jit(solution)/shard_map/scatter16/pallas_call | solution.py:539
  207.9 51.7 %gather16.2 = bf16[16,128,2048]{2,1,0:T(8,128)(2,1)} custom-call(bf16[128,2048]{1,0:T(8,128)(2,1)} %multiply_convert_fusion.x_ref), custom_call_target="tpu_custom_call" | custom-call | bytes 4000000 | tf_op jit(solution)/shard_map/gather16/pallas_call | solution.py:206
  272.2 18.3 %all-gather.13.cloned.1.call-done = bf16[1,1408,2048]{2,1,0:T(8,128)(2,1)} async-done(((bf16[1,704,2048]{2,1,0:T(8,128)(2,1)}), bf16[1,1408,2048]{2,1,0:T(8,128)(2,1)}) %all-gather.13.cloned.1.call-update) | async-done | bytes 5767184 | tf_op jit(solution)/shard_map/all_gather | solution.py:1336
  290.5 63.8 %mixture_forward.1 = (bf16[2048,2048]{1,0:T(8,128)(2,1)}, bf16[1024,2048]{1,0:T(8,128)(2,1)}, bf16[1024,1408]{1,0:T(8,128)(2,1)}, bf16[1024,1408]{1,0:T(8,128)(2...) custom-call(f32[1,256]{1,0:T(1,128)} %add_convert_fusion.2.pick_ref,, ...), custom_call_target="tpu_custom_call" | custom-call | bytes 4000000 | tf_op jit(solution)/shard_map/mixture_forward/pallas_call | solution.py:944
  354.3 6.1 fusion.45
  360.3 91.1 %mixture_backward.1 = (bf16[2048,2176]{1,0:T(8,128)(2,1)}, bf16[1024,2048]{1,0:T(8,128)(2,1)}, bf16[1024,1408]{1,0:T(8,128)(2,1)}, bf16[1024,1408]{1,0:T(8,128)(...) custom-call(f32[1,256]{1,0:T(1,128)} %add_convert_fusion.2.pick_ref, bf16[2048,2048]{1,0:T(8,128)(2,1)} %bitcast.157, ...), custom_call_target="tpu_custom_call" | custom-call | bytes 4000000 | tf_op jit(solution)/shard_map/mixture_backward/pallas_call | solution.py:970
  451.4 8.7 %convolution_convert_fusion.3 = bf16[512,2048]{1,0:T(8,128)(2,1)S(1)} fusion(bf16[2048,512]{1,0:T(8,128)(2,1)} %get-tuple-element.114, bf16[2048,2048]{1,0:T(8,128)(2,1)} %bitcast.159), kind=kOutput, calls=%fused_computation.4 | convolution fusion | flops 4296015872 | bytes 12582912 | tf_op jit(solution)/shard_map/dot_general | solution.py:1211
  463.2 10.7 %convolution_convert_fusion.2 = bf16[1408,2048]{1,0:T(8,128)(2,1)} fusion(bf16[1024,1408]{1,0:T(8,128)(2,1)} %get-tuple-element.90, bf16[1024,2048]{1,0:T(8,128)(2,1)} %get-tuple-element.91), kind=kOutput, calls=%fused_computation.2 | convolution fusion | flops 5908463616 | bytes 12845056 | tf_op jit(solution)/shard_map/dot_general | solution.py:1211
  473.9 11.0 %convolution_convert_fusion = bf16[2048,1408]{1,0:T(8,128)(2,1)} fusion(bf16[1024,2048]{1,0:T(8,128)(2,1)} %get-tuple-element.92, bf16[1024,1408]{1,0:T(8,128)(2,1)} %get-tuple-element.94), kind=kOutput, calls=%fused_computation | convolution fusion | flops 5908463616 | bytes 12845056 | tf_op jit(solution)/shard_map/dot_general | solution.py:1211
  484.8 11.0 %convolution_convert_fusion.1 = bf16[2048,1408]{1,0:T(8,128)(2,1)} fusion(bf16[1024,2048]{1,0:T(8,128)(2,1)} %get-tuple-element.92, bf16[1024,1408]{1,0:T(8,128)(2,1)} %get-tuple-element.93), kind=kOutput, calls=%fused_computation.1 | convolution fusion | flops 5908463616 | bytes 12845056 | tf_op jit(solution)/shard_map/dot_general | solution.py:1211
  510.2 52.9 %scatter16.3 = f32[128,2176]{1,0:T(8,128)S(1)} custom-call(bf16[16,128,2176]{2,1,0:T(8,128)(2,1)S(1)} %bitcast.140), custom_call_target="tpu_custom_call" | custom-call | bytes 4000000 | tf_op jit(solution)/shard_map/scatter16/pallas_call | solution.py:539
  567.9 51.8 %gather16.3 = bf16[16,128,2048]{2,1,0:T(8,128)(2,1)} custom-call(bf16[128,2048]{1,0:T(8,128)(2,1)} %fusion.40.x_ref), custom_call_target="tpu_custom_call" | custom-call | bytes 4000000 | tf_op jit(solution)/shard_map/gather16/pallas_call | solution.py:206
  619.7 20.4 %attend_back.1 = (bf16[16,2,64,2688]{3,2,1,0:T(8,128)(2,1)}, bf16[16,2,64,256]{3,2,1,0:T(8,128)(2,1)}, f32[128,2048]{1,0:T(8,128)}, f32[512,256]{1,0:T(8,128)}) custom-call(s32[2]{0:T(128)} %bitcast.149, bf16[16,2,64,2048]{3,2,1,0:T(8,128)(2,1)} %bitcast.170, bf16[2,1024,256]{2,1,0:T(8,128)(2,1)} %copy-done.6, bf16[2,1024,256]{2,1,0:T(8,128)(2,1)} %copy-done.8, ...), custom_call_target="tpu_custom_call" | custom-call | flops 14000000000 | bytes 25000000 | tf_op jit(solution)/shard_map/attend_back/pallas_call | solution.py:1181
  640.1 6.1 fusion.44
  649.8 82.8 %returning.1 = (f32[128,2688]{1,0:T(8,128)S(1)}, bf16[2,16,64,256]{3,2,1,0:T(8,128)(2,1)S(1)}, bf16[2,64,2048]{2,1,0:T(8,128)(2,1)S(1)}, bf16[1,16,64,256]{3,2,1,0:T(8,128)(2,1)S(1)}, bf16[1,64,2048]{2,1,0:T(8,128)(2,1)S(1)}) custom-call(bf16[16,128,2688]{2,1,0:T(8,128)(2,1)} %bitcast.166, bf16[2,16,64,256]{3,2,1,0:T(8,128)(2,1)S(1)} %pad_maximum_fusion.2.parts_ref, ...), custom_call_target="tpu_custom_call" | custom-call | bytes 4000000 | tf_op jit(solution)/shard_map/returning/pallas_call | solution.py:651
  749.6 3.9 fusion.16
  755.8 32.8 %closing.1 = (bf16[128,640]{1,0:T(8,128)(2,1)S(1)}, bf16[1,64,640]{2,1,0:T(8,128)(2,1)S(1)}) custom-call(bf16[16,128,640]{2,1,0:T(8,128)(2,1)S(1)} %bitcast.139), custom_call_target="tpu_custom_call" | custom-call | bytes 4000000 | tf_op jit(solution)/shard_map/closing/pallas_call | solution.py:718
  800.5 5.1 bitcast_convert_fusion
  805.6 4.7 bitcast_convert_fusion.1
  810.3 4.7 bitcast_convert_fusion.2
  (278 shorter events, 97.6 us)
Async XLA Ops:
  7.2 257.7 %all-gather.15.cloned.1.call-start = ((), (), s32[]{:S(2)}) async-start(), calls=%async_computation.11 | async-start | bytes 3244032 | tf_op jit(solution)/shard_map/all_gather | solution.py:1337
  9.5 262.6 %all-gather.9.cloned.1.call-start = ((), (), s32[]{:S(2)}) async-start(), calls=%async_computation.8 | async-start | bytes 8650752 | tf_op jit(solution)/shard_map/all_gather | solution.py:1334
  10.3 261.9 %all-gather.11.cloned.1.call-start = ((), (), s32[]{:S(2)}) async-start(), calls=%async_computation.9 | async-start | bytes 8650752 | tf_op jit(solution)/shard_map/all_gather | solution.py:1335
  11.1 279.4 %all-gather.13.cloned.1.call-start = ((), (), s32[]{:S(2)}) async-start(), calls=%async_computation.10 | async-start | bytes 8650752 | tf_op jit(solution)/shard_map/all_gather | solution.py:1336
  11.7 785.9 %reduce-scatter.11.cloned.1.call-start = ((), (), s32[]{:S(2)}) async-start(), calls=%async_computation.7 | async-start | bytes 3244032 | tf_op jit(solution)/shard_map/reduce_scatter | solution.py:1411
  149.3 56.2 %copy-start.10 = (f32[2,1024,1]{2,1,0:T(8,128)}, f32[2,1024,1]{2,1,0:T(8,128)S(1)}, u32[]{:S(2)}) copy-start(f32[2,1024,1]{2,1,0:T(8,128)S(1)} %get-tuple-element.98.lse_ref) | copy-start | bytes 24580
  149.3 56.2 %copy-start.12 = (bf16[16,2,64,128]{3,2,1,0:T(8,128)(2,1)}, bf16[16,2,64,128]{3,2,1,0:T(8,128)(2,1)S(1)}, u32[]{:S(2)}) copy-start(bf16[16,2,64,128]{3,2,1,0:T(8,128)(2,1)S(1)} %get-tuple-element.97.att_ref) | copy-start | bytes 1572868
  153.9 51.6 %copy-start.17 = (bf16[2,1,64,2048]{3,2,1,0:T(8,128)(2,1)S(1)}, bf16[2,1,64,2048]{3,2,1,0:T(8,128)(2,1)}, u32[]{:S(2)}) copy-start(bf16[2,1,64,2048]{3,2,1,0:T(8,128)(2,1)} %param.20) | copy-start | bytes 1572868
  205.8 53.8 %copy-start.48 = (f32[128]{0:T(128)}, f32[128]{0:T(128)S(1)}, u32[]{:S(2)}) copy-start(f32[128]{0:T(128)S(1)} %rsqrt.29) | copy-start | bytes 1540
  207.0 358.8 %copy-start.38 = (f32[128]{0:T(128)}, f32[128]{0:T(128)S(1)}, u32[]{:S(2)}) copy-start(f32[128]{0:T(128)S(1)} %add_rsqrt_fusion.2) | copy-start | bytes 1540
  207.9 54.7 %copy-start.19 = (bf16[2,1,64,2048]{3,2,1,0:T(8,128)(2,1)S(1)}, bf16[2,1,64,2048]{3,2,1,0:T(8,128)(2,1)}, u32[]{:S(2)}) copy-start(bf16[2,1,64,2048]{3,2,1,0:T(8,128)(2,1)} %param.21) | copy-start | bytes 1572868
  360.3 91.1 %copy-start.22 = (bf16[256,2048]{1,0:T(8,128)(2,1)}, bf16[256,2048]{1,0:T(8,128)(2,1)S(1)}, u32[]{:S(2)}) copy-start(bf16[256,2048]{1,0:T(8,128)(2,1)S(1)} %fusion.45) | copy-start | bytes 3145732
  463.1 337.3 %reduce-scatter.9.cloned.1.call-start = ((), (), s32[]{:S(2)}) async-start(), calls=%async_computation.6 | async-start | bytes 8650752 | tf_op jit(solution)/shard_map/reduce_scatter | solution.py:1404
  495.8 309.7 %reduce-scatter.7.cloned.1.call-start = ((), (), s32[]{:S(2)}) async-start(), calls=%async_computation.5 | async-start | bytes 8650752 | tf_op jit(solution)/shard_map/reduce_scatter | solution.py:1406
  496.6 313.7 %reduce-scatter.5.cloned.1.call-start = ((), (), s32[]{:S(2)}) async-start(), calls=%async_computation.4 | async-start | bytes 8650752 | tf_op jit(solution)/shard_map/reduce_scatter | solution.py:1405
  501.4 61.7 %copy-start.25 = (f32[1024,32]{1,0:T(8,128)}, f32[1024,32]{1,0:T(8,128)S(1)}, u32[]{:S(2)}) copy-start(f32[1024,32]{1,0:T(8,128)S(1)} %get-tuple-element.223.sin_ref) | copy-start | bytes 393220
  501.4 61.7 %copy-start.26 = (f32[1024,32]{1,0:T(8,128)}, f32[1024,32]{1,0:T(8,128)S(1)}, u32[]{:S(2)}) copy-start(f32[1024,32]{1,0:T(8,128)S(1)} %get-tuple-element.224.cos_ref) | copy-start | bytes 393220
  510.2 52.9 %copy-start.42 = (f32[128]{0:T(128)S(1)}, f32[128]{0:T(128)}, u32[]{:S(2)}) copy-start(f32[128]{0:T(128)} %copy-done.41) | copy-start | bytes 1540
  565.7 54.0 %copy-start.52 = (f32[128]{0:T(128)}, f32[128]{0:T(128)S(1)}, u32[]{:S(2)}) copy-start(f32[128]{0:T(128)S(1)} %broadcast_multiply_fusion.2) | copy-start | bytes 1540
  755.7 38.1 %copy-start.16 = (f32[128,2048]{1,0:T(8,128)S(1)}, f32[128,2048]{1,0:T(8,128)}, u32[]{:S(2)}) copy-start(f32[128,2048]{1,0:T(8,128)} %copy-done.15) | copy-start | bytes 3145732
  755.7 38.1 %copy-start.18 = (bf16[2,1,64,2048]{3,2,1,0:T(8,128)(2,1)S(1)}, bf16[2,1,64,2048]{3,2,1,0:T(8,128)(2,1)}, u32[]{:S(2)}) copy-start(bf16[2,1,64,2048]{3,2,1,0:T(8,128)(2,1)} %param.20) | copy-start | bytes 1572868
  755.7 38.1 %copy-start.39 = (f32[128]{0:T(128)S(1)}, f32[128]{0:T(128)}, u32[]{:S(2)}) copy-start(f32[128]{0:T(128)} %copy-done.38) | copy-start | bytes 1540
  755.7 38.1 %copy-start.43 = (f32[128]{0:T(128)S(1)}, f32[128]{0:T(128)}, u32[]{:S(2)}) copy-start(f32[128]{0:T(128)} %copy-done.41) | copy-start | bytes 1540
  755.7 38.1 %copy-start.46 = (bf16[128]{0:T(256)(128)(2,1)S(1)}, bf16[128]{0:T(256)(128)(2,1)}, u32[]{:S(2)}) copy-start(bf16[128]{0:T(256)(128)(2,1)} %copy-done.44) | copy-start | bytes 772
  (45 other events, 265.2 us)
Sparse Core Ops, SparseCore 0:
  10.1 55.1 all-gather.14
  66.9 71.6 all-gather.8
  140.1 74.4 all-gather.10
  216.0 74.4 all-gather.12
  463.3 30.6 reduce-scatter.10
  496.8 71.3 reduce-scatter.8
  571.1 71.4 reduce-scatter.6
  645.6 88.2 reduce-scatter.4

commit v5 on v4

--- a/solution.py
+++ b/solution.py
@@ -1,6 +1,7 @@
 import functools
 import jax
 import jax.numpy as jnp
+import numpy as np
 from jax import lax
 from jax.experimental import pallas as pl
 from jax.experimental.pallas import tpu as pltpu
@@ -19,8 +20,11 @@
     return me, z, x, c, me + 1 - 2 * c, me + 2 - 4 * x
 
 
-def enter(me, z, core, side):
+def enter(me, z, core, side, dp=1):
     barrier = pltpu.get_barrier_semaphore()
+    plane = lax.axis_index("dp")
+    for r in range(1, dp):
+        pl.semaphore_signal(barrier, inc=1, device_id={"dp": (plane + r) % dp}, device_id_type=MESH)
     for other in (core, side):
         pl.semaphore_signal(barrier, inc=1, device_id={"expert": other}, device_id_type=MESH)
 
@@ -32,7 +36,81 @@
     def _():
         pl.semaphore_signal(barrier, inc=1, device_id={"expert": me - 4}, device_id_type=MESH)
 
-    pl.semaphore_wait(barrier, 2 + (z < NZ - 1).astype(jnp.int32) + (z > 0).astype(jnp.int32))
+    pl.semaphore_wait(barrier, dp + 1 + (z < NZ - 1).astype(jnp.int32) + (z > 0).astype(jnp.int32))
+
+
+class Spread:
+    def __init__(self, dp, src, out, sems):
+        self.dp, self.src, self.out = dp, src, out
+        self.own, self.send, self.recv = sems
+        self.plane = lax.axis_index("dp")
+
+    @staticmethod
+    def scratch(dp):
+        dma = pltpu.SemaphoreType.DMA
+        return [dma, dma((dp,)), dma((dp,))]
+
+    def out_shape(dp, rows, v):
+        return jax.ShapeDtypeStruct((dp, rows, v.shape[1]), v.dtype)
+
+    def copy(self, r):
+        return pltpu.make_async_remote_copy(
+            src_ref=self.src, dst_ref=self.out.at[self.plane], send_sem=self.send.at[r], recv_sem=self.recv.at[r],
+            device_id={"dp": (self.plane + r) % self.dp}, device_id_type=MESH)
+
+    def arrival(self, r):
+        p = (self.plane - r + self.dp) % self.dp
+        return pltpu.make_async_remote_copy(
+            src_ref=self.src, dst_ref=self.out.at[p], send_sem=self.send.at[r], recv_sem=self.recv.at[r],
+            device_id={"dp": p}, device_id_type=MESH)
+
+    def start(self):
+        for r in range(1, self.dp):
+            self.copy(r).start()
+        self.kept = pltpu.make_async_copy(self.src, self.out.at[self.plane], self.own)
+        self.kept.start()
+
+    def finish(self):
+        self.kept.wait()
+        for r in range(1, self.dp):
+            self.arrival(r).wait_recv()
+            self.copy(r).wait_send()
+
+
+class Swap:
+    def __init__(self, dp, src, out, sems):
+        self.dp, self.src, self.out = dp, src, out
+        self.send, self.recv = sems
+        self.plane = lax.axis_index("dp")
+
+    @staticmethod
+    def scratch(dp):
+        dma = pltpu.SemaphoreType.DMA
+        return [dma((dp,)), dma((dp,))]
+
+    def out_shape(dp, rows, v):
+        return jax.ShapeDtypeStruct((dp - 1, rows, v.shape[2]), v.dtype)
+
+    def copy(self, r):
+        to = (self.plane + r) % self.dp
+        return pltpu.make_async_remote_copy(
+            src_ref=self.src.at[to], dst_ref=self.out.at[r - 1], send_sem=self.send.at[r], recv_sem=self.recv.at[r],
+            device_id={"dp": to}, device_id_type=MESH)
+
+    def start(self):
+        for r in range(1, self.dp):
+            self.copy(r).start()
+
+    def finish(self):
+        for r in range(1, self.dp):
+            self.copy(r).wait_recv()
+            self.copy(r).wait_send()
+
+
+def side_job(kind, dp, span, src, out, sems):
+    first, rows = span
+    part = pl.ds(first, rows)
+    return kind(dp, src.at[part] if kind is Spread else src.at[:, part], out, sems)
 
 
 def enter_all(me, plane, dp):
@@ -188,31 +266,45 @@
                     self.down(k, s).wait_send()
 
 
-def gather_kernel(chunks, x_ref, o_ref, *sems):
-    g = Gather(x_ref, o_ref, chunks, sems)
-    enter(g.me, g.z, g.core, g.side)
+def gather_kernel(chunks, dp, kind, span, x_ref, *refs):
+    job = None
+    ng = 9
+    if kind is None:
+        o_ref, *sems = refs
+    else:
+        src, o_ref, out, *sems = refs
+        job = side_job(kind, dp, span, src, out, sems[ng:])
+    g = Gather(x_ref, o_ref, chunks, sems[:ng])
+    enter(g.me, g.z, g.core, g.side, 1 if job is None else dp)
     g.start()
+    if job is not None:
+        job.start()
     for s in range(1, NZ + 1):
         g.round(s)
     g.finish()
+    if job is not None:
+        job.finish()
 
 
 COST = pl.CostEstimate(flops=0, bytes_accessed=4_000_000, transcendentals=0)
 ANY = pl.BlockSpec(memory_space=pl.ANY)
 
 
-def gather16(v, cid, chunks=4):
+def gather16(v, cid, chunks=4, dp=1, kind=None, span=None, side=None):
     rows, width = v.shape
-    return pl.pallas_call(
-        functools.partial(gather_kernel, chunks),
-        out_shape=jax.ShapeDtypeStruct((NE, rows, width), v.dtype),
-        in_specs=[ANY],
-        out_specs=ANY,
-        scratch_shapes=Gather.scratch(chunks),
+    extra = kind is not None
+    out = pl.pallas_call(
+        functools.partial(gather_kernel, chunks, dp, kind, span),
+        out_shape=(jax.ShapeDtypeStruct((NE, rows, width), v.dtype),)
+        + ((kind.out_shape(dp, span[1], side),) if extra else ()),
+        in_specs=[ANY] * (2 if extra else 1),
+        out_specs=(ANY,) * (2 if extra else 1),
+        scratch_shapes=Gather.scratch(chunks) + (kind.scratch(dp) if extra else []),
         compiler_params=pltpu.CompilerParams(collective_id=cid, has_side_effects=True),
         cost_estimate=COST,
         name="gather16",
-    )(v)
+    )(*((v, side) if extra else (v,)))
+    return out if extra else out[0]
 
 
 def opening_kernel(dp, chunks, x_ref, small_ref, parts_ref, out_ref,
@@ -523,30 +615,44 @@
                         self.down(t, i, k).wait_send()
 
 
-def scatter_kernel(chunks, p_ref, o_ref, *scratch):
-    s = Scatter(p_ref, o_ref, chunks, scratch)
-    enter(s.me, s.z, s.core, s.side)
+def scatter_kernel(chunks, dp, kind, span, p_ref, *refs):
+    job = None
+    ns = 14
+    if kind is None:
+        o_ref, *scratch = refs
+    else:
+        src, o_ref, out, *scratch = refs
+        job = side_job(kind, dp, span, src, out, scratch[ns:])
+    s = Scatter(p_ref, o_ref, chunks, scratch[:ns])
+    enter(s.me, s.z, s.core, s.side, 1 if job is None else dp)
     s.start()
+    if job is not None:
+        job.start()
     s.run()
     s.finish()
+    if job is not None:
+        job.finish()
 
 
 VMEM = pl.BlockSpec(memory_space=pltpu.VMEM)
 
 
-def scatter16(p, cid, chunks=2, out_dtype=jnp.float32):
+def scatter16(p, cid, chunks=2, out_dtype=jnp.float32, dp=1, kind=None, span=None, side=None):
     _, rows, width = p.shape
-    return pl.pallas_call(
-        functools.partial(scatter_kernel, chunks),
-        out_shape=jax.ShapeDtypeStruct((rows, width), out_dtype),
-        in_specs=[ANY],
-        out_specs=VMEM,
-        scratch_shapes=Scatter.scratch(rows, width, chunks, p.dtype),
+    extra = kind is not None
+    out = pl.pallas_call(
+        functools.partial(scatter_kernel, chunks, dp, kind, span),
+        out_shape=(jax.ShapeDtypeStruct((rows, width), out_dtype),)
+        + ((kind.out_shape(dp, span[1], side),) if extra else ()),
+        in_specs=[ANY] * (2 if extra else 1),
+        out_specs=(VMEM,) + ((ANY,) if extra else ()),
+        scratch_shapes=Scatter.scratch(rows, width, chunks, p.dtype) + (kind.scratch(dp) if extra else []),
         compiler_params=pltpu.CompilerParams(
-            collective_id=cid, has_side_effects=True, vmem_limit_bytes=32 * 1024 * 1024),
+            collective_id=cid, has_side_effects=True, vmem_limit_bytes=60 * 1024 * 1024),
         cost_estimate=COST,
         name="scatter16",
-    )(p)
+    )(*((p, side) if extra else (p,)))
+    return out if extra else out[0]
 
 
 def return_kernel(dp, chunks, p_ref, parts_ref, rows_ref, o_ref, parts_in, rows_in, parts_far, rows_far, *scratch):
@@ -658,7 +764,7 @@
         scratch_shapes=Scatter.scratch(n, width, chunks, p.dtype) + [
             dma((NE,)), dma((NE,)), dma((dp,)), dma((dp,)), dma, dma((dp,)), dma((2, dp)), dma((2, dp))],
         compiler_params=pltpu.CompilerParams(
-            collective_id=cid, has_side_effects=True, vmem_limit_bytes=48 * 1024 * 1024),
+            collective_id=cid, has_side_effects=True, vmem_limit_bytes=60 * 1024 * 1024),
         cost_estimate=COST,
         name="returning",
     )(p, parts, rows)
@@ -677,22 +783,7 @@
     ys, yr = scratch[ns:]
     plane = lax.axis_index("dp")
     rows = o_ref.shape[0] // dp
-    barrier = pltpu.get_barrier_semaphore()
-    for r in range(1, dp):
-        pl.semaphore_signal(barrier, inc=1, device_id={"dp": (plane + r) % dp}, device_id_type=MESH)
-    z = s.z
-    for other in (s.core, s.side):
-        pl.semaphore_signal(barrier, inc=1, device_id={"expert": other}, device_id_type=MESH)
-
-    @pl.when(z < NZ - 1)
-    def _():
-        pl.semaphore_signal(barrier, inc=1, device_id={"expert": s.me + 4}, device_id_type=MESH)
-
-    @pl.when(z > 0)
-    def _():
-        pl.semaphore_signal(barrier, inc=1, device_id={"expert": s.me - 4}, device_id_type=MESH)
-
-    pl.semaphore_wait(barrier, dp + 1 + (z < NZ - 1).astype(jnp.int32) + (z > 0).astype(jnp.int32))
+    enter(s.me, s.z, s.core, s.side, dp)
 
     def lift(r):
         to = (plane + r) % dp
@@ -750,6 +841,16 @@
 SHARE = 176
 
 
+def down_copies(a_ref, b_ref, out, sem):
+    dp, a, _ = a_ref.shape
+    rows = a + b_ref.shape[1]
+    copies = []
+    for d in range(dp):
+        copies.append(pltpu.make_async_copy(a_ref.at[d], out.at[pl.ds(d * rows, a)], sem.at[2 * d]))
+        copies.append(pltpu.make_async_copy(b_ref.at[d], out.at[pl.ds(d * rows + a, rows - a)], sem.at[2 * d + 1]))
+    return copies
+
+
 def one_hots(slot_row, slot_col, groups, slots):
     to_slot, to_token = [], []
     for g in range(groups):
@@ -774,10 +875,10 @@
         body(total // WIDE * WIDE, total % WIDE)
 
 
-def forward_kernel(chunks, pick_ref, mix_ref, routes_ref, slot_row, slot_col, valid_ref, wg_ref, wu_ref, wd_ref,
-                   fan_ref, sd_ref, dy_ref,
+def forward_kernel(chunks, pick_ref, mix_ref, routes_ref, slot_row, slot_col, valid_ref, wg_ref, wu_ref, fan_ref, sd_ref,
+                   wda_ref, wdb_ref, dy_ref,
                    out_ref, rows_ref, hid_ref, act_ref, slo_ref, eo_ref, sh_ref, sact_ref, sslo_ref, gate_ref,
-                   dy_all, *sems):
+                   dy_all, wd_ref, wd_sem, *sems):
     step = pl.program_id(0)
     tokens, width = mix_ref.shape
     groups, slots = tokens // 256, 128
@@ -788,6 +889,8 @@
     def _():
         enter(g.me, g.z, g.core, g.side)
         g.start()
+        for copy in down_copies(wda_ref, wdb_ref, wd_ref, wd_sem):
+            copy.start()
 
     mix = mix_ref[...]
     fanned = mm_t(mix, fan_ref[:TILE, :])
@@ -828,6 +931,12 @@
 
     over_columns(ff, fan_in)
 
+    @pl.when(step == 0)
+    def _():
+        for copy in down_copies(wda_ref, wdb_ref, wd_ref, wd_sem):
+            copy.wait()
+
+
     def fan_out(j, _):
         eo = mm(hid_ref[...], wd_ref[:, lanes(j)]).astype(BF)
         eo_ref[:, lanes(j)] = eo
@@ -849,9 +958,9 @@
         g.finish()
 
 
-def backward_kernel(chunks, pick_ref, dy_ref, slot_row, slot_col, wg_ref, wu_ref, wd_ref, fan_ref, sd_ref,
+def backward_kernel(chunks, pick_ref, dy_ref, slot_row, slot_col, wg_ref, wu_ref, fan_ref, sd_ref, wda_ref, wdb_ref,
                     act_ref, slo_ref, eo_ref, sact_ref, sslo_ref, gate_ref, part_ref,
-                    dh_ref, deo_ref, dg_ref, du_ref, ds_ref, sum_ref, *scratch):
+                    dh_ref, deo_ref, dg_ref, du_ref, ds_ref, sum_ref, wd_ref, wd_sem, *scratch):
     step = pl.program_id(0)
     tokens, width = dy_ref.shape
     groups, slots = tokens // 256, 128
@@ -861,6 +970,8 @@
     @pl.when(step == 0)
     def _():
         enter(sc.me, sc.z, sc.core, sc.side)
+        for copy in down_copies(wda_ref, wdb_ref, wd_ref, wd_sem):
+            copy.start()
         sc.start()
 
     d_sh = mm_t(dy_ref[...], sd_ref[...])
@@ -884,6 +995,8 @@
     def _():
         sc.first(0)
         sc.first(1)
+        for copy in down_copies(wda_ref, wdb_ref, wd_ref, wd_sem):
+            copy.wait()
 
     def back_out(start, size):
         cols = pl.ds(start, size)
@@ -893,19 +1006,10 @@
 
     over_columns(ff, back_out)
 
-    @pl.when(step == 1)
+    @pl.when(step == 0)
     def _():
-        sc.second(0)
         sc.first(2)
-
-    @pl.when(step == 2)
-    def _():
-        sc.second(1)
         sc.first(3)
-
-    @pl.when(step == 3)
-    def _():
-        sc.second(2)
 
     d_s = ds_ref[...]
 
@@ -921,6 +1025,16 @@
     high = d_gates.astype(BF).astype(F32)
     dh_ref[:, width:] = (high * pick_ref[:, :128] + (d_gates - high) * pick_ref[:, 128:]).astype(BF)
 
+    outer = (sc.z == 0) | (sc.z == NZ - 1)
+    for i in range(NZ - 1):
+        @pl.when((step == i) & outer)
+        def _():
+            sc.second(i)
+
+        @pl.when((step == min(i + 1, 2)) & jnp.logical_not(outer))
+        def _():
+            sc.second(i)
+
     @pl.when(step == 3)
     def _():
         sc.second(3)
@@ -935,10 +1049,10 @@
     return pl.BlockSpec((rows, w), lambda i: (i, 0))
 
 
-def mixture_forward(pick, mix, routes, slot, valid, wg, wu, wd, fan, sd, dy, cid, chunks=2):
+def mixture_forward(pick, mix, routes, slot, valid, wg, wu, wda, wdb, fan, sd, dy, cid, chunks=2):
     total, width = mix.shape
     step, half = total // 4, total // 8
-    ff = wd.shape[0]
+    ff = wg.shape[1]
     shape = jax.ShapeDtypeStruct
     rows = total // 2
     return pl.pallas_call(
@@ -949,21 +1063,22 @@
             shape((rows, ff), BF), shape((rows, width), BF), shape((total, TILE), BF), shape((total, TILE), BF),
             shape((total, TILE), BF), shape((total, 1), F32), shape((NE,) + dy.shape, BF)),
         in_specs=[whole(pick), tiles(step, width), tiles(step, routes.shape[1]), pl.BlockSpec((1, step), lambda i: (0, i)),
-                  tiles(step, 1), tiles(step, 1), whole(wg), whole(wu), whole(wd), whole(fan), whole(sd), ANY],
+                  tiles(step, 1), tiles(step, 1), whole(wg), whole(wu), whole(fan), whole(sd), ANY, ANY, ANY],
         out_specs=[tiles(step, width), tiles(half, width), tiles(half, ff), tiles(half, ff), tiles(half, ff),
                    tiles(half, width), tiles(step, TILE), tiles(step, TILE), tiles(step, TILE), tiles(step, 1), ANY],
-        scratch_shapes=Gather.scratch(chunks),
+        scratch_shapes=[pltpu.VMEM((ff, width), BF), pltpu.SemaphoreType.DMA((2 * wda.shape[0],))]
+        + Gather.scratch(chunks),
         compiler_params=pltpu.CompilerParams(
             collective_id=cid, has_side_effects=True, vmem_limit_bytes=60 * 1024 * 1024),
         cost_estimate=COST,
         name="mixture_forward",
-    )(pick, mix, routes, slot[None, :], slot[:, None], valid, wg, wu, wd, fan, sd, dy)
-
-
-def mixture_backward(pick, dy, slot, wg, wu, wd, fan, sd, act, slo, eo, sact, sslo, gate, part, cid, chunks=2):
+    )(pick, mix, routes, slot[None, :], slot[:, None], valid, wg, wu, fan, sd, wda, wdb, dy)
+
+
+def mixture_backward(pick, dy, slot, wg, wu, wda, wdb, fan, sd, act, slo, eo, sact, sslo, gate, part, cid, chunks=2):
     total, width = dy.shape
     step, half = total // 4, total // 8
-    ff = wd.shape[0]
+    ff = wg.shape[1]
     shape = jax.ShapeDtypeStruct
     rows = total // 2
     _, own, _ = part.shape
@@ -974,17 +1089,18 @@
             shape((total, width + 128), BF), shape((rows, width), BF), shape((rows, ff), BF), shape((rows, ff), BF),
             shape((total, 2 * TILE), BF), shape((own, width), F32)),
         in_specs=[whole(pick), tiles(step, width), pl.BlockSpec((1, step), lambda i: (0, i)), tiles(step, 1),
-                  whole(wg), whole(wu), whole(wd), whole(fan), whole(sd),
+                  whole(wg), whole(wu), whole(fan), whole(sd), ANY, ANY,
                   tiles(half, ff), tiles(half, ff), tiles(half, width), tiles(step, TILE), tiles(step, TILE),
                   tiles(step, 1), ANY],
         out_specs=[tiles(step, width + 128), tiles(half, width), tiles(half, ff), tiles(half, ff),
                    tiles(step, 2 * TILE), pl.BlockSpec((own, width), lambda i: (0, 0))],
-        scratch_shapes=Scatter.scratch(own, width, chunks, BF),
+        scratch_shapes=[pltpu.VMEM((ff, width), BF), pltpu.SemaphoreType.DMA((2 * wda.shape[0],))]
+        + Scatter.scratch(own, width, chunks, BF),
         compiler_params=pltpu.CompilerParams(
             collective_id=cid, has_side_effects=True, vmem_limit_bytes=60 * 1024 * 1024),
         cost_estimate=COST,
         name="mixture_backward",
-    )(pick, dy, slot[None, :], slot[:, None], wg, wu, wd, fan, sd, act, slo, eo, sact, sslo, gate, part)
+    )(pick, dy, slot[None, :], slot[:, None], wg, wu, fan, sd, wda, wdb, act, slo, eo, sact, sslo, gate, part)
 
 
 def mm_lead(a, b):
@@ -1219,11 +1335,10 @@
     )
 
 
-def rotary_tables(positions):
-    half_width = ROPE // 2
-    frequency = ROTARY_BASE ** (-jnp.arange(half_width, dtype=F32) * 2.0 / ROPE)
-    angles = positions[:, None] * frequency[None, :]
-    return (jnp.cos(angles), jnp.sin(angles))
+def rotary_tables(count):
+    frequency = ROTARY_BASE ** (-np.arange(ROPE // 2, dtype=np.float32) * np.float32(2.0) / np.float32(ROPE))
+    angles = np.arange(count, dtype=np.float32)[:, None] * frequency.astype(np.float32)[None, :]
+    return np.cos(angles).astype(np.float32), np.sin(angles).astype(np.float32)
 
 
 def rotate(values, cosine, sine_table):
@@ -1329,11 +1444,11 @@
     expand_head = parts_head[:, QK_NOPE + ROPE :].reshape(KV_RANK, QK_NOPE + V_DIM)
     output_head = output_head.reshape(V_DIM, width)
 
+    ff = gate_weight.shape[2]
     share_own = jnp.concatenate([shared_gate.T, shared_up.T, shared_down], axis=0)
     share_width = shared_down.shape[0]
     gate_full = lax.all_gather(gate_weight[0], "dp", axis=0, tiled=True)
     up_full = lax.all_gather(up_weight[0], "dp", axis=0, tiled=True)
-    down_full = lax.all_gather(down_weight[0], "dp", axis=0, tiled=True)
     share_full = lax.all_gather(share_own, "dp", axis=0)
     share_full = share_full.transpose(1, 0, 2).reshape(3 * share_width, width)
 
@@ -1344,16 +1459,9 @@
     valid_all = jnp.broadcast_to(
         all_positions < seq_lengths[None, :, None], (GROUPS, batches, here)
     ).reshape(total)
-    key_positions = jnp.arange(seq_total, dtype=jnp.int32)
-    cosine, sine_table = rotary_tables(key_positions.astype(F32))
-    cosine_own = lax.dynamic_slice_in_dim(cosine, me * here, here)
-    sine_own = lax.dynamic_slice_in_dim(sine_table, me * here, here)
-
-    def by_sequence(v):
-        return v.reshape(GROUPS, batches, here, v.shape[-1]).swapaxes(0, 1).reshape(batches, seq_total, -1)
-
-    def by_device(v):
-        return v.reshape(batches, GROUPS, here, v.shape[-1]).swapaxes(0, 1).reshape(total, -1)
+    cosine, sine_table = rotary_tables(seq_total)
+    cosine_own = lax.dynamic_slice_in_dim(jnp.asarray(cosine), me * here, here)
+    sine_own = lax.dynamic_slice_in_dim(jnp.asarray(sine_table), me * here, here)
 
     grad_own = out_cotangent.reshape(own, width) * valid_own[:, None].astype(BF)
     taken = jnp.any(routes_all == me, axis=1) & valid_all
@@ -1362,21 +1470,25 @@
     slot = jnp.where(taken, places.reshape(total), -1)
 
     def by_token(table):
-        return jnp.broadcast_to(
-            table.reshape(GROUPS, 1, here, -1), (GROUPS, batches, here, table.shape[1])).reshape(total, -1)
+        return jnp.asarray(np.broadcast_to(
+            table.reshape(GROUPS, 1, here, -1), (GROUPS, batches, here, table.shape[1])).reshape(total, -1))
 
     hidden_all, query, key, values, latent = project(
         x_all.reshape(GROUPS, own, width), gain_attn[None], gain_latent[None], parts_head, small, expand_head,
         by_token(cosine), by_token(sine_table), batches)
     attn_part, attended, log_total = attend(seq_lengths, query, key, values, output_head, GROUPS)
     attn_part = attn_part.reshape(GROUPS, own, width)
-    attn_out = scatter16(attn_part, 2)
+    down_own = down_weight[0]
+    cut = down_own.shape[0] // 32 * 16
+    spans = ((0, cut), (cut, down_own.shape[0] - cut))
+    attn_out, down_a = scatter16(attn_part, 2, dp=dp, kind=Spread, span=spans[0], side=down_own)
 
     x_wide = x_own.astype(F32)
     middle = x_wide + attn_out
     normed_mix, unit_mix, factor_mix = norm_forward(middle, gain_mixer)
     hidden_mix = normed_mix.astype(BF)
-    mix_all = gather16(hidden_mix, 3).reshape(total, width)
+    mix_all, down_b = gather16(hidden_mix, 3, dp=dp, kind=Spread, span=spans[1], side=down_own)
+    mix_all = mix_all.reshape(total, width)
 
     pad = TILE - share_width
     fan_share = jnp.concatenate(
@@ -1387,10 +1499,10 @@
     pick = jnp.concatenate([lane == me, lane == me + GROUPS], axis=1).astype(F32)
     out_part, rows, hidden, act, slope, result, share_hidden, share_act, share_slope, gates, grad_all = mixture_forward(
         pick, mix_all, routes_all, slot, valid_all.astype(F32)[:, None],
-        gate_full, up_full, down_full, fan_share, down_share, grad_own, 4)
+        gate_full, up_full, down_a, down_b, fan_share, down_share, grad_own, 4)
     grad_all = grad_all.reshape(total, width)
     mix_part, grad_result, grad_gate_in, grad_up_in, grad_share_in, mixed = mixture_backward(
-        pick, grad_all, slot, gate_full, up_full, down_full, fan_share, down_share, act, slope, result,
+        pick, grad_all, slot, gate_full, up_full, down_a, down_b, fan_share, down_share, act, slope, result,
         share_act, share_slope, gates, out_part.reshape(GROUPS, own, width), 8)
     grad_down = product_lead(hidden, grad_result).astype(BF)
     grad_gate = product_lead(rows, grad_gate_in).astype(BF)
@@ -1398,10 +1510,11 @@
     grad_share_fan = product_lead(grad_share_in, mix_all).astype(BF)
     grad_share_down = product_lead(share_hidden, grad_all).astype(BF)
     mix_part, grad_down, grad_gate, grad_up = lax.optimization_barrier((mix_part, grad_down, grad_gate, grad_up))
-    mix_sum = scatter16(mix_part.reshape(GROUPS, own, width + 128), 5)
+    grad_down = grad_down.reshape(dp, ff // dp, width)
+    mix_sum, far_a = scatter16(
+        mix_part.reshape(GROUPS, own, width + 128), 5, dp=dp, kind=Swap, span=spans[0], side=grad_down)
     layer_output = valid_own[:, None] * (middle + mixed)
 
-    out_down = lax.psum_scatter(grad_down, "dp", scatter_dimension=0, tiled=True)
     out_gate = lax.psum_scatter(grad_gate, "dp", scatter_dimension=0, tiled=True)
     out_up = lax.psum_scatter(grad_up, "dp", scatter_dimension=0, tiled=True)
     grad_share = jnp.concatenate(
@@ -1420,10 +1533,14 @@
     grad_middle_norm, grad_gain_mixer = norm_backward(grad_mix, unit_mix, factor_mix, gain_mixer)
     grad_middle = grad_own.astype(F32) + grad_middle_norm
 
-    grad_attn_all = gather16(grad_middle.astype(BF), 6).reshape(GROUPS, batches, here, width)
+    grad_attn_all, far_b = gather16(
+        grad_middle.astype(BF), 6, dp=dp, kind=Swap, span=spans[1], side=grad_down)
+    grad_attn_all = grad_attn_all.reshape(GROUPS, batches, here, width)
+    out_down = lax.dynamic_index_in_dim(grad_down, plane, 0, False).astype(F32)
+    out_down = out_down + jnp.sum(jnp.concatenate([far_a, far_b], axis=1).astype(F32), axis=0)
     back_part, grad_query, grad_output, grad_expand = attend_back(
         seq_lengths, grad_attn_all, query, key, values, latent, attended, log_total, output_head, parts_head,
-        expand_head, cosine, sine_table, 640)
+        expand_head, jnp.asarray(cosine), jnp.asarray(sine_table), 640)
     grad_query_w = product_lead(hidden_all, grad_query.reshape(total, TILE)).astype(BF)
     parts_grad = jnp.concatenate(
         [grad_query_w[:, : QK_NOPE + ROPE], grad_expand.astype(BF).reshape(width, ROPE)], axis=1)
@@ -1477,7 +1594,7 @@
         small_sum[:, 576:592],
         out_gate.astype(F32)[None],
         out_up.astype(F32)[None],
-        out_down.astype(F32)[None],
+        out_down[None],
         out_share[:share_width].T,
         out_share[share_width : 2 * share_width].T,
         out_share[2 * share_width :],

time: 830 us -> 827 us (level)
  Pallas kernels: 614 us -> 641 us
  waiting for transfers between devices: 21.3 us -> 1.99 us
  local copies, waits for them, and re-layouts: 57.5 us -> 48.5 us
    pallas_call x4, Pallas kernels: 208 us -> 254 us  [the longest x2 134 us: scatter16(): pl.pallas_call(functools.partial(scatter_kernel, chunks, dp, kind, span),...]
    all_gather x1 -> x0, waiting for transfers between devices: 18.3 us -> none  [per_device(): down_full = lax.all_gather(down_weight[0], 'dp', axis=0, tiled=True)]
    pallas_call x1, Pallas kernels: 91.1 us -> 74 us  [mixture_backward(): pl.pallas_call(functools.partial(backward_kernel, chunks), grid=(4,), out...]
    unnamed x132 -> x126, local copies, waits for them, and re-layouts: 17.3 us -> 8.36 us
  transfers between devices with their start and end apart: 8 -> 6, of which waited for: 1 -> 0; matrix products, arithmetic and copies ran while one was open for 16% -> 16% of each run, Pallas kernels for 56% -> 61%
where the time goes in v5:
time: 827 us; the launch traced here: 822 us
  Pallas kernels  641 us (78%)
  matrix products  63.9 us (8%)
  other arithmetic  51 us (6%)
  local copies, waits for them, and re-layouts  48.5 us (6%)
  between operations  15.4 us (2%)
    pallas_call x2, Pallas kernels, scatter16(): pl.pallas_call(functools.partial(scatter_kernel, chunks, dp, kind, span),...  134 us
    pallas_call x2, Pallas kernels, gather16(): pl.pallas_call(functools.partial(gather_kernel, chunks, dp, kind, span),...  121 us
    pallas_call x1, Pallas kernels, opening(): pl.pallas_call(functools.partial(opening_kernel, dp, chunks), out_shape=(...  88.2 us
    pallas_call x1, Pallas kernels, returning(): pl.pallas_call(functools.partial(return_kernel, dp, chunks), out_shape=(s...  83.6 us
    pallas_call x1, Pallas kernels, mixture_backward(): pl.pallas_call(functools.partial(backward_kernel, chunks), grid=(4,), out...  74 us
    pallas_call x1, Pallas kernels, mixture_forward(): pl.pallas_call(functools.partial(forward_kernel, chunks), grid=(4,), out_...  61.6 us
    dot_general x7, matrix products, product_lead(): lax.dot_general(left_side, right_side, (((0,), (0,)), ((), ())), preferre...  53.6 us
    pallas_call x1, Pallas kernels, closing(): pl.pallas_call(functools.partial(closing_kernel, dp, 1), out_shape=(shape...  32.6 us
  transfers between devices with their start and end apart: 6, of which 0 were waited for; matrix products, arithmetic and copies ran while one was open for 16% of the time, Pallas kernels for 61%

profile of v5, /device:TPU:0, one launch (start us, length us, event | category | flops | bytes accessed | tf_op | source)
XLA Modules:
  0.0 822.4 jit_solution(11044775711292422371)
XLA Ops:
  14.8 88.2 %opening.1 = (bf16[16,128,2048]{2,1,0:T(8,128)(2,1)}, bf16[2,16,64,640]{3,2,1,0:T(8,128)(2,1)}, bf16[2,16,64,256]{3,2,1,0:T(8,128)(2,1)}, bf16[2,64,2048]{2,1,0:...) custom-call(bf16[128,2048]{1,0:T(8,128)(2,1)} %bitcast.164, ...), custom_call_target="tpu_custom_call" | custom-call | bytes 4000000 | tf_op jit(solution)/shard_map/opening/pallas_call | solution.py:444
  118.5 16.8 %project.1 = (bf16[2048,2048]{1,0:T(8,128)(2,1)}, bf16[2,1024,256]{2,1,0:T(8,128)(2,1)S(1)}, bf16[2,1024,256]{2,1,0:T(8,128)(2,1)S(1)}, bf16[2,1024,128]{2,1,0:T(8,128)(2,1)S(1)}, bf16[2,1024,512]{2,1,0:T(8,128)(2,1)}) custom-call(bf16[16,128,2048]{2,1,0:T(8,128)(2,1)} %get-tuple-element.80.x_ref, f32[1,2048]{1,0:T(1,128)S(1)} %bitcast.139, ...), custom_call_target="tpu_custom_call" | custom-call | flops 7000000000 | bytes 20000000 | tf_op jit(solution)/shard_map/project/pallas_call | solution.py:1159
  135.3 9.9 %attend.1 = (bf16[16,2,64,2048]{3,2,1,0:T(8,128)(2,1)}, bf16[16,2,64,128]{3,2,1,0:T(8,128)(2,1)S(1)}, f32[2,1024,1]{2,1,0:T(8,128)S(1)}) custom-call(s32[2]{0:T(128)S(1)} %bitcast.143, bf16[2,1024,256]{2,1,0:T(8,128)(2,1)S(1)} %get-tuple-element.83.q_ref, bf16[2,1024,256]{2,1,0:T(8,128)(2,1)S(1)} %get-tuple-element.84.k_ref, ...), custom_call_target="tpu_custom_call" | custom-call | flops 4000000000 | bytes 15000000 | tf_op jit(solution)/shard_map/attend/pallas_call | solution.py:1217
  146.2 67.1 %scatter16.2 = (f32[128,2048]{1,0:T(8,128)}, bf16[2,352,2048]{2,1,0:T(8,128)(2,1)}) custom-call(bf16[16,128,2048]{2,1,0:T(8,128)(2,1)} %bitcast.163, bf16[704,2048]{1,0:T(8,128)(2,1)} %bitcast.156), custom_call_target="tpu_custom_call" | custom-call | bytes 4000000 | tf_op jit(solution)/shard_map/scatter16/pallas_call | solution.py:643
  216.7 65.3 %gather16.2 = (bf16[16,128,2048]{2,1,0:T(8,128)(2,1)}, bf16[2,352,2048]{2,1,0:T(8,128)(2,1)}) custom-call(bf16[128,2048]{1,0:T(8,128)(2,1)} %multiply_convert_fusion.x_ref, bf16[704,2048]{1,0:T(8,128)(2,1)} %bitcast.157), custom_call_target="tpu_custom_call" | custom-call | bytes 4000000 | tf_op jit(solution)/shard_map/gather16/pallas_call | solution.py:296
  287.1 3.8 copy.166
  296.0 61.6 %mixture_forward.1 = (bf16[2048,2048]{1,0:T(8,128)(2,1)}, bf16[1024,2048]{1,0:T(8,128)(2,1)}, bf16[1024,1408]{1,0:T(8,128)(2,1)}, bf16[1024,1408]{1,0:T(8,128)(2...) custom-call(f32[1,256]{1,0:T(1,128)} %add_convert_fusion.2.pick_ref,, ...), custom_call_target="tpu_custom_call" | custom-call | bytes 4000000 | tf_op jit(solution)/shard_map/mixture_forward/pallas_call | solution.py:1058
  357.6 6.1 fusion.44
  363.7 74.0 %mixture_backward.1 = (bf16[2048,2176]{1,0:T(8,128)(2,1)}, bf16[1024,2048]{1,0:T(8,128)(2,1)}, bf16[1024,1408]{1,0:T(8,128)(2,1)}, bf16[1024,1408]{1,0:T(8,128)(...) custom-call(f32[1,256]{1,0:T(1,128)} %add_convert_fusion.2.pick_ref, bf16[2048,2048]{1,0:T(8,128)(2,1)} %bitcast.148, ...), custom_call_target="tpu_custom_call" | custom-call | bytes 4000000 | tf_op jit(solution)/shard_map/mixture_backward/pallas_call | solution.py:1085
  437.7 8.8 %convolution_convert_fusion.3 = bf16[512,2048]{1,0:T(8,128)(2,1)S(1)} fusion(bf16[2048,512]{1,0:T(8,128)(2,1)} %get-tuple-element.130, bf16[2048,2048]{1,0:T(8,128)(2,1)} %bitcast.166), kind=kOutput, calls=%fused_computation.5 | convolution fusion | flops 4296015872 | bytes 12582912 | tf_op jit(solution)/shard_map/dot_general | solution.py:1327
  449.6 11.1 %convolution_convert_fusion.2 = bf16[1408,2048]{1,0:T(8,128)(2,1)} fusion(bf16[1024,1408]{1,0:T(8,128)(2,1)} %get-tuple-element.102, bf16[1024,2048]{1,0:T(8,128)(2,1)} %get-tuple-element.103), kind=kOutput, calls=%fused_computation.2 | convolution fusion | flops 5908463616 | bytes 12845056 | tf_op jit(solution)/shard_map/dot_general | solution.py:1327
  460.6 8.6 %convolution_convert_fusion = bf16[2048,1408]{1,0:T(8,128)(2,1)} fusion(bf16[1024,2048]{1,0:T(8,128)(2,1)S(1)} %copy-done.54, bf16[1024,1408]{1,0:T(8,128)(2,1)S(1)} %copy-done.55), kind=kOutput, calls=%fused_computation | convolution fusion | flops 5908463616 | bytes 12845056 | tf_op jit(solution)/shard_map/dot_general | solution.py:1327
  469.3 11.0 %convolution_convert_fusion.1 = bf16[2048,1408]{1,0:T(8,128)(2,1)} fusion(bf16[1024,2048]{1,0:T(8,128)(2,1)} %get-tuple-element.104, bf16[1024,1408]{1,0:T(8,128)(2,1)} %get-tuple-element.105), kind=kOutput, calls=%fused_computation.1 | convolution fusion | flops 5908463616 | bytes 12845056 | tf_op jit(solution)/shard_map/dot_general | solution.py:1327
  485.5 2.8 multiply_reduce_fusion.6
  488.7 66.7 %scatter16.3 = (f32[128,2176]{1,0:T(8,128)}, bf16[1,352,2048]{2,1,0:T(8,128)(2,1)}) custom-call(bf16[16,128,2176]{2,1,0:T(8,128)(2,1)} %bitcast.159, bf16[2,704,2048]{2,1,0:T(8,128)(2,1)} %bitcast.149), custom_call_target="tpu_custom_call" | custom-call | bytes 4000000 | tf_op jit(solution)/shard_map/scatter16/pallas_call | solution.py:643
  561.0 55.3 %gather16.3 = (bf16[16,128,2048]{2,1,0:T(8,128)(2,1)}, bf16[1,352,2048]{2,1,0:T(8,128)(2,1)}) custom-call(bf16[128,2048]{1,0:T(8,128)(2,1)} %fusion.39.x_ref, bf16[2,704,2048]{2,1,0:T(8,128)(2,1)} %bitcast.150), custom_call_target="tpu_custom_call" | custom-call | bytes 4000000 | tf_op jit(solution)/shard_map/gather16/pallas_call | solution.py:296
  616.4 20.4 %attend_back.1 = (bf16[16,2,64,2688]{3,2,1,0:T(8,128)(2,1)}, bf16[16,2,64,256]{3,2,1,0:T(8,128)(2,1)}, f32[128,2048]{1,0:T(8,128)}, f32[512,256]{1,0:T(8,128)}) custom-call(s32[2]{0:T(128)} %bitcast.140, bf16[16,2,64,2048]{3,2,1,0:T(8,128)(2,1)} %bitcast.203, bf16[2,1024,256]{2,1,0:T(8,128)(2,1)} %copy-done.6, bf16[2,1024,256]{2,1,0:T(8,128)(2,1)} %copy-done.7, ...), custom_call_target="tpu_custom_call" | custom-call | flops 14000000000 | bytes 25000000 | tf_op jit(solution)/shard_map/attend_back/pallas_call | solution.py:1297
  636.8 6.2 fusion.43
  651.0 83.6 %returning.1 = (f32[128,2688]{1,0:T(8,128)}, bf16[2,16,64,256]{3,2,1,0:T(8,128)(2,1)}, bf16[2,64,2048]{2,1,0:T(8,128)(2,1)}, bf16[1,16,64,256]{3,2,1,0:T(8,128)(2,1)}, bf16[1,64,2048]{2,1,0:T(8,128)(2,1)}) custom-call(bf16[16,128,2688]{2,1,0:T(8,128)(2,1)} %bitcast.158, bf16[2,16,64,256]{3,2,1,0:T(8,128)(2,1)} %pad_maximum_fusion.2.parts_ref, ...), custom_call_target="tpu_custom_call" | custom-call | bytes 4000000 | tf_op jit(solution)/shard_map/returning/pallas_call | solution.py:757
  752.3 4.1 fusion.16
  758.6 32.6 %closing.1 = (bf16[128,640]{1,0:T(8,128)(2,1)S(1)}, bf16[1,64,640]{2,1,0:T(8,128)(2,1)S(1)}) custom-call(bf16[16,128,640]{2,1,0:T(8,128)(2,1)S(1)} %bitcast.135), custom_call_target="tpu_custom_call" | custom-call | bytes 4000000 | tf_op jit(solution)/shard_map/closing/pallas_call | solution.py:809
  793.4 6.6 convert_add_fusion
  805.9 4.7 bitcast_convert_fusion
  810.6 4.7 bitcast_convert_fusion.1
  (259 shorter events, 87.2 us)
Async XLA Ops:
  7.2 279.9 %all-gather.11.cloned.1.call-start = ((), (), s32[]{:S(2)}) async-start(), calls=%async_computation.8 | async-start | bytes 3244032 | tf_op jit(solution)/shard_map/all_gather | solution.py:1452
  9.5 285.2 %all-gather.7.cloned.1.call-start = ((), (), s32[]{:S(2)}) async-start(), calls=%async_computation.6 | async-start | bytes 8650752 | tf_op jit(solution)/shard_map/all_gather | solution.py:1450
  10.4 284.4 %all-gather.9.cloned.1.call-start = ((), (), s32[]{:S(2)}) async-start(), calls=%async_computation.7 | async-start | bytes 8650752 | tf_op jit(solution)/shard_map/all_gather | solution.py:1451
  11.1 791.9 %reduce-scatter.8.cloned.1.call-start = ((), (), s32[]{:S(2)}) async-start(), calls=%async_computation.5 | async-start | bytes 3244032 | tf_op jit(solution)/shard_map/reduce_scatter | solution.py:1524
  117.2 18.1 %copy-start = (bf16[512,256]{1,0:T(8,128)(2,1)}, bf16[512,256]{1,0:T(8,128)(2,1)S(1)}, u32[]{:S(2)}) copy-start(bf16[512,256]{1,0:T(8,128)(2,1)S(1)} %reshape.550.we_ref) | copy-start | bytes 786436
  117.3 96.0 %copy-start.44 = (f32[128]{0:T(128)}, f32[128]{0:T(128)S(1)}, u32[]{:S(2)}) copy-start(f32[128]{0:T(128)S(1)} %rsqrt.29) | copy-start | bytes 1540
  118.5 16.8 %copy-start.3 = (bf16[2,64,2048]{2,1,0:T(8,128)(2,1)S(1)}, bf16[2,64,2048]{2,1,0:T(8,128)(2,1)}, u32[]{:S(2)}) copy-start(bf16[2,64,2048]{2,1,0:T(8,128)(2,1)} %get-tuple-element.86) | copy-start | bytes 1572868
  135.3 9.9 %copy-start.6 = (bf16[2,1024,256]{2,1,0:T(8,128)(2,1)}, bf16[2,1024,256]{2,1,0:T(8,128)(2,1)S(1)}, u32[]{:S(2)}) copy-start(bf16[2,1024,256]{2,1,0:T(8,128)(2,1)S(1)} %get-tuple-element.83.q_ref) | copy-start | bytes 3145732
  135.3 9.9 %copy-start.7 = (bf16[2,1024,256]{2,1,0:T(8,128)(2,1)}, bf16[2,1024,256]{2,1,0:T(8,128)(2,1)S(1)}, u32[]{:S(2)}) copy-start(bf16[2,1024,256]{2,1,0:T(8,128)(2,1)S(1)} %get-tuple-element.84.k_ref) | copy-start | bytes 3145732
  146.2 67.1 %copy-start.10 = (bf16[16,2,64,128]{3,2,1,0:T(8,128)(2,1)}, bf16[16,2,64,128]{3,2,1,0:T(8,128)(2,1)S(1)}, u32[]{:S(2)}) copy-start(bf16[16,2,64,128]{3,2,1,0:T(8,128)(2,1)S(1)} %get-tuple-element.112.att_ref) | copy-start | bytes 1572868
  146.2 67.1 %copy-start.14 = (bf16[2,1,64,2048]{3,2,1,0:T(8,128)(2,1)S(1)}, bf16[2,1,64,2048]{3,2,1,0:T(8,128)(2,1)}, u32[]{:S(2)}) copy-start(bf16[2,1,64,2048]{3,2,1,0:T(8,128)(2,1)} %param.24) | copy-start | bytes 1572868
  215.7 66.3 %copy-start.19 = (bf16[2048,16]{1,0:T(8,128)(2,1)S(1)}, bf16[2048,16]{1,0:T(8,128)(2,1)}, u32[]{:S(2)}) copy-start(bf16[2048,16]{1,0:T(8,128)(2,1)} %slice.172) | copy-start | bytes 196612
  215.7 66.2 %copy-start.36 = (f32[128]{0:T(128)}, f32[128]{0:T(128)S(1)}, u32[]{:S(2)}) copy-start(f32[128]{0:T(128)S(1)} %add_rsqrt_fusion.2) | copy-start | bytes 1540
  216.6 68.2 %copy-start.16 = (bf16[2,1,64,2048]{3,2,1,0:T(8,128)(2,1)S(1)}, bf16[2,1,64,2048]{3,2,1,0:T(8,128)(2,1)}, u32[]{:S(2)}) copy-start(bf16[2,1,64,2048]{3,2,1,0:T(8,128)(2,1)} %param.25) | copy-start | bytes 1572868
  216.6 69.1 %copy-start.25 = (pred[2048,1]{1,0:T(8,128)(4,1)S(1)}, pred[2048,1]{1,0:T(8,128)(4,1)}, u32[]{:S(2)}) copy-start(pred[2048,1]{1,0:T(8,128)(4,1)} %copy.136) | copy-start | bytes 6148
  282.3 274.4 %copy-start.38 = (f32[128]{0:T(128)}, f32[128]{0:T(128)S(1)}, u32[]{:S(2)}) copy-start(f32[128]{0:T(128)S(1)} %reshape.577) | copy-start | bytes 1540
  363.7 74.0 %copy-start.18 = (bf16[256,2048]{1,0:T(8,128)(2,1)}, bf16[256,2048]{1,0:T(8,128)(2,1)S(1)}, u32[]{:S(2)}) copy-start(bf16[256,2048]{1,0:T(8,128)(2,1)S(1)} %fusion.44) | copy-start | bytes 3145732
  449.5 356.4 %reduce-scatter.6.cloned.1.call-start = ((), (), s32[]{:S(2)}) async-start(), calls=%async_computation.4 | async-start | bytes 8650752 | tf_op jit(solution)/shard_map/reduce_scatter | solution.py:1519
  449.5 11.1 %copy-start.54 = (bf16[1024,2048]{1,0:T(8,128)(2,1)S(1)}, bf16[1024,2048]{1,0:T(8,128)(2,1)}, u32[]{:S(2)}) copy-start(bf16[1024,2048]{1,0:T(8,128)(2,1)} %get-tuple-element.104) | copy-start | bytes 12582916
  449.6 11.1 %copy-start.55 = (bf16[1024,1408]{1,0:T(8,128)(2,1)S(1)}, bf16[1024,1408]{1,0:T(8,128)(2,1)}, u32[]{:S(2)}) copy-start(bf16[1024,1408]{1,0:T(8,128)(2,1)} %get-tuple-element.106) | copy-start | bytes 8650756
  480.3 330.3 %reduce-scatter.4.cloned.1.call-start = ((), (), s32[]{:S(2)}) async-start(), calls=%async_computation.3 | async-start | bytes 8650752 | tf_op jit(solution)/shard_map/reduce_scatter | solution.py:1518
  488.7 69.0 %copy-start.37 = (f32[128]{0:T(128)S(1)}, f32[128]{0:T(128)}, u32[]{:S(2)}) copy-start(f32[128]{0:T(128)} %copy-done.36) | copy-start | bytes 1540
  559.8 56.6 %copy-start.46 = (f32[128]{0:T(128)}, f32[128]{0:T(128)S(1)}, u32[]{:S(2)}) copy-start(f32[128]{0:T(128)S(1)} %broadcast_multiply_fusion.2) | copy-start | bytes 1540
  738.7 13.6 %copy-start.15 = (bf16[2,1,64,2048]{3,2,1,0:T(8,128)(2,1)S(1)}, bf16[2,1,64,2048]{3,2,1,0:T(8,128)(2,1)}, u32[]{:S(2)}) copy-start(bf16[2,1,64,2048]{3,2,1,0:T(8,128)(2,1)} %param.24) | copy-start | bytes 1572868
  (40 other events, 190.4 us)
Sparse Core Ops, SparseCore 0:
  10.1 55.1 all-gather.10
  66.9 71.2 all-gather.6
  139.7 125.8 all-gather.8
  449.6 30.6 reduce-scatter.7
  482.6 121.6 reduce-scatter.5
  607.0 71.4 reduce-scatter.3

commit v6 on v5

--- a/solution.py
+++ b/solution.py
@@ -841,24 +841,80 @@
 SHARE = 176
 
 
-def down_copies(a_ref, b_ref, out, sem):
+def down_copies(a_ref, b_ref, out, sem, which):
     dp, a, _ = a_ref.shape
     rows = a + b_ref.shape[1]
+    if which == 0:
+        return [pltpu.make_async_copy(a_ref.at[d], out.at[pl.ds(d * rows, a)], sem.at[d]) for d in range(dp)]
+    return [pltpu.make_async_copy(b_ref.at[d], out.at[pl.ds(d * rows + a, rows - a)], sem.at[dp + d])
+            for d in range(dp)]
+
+
+def share_copies(share_ref, fan, down, sem):
+    dp, rows, w = share_ref.shape
+    n = rows // 3
     copies = []
     for d in range(dp):
-        copies.append(pltpu.make_async_copy(a_ref.at[d], out.at[pl.ds(d * rows, a)], sem.at[2 * d]))
-        copies.append(pltpu.make_async_copy(b_ref.at[d], out.at[pl.ds(d * rows + a, rows - a)], sem.at[2 * d + 1]))
+        cols = pl.ds(d * w, w)
+        for i, (dst, first) in enumerate(((fan, 0), (fan, TILE), (down, 0))):
+            copies.append(pltpu.make_async_copy(
+                share_ref.at[d, pl.ds(i * n, n)], dst.at[pl.ds(first, n), cols], sem.at[3 * d + i]))
     return copies
 
 
-def one_hots(slot_row, slot_col, groups, slots):
+def share_blank(fan, down):
+    pad = jnp.zeros((TILE - SHARE, fan.shape[1]), BF)
+    fan[SHARE:TILE] = pad
+    fan[TILE + SHARE:] = pad
+    down[SHARE:] = pad
+
+
+def mine_of(routes_ref, pick_ref):
+    tokens = routes_ref.shape[0]
+    lane16 = lax.broadcasted_iota(jnp.int32, (tokens, 16), 1)
+    mask = lane16 < 0
+    for k in range(routes_ref.shape[1]):
+        mask = mask | (lane16 == routes_ref[:, k:k + 1])
+    mine = jnp.sum(jnp.where(mask, pick_ref[:, :16], 0.0), axis=1, keepdims=True)
+    return mask, mine
+
+
+def valid_of(len_ref, first_device, tokens, batches, here):
+    n = lax.broadcasted_iota(jnp.int32, (tokens, 1), 0)
+    device = n // (batches * here)
+    batch = (n // here) % batches
+    position = (first_device + device) * here + n % here
+    length = jnp.zeros((tokens, 1), jnp.int32)
+    for b in range(batches):
+        length = jnp.where(batch == b, len_ref[b], length)
+    return (position < length).astype(F32)
+
+
+def one_hots(taken, groups, slots, here):
+    r = lax.broadcasted_iota(jnp.int32, (256, 256), 0)
+    c = lax.broadcasted_iota(jnp.int32, (256, 256), 1)
+    same = r // here == c // here
+    before = (same & (c < r)).astype(BF)
+    after = (same & (r < c)).astype(BF)
+    base_c = (lax.broadcasted_iota(jnp.int32, (256, slots), 0) // here * 32).astype(F32)
+    base_r = (lax.broadcasted_iota(jnp.int32, (slots, 256), 1) // here * 32).astype(F32)
+    lane = lax.broadcasted_iota(jnp.int32, (256, slots), 1).astype(F32)
+    row = lax.broadcasted_iota(jnp.int32, (slots, 256), 0).astype(F32)
+    ones = jnp.ones((256, slots), BF)
     to_slot, to_token = [], []
     for g in range(groups):
-        row = slot_row[:, g * 256:(g + 1) * 256]
-        col = slot_col[g * 256:(g + 1) * 256, :]
-        to_slot.append((lax.broadcasted_iota(jnp.int32, (slots, 256), 0) == row).astype(BF))
-        to_token.append((lax.broadcasted_iota(jnp.int32, (256, slots), 1) == col).astype(BF))
+        t = jnp.broadcast_to(taken[g * 256:(g + 1) * 256], (256, slots))
+        low = t.astype(BF)
+        place_c = mm(before, low) + base_c
+        place_r = mm_lead(low, after) + base_r
+        taken_r = mm_lead(low, (r == c).astype(BF))
+        to_token.append(jnp.where((place_c == lane) & (t > 0.5), 1.0, 0.0).astype(BF))
+        to_slot.append(jnp.where((place_r == row) & (taken_r > 0.5), 1.0, 0.0).astype(BF))
     return to_slot, to_token
+
+
+def mm_lead(a, b):
+    return lax.dot_general(a, b, (((0,), (0,)), ((), ())), preferred_element_type=F32)
 
 
 def lanes(j):
@@ -875,128 +931,158 @@
         body(total // WIDE * WIDE, total % WIDE)
 
 
-def forward_kernel(chunks, pick_ref, mix_ref, routes_ref, slot_row, slot_col, valid_ref, wg_ref, wu_ref, fan_ref, sd_ref,
-                   wda_ref, wdb_ref, dy_ref,
+def forward_kernel(chunks, dp, span, batches, here, len_ref, pick_ref, mix_ref, routes_ref, wg_ref, wu_ref, router_ref,
+                   share_ref, wda_ref, down_ref, dy_ref,
                    out_ref, rows_ref, hid_ref, act_ref, slo_ref, eo_ref, sh_ref, sact_ref, sslo_ref, gate_ref,
-                   dy_all, wd_ref, wd_sem, *sems):
+                   dy_all, wdb_ref,
+                   wd_ref, fan_ref, sd_ref, hid_buf, sh_buf, gate_buf, taken_buf, wd_sem, sh_sem, *sems):
     step = pl.program_id(0)
     tokens, width = mix_ref.shape
     groups, slots = tokens // 256, 128
+    half = groups * slots
     ff = hid_ref.shape[1]
-    g = Gather(dy_ref, dy_all, chunks, sems)
+    phase = pl.num_programs(0) // 2
+    g = Gather(dy_ref, dy_all, chunks, sems[:9])
+    job = side_job(Spread, dp, span, down_ref, wdb_ref, sems[9:])
 
     @pl.when(step == 0)
     def _():
-        enter(g.me, g.z, g.core, g.side)
+        enter(g.me, g.z, g.core, g.side, dp)
         g.start()
-        for copy in down_copies(wda_ref, wdb_ref, wd_ref, wd_sem):
+        job.start()
+        for copy in down_copies(wda_ref, wdb_ref, wd_ref, wd_sem, 0) + share_copies(share_ref, fan_ref, sd_ref, sh_sem):
             copy.start()
-
-    mix = mix_ref[...]
-    fanned = mm_t(mix, fan_ref[:TILE, :])
-    s_up = mm_t(mix, fan_ref[TILE:, :])
-    s_act, s_slope = silu_pair(fanned)
-    s_hidden = (s_act * s_up).astype(BF)
-    sh_ref[...] = s_hidden
-    sact_ref[...] = s_act.astype(BF)
-    sslo_ref[...] = (s_up * s_slope).astype(BF)
-    logits = fanned[:, SHARE:SHARE + 16]
-    lane16 = lax.broadcasted_iota(jnp.int32, (tokens, 16), 1)
-    mask = lane16 < 0
-    for k in range(routes_ref.shape[1]):
-        mask = mask | (lane16 == routes_ref[:, k:k + 1])
-    held = jnp.where(mask, logits, -1e30)
-    raised = jnp.where(mask, jnp.exp(held - jnp.max(held, axis=1, keepdims=True)), 0.0)
-    soft = raised / jnp.sum(raised, axis=1, keepdims=True)
-    gate = jnp.sum(soft * pick_ref[:, :16], axis=1, keepdims=True) * valid_ref[...]
-    gate_ref[...] = gate
-    to_slot, to_token = one_hots(slot_row, slot_col, groups, slots)
-
-    def dispatch(j, _):
-        for n in range(groups):
-            rows_ref[n * slots:(n + 1) * slots, lanes(j)] = mm(
-                to_slot[n], mix_ref[n * 256:(n + 1) * 256, lanes(j)]).astype(BF)
-        return 0
-
-    lax.fori_loop(0, width // WIDE, dispatch, 0)
-
-    def fan_in(start, size):
-        cols = pl.ds(start, size)
-        gate_in = mm(rows_ref[...], wg_ref[:, cols])
-        up_in = mm(rows_ref[...], wu_ref[:, cols])
-        act, slope = silu_pair(gate_in)
-        hid_ref[:, cols] = (act * up_in).astype(BF)
-        act_ref[:, cols] = act.astype(BF)
-        slo_ref[:, cols] = (up_in * slope).astype(BF)
-
-    over_columns(ff, fan_in)
-
-    @pl.when(step == 0)
+        share_blank(fan_ref, sd_ref)
+        fan_ref[SHARE:SHARE + 16] = router_ref[...]
+        for copy in share_copies(share_ref, fan_ref, sd_ref, sh_sem):
+            copy.wait()
+
+    @pl.when(step < phase)
     def _():
-        for copy in down_copies(wda_ref, wdb_ref, wd_ref, wd_sem):
-            copy.wait()
-
-
-    def fan_out(j, _):
-        eo = mm(hid_ref[...], wd_ref[:, lanes(j)]).astype(BF)
-        eo_ref[:, lanes(j)] = eo
-        shared = mm(s_hidden, sd_ref[:, lanes(j)])
-        picked = jnp.concatenate(
-            [mm(to_token[n], eo[n * slots:(n + 1) * slots]) for n in range(groups)], axis=0)
-        out_ref[:, lanes(j)] = (shared + gate * picked).astype(BF)
-        return 0
-
-    lax.fori_loop(0, width // WIDE, fan_out, 0)
-    steps = pl.num_programs(0)
-    for r in range(1, NZ + 1):
-        @pl.when(step == r - 1)
+        mix = mix_ref[...]
+        fanned = mm_t(mix, fan_ref[:TILE, :])
+        s_up = mm_t(mix, fan_ref[TILE:, :])
+        s_act, s_slope = silu_pair(fanned)
+        s_hidden = (s_act * s_up).astype(BF)
+        at = pl.ds(pl.multiple_of(step * tokens, tokens), tokens)
+        sh_ref[...] = s_hidden
+        sh_buf[at] = s_hidden
+        sact_ref[...] = s_act.astype(BF)
+        sslo_ref[...] = (s_up * s_slope).astype(BF)
+        logits = fanned[:, SHARE:SHARE + 16]
+        mask, mine = mine_of(routes_ref, pick_ref)
+        taken = mine * valid_of(len_ref, step * (tokens // (batches * here)), tokens, batches, here)
+        held = jnp.where(mask, logits, -1e30)
+        raised = jnp.where(mask, jnp.exp(held - jnp.max(held, axis=1, keepdims=True)), 0.0)
+        soft = raised / jnp.sum(raised, axis=1, keepdims=True)
+        gate = jnp.sum(soft * pick_ref[:, :16], axis=1, keepdims=True) * taken
+        gate_ref[...] = jnp.concatenate([gate, taken], axis=1)
+        gate_buf[at] = gate
+        taken_buf[at] = taken
+        to_slot, _ = one_hots(taken, groups, slots, here)
+
+        def dispatch(j, _):
+            for n in range(groups):
+                rows_ref[n * slots:(n + 1) * slots, lanes(j)] = mm(
+                    to_slot[n], mix_ref[n * 256:(n + 1) * 256, lanes(j)]).astype(BF)
+            return 0
+
+        lax.fori_loop(0, width // WIDE, dispatch, 0)
+        rows_at = pl.ds(pl.multiple_of(step * half, half), half)
+
+        def fan_in(start, size):
+            cols = pl.ds(start, size)
+            gate_in = mm(rows_ref[...], wg_ref[:, cols])
+            up_in = mm(rows_ref[...], wu_ref[:, cols])
+            act, slope = silu_pair(gate_in)
+            hidden = (act * up_in).astype(BF)
+            hid_ref[:, cols] = hidden
+            hid_buf[rows_at, cols] = hidden
+            act_ref[:, cols] = act.astype(BF)
+            slo_ref[:, cols] = (up_in * slope).astype(BF)
+
+        over_columns(ff, fan_in)
+
+    @pl.when(step == phase)
+    def _():
+        job.finish()
+        for copy in down_copies(wda_ref, wdb_ref, wd_ref, wd_sem, 1):
+            copy.start()
+        for which in range(2):
+            for copy in down_copies(wda_ref, wdb_ref, wd_ref, wd_sem, which):
+                copy.wait()
+
+    @pl.when(step >= phase)
+    def _():
+        tile = step - phase
+        at = pl.ds(pl.multiple_of(tile * tokens, tokens), tokens)
+        rows_at = pl.ds(pl.multiple_of(tile * half, half), half)
+        gate = gate_buf[at]
+        s_hidden = sh_buf[at]
+        _, to_token = one_hots(taken_buf[at], groups, slots, here)
+
+        def fan_out(j, _):
+            eo = mm(hid_buf[rows_at], wd_ref[:, lanes(j)]).astype(BF)
+            eo_ref[:, lanes(j)] = eo
+            shared = mm(s_hidden, sd_ref[:, lanes(j)])
+            picked = jnp.concatenate(
+                [mm(to_token[n], eo[n * slots:(n + 1) * slots]) for n in range(groups)], axis=0)
+            out_ref[:, lanes(j)] = (shared + gate * picked).astype(BF)
+            return 0
+
+        lax.fori_loop(0, width // WIDE, fan_out, 0)
+
+    for r, s in ((1, 1), (2, 3), (3, 5), (4, 7)):
+        @pl.when(step == s)
         def _():
             g.round(r)
 
-    @pl.when(step == steps - 1)
+    @pl.when(step == 2 * phase - 1)
     def _():
         g.finish()
 
 
-def backward_kernel(chunks, pick_ref, dy_ref, slot_row, slot_col, wg_ref, wu_ref, fan_ref, sd_ref, wda_ref, wdb_ref,
-                    act_ref, slo_ref, eo_ref, sact_ref, sslo_ref, gate_ref, part_ref,
-                    dh_ref, deo_ref, dg_ref, du_ref, ds_ref, sum_ref, wd_ref, wd_sem, *scratch):
+def backward_kernel(here, pick_ref, dy_ref, mix_ref, sh_ref, wg_ref, wu_ref, share_ref, wda_ref, wdb_ref,
+                    act_ref, slo_ref, eo_ref, sact_ref, sslo_ref, gate_ref,
+                    dh_ref, deo_ref, dg_ref, du_ref, gshare_ref,
+                    wd_ref, fan_ref, sd_ref, gfan, gsd, wd_sem, sh_sem):
     step = pl.program_id(0)
     tokens, width = dy_ref.shape
     groups, slots = tokens // 256, 128
     ff = dg_ref.shape[1]
-    sc = Scatter(part_ref, sum_ref, chunks, scratch)
 
     @pl.when(step == 0)
     def _():
-        enter(sc.me, sc.z, sc.core, sc.side)
-        for copy in down_copies(wda_ref, wdb_ref, wd_ref, wd_sem):
+        copies = share_copies(share_ref, fan_ref, sd_ref, sh_sem)
+        for which in range(2):
+            copies += down_copies(wda_ref, wdb_ref, wd_ref, wd_sem, which)
+        for copy in copies:
             copy.start()
-        sc.start()
+        share_blank(fan_ref, sd_ref)
+        gfan[...] = jnp.zeros_like(gfan)
+        gsd[...] = jnp.zeros_like(gsd)
+        for copy in copies:
+            copy.wait()
 
     d_sh = mm_t(dy_ref[...], sd_ref[...])
-    ds_ref[:, :TILE] = (d_sh * sslo_ref[...].astype(F32)).astype(BF)
-    ds_ref[:, TILE:] = (d_sh * sact_ref[...].astype(F32)).astype(BF)
-    to_slot, to_token = one_hots(slot_row, slot_col, groups, slots)
-    gate = gate_ref[...]
+    d_s = jnp.concatenate([(d_sh * sslo_ref[...].astype(F32)).astype(BF),
+                           (d_sh * sact_ref[...].astype(F32)).astype(BF)], axis=1)
+    gate, taken = gate_ref[:, :1], gate_ref[:, 1:]
+    to_slot, to_token = one_hots(taken, groups, slots, here)
 
     def dispatch(j, total):
-        dy = dy_ref[:, lanes(j)].astype(F32)
+        low = dy_ref[:, lanes(j)]
+        dy = low.astype(F32)
         gated = (gate * dy).astype(BF)
         for n in range(groups):
             deo_ref[n * slots:(n + 1) * slots, lanes(j)] = mm(to_slot[n], gated[n * 256:(n + 1) * 256]).astype(BF)
         picked = jnp.concatenate(
             [mm(to_token[n], eo_ref[n * slots:(n + 1) * slots, lanes(j)]) for n in range(groups)], axis=0)
+        gfan[:, lanes(j)] += mm_lead(d_s, mix_ref[:, lanes(j)])
+        gsd[:, lanes(j)] += mm_lead(sh_ref[...], low)
         return total + jnp.sum(dy * picked, axis=1, keepdims=True)
 
     d_gates = lax.fori_loop(0, width // WIDE, dispatch, jnp.zeros((tokens, 1), F32))
-
-    @pl.when(step == 0)
-    def _():
-        sc.first(0)
-        sc.first(1)
-        for copy in down_copies(wda_ref, wdb_ref, wd_ref, wd_sem):
-            copy.wait()
 
     def back_out(start, size):
         cols = pl.ds(start, size)
@@ -1006,105 +1092,106 @@
 
     over_columns(ff, back_out)
 
-    @pl.when(step == 0)
-    def _():
-        sc.first(2)
-        sc.first(3)
-
-    d_s = ds_ref[...]
-
     def back_in(j, _):
         d_rows = (mm_t(dg_ref[...], wg_ref[lanes(j), :]) + mm_t(du_ref[...], wu_ref[lanes(j), :])).astype(BF)
         shared = mm(d_s, fan_ref[:, lanes(j)])
-        taken = jnp.concatenate(
+        taken_rows = jnp.concatenate(
             [mm(to_token[n], d_rows[n * slots:(n + 1) * slots]) for n in range(groups)], axis=0)
-        dh_ref[:, lanes(j)] = (shared + taken).astype(BF)
+        dh_ref[:, lanes(j)] = (shared + taken_rows).astype(BF)
         return 0
 
     lax.fori_loop(0, width // WIDE, back_in, 0)
     high = d_gates.astype(BF).astype(F32)
     dh_ref[:, width:] = (high * pick_ref[:, :128] + (d_gates - high) * pick_ref[:, 128:]).astype(BF)
 
-    outer = (sc.z == 0) | (sc.z == NZ - 1)
-    for i in range(NZ - 1):
-        @pl.when((step == i) & outer)
-        def _():
-            sc.second(i)
-
-        @pl.when((step == min(i + 1, 2)) & jnp.logical_not(outer))
-        def _():
-            sc.second(i)
-
-    @pl.when(step == 3)
+    @pl.when(step == pl.num_programs(0) - 1)
     def _():
-        sc.second(3)
-        sc.finish()
+        dp, rows, w = share_ref.shape
+        n = rows // 3
+        for d in range(dp):
+            cols = slice(d * w, (d + 1) * w)
+            gshare_ref[d, :n] = gfan[:n, cols].astype(BF)
+            gshare_ref[d, n:2 * n] = gfan[TILE:TILE + n, cols].astype(BF)
+            gshare_ref[d, 2 * n:] = gsd[:n, cols].astype(BF)
 
 
 def whole(v):
-    return pl.BlockSpec(v.shape, lambda i: (0, 0), pipeline_mode=pl.Buffered(buffer_count=1))
+    zeros = (0,) * v.ndim
+    return pl.BlockSpec(v.shape, lambda i: zeros, pipeline_mode=pl.Buffered(buffer_count=1))
 
 
 def tiles(rows, w):
     return pl.BlockSpec((rows, w), lambda i: (i, 0))
 
 
-def mixture_forward(pick, mix, routes, slot, valid, wg, wu, wda, wdb, fan, sd, dy, cid, chunks=2):
+SMEM = pl.BlockSpec(memory_space=pltpu.SMEM)
+
+
+def mixture_forward(dp, batches, here, lengths, pick, mix, routes, wg, wu, router, share, wda, span, down, dy, cid,
+                    chunks=2):
     total, width = mix.shape
     step, half = total // 4, total // 8
     ff = wg.shape[1]
     shape = jax.ShapeDtypeStruct
     rows = total // 2
+    dma = pltpu.SemaphoreType.DMA
+
+    def early(n, w):
+        return pl.BlockSpec((n, w), lambda i: (jnp.minimum(i, 3), 0))
+
+    def late(n, w):
+        return pl.BlockSpec((n, w), lambda i: (jnp.maximum(i - 4, 0), 0))
+
     return pl.pallas_call(
-        functools.partial(forward_kernel, chunks),
-        grid=(4,),
+        functools.partial(forward_kernel, chunks, dp, span, batches, here),
+        grid=(8,),
         out_shape=(
             shape((total, width), BF), shape((rows, width), BF), shape((rows, ff), BF), shape((rows, ff), BF),
             shape((rows, ff), BF), shape((rows, width), BF), shape((total, TILE), BF), shape((total, TILE), BF),
-            shape((total, TILE), BF), shape((total, 1), F32), shape((NE,) + dy.shape, BF)),
-        in_specs=[whole(pick), tiles(step, width), tiles(step, routes.shape[1]), pl.BlockSpec((1, step), lambda i: (0, i)),
-                  tiles(step, 1), tiles(step, 1), whole(wg), whole(wu), whole(fan), whole(sd), ANY, ANY, ANY],
-        out_specs=[tiles(step, width), tiles(half, width), tiles(half, ff), tiles(half, ff), tiles(half, ff),
-                   tiles(half, width), tiles(step, TILE), tiles(step, TILE), tiles(step, TILE), tiles(step, 1), ANY],
-        scratch_shapes=[pltpu.VMEM((ff, width), BF), pltpu.SemaphoreType.DMA((2 * wda.shape[0],))]
-        + Gather.scratch(chunks),
+            shape((total, TILE), BF), shape((total, 2), F32), shape((NE,) + dy.shape, BF),
+            shape((dp, span[1], width), BF)),
+        in_specs=[SMEM, whole(pick), early(step, width), early(step, routes.shape[1]), whole(wg), whole(wu),
+                  whole(router), ANY, ANY, ANY, ANY],
+        out_specs=[late(step, width), early(half, width), early(half, ff), early(half, ff), early(half, ff),
+                   late(half, width), early(step, TILE), early(step, TILE), early(step, TILE), early(step, 2), ANY, ANY],
+        scratch_shapes=[
+            pltpu.VMEM((ff, width), BF), pltpu.VMEM((2 * TILE, width), BF), pltpu.VMEM((TILE, width), BF),
+            pltpu.VMEM((rows, ff), BF), pltpu.VMEM((total, TILE), BF), pltpu.VMEM((total, 1), F32),
+            pltpu.VMEM((total, 1), F32), dma((2 * dp,)), dma((3 * dp,))] + Gather.scratch(chunks) + Spread.scratch(dp),
         compiler_params=pltpu.CompilerParams(
             collective_id=cid, has_side_effects=True, vmem_limit_bytes=60 * 1024 * 1024),
         cost_estimate=COST,
         name="mixture_forward",
-    )(pick, mix, routes, slot[None, :], slot[:, None], valid, wg, wu, fan, sd, wda, wdb, dy)
-
-
-def mixture_backward(pick, dy, slot, wg, wu, wda, wdb, fan, sd, act, slo, eo, sact, sslo, gate, part, cid, chunks=2):
+    )(lengths, pick, mix, routes, wg, wu, router, share, wda, down, dy)
+
+
+def mixture_backward(here, pick, dy, mix, sh, wg, wu, share, wda, wdb, act, slo, eo, sact, sslo, gate):
     total, width = dy.shape
     step, half = total // 4, total // 8
     ff = wg.shape[1]
     shape = jax.ShapeDtypeStruct
     rows = total // 2
-    _, own, _ = part.shape
+    dp = wda.shape[0]
+    dma = pltpu.SemaphoreType.DMA
     return pl.pallas_call(
-        functools.partial(backward_kernel, chunks),
+        functools.partial(backward_kernel, here),
         grid=(4,),
         out_shape=(
             shape((total, width + 128), BF), shape((rows, width), BF), shape((rows, ff), BF), shape((rows, ff), BF),
-            shape((total, 2 * TILE), BF), shape((own, width), F32)),
-        in_specs=[whole(pick), tiles(step, width), pl.BlockSpec((1, step), lambda i: (0, i)), tiles(step, 1),
-                  whole(wg), whole(wu), whole(fan), whole(sd), ANY, ANY,
+            shape(share.shape, BF)),
+        in_specs=[whole(pick), tiles(step, width), tiles(step, width), tiles(step, TILE), whole(wg), whole(wu),
+                  ANY, ANY, ANY,
                   tiles(half, ff), tiles(half, ff), tiles(half, width), tiles(step, TILE), tiles(step, TILE),
-                  tiles(step, 1), ANY],
+                  tiles(step, 2)],
         out_specs=[tiles(step, width + 128), tiles(half, width), tiles(half, ff), tiles(half, ff),
-                   tiles(step, 2 * TILE), pl.BlockSpec((own, width), lambda i: (0, 0))],
-        scratch_shapes=[pltpu.VMEM((ff, width), BF), pltpu.SemaphoreType.DMA((2 * wda.shape[0],))]
-        + Scatter.scratch(own, width, chunks, BF),
-        compiler_params=pltpu.CompilerParams(
-            collective_id=cid, has_side_effects=True, vmem_limit_bytes=60 * 1024 * 1024),
+                   pl.BlockSpec(share.shape, lambda i: (0, 0, 0))],
+        scratch_shapes=[
+            pltpu.VMEM((ff, width), BF), pltpu.VMEM((2 * TILE, width), BF), pltpu.VMEM((TILE, width), BF),
+            pltpu.VMEM((2 * TILE, width), F32), pltpu.VMEM((TILE, width), F32), dma((2 * dp,)), dma((3 * dp,))],
+        compiler_params=pltpu.CompilerParams(vmem_limit_bytes=60 * 1024 * 1024),
         cost_estimate=COST,
         name="mixture_backward",
-    )(pick, dy, slot[None, :], slot[:, None], wg, wu, fan, sd, wda, wdb, act, slo, eo, sact, sslo, gate, part)
-
-
-def mm_lead(a, b):
-    return lax.dot_general(a, b, (((0,), (0,)), ((), ())), preferred_element_type=F32)
+    )(pick, dy, mix, sh, wg, wu, share, wda, wdb, act, slo, eo, sact, sslo, gate)
 
 
 def turn(v, cosine, sine):
@@ -1450,24 +1537,14 @@
     gate_full = lax.all_gather(gate_weight[0], "dp", axis=0, tiled=True)
     up_full = lax.all_gather(up_weight[0], "dp", axis=0, tiled=True)
     share_full = lax.all_gather(share_own, "dp", axis=0)
-    share_full = share_full.transpose(1, 0, 2).reshape(3 * share_width, width)
-
     seq_lengths = lengths.reshape(batches)
     own_positions = me * here + jnp.arange(here, dtype=jnp.int32)
     valid_own = (own_positions[None, :] < seq_lengths[:, None]).reshape(own).astype(F32)
-    all_positions = jnp.arange(seq_total, dtype=jnp.int32).reshape(GROUPS, 1, here)
-    valid_all = jnp.broadcast_to(
-        all_positions < seq_lengths[None, :, None], (GROUPS, batches, here)
-    ).reshape(total)
     cosine, sine_table = rotary_tables(seq_total)
     cosine_own = lax.dynamic_slice_in_dim(jnp.asarray(cosine), me * here, here)
     sine_own = lax.dynamic_slice_in_dim(jnp.asarray(sine_table), me * here, here)
 
     grad_own = out_cotangent.reshape(own, width) * valid_own[:, None].astype(BF)
-    taken = jnp.any(routes_all == me, axis=1) & valid_all
-    places = jnp.cumsum(taken.reshape(-1, here).astype(jnp.int32), axis=1) - 1
-    places = places + 32 * (jnp.arange(places.shape[0], dtype=jnp.int32) % 4)[:, None]
-    slot = jnp.where(taken, places.reshape(total), -1)
 
     def by_token(table):
         return jnp.asarray(np.broadcast_to(
@@ -1479,48 +1556,38 @@
     attn_part, attended, log_total = attend(seq_lengths, query, key, values, output_head, GROUPS)
     attn_part = attn_part.reshape(GROUPS, own, width)
     down_own = down_weight[0]
-    cut = down_own.shape[0] // 32 * 16
+    cut = down_own.shape[0] * 3 // 80 * 16
     spans = ((0, cut), (cut, down_own.shape[0] - cut))
-    attn_out, down_a = scatter16(attn_part, 2, dp=dp, kind=Spread, span=spans[0], side=down_own)
+    attn_out = scatter16(attn_part, 2)
 
     x_wide = x_own.astype(F32)
     middle = x_wide + attn_out
     normed_mix, unit_mix, factor_mix = norm_forward(middle, gain_mixer)
     hidden_mix = normed_mix.astype(BF)
-    mix_all, down_b = gather16(hidden_mix, 3, dp=dp, kind=Spread, span=spans[1], side=down_own)
+    mix_all, down_a = gather16(hidden_mix, 3, dp=dp, kind=Spread, span=spans[0], side=down_own)
     mix_all = mix_all.reshape(total, width)
 
-    pad = TILE - share_width
-    fan_share = jnp.concatenate(
-        [share_full[:share_width], router_full.T, jnp.zeros((pad - GROUPS, width), BF),
-         share_full[share_width : 2 * share_width], jnp.zeros((pad, width), BF)], axis=0)
-    down_share = jnp.concatenate([share_full[2 * share_width :], jnp.zeros((pad, width), BF)], axis=0)
     lane = jnp.arange(128)[None, :]
     pick = jnp.concatenate([lane == me, lane == me + GROUPS], axis=1).astype(F32)
-    out_part, rows, hidden, act, slope, result, share_hidden, share_act, share_slope, gates, grad_all = mixture_forward(
-        pick, mix_all, routes_all, slot, valid_all.astype(F32)[:, None],
-        gate_full, up_full, down_a, down_b, fan_share, down_share, grad_own, 4)
+    (out_part, rows, hidden, act, slope, result, share_hidden, share_act, share_slope, gates, grad_all,
+     down_b) = mixture_forward(
+        dp, batches, here, seq_lengths, pick, mix_all, routes_all, gate_full, up_full, router_full.T, share_full,
+        down_a, spans[1], down_own, grad_own, 4)
     grad_all = grad_all.reshape(total, width)
-    mix_part, grad_result, grad_gate_in, grad_up_in, grad_share_in, mixed = mixture_backward(
-        pick, grad_all, slot, gate_full, up_full, down_a, down_b, fan_share, down_share, act, slope, result,
-        share_act, share_slope, gates, out_part.reshape(GROUPS, own, width), 8)
+    mixed = lax.psum_scatter(out_part, "expert", scatter_dimension=0, tiled=True).astype(F32)
+    mix_part, grad_result, grad_gate_in, grad_up_in, grad_share = mixture_backward(
+        here, pick, grad_all, mix_all, share_hidden, gate_full, up_full, share_full, down_a, down_b, act, slope, result,
+        share_act, share_slope, gates)
     grad_down = product_lead(hidden, grad_result).astype(BF)
     grad_gate = product_lead(rows, grad_gate_in).astype(BF)
     grad_up = product_lead(rows, grad_up_in).astype(BF)
-    grad_share_fan = product_lead(grad_share_in, mix_all).astype(BF)
-    grad_share_down = product_lead(share_hidden, grad_all).astype(BF)
     mix_part, grad_down, grad_gate, grad_up = lax.optimization_barrier((mix_part, grad_down, grad_gate, grad_up))
-    grad_down = grad_down.reshape(dp, ff // dp, width)
-    mix_sum, far_a = scatter16(
-        mix_part.reshape(GROUPS, own, width + 128), 5, dp=dp, kind=Swap, span=spans[0], side=grad_down)
+    mix_sum = scatter16(mix_part.reshape(GROUPS, own, width + 128), 5)
     layer_output = valid_own[:, None] * (middle + mixed)
 
+    out_down = lax.psum_scatter(grad_down, "dp", scatter_dimension=0, tiled=True)
     out_gate = lax.psum_scatter(grad_gate, "dp", scatter_dimension=0, tiled=True)
     out_up = lax.psum_scatter(grad_up, "dp", scatter_dimension=0, tiled=True)
-    grad_share = jnp.concatenate(
-        [grad_share_fan[:share_width], grad_share_fan[TILE : TILE + share_width], grad_share_down[:share_width]],
-        axis=0)
-    grad_share = grad_share.reshape(3 * share_width, dp, width // dp).swapaxes(0, 1)
     out_share = lax.psum_scatter(grad_share, "dp", scatter_dimension=0, tiled=False).astype(F32)
 
     mask_own = selected_experts(routes_own)
@@ -1533,11 +1600,7 @@
     grad_middle_norm, grad_gain_mixer = norm_backward(grad_mix, unit_mix, factor_mix, gain_mixer)
     grad_middle = grad_own.astype(F32) + grad_middle_norm
 
-    grad_attn_all, far_b = gather16(
-        grad_middle.astype(BF), 6, dp=dp, kind=Swap, span=spans[1], side=grad_down)
-    grad_attn_all = grad_attn_all.reshape(GROUPS, batches, here, width)
-    out_down = lax.dynamic_index_in_dim(grad_down, plane, 0, False).astype(F32)
-    out_down = out_down + jnp.sum(jnp.concatenate([far_a, far_b], axis=1).astype(F32), axis=0)
+    grad_attn_all = gather16(grad_middle.astype(BF), 6).reshape(GROUPS, batches, here, width)
     back_part, grad_query, grad_output, grad_expand = attend_back(
         seq_lengths, grad_attn_all, query, key, values, latent, attended, log_total, output_head, parts_head,
         expand_head, jnp.asarray(cosine), jnp.asarray(sine_table), 640)
@@ -1594,7 +1657,7 @@
         small_sum[:, 576:592],
         out_gate.astype(F32)[None],
         out_up.astype(F32)[None],
-        out_down[None],
+        out_down.astype(F32)[None],
         out_share[:share_width].T,
         out_share[share_width : 2 * share_width].T,
         out_share[2 * share_width :],

time: 827 us -> 830 us (level)
  waiting for transfers between devices: 1.99 us -> 18.8 us
  local copies, waits for them, and re-layouts: 48.5 us -> 36.3 us
  Pallas kernels: 641 us -> 653 us
  matrix products: 63.9 us -> 52.2 us
    pallas_call x2, Pallas kernels: 134 us -> 107 us  [scatter16(): pl.pallas_call(functools.partial(scatter_kernel, chunks, dp, kind, span),...]
    pallas_call x2, Pallas kernels: 136 us -> 155 us  [the longest x1 88 us: mixture_forward(): pl.pallas_call(functools.partial(forward_kernel, chunks, dp, span, batche...]
    pallas_call x1, Pallas kernels: 32.6 us -> 50.6 us  [closing(): pl.pallas_call(functools.partial(closing_kernel, dp, 1), out_shape=(shape...]
    reduce_scatter x0 -> x2, waiting for transfers between devices: none -> 15.5 us  [the longest x1 15.5 us: per_device(): lax.psum_scatter(out_part, 'expert', scatter_dimension=0, tiled=True)]
    dot_general x7 -> x5, matrix products: 53.6 us -> 40.5 us  [product_lead(): lax.dot_general(left_side, right_side, (((0,), (0,)), ((), ())), preferre...]
  transfers between devices with their start and end apart: 6 -> 8, of which waited for: 0 -> 1; matrix products, arithmetic and copies ran while one was open for 16% -> 16% of each run, Pallas kernels for 61% -> 60%
where the time goes in v6:
time: 830 us; the launch traced here: 825 us
  Pallas kernels  653 us (79%)
  matrix products  52.2 us (6%)
  other arithmetic  49.3 us (6%)
  local copies, waits for them, and re-layouts  36.3 us (4%)
  waiting for transfers between devices  18.8 us (2%)
  between operations  15.1 us (2%)
    pallas_call x2, Pallas kernels, gather16(): pl.pallas_call(functools.partial(gather_kernel, chunks, dp, kind, span),...  124 us
    pallas_call x2, Pallas kernels, scatter16(): pl.pallas_call(functools.partial(scatter_kernel, chunks, dp, kind, span),...  107 us
    pallas_call x1, Pallas kernels, opening(): pl.pallas_call(functools.partial(opening_kernel, dp, chunks), out_shape=(...  88.3 us
    pallas_call x1, Pallas kernels, mixture_forward(): pl.pallas_call(functools.partial(forward_kernel, chunks, dp, span, batche...  88 us
    pallas_call x1, Pallas kernels, returning(): pl.pallas_call(functools.partial(return_kernel, dp, chunks), out_shape=(s...  81.7 us
    pallas_call x1, Pallas kernels, mixture_backward(): pl.pallas_call(functools.partial(backward_kernel, here), grid=(4,), out_s...  66.8 us
    pallas_call x1, Pallas kernels, closing(): pl.pallas_call(functools.partial(closing_kernel, dp, 1), out_shape=(shape...  50.6 us
    dot_general x5, matrix products, product_lead(): lax.dot_general(left_side, right_side, (((0,), (0,)), ((), ())), preferre...  40.5 us
  transfers between devices with their start and end apart: 8, of which 1 were waited for; matrix products, arithmetic and copies ran while one was open for 16% of the time, Pallas kernels for 60%

profile of v6, /device:TPU:0, one launch (start us, length us, event | category | flops | bytes accessed | tf_op | source)
XLA Modules:
  0.0 825.4 jit_solution(16439596374234586748)
XLA Ops:
  14.5 88.3 %opening.1 = (bf16[16,128,2048]{2,1,0:T(8,128)(2,1)}, bf16[2,16,64,640]{3,2,1,0:T(8,128)(2,1)}, bf16[2,16,64,256]{3,2,1,0:T(8,128)(2,1)}, bf16[2,64,2048]{2,1,0:...) custom-call(bf16[128,2048]{1,0:T(8,128)(2,1)} %bitcast.140, ...), custom_call_target="tpu_custom_call" | custom-call | bytes 4000000 | tf_op jit(solution)/shard_map/opening/pallas_call | solution.py:444
  111.5 16.9 %project.1 = (bf16[2048,2048]{1,0:T(8,128)(2,1)}, bf16[2,1024,256]{2,1,0:T(8,128)(2,1)S(1)}, bf16[2,1024,256]{2,1,0:T(8,128)(2,1)S(1)}, bf16[2,1024,128]{2,1,0:T(8,128)(2,1)S(1)}, bf16[2,1024,512]{2,1,0:T(8,128)(2,1)}) custom-call(bf16[16,128,2048]{2,1,0:T(8,128)(2,1)} %get-tuple-element.74.x_ref, f32[1,2048]{1,0:T(1,128)S(1)} %bitcast.118, ...), custom_call_target="tpu_custom_call" | custom-call | flops 7000000000 | bytes 20000000 | tf_op jit(solution)/shard_map/project/pallas_call | solution.py:1246
  128.4 9.9 %attend.1 = (bf16[16,2,64,2048]{3,2,1,0:T(8,128)(2,1)}, bf16[16,2,64,128]{3,2,1,0:T(8,128)(2,1)S(1)}, f32[2,1024,1]{2,1,0:T(8,128)S(1)}) custom-call(s32[2]{0:T(128)S(1)} %bitcast.121, bf16[2,1024,256]{2,1,0:T(8,128)(2,1)S(1)} %get-tuple-element.77.q_ref, bf16[2,1024,256]{2,1,0:T(8,128)(2,1)S(1)} %get-tuple-element.78.k_ref, ...), custom_call_target="tpu_custom_call" | custom-call | flops 4000000000 | bytes 15000000 | tf_op jit(solution)/shard_map/attend/pallas_call | solution.py:1304
  139.3 52.6 %scatter16.2 = f32[128,2048]{1,0:T(8,128)} custom-call(bf16[16,128,2048]{2,1,0:T(8,128)(2,1)} %bitcast.137), custom_call_target="tpu_custom_call" | custom-call | bytes 4000000 | tf_op jit(solution)/shard_map/scatter16/pallas_call | solution.py:643
  198.1 72.5 %gather16.2 = (bf16[16,128,2048]{2,1,0:T(8,128)(2,1)}, bf16[2,416,2048]{2,1,0:T(8,128)(2,1)}) custom-call(bf16[128,2048]{1,0:T(8,128)(2,1)} %multiply_convert_fusion.x_ref, bf16[704,2048]{1,0:T(8,128)(2,1)} %bitcast.131), custom_call_target="tpu_custom_call" | custom-call | bytes 4000000 | tf_op jit(solution)/shard_map/gather16/pallas_call | solution.py:296
  272.1 88.0 %mixture_forward.1 = (bf16[2048,2048]{1,0:T(8,128)(2,1)}, bf16[1024,2048]{1,0:T(8,128)(2,1)}, bf16[1024,1408]{1,0:T(8,128)(2,1)}, bf16[1024,1408]{1,0:T(8,128)(2...) custom-call(s32[2]{0:T(128)} %bitcast.119, ...), custom_call_target="tpu_custom_call" | custom-call | bytes 4000000 | tf_op jit(solution)/shard_map/mixture_forward/pallas_call | solution.py:1145
  360.1 66.8 %mixture_backward.1 = (bf16[2048,2176]{1,0:T(8,128)(2,1)}, bf16[1024,2048]{1,0:T(8,128)(2,1)}, bf16[1024,1408]{1,0:T(8,128)(2,1)}, bf16[1024,1408]{1,0:T(8,128)(2,1)}, bf16[2,528,1024]{2,1,0:T(8,128)(2,1)}) custom-call(f32[1,256]{1,0:T(1,128)} %add_convert_fusion.2.pick_ref, bf16[2048,2048]{1,0:T(8,128)(2,1)} %bitcast.139, bf16[2048,2048]{1,0:T(8,128)(2,1)} %bitcast.126, ...), custom_call_target="tpu_custom_call" | custom-call | bytes 4000000 | tf_op jit(solution)/shard_map/mixture_backward/pallas_call | solution.py:1176
  427.0 10.6 %convolution_convert_fusion.2 = bf16[1408,2048]{1,0:T(8,128)(2,1)} fusion(bf16[1024,1408]{1,0:T(8,128)(2,1)} %get-tuple-element.95, bf16[1024,2048]{1,0:T(8,128)(2,1)} %get-tuple-element.96), kind=kOutput, calls=%fused_computation.2 | convolution fusion | flops 5908463616 | bytes 12845056 | tf_op jit(solution)/shard_map/dot_general | solution.py:1414
  437.6 11.0 %convolution_convert_fusion = bf16[2048,1408]{1,0:T(8,128)(2,1)} fusion(bf16[1024,2048]{1,0:T(8,128)(2,1)} %get-tuple-element.97, bf16[1024,1408]{1,0:T(8,128)(2,1)} %get-tuple-element.99), kind=kOutput, calls=%fused_computation | convolution fusion | flops 5908463616 | bytes 12845056 | tf_op jit(solution)/shard_map/dot_general | solution.py:1414
  448.6 11.0 %convolution_convert_fusion.1 = bf16[2048,1408]{1,0:T(8,128)(2,1)} fusion(bf16[1024,2048]{1,0:T(8,128)(2,1)} %get-tuple-element.97, bf16[1024,1408]{1,0:T(8,128)(2,1)} %get-tuple-element.98), kind=kOutput, calls=%fused_computation.1 | convolution fusion | flops 5908463616 | bytes 12845056 | tf_op jit(solution)/shard_map/dot_general | solution.py:1414
  466.9 3.0 multiply_reduce_fusion.6
  470.4 54.4 %scatter16.3 = f32[128,2176]{1,0:T(8,128)} custom-call(bf16[16,128,2176]{2,1,0:T(8,128)(2,1)} %bitcast.134), custom_call_target="tpu_custom_call" | custom-call | bytes 4000000 | tf_op jit(solution)/shard_map/scatter16/pallas_call | solution.py:643
  530.9 51.4 %gather16.3 = bf16[16,128,2048]{2,1,0:T(8,128)(2,1)} custom-call(bf16[128,2048]{1,0:T(8,128)(2,1)} %fusion.37.x_ref), custom_call_target="tpu_custom_call" | custom-call | bytes 4000000 | tf_op jit(solution)/shard_map/gather16/pallas_call | solution.py:296
  582.3 20.5 %attend_back.1 = (bf16[16,2,64,2688]{3,2,1,0:T(8,128)(2,1)}, bf16[16,2,64,256]{3,2,1,0:T(8,128)(2,1)}, f32[128,2048]{1,0:T(8,128)}, f32[512,256]{1,0:T(8,128)}) custom-call(s32[2]{0:T(128)} %bitcast.120, bf16[16,2,64,2048]{3,2,1,0:T(8,128)(2,1)} %bitcast.138, bf16[2,1024,256]{2,1,0:T(8,128)(2,1)} %copy-done.6, bf16[2,1024,256]{2,1,0:T(8,128)(2,1)} %copy-done.7, ...), custom_call_target="tpu_custom_call" | custom-call | flops 14000000000 | bytes 25000000 | tf_op jit(solution)/shard_map/attend_back/pallas_call | solution.py:1384
  602.8 6.0 fusion.39
  616.4 2.7 pad_maximum_fusion.1.parts_ref
  619.1 81.7 %returning.1 = (f32[128,2688]{1,0:T(8,128)}, bf16[2,16,64,256]{3,2,1,0:T(8,128)(2,1)}, bf16[2,64,2048]{2,1,0:T(8,128)(2,1)}, bf16[1,16,64,256]{3,2,1,0:T(8,128)(2,1)}, bf16[1,64,2048]{2,1,0:T(8,128)(2,1)}) custom-call(bf16[16,128,2688]{2,1,0:T(8,128)(2,1)} %bitcast.133, bf16[2,16,64,256]{3,2,1,0:T(8,128)(2,1)} %pad_maximum_fusion.1.parts_ref, ...), custom_call_target="tpu_custom_call" | custom-call | bytes 4000000 | tf_op jit(solution)/shard_map/returning/pallas_call | solution.py:757
  720.5 4.5 fusion.16
  727.2 50.6 %closing.1 = (bf16[128,640]{1,0:T(8,128)(2,1)S(1)}, bf16[1,64,640]{2,1,0:T(8,128)(2,1)S(1)}) custom-call(bf16[16,128,640]{2,1,0:T(8,128)(2,1)S(1)} %bitcast.114), custom_call_target="tpu_custom_call" | custom-call | bytes 4000000 | tf_op jit(solution)/shard_map/closing/pallas_call | solution.py:809
  784.8 5.2 bitcast_convert_fusion
  790.0 4.7 bitcast_convert_fusion.1
  794.8 4.7 bitcast_convert_fusion.2
  799.5 15.5 %reduce-scatter.6.cloned.1.call-done = bf16[128,2048]{1,0:T(8,128)(2,1)} async-done(((bf16[2048,2048]{1,0:T(8,128)(2,1)}), bf16[128,2048]{1,0:T(8,128)(2,1)}) %reduce-scatter.6.cloned.1.call-update) | async-done | bytes 524304 | tf_op jit(solution)/shard_map/reduce_scatter | solution.py:1577
  815.0 3.4 fusion.15
  (201 shorter events, 74.5 us)
Async XLA Ops:
  7.2 264.9 %all-gather.11.cloned.1.call-start = ((), (), s32[]{:S(2)}) async-start(), calls=%async_computation.12 | async-start | bytes 3244032 | tf_op jit(solution)/shard_map/all_gather | solution.py:1539
  9.5 262.5 %all-gather.7.cloned.1.call-start = ((), (), s32[]{:S(2)}) async-start(), calls=%async_computation.10 | async-start | bytes 8650752 | tf_op jit(solution)/shard_map/all_gather | solution.py:1537
  10.4 261.7 %all-gather.9.cloned.1.call-start = ((), (), s32[]{:S(2)}) async-start(), calls=%async_computation.11 | async-start | bytes 8650752 | tf_op jit(solution)/shard_map/all_gather | solution.py:1538
  11.1 770.8 %reduce-scatter.14.cloned.1.call-start = ((), (), s32[]{:S(2)}) async-start(), calls=%async_computation.9 | async-start | bytes 3244032 | tf_op jit(solution)/shard_map/reduce_scatter | solution.py:1591
  14.5 95.7 %copy-start.4 = (f32[2048,32]{1,0:T(8,128)S(1)}, f32[2048,32]{1,0:T(8,128)}, u32[]{:S(2)}) copy-start(f32[2048,32]{1,0:T(8,128)} %constant.97.clone.cos_ref) | copy-start | bytes 786436
  108.1 20.2 %copy-start = (bf16[512,256]{1,0:T(8,128)(2,1)}, bf16[512,256]{1,0:T(8,128)(2,1)S(1)}, u32[]{:S(2)}) copy-start(bf16[512,256]{1,0:T(8,128)(2,1)S(1)} %reshape.340.we_ref) | copy-start | bytes 786436
  111.5 16.9 %copy-start.2 = (s32[2,1]{0,1:T(1,128)S(1)}, s32[2,1]{0,1:T(1,128)}, u32[]{:S(2)}) copy-start(s32[2,1]{0,1:T(1,128)} %param.26) | copy-start | bytes 28
  111.5 16.9 %copy-start.3 = (bf16[2,64,2048]{2,1,0:T(8,128)(2,1)S(1)}, bf16[2,64,2048]{2,1,0:T(8,128)(2,1)}, u32[]{:S(2)}) copy-start(bf16[2,64,2048]{2,1,0:T(8,128)(2,1)} %get-tuple-element.80) | copy-start | bytes 1572868
  139.3 52.6 %copy-start.10 = (bf16[16,2,64,128]{3,2,1,0:T(8,128)(2,1)}, bf16[16,2,64,128]{3,2,1,0:T(8,128)(2,1)S(1)}, u32[]{:S(2)}) copy-start(bf16[16,2,64,128]{3,2,1,0:T(8,128)(2,1)S(1)} %get-tuple-element.102.att_ref) | copy-start | bytes 1572868
  139.3 52.6 %copy-start.11 = (bf16[2,1,64,2048]{3,2,1,0:T(8,128)(2,1)S(1)}, bf16[2,1,64,2048]{3,2,1,0:T(8,128)(2,1)}, u32[]{:S(2)}) copy-start(bf16[2,1,64,2048]{3,2,1,0:T(8,128)(2,1)} %param.24) | copy-start | bytes 1572868
  195.1 330.9 %copy-start.29 = (f32[128]{0:T(128)}, f32[128]{0:T(128)S(1)}, u32[]{:S(2)}) copy-start(f32[128]{0:T(128)S(1)} %reshape.361) | copy-start | bytes 1540
  195.2 334.6 %copy-start.31 = (bf16[128]{0:T(256)(128)(2,1)}, bf16[128]{0:T(256)(128)(2,1)S(1)}, u32[]{:S(2)}) copy-start(bf16[128]{0:T(256)(128)(2,1)S(1)} %convert_element_type.176) | copy-start | bytes 772
  197.1 74.0 %copy-start.12 = (bf16[2,1,64,2048]{3,2,1,0:T(8,128)(2,1)S(1)}, bf16[2,1,64,2048]{3,2,1,0:T(8,128)(2,1)}, u32[]{:S(2)}) copy-start(bf16[2,1,64,2048]{3,2,1,0:T(8,128)(2,1)} %param.25) | copy-start | bytes 1572868
  197.1 332.6 %copy-start.27 = (f32[128]{0:T(128)}, f32[128]{0:T(128)S(1)}, u32[]{:S(2)}) copy-start(f32[128]{0:T(128)S(1)} %add_rsqrt_fusion.2) | copy-start | bytes 1540
  427.0 357.8 %reduce-scatter.12.cloned.1.call-start = ((), (), s32[]{:S(2)}) async-start(), calls=%async_computation.8 | async-start | bytes 8650752 | tf_op jit(solution)/shard_map/reduce_scatter | solution.py:1588
  459.6 330.4 %reduce-scatter.10.cloned.1.call-start = ((), (), s32[]{:S(2)}) async-start(), calls=%async_computation.7 | async-start | bytes 8650752 | tf_op jit(solution)/shard_map/reduce_scatter | solution.py:1590
  460.2 334.6 %reduce-scatter.8.cloned.1.call-start = ((), (), s32[]{:S(2)}) async-start(), calls=%async_computation.6 | async-start | bytes 8650752 | tf_op jit(solution)/shard_map/reduce_scatter | solution.py:1589
  461.0 354.0 %reduce-scatter.6.cloned.1.call-start = ((), (), s32[]{:S(2)}) async-start(), calls=%async_computation.5 | async-start | bytes 8912896 | tf_op jit(solution)/shard_map/reduce_scatter | solution.py:1577
  529.7 52.6 %copy-start.36 = (f32[128]{0:T(128)}, f32[128]{0:T(128)S(1)}, u32[]{:S(2)}) copy-start(f32[128]{0:T(128)S(1)} %broadcast_multiply_fusion.2) | copy-start | bytes 1540
  794.7 20.3 %copy-start.28 = (f32[128]{0:T(128)S(1)}, f32[128]{0:T(128)}, u32[]{:S(2)}) copy-start(f32[128]{0:T(128)} %copy-done.27) | copy-start | bytes 1540
  794.7 20.3 %copy-start.30 = (f32[128]{0:T(128)S(1)}, f32[128]{0:T(128)}, u32[]{:S(2)}) copy-start(f32[128]{0:T(128)} %copy-done.29) | copy-start | bytes 1540
  794.7 20.3 %copy-start.32 = (bf16[128]{0:T(256)(128)(2,1)S(1)}, bf16[128]{0:T(256)(128)(2,1)}, u32[]{:S(2)}) copy-start(bf16[128]{0:T(256)(128)(2,1)} %copy-done.31) | copy-start | bytes 772
  794.7 20.3 %copy-start.35 = (f32[128]{0:T(128)S(1)}, f32[128]{0:T(128)}, u32[]{:S(2)}) copy-start(f32[128]{0:T(128)} %copy-done.34) | copy-start | bytes 1540
  794.7 20.3 %copy-start.37 = (f32[128]{0:T(128)S(1)}, f32[128]{0:T(128)}, u32[]{:S(2)}) copy-start(f32[128]{0:T(128)} %copy-done.36) | copy-start | bytes 1540
  (28 other events, 125.2 us)
Sparse Core Ops, SparseCore 0:
  10.1 55.0 all-gather.10
  66.8 71.1 all-gather.6
  139.6 87.0 all-gather.8
  427.1 30.6 reduce-scatter.13
  460.6 71.3 reduce-scatter.11
  534.8 71.3 reduce-scatter.9
  609.1 88.2 reduce-scatter.7
  701.4 113.4 reduce-scatter.5

commit v7 on v6

--- a/solution.py
+++ b/solution.py
@@ -50,9 +50,6 @@
         dma = pltpu.SemaphoreType.DMA
         return [dma, dma((dp,)), dma((dp,))]
 
-    def out_shape(dp, rows, v):
-        return jax.ShapeDtypeStruct((dp, rows, v.shape[1]), v.dtype)
-
     def copy(self, r):
         return pltpu.make_async_remote_copy(
             src_ref=self.src, dst_ref=self.out.at[self.plane], send_sem=self.send.at[r], recv_sem=self.recv.at[r],
@@ -77,40 +74,8 @@
             self.copy(r).wait_send()
 
 
-class Swap:
-    def __init__(self, dp, src, out, sems):
-        self.dp, self.src, self.out = dp, src, out
-        self.send, self.recv = sems
-        self.plane = lax.axis_index("dp")
-
-    @staticmethod
-    def scratch(dp):
-        dma = pltpu.SemaphoreType.DMA
-        return [dma((dp,)), dma((dp,))]
-
-    def out_shape(dp, rows, v):
-        return jax.ShapeDtypeStruct((dp - 1, rows, v.shape[2]), v.dtype)
-
-    def copy(self, r):
-        to = (self.plane + r) % self.dp
-        return pltpu.make_async_remote_copy(
-            src_ref=self.src.at[to], dst_ref=self.out.at[r - 1], send_sem=self.send.at[r], recv_sem=self.recv.at[r],
-            device_id={"dp": to}, device_id_type=MESH)
-
-    def start(self):
-        for r in range(1, self.dp):
-            self.copy(r).start()
-
-    def finish(self):
-        for r in range(1, self.dp):
-            self.copy(r).wait_recv()
-            self.copy(r).wait_send()
-
-
-def side_job(kind, dp, span, src, out, sems):
-    first, rows = span
-    part = pl.ds(first, rows)
-    return kind(dp, src.at[part] if kind is Spread else src.at[:, part], out, sems)
+def side_job(dp, span, src, out, sems):
+    return Spread(dp, src.at[pl.ds(span[0], span[1])], out, sems)
 
 
 def enter_all(me, plane, dp):
@@ -128,13 +93,22 @@
     def __init__(self, src, out, chunks, sems, view=lambda ref, b: ref.at[b]):
         self.src, self.out, self.chunks, self.view = src, out, chunks, view
         self.rows = src.shape[0] // chunks
-        self.own_sem, self.us, self.ur, self.ds, self.dr, self.xs, self.xr, self.cs, self.cr = sems
+        (self.own_sem, self.us, self.ur, self.ds, self.dr, self.bus, self.bur, self.bds, self.bdr,
+         self.xs, self.xr, self.cs, self.cr) = sems
         self.me, self.z, self.x, self.c, self.core, self.side = place()
+
+    COUNT = 13
 
     @staticmethod
     def scratch(chunks):
         dma = pltpu.SemaphoreType.DMA
-        return [dma] + [dma((4, chunks))] * 4 + [dma((7, chunks))] * 2 + [dma((14, chunks))] * 2
+        return [dma] + [dma((4, chunks))] * 8 + [dma((7, chunks))] * 2 + [dma((14, chunks))] * 2
+
+    def alt(self, k):
+        return k >= (self.chunks + 1) // 2
+
+    def order(self):
+        return range(self.chunks - 1, -1, -1)
 
     def copy(self, block, k, src, send, recv, to):
         src_ref = self.src if src is None else self.view(self.out, src)
@@ -155,19 +129,22 @@
     def down(self, k, s, src=None):
         return self.copy(self.me + 4 * s, k, src, self.ds.at[s, k], self.dr.at[s, k], self.me - 4)
 
+    def up_b(self, k, s):
+        b = self.side - 4 * s
+        return self.copy(b, k, b, self.bus.at[s, k], self.bur.at[s, k], self.me + 4)
+
+    def down_b(self, k, s):
+        b = self.side + 4 * s
+        return self.copy(b, k, b, self.bds.at[s, k], self.bdr.at[s, k], self.me - 4)
+
     def across(self, k, slot, block, src=None):
         return self.copy(block, k, src, self.xs.at[slot, k], self.xr.at[slot, k], self.side)
 
     def over(self, k, slot, block, src=None):
         return self.copy(block, k, src, self.cs.at[slot, k], self.cr.at[slot, k], self.core)
 
-    def up_in(self, k, s):
-        b = self.me - 4 * s
-        return self.copy(b, k, b, self.us.at[s - 1, k], self.ur.at[s - 1, k], self.side)
-
-    def dn_in(self, k, s):
-        b = self.me + 4 * s
-        return self.copy(b, k, b, self.ds.at[s - 1, k], self.dr.at[s - 1, k], self.side)
+    def arrived(self, b, k, sems, s):
+        return self.copy(b, k, b, sems[0].at[s - 1, k], sems[1].at[s - 1, k], self.side)
 
     def shift(self, base, slot):
         return base - 4 * slot if slot <= 3 else base + 4 * (slot - 3)
@@ -183,11 +160,16 @@
             return self.z >= 0
         return self.z >= slot if slot <= 3 else self.z + (slot - 3) <= NZ - 1
 
+    def crosses(self, k, slot):
+        if slot == 0 or not self.alt(k):
+            return self.has(slot)
+        return self.z > slot if slot <= 3 else self.z + (slot - 3) < NZ - 1
+
     def start(self):
         z, me = self.z, self.me
         self.own = pltpu.make_async_copy(self.src, self.view(self.out, me), self.own_sem)
         self.own.start()
-        for k in range(self.chunks):
+        for k in self.order():
             self.across(k, 0, me).start()
 
             @pl.when(z < NZ - 1)
@@ -206,8 +188,11 @@
         @pl.when(z >= s)
         def _():
             b = me - 4 * s
-            self.up_in(k, s).wait_recv()
-            self.across(k, s, b, b).start()
+            self.arrived(b, k, (self.us, self.ur), s).wait_recv()
+
+            @pl.when(self.crosses(k, s))
+            def _():
+                self.across(k, s, b, b).start()
 
             @pl.when(z < NZ - 1)
             def _():
@@ -218,8 +203,11 @@
         @pl.when(z + s <= NZ - 1)
         def _():
             b = me + 4 * s
-            self.dn_in(k, s).wait_recv()
-            self.across(k, 3 + s, b, b).start()
+            self.arrived(b, k, (self.ds, self.dr), s).wait_recv()
+
+            @pl.when(self.crosses(k, 3 + s))
+            def _():
+                self.across(k, 3 + s, b, b).start()
 
             @pl.when(z > 0)
             def _():
@@ -227,25 +215,63 @@
 
             self.over(k, 3 + s, b, b).start()
 
+    def line_b(self, k, s):
+        z = self.z
+
+        @pl.when(z == s)
+        def _():
+            b = self.side - 4 * s
+            self.arrived(b, k, (self.bus, self.bur), s).wait_recv()
+
+            @pl.when(z < NZ - 1)
+            def _():
+                self.up_b(k, s).start()
+
+            self.over(k, 7 + s, b, b).start()
+
+        @pl.when(z + s == NZ - 1)
+        def _():
+            b = self.side + 4 * s
+            self.arrived(b, k, (self.bds, self.bdr), s).wait_recv()
+
+            @pl.when(z > 0)
+            def _():
+                self.down_b(k, s).start()
+
+            self.over(k, 10 + s, b, b).start()
+
     def from_side(self, k, slot):
-        @pl.when(self.has(slot))
+        @pl.when(self.crosses(k, slot))
         def _():
             b = self.shift(self.side, slot)
             self.across(k, slot, b, b).wait_recv()
+            if slot == 0 and self.alt(k):
+                @pl.when(self.z == 0)
+                def _():
+                    self.up_b(k, 0).start()
+
+                @pl.when(self.z == NZ - 1)
+                def _():
+                    self.down_b(k, 0).start()
+
             self.over(k, 7 + slot, b, b).start()
 
     def round(self, s):
         if s < NZ:
-            for k in range(self.chunks):
+            for k in self.order():
                 self.line(k, s)
-        for k in range(self.chunks):
+        for k in self.order():
             for slot in ((0,) if s == 1 else (s - 1, s + 2)):
                 self.from_side(k, slot)
+        if s > 1:
+            for k in self.order():
+                if self.alt(k):
+                    self.line_b(k, s - 1)
 
     def finish(self):
         z = self.z
         self.own.wait()
-        for k in range(self.chunks):
+        for k in self.order():
             for slot in range(14):
                 @pl.when(self.has(slot))
                 def _():
@@ -253,7 +279,7 @@
                     self.over(k, slot, b, b).wait_recv()
                     self.over(k, slot, b, b).wait_send()
             for slot in range(7):
-                @pl.when(self.has(slot))
+                @pl.when(self.crosses(k, slot))
                 def _():
                     self.across(k, slot, self.me).wait_send()
             for s in range(NZ - 1):
@@ -265,15 +291,24 @@
                 def _():
                     self.down(k, s).wait_send()
 
-
-def gather_kernel(chunks, dp, kind, span, x_ref, *refs):
+                if self.alt(k):
+                    @pl.when(z == s)
+                    def _():
+                        self.up_b(k, s).wait_send()
+
+                    @pl.when(z + s == NZ - 1)
+                    def _():
+                        self.down_b(k, s).wait_send()
+
+
+def gather_kernel(chunks, dp, span, x_ref, *refs):
     job = None
-    ng = 9
-    if kind is None:
+    ng = Gather.COUNT
+    if span is None:
         o_ref, *sems = refs
     else:
         src, o_ref, out, *sems = refs
-        job = side_job(kind, dp, span, src, out, sems[ng:])
+        job = side_job(dp, span, src, out, sems[ng:])
     g = Gather(x_ref, o_ref, chunks, sems[:ng])
     enter(g.me, g.z, g.core, g.side, 1 if job is None else dp)
     g.start()
@@ -290,16 +325,16 @@
 ANY = pl.BlockSpec(memory_space=pl.ANY)
 
 
-def gather16(v, cid, chunks=4, dp=1, kind=None, span=None, side=None):
+def gather16(v, cid, chunks=2, dp=1, span=None, side=None):
     rows, width = v.shape
-    extra = kind is not None
+    extra = span is not None
     out = pl.pallas_call(
-        functools.partial(gather_kernel, chunks, dp, kind, span),
+        functools.partial(gather_kernel, chunks, dp, span),
         out_shape=(jax.ShapeDtypeStruct((NE, rows, width), v.dtype),)
-        + ((kind.out_shape(dp, span[1], side),) if extra else ()),
+        + ((jax.ShapeDtypeStruct((dp, span[1], side.shape[1]), side.dtype),) if extra else ()),
         in_specs=[ANY] * (2 if extra else 1),
         out_specs=(ANY,) * (2 if extra else 1),
-        scratch_shapes=Gather.scratch(chunks) + (kind.scratch(dp) if extra else []),
+        scratch_shapes=Gather.scratch(chunks) + (Spread.scratch(dp) if extra else []),
         compiler_params=pltpu.CompilerParams(collective_id=cid, has_side_effects=True),
         cost_estimate=COST,
         name="gather16",
@@ -309,7 +344,7 @@
 
 def opening_kernel(dp, chunks, x_ref, small_ref, parts_ref, out_ref,
                    x_all, small_all, parts_head, out_head, small_dp, parts_dp, out_dp, *sems):
-    ng = 9
+    ng = Gather.COUNT
     gx = Gather(x_ref, x_all, chunks, sems[:ng])
     gs = Gather(small_dp, small_all, 1, sems[ng:2 * ng], lambda ref, b: ref.at[:, b])
     loc, ys, yr, ps, pr, os_, or_, pl_sem, ol_sem = sems[2 * ng:]
@@ -435,7 +470,7 @@
     gs.finish()
 
 
-def opening(dp, x, small, parts, out, cid, chunks=4):
+def opening(dp, x, small, parts, out, cid, chunks=2):
     dma = pltpu.SemaphoreType.DMA
     rows, ws = small.shape
     bf = x.dtype
@@ -465,6 +500,8 @@
 
 
 class Scatter:
+    COUNT = 14
+
     def __init__(self, p_ref, o_ref, chunks, scratch):
         self.p, self.o, self.chunks = p_ref, o_ref, chunks
         (self.cbuf, self.own, self.xbuf, self.ubuf, self.dbuf, self.ld, self.cs, self.cr, self.xs, self.xr,
@@ -589,12 +626,14 @@
                 def _():
                     o[s] = (base() + self.ubuf[t, s].astype(f32)).astype(o.dtype)
 
-    def run(self):
+    def run(self, between=lambda: None):
         self.first(0)
         for i in range(NZ):
             if i + 1 < NZ:
                 self.first(i + 1)
+            between()
             self.second(i)
+            between()
 
     def finish(self):
         z = self.z
@@ -615,48 +654,34 @@
                         self.down(t, i, k).wait_send()
 
 
-def scatter_kernel(chunks, dp, kind, span, p_ref, *refs):
-    job = None
-    ns = 14
-    if kind is None:
-        o_ref, *scratch = refs
-    else:
-        src, o_ref, out, *scratch = refs
-        job = side_job(kind, dp, span, src, out, scratch[ns:])
-    s = Scatter(p_ref, o_ref, chunks, scratch[:ns])
-    enter(s.me, s.z, s.core, s.side, 1 if job is None else dp)
+def scatter_kernel(chunks, p_ref, o_ref, *scratch):
+    s = Scatter(p_ref, o_ref, chunks, scratch)
+    enter(s.me, s.z, s.core, s.side)
     s.start()
-    if job is not None:
-        job.start()
     s.run()
     s.finish()
-    if job is not None:
-        job.finish()
 
 
 VMEM = pl.BlockSpec(memory_space=pltpu.VMEM)
 
 
-def scatter16(p, cid, chunks=2, out_dtype=jnp.float32, dp=1, kind=None, span=None, side=None):
+def scatter16(p, cid, chunks=2):
     _, rows, width = p.shape
-    extra = kind is not None
-    out = pl.pallas_call(
-        functools.partial(scatter_kernel, chunks, dp, kind, span),
-        out_shape=(jax.ShapeDtypeStruct((rows, width), out_dtype),)
-        + ((kind.out_shape(dp, span[1], side),) if extra else ()),
-        in_specs=[ANY] * (2 if extra else 1),
-        out_specs=(VMEM,) + ((ANY,) if extra else ()),
-        scratch_shapes=Scatter.scratch(rows, width, chunks, p.dtype) + (kind.scratch(dp) if extra else []),
+    return pl.pallas_call(
+        functools.partial(scatter_kernel, chunks),
+        out_shape=jax.ShapeDtypeStruct((rows, width), jnp.float32),
+        in_specs=[ANY],
+        out_specs=VMEM,
+        scratch_shapes=Scatter.scratch(rows, width, chunks, p.dtype),
         compiler_params=pltpu.CompilerParams(
             collective_id=cid, has_side_effects=True, vmem_limit_bytes=60 * 1024 * 1024),
         cost_estimate=COST,
         name="scatter16",
-    )(*((p, side) if extra else (p,)))
-    return out if extra else out[0]
+    )(p)
 
 
 def return_kernel(dp, chunks, p_ref, parts_ref, rows_ref, o_ref, parts_in, rows_in, parts_far, rows_far, *scratch):
-    ns = 14
+    ns = Scatter.COUNT
     s = Scatter(p_ref, o_ref, chunks, scratch[:ns])
     ps, pr, os_, or_, pl_sem, ol_sem, ys, yr = scratch[ns:]
     me = s.me
@@ -778,7 +803,7 @@
 
 
 def closing_kernel(dp, chunks, p_ref, o_ref, far_ref, *scratch):
-    ns = 14
+    ns = Scatter.COUNT
     s = Scatter(p_ref, o_ref, chunks, scratch[:ns])
     ys, yr = scratch[ns:]
     plane = lax.axis_index("dp")
@@ -942,8 +967,8 @@
     half = groups * slots
     ff = hid_ref.shape[1]
     phase = pl.num_programs(0) // 2
-    g = Gather(dy_ref, dy_all, chunks, sems[:9])
-    job = side_job(Spread, dp, span, down_ref, wdb_ref, sems[9:])
+    g = Gather(dy_ref, dy_all, chunks, sems[:Gather.COUNT])
+    job = side_job(dp, span, down_ref, wdb_ref, sems[Gather.COUNT:])
 
     @pl.when(step == 0)
     def _():
@@ -1042,44 +1067,48 @@
         g.finish()
 
 
-def backward_kernel(here, pick_ref, dy_ref, mix_ref, sh_ref, wg_ref, wu_ref, share_ref, wda_ref, wdb_ref,
-                    act_ref, slo_ref, eo_ref, sact_ref, sslo_ref, gate_ref,
-                    dh_ref, deo_ref, dg_ref, du_ref, gshare_ref,
-                    wd_ref, fan_ref, sd_ref, gfan, gsd, wd_sem, sh_sem):
+def backward_kernel(here, chunks, pick_ref, dy_ref, wg_ref, wu_ref, share_ref, wda_ref, wdb_ref,
+                    act_ref, slo_ref, eo_ref, sact_ref, sslo_ref, gate_ref, part_ref,
+                    dh_ref, deo_ref, dg_ref, du_ref, ds_ref, sum_ref,
+                    wd_ref, fan_ref, sd_ref, wd_sem, sh_sem, *scratch):
     step = pl.program_id(0)
     tokens, width = dy_ref.shape
     groups, slots = tokens // 256, 128
     ff = dg_ref.shape[1]
+    sc = Scatter(part_ref, sum_ref, chunks, scratch)
 
     @pl.when(step == 0)
     def _():
+        enter(sc.me, sc.z, sc.core, sc.side)
         copies = share_copies(share_ref, fan_ref, sd_ref, sh_sem)
         for which in range(2):
             copies += down_copies(wda_ref, wdb_ref, wd_ref, wd_sem, which)
         for copy in copies:
             copy.start()
+        sc.start()
         share_blank(fan_ref, sd_ref)
-        gfan[...] = jnp.zeros_like(gfan)
-        gsd[...] = jnp.zeros_like(gsd)
         for copy in copies:
             copy.wait()
 
     d_sh = mm_t(dy_ref[...], sd_ref[...])
     d_s = jnp.concatenate([(d_sh * sslo_ref[...].astype(F32)).astype(BF),
                            (d_sh * sact_ref[...].astype(F32)).astype(BF)], axis=1)
+    ds_ref[...] = d_s
     gate, taken = gate_ref[:, :1], gate_ref[:, 1:]
     to_slot, to_token = one_hots(taken, groups, slots, here)
 
+    @pl.when(step == 0)
+    def _():
+        sc.first(0)
+        sc.first(1)
+
     def dispatch(j, total):
-        low = dy_ref[:, lanes(j)]
-        dy = low.astype(F32)
+        dy = dy_ref[:, lanes(j)].astype(F32)
         gated = (gate * dy).astype(BF)
         for n in range(groups):
             deo_ref[n * slots:(n + 1) * slots, lanes(j)] = mm(to_slot[n], gated[n * 256:(n + 1) * 256]).astype(BF)
         picked = jnp.concatenate(
             [mm(to_token[n], eo_ref[n * slots:(n + 1) * slots, lanes(j)]) for n in range(groups)], axis=0)
-        gfan[:, lanes(j)] += mm_lead(d_s, mix_ref[:, lanes(j)])
-        gsd[:, lanes(j)] += mm_lead(sh_ref[...], low)
         return total + jnp.sum(dy * picked, axis=1, keepdims=True)
 
     d_gates = lax.fori_loop(0, width // WIDE, dispatch, jnp.zeros((tokens, 1), F32))
@@ -1091,6 +1120,11 @@
         du_ref[:, cols] = (d_eh * act_ref[:, cols].astype(F32)).astype(BF)
 
     over_columns(ff, back_out)
+
+    @pl.when(step == 0)
+    def _():
+        sc.first(2)
+        sc.first(3)
 
     def back_in(j, _):
         d_rows = (mm_t(dg_ref[...], wg_ref[lanes(j), :]) + mm_t(du_ref[...], wu_ref[lanes(j), :])).astype(BF)
@@ -1104,15 +1138,20 @@
     high = d_gates.astype(BF).astype(F32)
     dh_ref[:, width:] = (high * pick_ref[:, :128] + (d_gates - high) * pick_ref[:, 128:]).astype(BF)
 
-    @pl.when(step == pl.num_programs(0) - 1)
+    outer = (sc.z == 0) | (sc.z == NZ - 1)
+    for i in range(NZ - 1):
+        @pl.when((step == i) & outer)
+        def _():
+            sc.second(i)
+
+        @pl.when((step == min(i + 1, 2)) & jnp.logical_not(outer))
+        def _():
+            sc.second(i)
+
+    @pl.when(step == NZ - 1)
     def _():
-        dp, rows, w = share_ref.shape
-        n = rows // 3
-        for d in range(dp):
-            cols = slice(d * w, (d + 1) * w)
-            gshare_ref[d, :n] = gfan[:n, cols].astype(BF)
-            gshare_ref[d, n:2 * n] = gfan[TILE:TILE + n, cols].astype(BF)
-            gshare_ref[d, 2 * n:] = gsd[:n, cols].astype(BF)
+        sc.second(NZ - 1)
+        sc.finish()
 
 
 def whole(v):
@@ -1165,33 +1204,119 @@
     )(lengths, pick, mix, routes, wg, wu, router, share, wda, down, dy)
 
 
-def mixture_backward(here, pick, dy, mix, sh, wg, wu, share, wda, wdb, act, slo, eo, sact, sslo, gate):
+def mixture_backward(here, pick, dy, wg, wu, share, wda, wdb, act, slo, eo, sact, sslo, gate, part, cid, chunks=2):
     total, width = dy.shape
-    step, half = total // 4, total // 8
+    step, half = total // NZ, total // NZ // 2
     ff = wg.shape[1]
     shape = jax.ShapeDtypeStruct
     rows = total // 2
     dp = wda.shape[0]
+    _, own, _ = part.shape
     dma = pltpu.SemaphoreType.DMA
     return pl.pallas_call(
-        functools.partial(backward_kernel, here),
-        grid=(4,),
+        functools.partial(backward_kernel, here, chunks),
+        grid=(NZ,),
         out_shape=(
             shape((total, width + 128), BF), shape((rows, width), BF), shape((rows, ff), BF), shape((rows, ff), BF),
-            shape(share.shape, BF)),
-        in_specs=[whole(pick), tiles(step, width), tiles(step, width), tiles(step, TILE), whole(wg), whole(wu),
-                  ANY, ANY, ANY,
+            shape((total, 2 * TILE), BF), shape((own, width), F32)),
+        in_specs=[whole(pick), tiles(step, width), whole(wg), whole(wu), ANY, ANY, ANY,
                   tiles(half, ff), tiles(half, ff), tiles(half, width), tiles(step, TILE), tiles(step, TILE),
-                  tiles(step, 2)],
+                  tiles(step, 2), ANY],
         out_specs=[tiles(step, width + 128), tiles(half, width), tiles(half, ff), tiles(half, ff),
-                   pl.BlockSpec(share.shape, lambda i: (0, 0, 0))],
+                   tiles(step, 2 * TILE), pl.BlockSpec((own, width), lambda i: (0, 0))],
         scratch_shapes=[
             pltpu.VMEM((ff, width), BF), pltpu.VMEM((2 * TILE, width), BF), pltpu.VMEM((TILE, width), BF),
-            pltpu.VMEM((2 * TILE, width), F32), pltpu.VMEM((TILE, width), F32), dma((2 * dp,)), dma((3 * dp,))],
-        compiler_params=pltpu.CompilerParams(vmem_limit_bytes=60 * 1024 * 1024),
+            dma((2 * dp,)), dma((3 * dp,))] + Scatter.scratch(own, width, chunks, BF),
+        compiler_params=pltpu.CompilerParams(
+            collective_id=cid, has_side_effects=True, vmem_limit_bytes=62 * 1024 * 1024),
         cost_estimate=COST,
         name="mixture_backward",
-    )(pick, dy, mix, sh, wg, wu, share, wda, wdb, act, slo, eo, sact, sslo, gate)
+    )(pick, dy, wg, wu, share, wda, wdb, act, slo, eo, sact, sslo, gate, part)
+
+
+class ShareWork:
+    ROWS = 256
+
+    def __init__(self, ds_ref, sh_ref, mix_ref, dy_ref, out_ref, scratch):
+        self.sources = (ds_ref, sh_ref, mix_ref, dy_ref)
+        self.out = out_ref
+        *self.buffers, self.gfan, self.gsd, self.sem = scratch
+        self.steps = mix_ref.shape[0] // self.ROWS
+        self.done = 0
+
+    @staticmethod
+    def scratch(width):
+        r = ShareWork.ROWS
+        return [pltpu.VMEM((2, r, w), BF) for w in (2 * TILE, TILE, width, width)] + [
+            pltpu.VMEM((2 * TILE, width), F32), pltpu.VMEM((TILE, width), F32), pltpu.SemaphoreType.DMA((2, 4))]
+
+    COUNT = 7
+
+    def copies(self, n):
+        return [pltpu.make_async_copy(src.at[pl.ds(n * self.ROWS, self.ROWS)], buf.at[n % 2], self.sem.at[n % 2, i])
+                for i, (src, buf) in enumerate(zip(self.sources, self.buffers))]
+
+    def start(self):
+        for copy in self.copies(0):
+            copy.start()
+        self.gfan[...] = jnp.zeros_like(self.gfan)
+        self.gsd[...] = jnp.zeros_like(self.gsd)
+
+    def step(self):
+        n = self.done
+        if n == self.steps:
+            return
+        self.done += 1
+        for copy in self.copies(n):
+            copy.wait()
+        if n + 1 < self.steps:
+            for copy in self.copies(n + 1):
+                copy.start()
+        ds, sh, mix, dy = self.buffers
+
+        def columns(j, _):
+            self.gfan[:, lanes(j)] += mm_lead(ds[n % 2], mix[n % 2, :, lanes(j)])
+            self.gsd[:, lanes(j)] += mm_lead(sh[n % 2], dy[n % 2, :, lanes(j)])
+            return 0
+
+        lax.fori_loop(0, mix.shape[2] // WIDE, columns, 0)
+
+    def finish(self):
+        while self.done < self.steps:
+            self.step()
+        dp, rows, w = self.out.shape
+        n = rows // 3
+        for d in range(dp):
+            cols = slice(d * w, (d + 1) * w)
+            self.out[d, :n] = self.gfan[:n, cols].astype(BF)
+            self.out[d, n:2 * n] = self.gfan[TILE:TILE + n, cols].astype(BF)
+            self.out[d, 2 * n:] = self.gsd[:n, cols].astype(BF)
+
+
+def scatter_share_kernel(chunks, p_ref, ds_ref, sh_ref, mix_ref, dy_ref, o_ref, g_ref, *scratch):
+    s = Scatter(p_ref, o_ref, chunks, scratch[:Scatter.COUNT])
+    work = ShareWork(ds_ref, sh_ref, mix_ref, dy_ref, g_ref, scratch[Scatter.COUNT:])
+    enter(s.me, s.z, s.core, s.side)
+    s.start()
+    work.start()
+    s.run(work.step)
+    work.finish()
+    s.finish()
+
+
+def scatter_share(p, ds, sh, mix, dy, share_shape, cid, chunks=2):
+    _, rows, width = p.shape
+    return pl.pallas_call(
+        functools.partial(scatter_share_kernel, chunks),
+        out_shape=(jax.ShapeDtypeStruct((rows, width), F32), jax.ShapeDtypeStruct(share_shape, BF)),
+        in_specs=[ANY] * 5,
+        out_specs=(VMEM, VMEM),
+        scratch_shapes=Scatter.scratch(rows, width, chunks, p.dtype) + ShareWork.scratch(mix.shape[1]),
+        compiler_params=pltpu.CompilerParams(
+            collective_id=cid, has_side_effects=True, vmem_limit_bytes=60 * 1024 * 1024),
+        cost_estimate=COST,
+        name="scatter_share",
+    )(p, ds, sh, mix, dy)
 
 
 def turn(v, cosine, sine):
@@ -1556,7 +1681,7 @@
     attn_part, attended, log_total = attend(seq_lengths, query, key, values, output_head, GROUPS)
     attn_part = attn_part.reshape(GROUPS, own, width)
     down_own = down_weight[0]
-    cut = down_own.shape[0] * 3 // 80 * 16
+    cut = down_own.shape[0] * 9 // 320 * 16
     spans = ((0, cut), (cut, down_own.shape[0] - cut))
     attn_out = scatter16(attn_part, 2)
 
@@ -1564,7 +1689,7 @@
     middle = x_wide + attn_out
     normed_mix, unit_mix, factor_mix = norm_forward(middle, gain_mixer)
     hidden_mix = normed_mix.astype(BF)
-    mix_all, down_a = gather16(hidden_mix, 3, dp=dp, kind=Spread, span=spans[0], side=down_own)
+    mix_all, down_a = gather16(hidden_mix, 3, dp=dp, span=spans[0], side=down_own)
     mix_all = mix_all.reshape(total, width)
 
     lane = jnp.arange(128)[None, :]
@@ -1574,15 +1699,15 @@
         dp, batches, here, seq_lengths, pick, mix_all, routes_all, gate_full, up_full, router_full.T, share_full,
         down_a, spans[1], down_own, grad_own, 4)
     grad_all = grad_all.reshape(total, width)
-    mixed = lax.psum_scatter(out_part, "expert", scatter_dimension=0, tiled=True).astype(F32)
-    mix_part, grad_result, grad_gate_in, grad_up_in, grad_share = mixture_backward(
-        here, pick, grad_all, mix_all, share_hidden, gate_full, up_full, share_full, down_a, down_b, act, slope, result,
-        share_act, share_slope, gates)
+    mix_part, grad_result, grad_gate_in, grad_up_in, grad_share_in, mixed = mixture_backward(
+        here, pick, grad_all, gate_full, up_full, share_full, down_a, down_b, act, slope, result,
+        share_act, share_slope, gates, out_part.reshape(GROUPS, own, width), 8)
     grad_down = product_lead(hidden, grad_result).astype(BF)
     grad_gate = product_lead(rows, grad_gate_in).astype(BF)
     grad_up = product_lead(rows, grad_up_in).astype(BF)
     mix_part, grad_down, grad_gate, grad_up = lax.optimization_barrier((mix_part, grad_down, grad_gate, grad_up))
-    mix_sum = scatter16(mix_part.reshape(GROUPS, own, width + 128), 5)
+    mix_sum, grad_share = scatter_share(
+        mix_part.reshape(GROUPS, own, width + 128), grad_share_in, share_hidden, mix_all, grad_all, share_full.shape, 5)
     layer_output = valid_own[:, None] * (middle + mixed)
 
     out_down = lax.psum_scatter(grad_down, "dp", scatter_dimension=0, tiled=True)

time: 830 us -> 808 us (0.973)
  Pallas kernels: 653 us -> 635 us
    reduce_scatter x1, waiting for transfers between devices: 0.02 us -> 19.2 us  [per_device(): lax.psum_scatter(grad_gate, 'dp', scatter_dimension=0, tiled=True)]
    pallas_call x5, Pallas kernels: 298 us -> 279 us  [the longest x2 104 us: gather16(): pl.pallas_call(functools.partial(gather_kernel, chunks, dp, span), out_sh...]
    reduce_scatter x1 -> x0, waiting for transfers between devices: 15.5 us -> none  [per_device(): lax.psum_scatter(out_part, 'expert', scatter_dimension=0, tiled=True)]
    pallas_call x1, Pallas kernels: 50.6 us -> 35.5 us  [closing(): pl.pallas_call(functools.partial(closing_kernel, dp, 1), out_shape=(shape...]
    pallas_call x1, Pallas kernels: 88 us -> 99.2 us  [mixture_forward(): pl.pallas_call(functools.partial(forward_kernel, chunks, dp, span, batche...]
  transfers between devices with their start and end apart: 8 -> 7, of which waited for: 1 -> 1; matrix products, arithmetic and copies ran while one was open for 16% -> 10% of each run, Pallas kernels for 60% -> 52%
where the time goes in v7:
time: 808 us; the launch traced here: 799 us
  Pallas kernels  635 us (79%)
  matrix products  50.5 us (6%)
  other arithmetic  45 us (6%)
  local copies, waits for them, and re-layouts  30.4 us (4%)
  waiting for transfers between devices  22.4 us (3%)
  between operations  15.2 us (2%)
    pallas_call x2, Pallas kernels, gather16(): pl.pallas_call(functools.partial(gather_kernel, chunks, dp, span), out_sh...  104 us
    pallas_call x1, Pallas kernels, mixture_forward(): pl.pallas_call(functools.partial(forward_kernel, chunks, dp, span, batche...  99.2 us
    pallas_call x1, Pallas kernels, opening(): pl.pallas_call(functools.partial(opening_kernel, dp, chunks), out_shape=(...  89.9 us
    pallas_call x1, Pallas kernels, returning(): pl.pallas_call(functools.partial(return_kernel, dp, chunks), out_shape=(s...  83.9 us
    pallas_call x1, Pallas kernels, mixture_backward(): pl.pallas_call(functools.partial(backward_kernel, here, chunks), grid=(NZ...  65.5 us
    pallas_call x1, Pallas kernels, scatter_share(): pl.pallas_call(functools.partial(scatter_share_kernel, chunks), out_shape...  58.6 us
    pallas_call x1, Pallas kernels, scatter16(): pl.pallas_call(functools.partial(scatter_kernel, chunks), out_shape=jax.S...  51.6 us
    dot_general x5, matrix products, product_lead(): lax.dot_general(left_side, right_side, (((0,), (0,)), ((), ())), preferre...  40.5 us
  transfers between devices with their start and end apart: 7, of which 1 were waited for; matrix products, arithmetic and copies ran while one was open for 10% of the time, Pallas kernels for 52%

profile of v7, /device:TPU:0, one launch (start us, length us, event | category | flops | bytes accessed | tf_op | source)
XLA Modules:
  0.0 799.0 jit_solution(6781208249519767536)
XLA Ops:
  14.5 89.9 %opening.1 = (bf16[16,128,2048]{2,1,0:T(8,128)(2,1)}, bf16[2,16,64,640]{3,2,1,0:T(8,128)(2,1)}, bf16[2,16,64,256]{3,2,1,0:T(8,128)(2,1)}, bf16[2,64,2048]{2,1,0:...) custom-call(bf16[128,2048]{1,0:T(8,128)(2,1)} %bitcast.142, ...), custom_call_target="tpu_custom_call" | custom-call | bytes 4000000 | tf_op jit(solution)/shard_map/opening/pallas_call | solution.py:479
  113.1 16.6 %project.1 = (bf16[2048,2048]{1,0:T(8,128)(2,1)}, bf16[2,1024,256]{2,1,0:T(8,128)(2,1)S(1)}, bf16[2,1024,256]{2,1,0:T(8,128)(2,1)S(1)}, bf16[2,1024,128]{2,1,0:T(8,128)(2,1)S(1)}, bf16[2,1024,512]{2,1,0:T(8,128)(2,1)}) custom-call(bf16[16,128,2048]{2,1,0:T(8,128)(2,1)} %get-tuple-element.77.x_ref, f32[1,2048]{1,0:T(1,128)S(1)} %bitcast.119, ...), custom_call_target="tpu_custom_call" | custom-call | flops 7000000000 | bytes 20000000 | tf_op jit(solution)/shard_map/project/pallas_call | solution.py:1371
  129.8 9.9 %attend.1 = (bf16[16,2,64,2048]{3,2,1,0:T(8,128)(2,1)}, bf16[16,2,64,128]{3,2,1,0:T(8,128)(2,1)S(1)}, f32[2,1024,1]{2,1,0:T(8,128)S(1)}) custom-call(s32[2]{0:T(128)S(1)} %bitcast.122, bf16[2,1024,256]{2,1,0:T(8,128)(2,1)S(1)} %get-tuple-element.80.q_ref, bf16[2,1024,256]{2,1,0:T(8,128)(2,1)S(1)} %get-tuple-element.81.k_ref, ...), custom_call_target="tpu_custom_call" | custom-call | flops 4000000000 | bytes 15000000 | tf_op jit(solution)/shard_map/attend/pallas_call | solution.py:1429
  141.5 51.6 %scatter16.1 = f32[128,2048]{1,0:T(8,128)} custom-call(bf16[16,128,2048]{2,1,0:T(8,128)(2,1)} %bitcast.140), custom_call_target="tpu_custom_call" | custom-call | bytes 4000000 | tf_op jit(solution)/shard_map/scatter16/pallas_call | solution.py:670
  199.1 57.6 %gather16.2 = (bf16[16,128,2048]{2,1,0:T(8,128)(2,1)}, bf16[2,304,2048]{2,1,0:T(8,128)(2,1)}) custom-call(bf16[128,2048]{1,0:T(8,128)(2,1)} %multiply_convert_fusion.x_ref, bf16[704,2048]{1,0:T(8,128)(2,1)} %bitcast.134), custom_call_target="tpu_custom_call" | custom-call | bytes 4000000 | tf_op jit(solution)/shard_map/gather16/pallas_call | solution.py:331
  258.2 99.2 %mixture_forward.1 = (bf16[2048,2048]{1,0:T(8,128)(2,1)}, bf16[1024,2048]{1,0:T(8,128)(2,1)}, bf16[1024,1408]{1,0:T(8,128)(2,1)}, bf16[1024,1408]{1,0:T(8,128)(2...) custom-call(s32[2]{0:T(128)} %bitcast.120, ...), custom_call_target="tpu_custom_call" | custom-call | bytes 4000000 | tf_op jit(solution)/shard_map/mixture_forward/pallas_call | solution.py:1184
  357.4 65.5 %mixture_backward.1 = (bf16[2048,2176]{1,0:T(8,128)(2,1)}, bf16[1024,2048]{1,0:T(8,128)(2,1)}, bf16[1024,1408]{1,0:T(8,128)(2,1)}, bf16[1024,1408]{1,0:T(8,128)(...) custom-call(f32[1,256]{1,0:T(1,128)} %add_convert_fusion.2.pick_ref, bf16[2048,2048]{1,0:T(8,128)(2,1)} %bitcast.128, ...), custom_call_target="tpu_custom_call" | custom-call | bytes 4000000 | tf_op jit(solution)/shard_map/mixture_backward/pallas_call | solution.py:1216
  423.0 11.2 %convolution_convert_fusion = bf16[2048,1408]{1,0:T(8,128)(2,1)} fusion(bf16[1024,2048]{1,0:T(8,128)(2,1)} %get-tuple-element.100, bf16[1024,1408]{1,0:T(8,128)(2,1)} %get-tuple-element.102), kind=kOutput, calls=%fused_computation | convolution fusion | flops 5908463616 | bytes 12845056 | tf_op jit(solution)/shard_map/dot_general | solution.py:1539
  434.2 11.0 %convolution_convert_fusion.1 = bf16[2048,1408]{1,0:T(8,128)(2,1)} fusion(bf16[1024,2048]{1,0:T(8,128)(2,1)} %get-tuple-element.100, bf16[1024,1408]{1,0:T(8,128)(2,1)} %get-tuple-element.101), kind=kOutput, calls=%fused_computation.1 | convolution fusion | flops 5908463616 | bytes 12845056 | tf_op jit(solution)/shard_map/dot_general | solution.py:1539
  445.2 10.4 %convolution_convert_fusion.2 = bf16[1408,2048]{1,0:T(8,128)(2,1)} fusion(bf16[1024,1408]{1,0:T(8,128)(2,1)} %get-tuple-element.98, bf16[1024,2048]{1,0:T(8,128)(2,1)} %get-tuple-element.99), kind=kOutput, calls=%fused_computation.2 | convolution fusion | flops 5908463616 | bytes 12845056 | tf_op jit(solution)/shard_map/dot_general | solution.py:1539
  455.6 58.6 %scatter_share.1 = (f32[128,2176]{1,0:T(8,128)}, bf16[2,528,1024]{2,1,0:T(8,128)(2,1)}) custom-call(bf16[16,128,2176]{2,1,0:T(8,128)(2,1)} %bitcast.137, bf16[2048,512]{1,0:T(8,128)(2,1)} %get-tuple-element.104.ds_ref, bf16[2048,256]{1,0:T(8,128)(2,1)} %get-tuple-element.105.sh_ref, bf16[2048,2048]{1,0:T(8,128)(2,1)} %bitcast.127, bf16[2048,2048]{1,0:T(8,128)(2,1)} %bitcast.129), custom_call_target="tpu_custom_call" | custom-call | bytes 4000000 | tf_op jit(solution)/shard_map/scatter_share/pallas_call | solution.py:1309
  526.8 45.9 %gather16.3 = bf16[16,128,2048]{2,1,0:T(8,128)(2,1)} custom-call(bf16[128,2048]{1,0:T(8,128)(2,1)} %fusion.37.x_ref), custom_call_target="tpu_custom_call" | custom-call | bytes 4000000 | tf_op jit(solution)/shard_map/gather16/pallas_call | solution.py:331
  572.7 20.9 %attend_back.1 = (bf16[16,2,64,2688]{3,2,1,0:T(8,128)(2,1)}, bf16[16,2,64,256]{3,2,1,0:T(8,128)(2,1)}, f32[128,2048]{1,0:T(8,128)}, f32[512,256]{1,0:T(8,128)}) custom-call(s32[2]{0:T(128)} %bitcast.121, bf16[16,2,64,2048]{3,2,1,0:T(8,128)(2,1)} %bitcast.141, bf16[2,1024,256]{2,1,0:T(8,128)(2,1)} %copy-done.6, bf16[2,1024,256]{2,1,0:T(8,128)(2,1)} %copy-done.7, ...), custom_call_target="tpu_custom_call" | custom-call | flops 14000000000 | bytes 25000000 | tf_op jit(solution)/shard_map/attend_back/pallas_call | solution.py:1509
  593.6 6.0 fusion.39
  607.0 2.7 pad_maximum_fusion.1.parts_ref
  609.7 83.9 %returning.1 = (f32[128,2688]{1,0:T(8,128)}, bf16[2,16,64,256]{3,2,1,0:T(8,128)(2,1)}, bf16[2,64,2048]{2,1,0:T(8,128)(2,1)}, bf16[1,16,64,256]{3,2,1,0:T(8,128)(2,1)}, bf16[1,64,2048]{2,1,0:T(8,128)(2,1)}) custom-call(bf16[16,128,2688]{2,1,0:T(8,128)(2,1)} %bitcast.136, bf16[2,16,64,256]{3,2,1,0:T(8,128)(2,1)} %pad_maximum_fusion.1.parts_ref, ...), custom_call_target="tpu_custom_call" | custom-call | bytes 4000000 | tf_op jit(solution)/shard_map/returning/pallas_call | solution.py:782
  697.6 2.5 reshape.362
  705.6 4.1 fusion.16
  711.8 35.5 %closing.1 = (bf16[128,640]{1,0:T(8,128)(2,1)S(1)}, bf16[1,64,640]{2,1,0:T(8,128)(2,1)S(1)}) custom-call(bf16[16,128,640]{2,1,0:T(8,128)(2,1)S(1)} %bitcast.115), custom_call_target="tpu_custom_call" | custom-call | bytes 4000000 | tf_op jit(solution)/shard_map/closing/pallas_call | solution.py:834
  751.3 3.7 fusion.15
  757.9 5.1 bitcast_convert_fusion
  763.0 4.8 bitcast_convert_fusion.1
  767.8 19.2 %reduce-scatter.5.cloned.1.call-done = bf16[1024,1408]{1,0:T(8,128)(2,1)} async-done(((bf16[2048,1408]{1,0:T(8,128)(2,1)}), bf16[1024,1408]{1,0:T(8,128)(2,1)}) %reduce-scatter.5.cloned.1.call-update) | async-done | bytes 2883600 | tf_op jit(solution)/shard_map/reduce_scatter | solution.py:1714
  787.0 4.7 bitcast_convert_fusion.2
  (170 shorter events, 63.1 us)
Async XLA Ops:
  7.2 251.0 %all-gather.11.cloned.1.call-start = ((), (), s32[]{:S(2)}) async-start(), calls=%async_computation.10 | async-start | bytes 3244032 | tf_op jit(solution)/shard_map/all_gather | solution.py:1664
  9.5 248.7 %all-gather.7.cloned.1.call-start = ((), (), s32[]{:S(2)}) async-start(), calls=%async_computation.8 | async-start | bytes 8650752 | tf_op jit(solution)/shard_map/all_gather | solution.py:1662
  10.4 247.8 %all-gather.9.cloned.1.call-start = ((), (), s32[]{:S(2)}) async-start(), calls=%async_computation.9 | async-start | bytes 8650752 | tf_op jit(solution)/shard_map/all_gather | solution.py:1663
  11.1 743.9 %reduce-scatter.11.cloned.1.call-start = ((), (), s32[]{:S(2)}) async-start(), calls=%async_computation.7 | async-start | bytes 3244032 | tf_op jit(solution)/shard_map/reduce_scatter | solution.py:1716
  14.5 97.3 %copy-start.4 = (f32[2048,32]{1,0:T(8,128)S(1)}, f32[2048,32]{1,0:T(8,128)}, u32[]{:S(2)}) copy-start(f32[2048,32]{1,0:T(8,128)} %constant.97.clone.cos_ref) | copy-start | bytes 786436
  104.5 7.4 copy-start.1
  109.8 19.9 %copy-start = (bf16[512,256]{1,0:T(8,128)(2,1)}, bf16[512,256]{1,0:T(8,128)(2,1)S(1)}, u32[]{:S(2)}) copy-start(bf16[512,256]{1,0:T(8,128)(2,1)S(1)} %reshape.343.we_ref) | copy-start | bytes 786436
  113.1 16.7 %copy-start.2 = (s32[2,1]{0,1:T(1,128)S(1)}, s32[2,1]{0,1:T(1,128)}, u32[]{:S(2)}) copy-start(s32[2,1]{0,1:T(1,128)} %param.26) | copy-start | bytes 28
  113.1 16.7 %copy-start.3 = (bf16[2,64,2048]{2,1,0:T(8,128)(2,1)S(1)}, bf16[2,64,2048]{2,1,0:T(8,128)(2,1)}, u32[]{:S(2)}) copy-start(bf16[2,64,2048]{2,1,0:T(8,128)(2,1)} %get-tuple-element.83) | copy-start | bytes 1572868
  129.8 10.0 %copy-start.6 = (bf16[2,1024,256]{2,1,0:T(8,128)(2,1)}, bf16[2,1024,256]{2,1,0:T(8,128)(2,1)S(1)}, u32[]{:S(2)}) copy-start(bf16[2,1024,256]{2,1,0:T(8,128)(2,1)S(1)} %get-tuple-element.80.q_ref) | copy-start | bytes 3145732
  129.8 10.0 %copy-start.7 = (bf16[2,1024,256]{2,1,0:T(8,128)(2,1)}, bf16[2,1024,256]{2,1,0:T(8,128)(2,1)S(1)}, u32[]{:S(2)}) copy-start(bf16[2,1024,256]{2,1,0:T(8,128)(2,1)S(1)} %get-tuple-element.81.k_ref) | copy-start | bytes 3145732
  129.8 10.0 %copy-start.9 = (bf16[2,1024,128]{2,1,0:T(8,128)(2,1)}, bf16[2,1024,128]{2,1,0:T(8,128)(2,1)S(1)}, u32[]{:S(2)}) copy-start(bf16[2,1024,128]{2,1,0:T(8,128)(2,1)S(1)} %get-tuple-element.82.v_ref) | copy-start | bytes 1572868
  141.5 51.6 %copy-start.11 = (bf16[2,1,64,2048]{3,2,1,0:T(8,128)(2,1)S(1)}, bf16[2,1,64,2048]{3,2,1,0:T(8,128)(2,1)}, u32[]{:S(2)}) copy-start(bf16[2,1,64,2048]{3,2,1,0:T(8,128)(2,1)} %param.24) | copy-start | bytes 1572868
  141.5 51.9 %copy-start.12 = (bf16[2,16,64,640]{3,2,1,0:T(8,128)(2,1)S(1)}, bf16[2,16,64,640]{3,2,1,0:T(8,128)(2,1)}, u32[]{:S(2)}) copy-start(bf16[2,16,64,640]{3,2,1,0:T(8,128)(2,1)} %get-tuple-element.78) | copy-start | bytes 7864324
  198.1 59.2 %copy-start.13 = (bf16[2,1,64,2048]{3,2,1,0:T(8,128)(2,1)S(1)}, bf16[2,1,64,2048]{3,2,1,0:T(8,128)(2,1)}, u32[]{:S(2)}) copy-start(bf16[2,1,64,2048]{3,2,1,0:T(8,128)(2,1)} %param.25) | copy-start | bytes 1572868
  514.2 243.7 %reduce-scatter.9.cloned.1.call-start = ((), (), s32[]{:S(2)}) async-start(), calls=%async_computation.6 | async-start | bytes 8650752 | tf_op jit(solution)/shard_map/reduce_scatter | solution.py:1713
  514.8 248.2 %reduce-scatter.7.cloned.1.call-start = ((), (), s32[]{:S(2)}) async-start(), calls=%async_computation.5 | async-start | bytes 8650752 | tf_op jit(solution)/shard_map/reduce_scatter | solution.py:1715
  515.4 3.6 copy-start.18
  515.4 271.7 %reduce-scatter.5.cloned.1.call-start = ((), (), s32[]{:S(2)}) async-start(), calls=%async_computation.4 | async-start | bytes 8650752 | tf_op jit(solution)/shard_map/reduce_scatter | solution.py:1714
  521.3 4.3 copy-start.14
  705.5 4.1 copy-start.17
  705.6 4.1 copy-start.19
  711.5 38.0 %copy-start.22 = (bf16[1,64,2048]{2,1,0:T(8,128)(2,1)S(1)}, bf16[1,64,2048]{2,1,0:T(8,128)(2,1)}, u32[]{:S(2)}) copy-start(bf16[1,64,2048]{2,1,0:T(8,128)(2,1)} %get-tuple-element.121) | copy-start | bytes 786436
  747.3 7.6 copy-start.20
  (13 other events, 24.7 us)
Sparse Core Ops, SparseCore 0:
  10.1 55.0 all-gather.10
  66.8 71.1 all-gather.6
  139.6 85.3 all-gather.8
  514.3 31.3 reduce-scatter.10
  548.5 71.3 reduce-scatter.8
  622.6 88.2 reduce-scatter.6
  713.9 73.1 reduce-scatter.4

commit v8 on v7

--- a/solution.py
+++ b/solution.py
@@ -654,30 +654,44 @@
                         self.down(t, i, k).wait_send()
 
 
-def scatter_kernel(chunks, p_ref, o_ref, *scratch):
-    s = Scatter(p_ref, o_ref, chunks, scratch)
-    enter(s.me, s.z, s.core, s.side)
+def scatter_kernel(chunks, dp, span, p_ref, *refs):
+    job = None
+    ns = Scatter.COUNT
+    if span is None:
+        o_ref, *scratch = refs
+    else:
+        src, o_ref, out, *scratch = refs
+        job = side_job(dp, span, src, out, scratch[ns:])
+    s = Scatter(p_ref, o_ref, chunks, scratch[:ns])
+    enter(s.me, s.z, s.core, s.side, 1 if job is None else dp)
     s.start()
+    if job is not None:
+        job.start()
     s.run()
     s.finish()
+    if job is not None:
+        job.finish()
 
 
 VMEM = pl.BlockSpec(memory_space=pltpu.VMEM)
 
 
-def scatter16(p, cid, chunks=2):
+def scatter16(p, cid, chunks=2, dp=1, span=None, side=None):
     _, rows, width = p.shape
-    return pl.pallas_call(
-        functools.partial(scatter_kernel, chunks),
-        out_shape=jax.ShapeDtypeStruct((rows, width), jnp.float32),
-        in_specs=[ANY],
-        out_specs=VMEM,
-        scratch_shapes=Scatter.scratch(rows, width, chunks, p.dtype),
+    extra = span is not None
+    out = pl.pallas_call(
+        functools.partial(scatter_kernel, chunks, dp, span),
+        out_shape=(jax.ShapeDtypeStruct((rows, width), jnp.float32),)
+        + ((jax.ShapeDtypeStruct((dp, span[1], side.shape[1]), side.dtype),) if extra else ()),
+        in_specs=[ANY] * (2 if extra else 1),
+        out_specs=(VMEM,) + ((ANY,) if extra else ()),
+        scratch_shapes=Scatter.scratch(rows, width, chunks, p.dtype) + (Spread.scratch(dp) if extra else []),
         compiler_params=pltpu.CompilerParams(
             collective_id=cid, has_side_effects=True, vmem_limit_bytes=60 * 1024 * 1024),
         cost_estimate=COST,
         name="scatter16",
-    )(p)
+    )(*((p, side) if extra else (p,)))
+    return out if extra else out[0]
 
 
 def return_kernel(dp, chunks, p_ref, parts_ref, rows_ref, o_ref, parts_in, rows_in, parts_far, rows_far, *scratch):
@@ -866,13 +880,15 @@
 SHARE = 176
 
 
-def down_copies(a_ref, b_ref, out, sem, which):
-    dp, a, _ = a_ref.shape
-    rows = a + b_ref.shape[1]
-    if which == 0:
-        return [pltpu.make_async_copy(a_ref.at[d], out.at[pl.ds(d * rows, a)], sem.at[d]) for d in range(dp)]
-    return [pltpu.make_async_copy(b_ref.at[d], out.at[pl.ds(d * rows + a, rows - a)], sem.at[dp + d])
-            for d in range(dp)]
+def down_copies(parts, out, sem, which):
+    dp = parts[0].shape[0]
+    sizes = [part.shape[1] for part in parts]
+    rows, first = sum(sizes), sum(sizes[:which])
+    return [
+        pltpu.make_async_copy(
+            parts[which].at[d], out.at[pl.ds(d * rows + first, sizes[which])], sem.at[len(parts) * d + which])
+        for d in range(dp)
+    ]
 
 
 def share_copies(share_ref, fan, down, sem):
@@ -957,9 +973,9 @@
 
 
 def forward_kernel(chunks, dp, span, batches, here, len_ref, pick_ref, mix_ref, routes_ref, wg_ref, wu_ref, router_ref,
-                   share_ref, wda_ref, down_ref, dy_ref,
+                   share_ref, wda_ref, wdb_ref, down_ref, dy_ref,
                    out_ref, rows_ref, hid_ref, act_ref, slo_ref, eo_ref, sh_ref, sact_ref, sslo_ref, gate_ref,
-                   dy_all, wdb_ref,
+                   dy_all, wdc_ref,
                    wd_ref, fan_ref, sd_ref, hid_buf, sh_buf, gate_buf, taken_buf, wd_sem, sh_sem, *sems):
     step = pl.program_id(0)
     tokens, width = mix_ref.shape
@@ -968,18 +984,20 @@
     ff = hid_ref.shape[1]
     phase = pl.num_programs(0) // 2
     g = Gather(dy_ref, dy_all, chunks, sems[:Gather.COUNT])
-    job = side_job(dp, span, down_ref, wdb_ref, sems[Gather.COUNT:])
+    job = side_job(dp, span, down_ref, wdc_ref, sems[Gather.COUNT:])
+    parts = (wda_ref, wdb_ref, wdc_ref)
 
     @pl.when(step == 0)
     def _():
         enter(g.me, g.z, g.core, g.side, dp)
         g.start()
         job.start()
-        for copy in down_copies(wda_ref, wdb_ref, wd_ref, wd_sem, 0) + share_copies(share_ref, fan_ref, sd_ref, sh_sem):
+        copies = share_copies(share_ref, fan_ref, sd_ref, sh_sem)
+        for copy in copies + down_copies(parts, wd_ref, wd_sem, 0) + down_copies(parts, wd_ref, wd_sem, 1):
             copy.start()
         share_blank(fan_ref, sd_ref)
         fan_ref[SHARE:SHARE + 16] = router_ref[...]
-        for copy in share_copies(share_ref, fan_ref, sd_ref, sh_sem):
+        for copy in copies:
             copy.wait()
 
     @pl.when(step < phase)
@@ -1031,10 +1049,10 @@
     @pl.when(step == phase)
     def _():
         job.finish()
-        for copy in down_copies(wda_ref, wdb_ref, wd_ref, wd_sem, 1):
+        for copy in down_copies(parts, wd_ref, wd_sem, 2):
             copy.start()
-        for which in range(2):
-            for copy in down_copies(wda_ref, wdb_ref, wd_ref, wd_sem, which):
+        for which in range(3):
+            for copy in down_copies(parts, wd_ref, wd_sem, which):
                 copy.wait()
 
     @pl.when(step >= phase)
@@ -1057,7 +1075,7 @@
 
         lax.fori_loop(0, width // WIDE, fan_out, 0)
 
-    for r, s in ((1, 1), (2, 3), (3, 5), (4, 7)):
+    for r, s in ((1, 1), (2, 2), (3, 4), (4, 6)):
         @pl.when(step == s)
         def _():
             g.round(r)
@@ -1067,7 +1085,7 @@
         g.finish()
 
 
-def backward_kernel(here, chunks, pick_ref, dy_ref, wg_ref, wu_ref, share_ref, wda_ref, wdb_ref,
+def backward_kernel(here, chunks, pick_ref, dy_ref, wg_ref, wu_ref, share_ref, wda_ref, wdb_ref, wdc_ref,
                     act_ref, slo_ref, eo_ref, sact_ref, sslo_ref, gate_ref, part_ref,
                     dh_ref, deo_ref, dg_ref, du_ref, ds_ref, sum_ref,
                     wd_ref, fan_ref, sd_ref, wd_sem, sh_sem, *scratch):
@@ -1081,8 +1099,8 @@
     def _():
         enter(sc.me, sc.z, sc.core, sc.side)
         copies = share_copies(share_ref, fan_ref, sd_ref, sh_sem)
-        for which in range(2):
-            copies += down_copies(wda_ref, wdb_ref, wd_ref, wd_sem, which)
+        for which in range(3):
+            copies += down_copies((wda_ref, wdb_ref, wdc_ref), wd_ref, wd_sem, which)
         for copy in copies:
             copy.start()
         sc.start()
@@ -1166,7 +1184,7 @@
 SMEM = pl.BlockSpec(memory_space=pltpu.SMEM)
 
 
-def mixture_forward(dp, batches, here, lengths, pick, mix, routes, wg, wu, router, share, wda, span, down, dy, cid,
+def mixture_forward(dp, batches, here, lengths, pick, mix, routes, wg, wu, router, share, wda, wdb, span, down, dy, cid,
                     chunks=2):
     total, width = mix.shape
     step, half = total // 4, total // 8
@@ -1190,21 +1208,21 @@
             shape((total, TILE), BF), shape((total, 2), F32), shape((NE,) + dy.shape, BF),
             shape((dp, span[1], width), BF)),
         in_specs=[SMEM, whole(pick), early(step, width), early(step, routes.shape[1]), whole(wg), whole(wu),
-                  whole(router), ANY, ANY, ANY, ANY],
+                  whole(router), ANY, ANY, ANY, ANY, ANY],
         out_specs=[late(step, width), early(half, width), early(half, ff), early(half, ff), early(half, ff),
                    late(half, width), early(step, TILE), early(step, TILE), early(step, TILE), early(step, 2), ANY, ANY],
         scratch_shapes=[
             pltpu.VMEM((ff, width), BF), pltpu.VMEM((2 * TILE, width), BF), pltpu.VMEM((TILE, width), BF),
             pltpu.VMEM((rows, ff), BF), pltpu.VMEM((total, TILE), BF), pltpu.VMEM((total, 1), F32),
-            pltpu.VMEM((total, 1), F32), dma((2 * dp,)), dma((3 * dp,))] + Gather.scratch(chunks) + Spread.scratch(dp),
+            pltpu.VMEM((total, 1), F32), dma((3 * dp,)), dma((3 * dp,))] + Gather.scratch(chunks) + Spread.scratch(dp),
         compiler_params=pltpu.CompilerParams(
             collective_id=cid, has_side_effects=True, vmem_limit_bytes=60 * 1024 * 1024),
         cost_estimate=COST,
         name="mixture_forward",
-    )(lengths, pick, mix, routes, wg, wu, router, share, wda, down, dy)
-
-
-def mixture_backward(here, pick, dy, wg, wu, share, wda, wdb, act, slo, eo, sact, sslo, gate, part, cid, chunks=2):
+    )(lengths, pick, mix, routes, wg, wu, router, share, wda, wdb, down, dy)
+
+
+def mixture_backward(here, pick, dy, wg, wu, share, wda, wdb, wdc, act, slo, eo, sact, sslo, gate, part, cid, chunks=2):
     total, width = dy.shape
     step, half = total // NZ, total // NZ // 2
     ff = wg.shape[1]
@@ -1219,19 +1237,19 @@
         out_shape=(
             shape((total, width + 128), BF), shape((rows, width), BF), shape((rows, ff), BF), shape((rows, ff), BF),
             shape((total, 2 * TILE), BF), shape((own, width), F32)),
-        in_specs=[whole(pick), tiles(step, width), whole(wg), whole(wu), ANY, ANY, ANY,
+        in_specs=[whole(pick), tiles(step, width), whole(wg), whole(wu), ANY, ANY, ANY, ANY,
                   tiles(half, ff), tiles(half, ff), tiles(half, width), tiles(step, TILE), tiles(step, TILE),
                   tiles(step, 2), ANY],
         out_specs=[tiles(step, width + 128), tiles(half, width), tiles(half, ff), tiles(half, ff),
                    tiles(step, 2 * TILE), pl.BlockSpec((own, width), lambda i: (0, 0))],
         scratch_shapes=[
             pltpu.VMEM((ff, width), BF), pltpu.VMEM((2 * TILE, width), BF), pltpu.VMEM((TILE, width), BF),
-            dma((2 * dp,)), dma((3 * dp,))] + Scatter.scratch(own, width, chunks, BF),
+            dma((3 * dp,)), dma((3 * dp,))] + Scatter.scratch(own, width, chunks, BF),
         compiler_params=pltpu.CompilerParams(
             collective_id=cid, has_side_effects=True, vmem_limit_bytes=62 * 1024 * 1024),
         cost_estimate=COST,
         name="mixture_backward",
-    )(pick, dy, wg, wu, share, wda, wdb, act, slo, eo, sact, sslo, gate, part)
+    )(pick, dy, wg, wu, share, wda, wdb, wdc, act, slo, eo, sact, sslo, gate, part)
 
 
 class ShareWork:
@@ -1681,31 +1699,32 @@
     attn_part, attended, log_total = attend(seq_lengths, query, key, values, output_head, GROUPS)
     attn_part = attn_part.reshape(GROUPS, own, width)
     down_own = down_weight[0]
-    cut = down_own.shape[0] * 9 // 320 * 16
-    spans = ((0, cut), (cut, down_own.shape[0] - cut))
-    attn_out = scatter16(attn_part, 2)
+    cut = down_own.shape[0] * 3 // 160 * 16
+    cuts = (0, cut, 2 * cut + cut // 48 * 16, down_own.shape[0])
+    spans = [(first, last - first) for first, last in zip(cuts, cuts[1:])]
+    attn_out, down_a = scatter16(attn_part, 2, dp=dp, span=spans[0], side=down_own)
 
     x_wide = x_own.astype(F32)
     middle = x_wide + attn_out
     normed_mix, unit_mix, factor_mix = norm_forward(middle, gain_mixer)
     hidden_mix = normed_mix.astype(BF)
-    mix_all, down_a = gather16(hidden_mix, 3, dp=dp, span=spans[0], side=down_own)
+    mix_all, down_b = gather16(hidden_mix, 3, dp=dp, span=spans[1], side=down_own)
     mix_all = mix_all.reshape(total, width)
 
     lane = jnp.arange(128)[None, :]
     pick = jnp.concatenate([lane == me, lane == me + GROUPS], axis=1).astype(F32)
     (out_part, rows, hidden, act, slope, result, share_hidden, share_act, share_slope, gates, grad_all,
-     down_b) = mixture_forward(
+     down_c) = mixture_forward(
         dp, batches, here, seq_lengths, pick, mix_all, routes_all, gate_full, up_full, router_full.T, share_full,
-        down_a, spans[1], down_own, grad_own, 4)
+        down_a, down_b, spans[2], down_own, grad_own, 4)
     grad_all = grad_all.reshape(total, width)
     mix_part, grad_result, grad_gate_in, grad_up_in, grad_share_in, mixed = mixture_backward(
-        here, pick, grad_all, gate_full, up_full, share_full, down_a, down_b, act, slope, result,
+        here, pick, grad_all, gate_full, up_full, share_full, down_a, down_b, down_c, act, slope, result,
         share_act, share_slope, gates, out_part.reshape(GROUPS, own, width), 8)
     grad_down = product_lead(hidden, grad_result).astype(BF)
     grad_gate = product_lead(rows, grad_gate_in).astype(BF)
     grad_up = product_lead(rows, grad_up_in).astype(BF)
-    mix_part, grad_down, grad_gate, grad_up = lax.optimization_barrier((mix_part, grad_down, grad_gate, grad_up))
+    mix_part, _, _, _ = lax.optimization_barrier((mix_part, grad_down, grad_gate, grad_up))
     mix_sum, grad_share = scatter_share(
         mix_part.reshape(GROUPS, own, width + 128), grad_share_in, share_hidden, mix_all, grad_all, share_full.shape, 5)
     layer_output = valid_own[:, None] * (middle + mixed)
@@ -1713,6 +1732,7 @@
     out_down = lax.psum_scatter(grad_down, "dp", scatter_dimension=0, tiled=True)
     out_gate = lax.psum_scatter(grad_gate, "dp", scatter_dimension=0, tiled=True)
     out_up = lax.psum_scatter(grad_up, "dp", scatter_dimension=0, tiled=True)
+    grad_share, out_down, out_gate, out_up = lax.optimization_barrier((grad_share, out_down, out_gate, out_up))
     out_share = lax.psum_scatter(grad_share, "dp", scatter_dimension=0, tiled=False).astype(F32)
 
     mask_own = selected_experts(routes_own)

time: 808 us -> 768 us (0.950)
  Pallas kernels: 635 us -> 605 us
  waiting for transfers between devices: 22.4 us -> 1.47 us
    pallas_call x1, Pallas kernels: 99.2 us -> 75.1 us  [mixture_forward(): pl.pallas_call(functools.partial(forward_kernel, chunks, dp, span, batche...]
    reduce_scatter x1, waiting for transfers between devices: 19.2 us -> 0.01 us  [per_device(): lax.psum_scatter(grad_gate, 'dp', scatter_dimension=0, tiled=True)]
  transfers between devices with their start and end apart: 7 -> 7, of which waited for: 1 -> 0; matrix products, arithmetic and copies ran while one was open for 10% -> 15% of each run, Pallas kernels for 52% -> 61%
where the time goes in v8:
time: 768 us; the launch traced here: 758 us
  Pallas kernels  605 us (79%)
  matrix products  52.8 us (7%)
  other arithmetic  45 us (6%)
  local copies, waits for them, and re-layouts  38.2 us (5%)
  between operations  15.3 us (2%)
    pallas_call x2, Pallas kernels, gather16(): pl.pallas_call(functools.partial(gather_kernel, chunks, dp, span), out_sh...  99.5 us
    pallas_call x1, Pallas kernels, opening(): pl.pallas_call(functools.partial(opening_kernel, dp, chunks), out_shape=(...  89.9 us
    pallas_call x1, Pallas kernels, returning(): pl.pallas_call(functools.partial(return_kernel, dp, chunks), out_shape=(s...  82.7 us
    pallas_call x1, Pallas kernels, mixture_forward(): pl.pallas_call(functools.partial(forward_kernel, chunks, dp, span, batche...  75.1 us
    pallas_call x1, Pallas kernels, mixture_backward(): pl.pallas_call(functools.partial(backward_kernel, here, chunks), grid=(NZ...  65.9 us
    pallas_call x1, Pallas kernels, scatter_share(): pl.pallas_call(functools.partial(scatter_share_kernel, chunks), out_shape...  58.4 us
    pallas_call x1, Pallas kernels, scatter16(): pl.pallas_call(functools.partial(scatter_kernel, chunks, dp, span), out_s...  52.6 us
    dot_general x5, matrix products, product_lead(): lax.dot_general(left_side, right_side, (((0,), (0,)), ((), ())), preferre...  41.9 us
  transfers between devices with their start and end apart: 7, of which 0 were waited for; matrix products, arithmetic and copies ran while one was open for 15% of the time, Pallas kernels for 61%

profile of v8, /device:TPU:0, one launch (start us, length us, event | category | flops | bytes accessed | tf_op | source)
XLA Modules:
  0.0 758.3 jit_solution(12543499609957278894)
XLA Ops:
  14.5 89.9 %opening.1 = (bf16[16,128,2048]{2,1,0:T(8,128)(2,1)}, bf16[2,16,64,640]{3,2,1,0:T(8,128)(2,1)}, bf16[2,16,64,256]{3,2,1,0:T(8,128)(2,1)}, bf16[2,64,2048]{2,1,0:...) custom-call(bf16[128,2048]{1,0:T(8,128)(2,1)} %bitcast.143, ...), custom_call_target="tpu_custom_call" | custom-call | bytes 4000000 | tf_op jit(solution)/shard_map/opening/pallas_call | solution.py:479
  114.5 16.9 %project.1 = (bf16[2048,2048]{1,0:T(8,128)(2,1)}, bf16[2,1024,256]{2,1,0:T(8,128)(2,1)S(1)}, bf16[2,1024,256]{2,1,0:T(8,128)(2,1)S(1)}, bf16[2,1024,128]{2,1,0:T(8,128)(2,1)S(1)}, bf16[2,1024,512]{2,1,0:T(8,128)(2,1)}) custom-call(bf16[16,128,2048]{2,1,0:T(8,128)(2,1)} %get-tuple-element.80.x_ref, f32[1,2048]{1,0:T(1,128)S(1)} %bitcast.119, ...), custom_call_target="tpu_custom_call" | custom-call | flops 7000000000 | bytes 20000000 | tf_op jit(solution)/shard_map/project/pallas_call | solution.py:1389
  131.5 9.9 %attend.1 = (bf16[16,2,64,2048]{3,2,1,0:T(8,128)(2,1)}, bf16[16,2,64,128]{3,2,1,0:T(8,128)(2,1)S(1)}, f32[2,1024,1]{2,1,0:T(8,128)S(1)}) custom-call(s32[2]{0:T(128)S(1)} %bitcast.122, bf16[2,1024,256]{2,1,0:T(8,128)(2,1)S(1)} %get-tuple-element.83.q_ref, bf16[2,1024,256]{2,1,0:T(8,128)(2,1)S(1)} %get-tuple-element.84.k_ref, ...), custom_call_target="tpu_custom_call" | custom-call | flops 4000000000 | bytes 15000000 | tf_op jit(solution)/shard_map/attend/pallas_call | solution.py:1447
  143.1 52.6 %scatter16.1 = (f32[128,2048]{1,0:T(8,128)}, bf16[2,208,2048]{2,1,0:T(8,128)(2,1)}) custom-call(bf16[16,128,2048]{2,1,0:T(8,128)(2,1)} %bitcast.142, bf16[704,2048]{1,0:T(8,128)(2,1)} %bitcast.130), custom_call_target="tpu_custom_call" | custom-call | bytes 4000000 | tf_op jit(solution)/shard_map/scatter16/pallas_call | solution.py:682
  199.0 52.7 %gather16.2 = (bf16[16,128,2048]{2,1,0:T(8,128)(2,1)}, bf16[2,272,2048]{2,1,0:T(8,128)(2,1)}) custom-call(bf16[128,2048]{1,0:T(8,128)(2,1)} %multiply_convert_fusion.x_ref, bf16[704,2048]{1,0:T(8,128)(2,1)} %bitcast.131), custom_call_target="tpu_custom_call" | custom-call | bytes 4000000 | tf_op jit(solution)/shard_map/gather16/pallas_call | solution.py:331
  257.1 75.1 %mixture_forward.1 = (bf16[2048,2048]{1,0:T(8,128)(2,1)}, bf16[1024,2048]{1,0:T(8,128)(2,1)}, bf16[1024,1408]{1,0:T(8,128)(2,1)}, bf16[1024,1408]{1,0:T(8,128)(2...) custom-call(s32[2]{0:T(128)} %bitcast.120, ...), custom_call_target="tpu_custom_call" | custom-call | bytes 4000000 | tf_op jit(solution)/shard_map/mixture_forward/pallas_call | solution.py:1202
  332.2 65.9 %mixture_backward.1 = (bf16[2048,2176]{1,0:T(8,128)(2,1)}, bf16[1024,2048]{1,0:T(8,128)(2,1)}, bf16[1024,1408]{1,0:T(8,128)(2,1)}, bf16[1024,1408]{1,0:T(8,128)(...) custom-call(f32[1,256]{1,0:T(1,128)} %add_convert_fusion.2.pick_ref, bf16[2048,2048]{1,0:T(8,128)(2,1)} %bitcast.128, ...), custom_call_target="tpu_custom_call" | custom-call | bytes 4000000 | tf_op jit(solution)/shard_map/mixture_backward/pallas_call | solution.py:1234
  398.1 11.2 %convolution_convert_fusion = bf16[2048,1408]{1,0:T(8,128)(2,1)} fusion(bf16[1024,2048]{1,0:T(8,128)(2,1)} %get-tuple-element.105, bf16[1024,1408]{1,0:T(8,128)(2,1)} %get-tuple-element.107), kind=kOutput, calls=%fused_computation | convolution fusion | flops 5908463616 | bytes 12845056 | tf_op jit(solution)/shard_map/dot_general | solution.py:1557
  409.4 11.0 %convolution_convert_fusion.1 = bf16[2048,1408]{1,0:T(8,128)(2,1)} fusion(bf16[1024,2048]{1,0:T(8,128)(2,1)} %get-tuple-element.105, bf16[1024,1408]{1,0:T(8,128)(2,1)} %get-tuple-element.106), kind=kOutput, calls=%fused_computation.1 | convolution fusion | flops 5908463616 | bytes 12845056 | tf_op jit(solution)/shard_map/dot_general | solution.py:1557
  420.5 10.4 %convolution_convert_fusion.2 = bf16[1408,2048]{1,0:T(8,128)(2,1)} fusion(bf16[1024,1408]{1,0:T(8,128)(2,1)} %get-tuple-element.103, bf16[1024,2048]{1,0:T(8,128)(2,1)} %get-tuple-element.104), kind=kOutput, calls=%fused_computation.2 | convolution fusion | flops 5908463616 | bytes 12845056 | tf_op jit(solution)/shard_map/dot_general | solution.py:1557
  436.2 2.8 multiply_reduce_fusion.6
  439.5 58.4 %scatter_share.1 = (f32[128,2176]{1,0:T(8,128)}, bf16[2,528,1024]{2,1,0:T(8,128)(2,1)}) custom-call(bf16[16,128,2176]{2,1,0:T(8,128)(2,1)} %bitcast.138, bf16[2048,512]{1,0:T(8,128)(2,1)} %get-tuple-element.109.ds_ref, bf16[2048,256]{1,0:T(8,128)(2,1)} %get-tuple-element.110.sh_ref, bf16[2048,2048]{1,0:T(8,128)(2,1)} %bitcast.127, bf16[2048,2048]{1,0:T(8,128)(2,1)} %bitcast.129), custom_call_target="tpu_custom_call" | custom-call | bytes 4000000 | tf_op jit(solution)/shard_map/scatter_share/pallas_call | solution.py:1327
  504.0 46.7 %gather16.3 = bf16[16,128,2048]{2,1,0:T(8,128)(2,1)} custom-call(bf16[128,2048]{1,0:T(8,128)(2,1)} %fusion.37.x_ref), custom_call_target="tpu_custom_call" | custom-call | bytes 4000000 | tf_op jit(solution)/shard_map/gather16/pallas_call | solution.py:331
  550.7 20.5 %attend_back.1 = (bf16[16,2,64,2688]{3,2,1,0:T(8,128)(2,1)}, bf16[16,2,64,256]{3,2,1,0:T(8,128)(2,1)}, f32[128,2048]{1,0:T(8,128)}, f32[512,256]{1,0:T(8,128)}) custom-call(s32[2]{0:T(128)} %bitcast.121, bf16[16,2,64,2048]{3,2,1,0:T(8,128)(2,1)} %bitcast.141, bf16[2,1024,256]{2,1,0:T(8,128)(2,1)} %copy-done.6, bf16[2,1024,256]{2,1,0:T(8,128)(2,1)} %copy-done.7, ...), custom_call_target="tpu_custom_call" | custom-call | flops 14000000000 | bytes 25000000 | tf_op jit(solution)/shard_map/attend_back/pallas_call | solution.py:1527
  571.2 6.3 fusion.39
  585.0 2.7 pad_maximum_fusion.1.parts_ref
  587.7 82.7 %returning.1 = (f32[128,2688]{1,0:T(8,128)}, bf16[2,16,64,256]{3,2,1,0:T(8,128)(2,1)}, bf16[2,64,2048]{2,1,0:T(8,128)(2,1)}, bf16[1,16,64,256]{3,2,1,0:T(8,128)(2,1)}, bf16[1,64,2048]{2,1,0:T(8,128)(2,1)}) custom-call(bf16[16,128,2688]{2,1,0:T(8,128)(2,1)} %bitcast.137, bf16[2,16,64,256]{3,2,1,0:T(8,128)(2,1)} %pad_maximum_fusion.1.parts_ref, ...), custom_call_target="tpu_custom_call" | custom-call | bytes 4000000 | tf_op jit(solution)/shard_map/returning/pallas_call | solution.py:796
  690.0 4.0 fusion.16
  694.1 2.9 add_convert_fusion
  697.3 33.8 %closing.1 = (bf16[128,640]{1,0:T(8,128)(2,1)S(1)}, bf16[1,64,640]{2,1,0:T(8,128)(2,1)S(1)}) custom-call(bf16[16,128,640]{2,1,0:T(8,128)(2,1)S(1)} %bitcast.115), custom_call_target="tpu_custom_call" | custom-call | bytes 4000000 | tf_op jit(solution)/shard_map/closing/pallas_call | solution.py:848
  735.2 3.7 fusion.15
  739.0 3.3 bitcast_convert_fusion
  742.3 2.9 bitcast_convert_fusion.1
  745.3 2.9 bitcast_convert_fusion.2
  (200 shorter events, 73.7 us)
Async XLA Ops:
  7.2 249.9 %all-gather.11.cloned.1.call-start = ((), (), s32[]{:S(2)}) async-start(), calls=%async_computation.10 | async-start | bytes 3244032 | tf_op jit(solution)/shard_map/all_gather | solution.py:1682
  9.5 247.6 %all-gather.7.cloned.1.call-start = ((), (), s32[]{:S(2)}) async-start(), calls=%async_computation.8 | async-start | bytes 8650752 | tf_op jit(solution)/shard_map/all_gather | solution.py:1680
  10.4 246.7 %all-gather.9.cloned.1.call-start = ((), (), s32[]{:S(2)}) async-start(), calls=%async_computation.9 | async-start | bytes 8650752 | tf_op jit(solution)/shard_map/all_gather | solution.py:1681
  11.1 682.9 %reduce-scatter.9.cloned.1.call-start = ((), (), s32[]{:S(2)}) async-start(), calls=%async_computation.6 | async-start | bytes 8650752 | tf_op jit(solution)/shard_map/reduce_scatter | solution.py:1734
  13.6 97.4 %copy-start.11 = (bf16[2,1,64,2048]{3,2,1,0:T(8,128)(2,1)S(1)}, bf16[2,1,64,2048]{3,2,1,0:T(8,128)(2,1)}, u32[]{:S(2)}) copy-start(bf16[2,1,64,2048]{3,2,1,0:T(8,128)(2,1)} %param.24) | copy-start | bytes 1572868
  111.0 20.4 %copy-start = (bf16[512,256]{1,0:T(8,128)(2,1)}, bf16[512,256]{1,0:T(8,128)(2,1)S(1)}, u32[]{:S(2)}) copy-start(bf16[512,256]{1,0:T(8,128)(2,1)S(1)} %reshape.343.we_ref) | copy-start | bytes 786436
  111.3 84.4 %copy-start.35 = (f32[128]{0:T(128)}, f32[128]{0:T(128)S(1)}, u32[]{:S(2)}) copy-start(f32[128]{0:T(128)S(1)} %rsqrt.29) | copy-start | bytes 1540
  114.5 16.9 %copy-start.2 = (s32[2,1]{0,1:T(1,128)S(1)}, s32[2,1]{0,1:T(1,128)}, u32[]{:S(2)}) copy-start(s32[2,1]{0,1:T(1,128)} %param.26) | copy-start | bytes 28
  114.5 16.9 %copy-start.3 = (bf16[2,64,2048]{2,1,0:T(8,128)(2,1)S(1)}, bf16[2,64,2048]{2,1,0:T(8,128)(2,1)}, u32[]{:S(2)}) copy-start(bf16[2,64,2048]{2,1,0:T(8,128)(2,1)} %get-tuple-element.86) | copy-start | bytes 1572868
  131.4 9.9 %copy-start.6 = (bf16[2,1024,256]{2,1,0:T(8,128)(2,1)}, bf16[2,1024,256]{2,1,0:T(8,128)(2,1)S(1)}, u32[]{:S(2)}) copy-start(bf16[2,1024,256]{2,1,0:T(8,128)(2,1)S(1)} %get-tuple-element.83.q_ref) | copy-start | bytes 3145732
  131.4 9.9 %copy-start.7 = (bf16[2,1024,256]{2,1,0:T(8,128)(2,1)}, bf16[2,1024,256]{2,1,0:T(8,128)(2,1)S(1)}, u32[]{:S(2)}) copy-start(bf16[2,1024,256]{2,1,0:T(8,128)(2,1)S(1)} %get-tuple-element.84.k_ref) | copy-start | bytes 3145732
  143.1 52.6 %copy-start.12 = (bf16[2,1,64,2048]{3,2,1,0:T(8,128)(2,1)S(1)}, bf16[2,1,64,2048]{3,2,1,0:T(8,128)(2,1)}, u32[]{:S(2)}) copy-start(bf16[2,1,64,2048]{3,2,1,0:T(8,128)(2,1)} %param.24) | copy-start | bytes 1572868
  198.1 304.7 %copy-start.27 = (f32[128]{0:T(128)}, f32[128]{0:T(128)S(1)}, u32[]{:S(2)}) copy-start(f32[128]{0:T(128)S(1)} %add_rsqrt_fusion.2) | copy-start | bytes 1540
  254.8 244.3 %copy-start.30 = (f32[128]{0:T(128)}, f32[128]{0:T(128)S(1)}, u32[]{:S(2)}) copy-start(f32[128]{0:T(128)S(1)} %reshape.365) | copy-start | bytes 1540
  254.8 248.0 %copy-start.32 = (bf16[128]{0:T(256)(128)(2,1)}, bf16[128]{0:T(256)(128)(2,1)S(1)}, u32[]{:S(2)}) copy-start(bf16[128]{0:T(256)(128)(2,1)S(1)} %convert_element_type.173) | copy-start | bytes 772
  409.4 284.6 %reduce-scatter.7.cloned.1.call-start = ((), (), s32[]{:S(2)}) async-start(), calls=%async_computation.5 | async-start | bytes 8650752 | tf_op jit(solution)/shard_map/reduce_scatter | solution.py:1733
  420.4 273.6 %reduce-scatter.5.cloned.1.call-start = ((), (), s32[]{:S(2)}) async-start(), calls=%async_computation.4 | async-start | bytes 8650752 | tf_op jit(solution)/shard_map/reduce_scatter | solution.py:1732
  430.9 317.2 %reduce-scatter.11.cloned.1.call-start = ((), (), s32[]{:S(2)}) async-start(), calls=%async_computation.7 | async-start | bytes 3244032 | tf_op jit(solution)/shard_map/reduce_scatter | solution.py:1736
  502.8 47.9 %copy-start.37 = (f32[128]{0:T(128)}, f32[128]{0:T(128)S(1)}, u32[]{:S(2)}) copy-start(f32[128]{0:T(128)S(1)} %broadcast_multiply_fusion.2) | copy-start | bytes 1540
  697.2 38.0 %copy-start.28 = (f32[128]{0:T(128)S(1)}, f32[128]{0:T(128)}, u32[]{:S(2)}) copy-start(f32[128]{0:T(128)} %copy-done.27) | copy-start | bytes 1540
  697.2 38.0 %copy-start.31 = (f32[128]{0:T(128)S(1)}, f32[128]{0:T(128)}, u32[]{:S(2)}) copy-start(f32[128]{0:T(128)} %copy-done.30) | copy-start | bytes 1540
  697.3 38.0 %copy-start.33 = (bf16[128]{0:T(256)(128)(2,1)S(1)}, bf16[128]{0:T(256)(128)(2,1)}, u32[]{:S(2)}) copy-start(bf16[128]{0:T(256)(128)(2,1)} %copy-done.32) | copy-start | bytes 772
  697.3 38.0 %copy-start.36 = (f32[128]{0:T(128)S(1)}, f32[128]{0:T(128)}, u32[]{:S(2)}) copy-start(f32[128]{0:T(128)} %copy-done.35) | copy-start | bytes 1540
  697.3 38.0 %copy-start.38 = (f32[128]{0:T(128)S(1)}, f32[128]{0:T(128)}, u32[]{:S(2)}) copy-start(f32[128]{0:T(128)} %copy-done.37) | copy-start | bytes 1540
  (28 other events, 111.8 us)
Sparse Core Ops, SparseCore 0:
  10.1 55.0 all-gather.10
  66.8 71.1 all-gather.6
  139.5 111.8 all-gather.8
  409.5 69.4 reduce-scatter.8
  481.8 71.3 reduce-scatter.6
  556.0 72.5 reduce-scatter.4
  694.1 37.7 reduce-scatter.10

commit v9 on v8

--- a/solution.py
+++ b/solution.py
@@ -74,8 +74,47 @@
             self.copy(r).wait_send()
 
 
+class Swap:
+    def __init__(self, dp, src, out, sems):
+        self.dp, self.src, self.out = dp, src, out
+        self.send, self.recv = sems
+        self.plane = lax.axis_index("dp")
+
+    @staticmethod
+    def scratch(dp):
+        dma = pltpu.SemaphoreType.DMA
+        return [dma((dp,)), dma((dp,))]
+
+    def copy(self, r):
+        to = (self.plane + r) % self.dp
+        return pltpu.make_async_remote_copy(
+            src_ref=self.src.at[to], dst_ref=self.out.at[r - 1], send_sem=self.send.at[r], recv_sem=self.recv.at[r],
+            device_id={"dp": to}, device_id_type=MESH)
+
+    def start(self):
+        for r in range(1, self.dp):
+            self.copy(r).start()
+
+    def finish(self):
+        for r in range(1, self.dp):
+            self.copy(r).wait_recv()
+            self.copy(r).wait_send()
+
+
 def side_job(dp, span, src, out, sems):
+    if span is None:
+        return Swap(dp, src, out, sems)
     return Spread(dp, src.at[pl.ds(span[0], span[1])], out, sems)
+
+
+def side_shape(dp, span, side):
+    if span is None:
+        return jax.ShapeDtypeStruct((dp - 1,) + side.shape[1:], side.dtype)
+    return jax.ShapeDtypeStruct((dp, span[1], side.shape[1]), side.dtype)
+
+
+def side_scratch(dp, span):
+    return (Swap if span is None else Spread).scratch(dp)
 
 
 def enter_all(me, plane, dp):
@@ -301,10 +340,10 @@
                         self.down_b(k, s).wait_send()
 
 
-def gather_kernel(chunks, dp, span, x_ref, *refs):
+def gather_kernel(chunks, dp, span, extra, x_ref, *refs):
     job = None
     ng = Gather.COUNT
-    if span is None:
+    if not extra:
         o_ref, *sems = refs
     else:
         src, o_ref, out, *sems = refs
@@ -327,14 +366,14 @@
 
 def gather16(v, cid, chunks=2, dp=1, span=None, side=None):
     rows, width = v.shape
-    extra = span is not None
+    extra = side is not None
     out = pl.pallas_call(
-        functools.partial(gather_kernel, chunks, dp, span),
+        functools.partial(gather_kernel, chunks, dp, span, extra),
         out_shape=(jax.ShapeDtypeStruct((NE, rows, width), v.dtype),)
-        + ((jax.ShapeDtypeStruct((dp, span[1], side.shape[1]), side.dtype),) if extra else ()),
+        + ((side_shape(dp, span, side),) if extra else ()),
         in_specs=[ANY] * (2 if extra else 1),
         out_specs=(ANY,) * (2 if extra else 1),
-        scratch_shapes=Gather.scratch(chunks) + (Spread.scratch(dp) if extra else []),
+        scratch_shapes=Gather.scratch(chunks) + (side_scratch(dp, span) if extra else []),
         compiler_params=pltpu.CompilerParams(collective_id=cid, has_side_effects=True),
         cost_estimate=COST,
         name="gather16",
@@ -654,10 +693,10 @@
                         self.down(t, i, k).wait_send()
 
 
-def scatter_kernel(chunks, dp, span, p_ref, *refs):
+def scatter_kernel(chunks, dp, span, extra, p_ref, *refs):
     job = None
     ns = Scatter.COUNT
-    if span is None:
+    if not extra:
         o_ref, *scratch = refs
     else:
         src, o_ref, out, *scratch = refs
@@ -678,14 +717,14 @@
 
 def scatter16(p, cid, chunks=2, dp=1, span=None, side=None):
     _, rows, width = p.shape
-    extra = span is not None
+    extra = side is not None
     out = pl.pallas_call(
-        functools.partial(scatter_kernel, chunks, dp, span),
+        functools.partial(scatter_kernel, chunks, dp, span, extra),
         out_shape=(jax.ShapeDtypeStruct((rows, width), jnp.float32),)
-        + ((jax.ShapeDtypeStruct((dp, span[1], side.shape[1]), side.dtype),) if extra else ()),
+        + ((side_shape(dp, span, side),) if extra else ()),
         in_specs=[ANY] * (2 if extra else 1),
         out_specs=(VMEM,) + ((ANY,) if extra else ()),
-        scratch_shapes=Scatter.scratch(rows, width, chunks, p.dtype) + (Spread.scratch(dp) if extra else []),
+        scratch_shapes=Scatter.scratch(rows, width, chunks, p.dtype) + (side_scratch(dp, span) if extra else []),
         compiler_params=pltpu.CompilerParams(
             collective_id=cid, has_side_effects=True, vmem_limit_bytes=60 * 1024 * 1024),
         cost_estimate=COST,
@@ -694,135 +733,67 @@
     return out if extra else out[0]
 
 
-def return_kernel(dp, chunks, p_ref, parts_ref, rows_ref, o_ref, parts_in, rows_in, parts_far, rows_far, *scratch):
+def return_kernel(dp, chunks, p_ref, parts_ref, rows_ref, o_ref, parts_far, rows_far, *scratch):
     ns = Scatter.COUNT
     s = Scatter(p_ref, o_ref, chunks, scratch[:ns])
-    ps, pr, os_, or_, pl_sem, ol_sem, ys, yr = scratch[ns:]
-    me = s.me
+    swap = Swap(dp, parts_ref, parts_far, scratch[ns:ns + 2])
+    rs, rr = scratch[ns + 2:]
     plane = lax.axis_index("dp")
-    enter_all(me, plane, dp)
-
-    def part(r):
-        e = (me + r) % NE
+    keeper = s.me * dp // NE
+    enter(s.me, s.z, s.core, s.side, dp)
+
+    def row(r):
         return pltpu.make_async_remote_copy(
-            src_ref=parts_ref.at[:, e], dst_ref=parts_in.at[:, me],
-            send_sem=ps.at[r], recv_sem=pr.at[r],
-            device_id={"expert": e}, device_id_type=MESH)
-
-    def part_in(r):
-        h = (me - r + NE) % NE
-        return pltpu.make_async_remote_copy(
-            src_ref=parts_in.at[:, h], dst_ref=parts_in.at[:, h],
-            send_sem=ps.at[r], recv_sem=pr.at[r],
-            device_id={"expert": h}, device_id_type=MESH)
-
-    def part_kept():
-        return pltpu.make_async_copy(parts_ref.at[:, me], parts_in.at[:, me], pl_sem)
-
-    def row(j):
-        b = dp * me + j
-        return pltpu.make_async_remote_copy(
-            src_ref=rows_ref.at[j], dst_ref=rows_in.at[b // NE],
-            send_sem=os_.at[j], recv_sem=or_.at[b // NE],
-            device_id={"expert": b % NE}, device_id_type=MESH)
-
-    def row_kept(j):
-        b = dp * me + j
-        return pltpu.make_async_copy(rows_ref.at[j], rows_in.at[b // NE], ol_sem.at[j])
-
-    def row_in(d):
-        return pltpu.make_async_remote_copy(
-            src_ref=rows_in.at[d], dst_ref=rows_in.at[d], send_sem=os_.at[d], recv_sem=or_.at[d],
-            device_id={"expert": s.core}, device_id_type=MESH)
-
-    def lift(i, r):
-        to = (plane + r) % dp
-        src, dst = ((parts_in.at[to], parts_far.at[r - 1]), (rows_in.at[to], rows_far.at[r - 1]))[i]
-        return pltpu.make_async_remote_copy(
-            src_ref=src, dst_ref=dst, send_sem=ys.at[i, r], recv_sem=yr.at[i, r],
-            device_id={"dp": to}, device_id_type=MESH)
+            src_ref=rows_ref, dst_ref=rows_far.at[r - 1], send_sem=rs.at[r], recv_sem=rr.at[r],
+            device_id={"dp": (plane + r) % dp}, device_id_type=MESH)
 
     s.start()
-    for r in range(1, NE):
-        part(r).start()
-    part_kept().start()
-    for j in range(dp):
-        @pl.when((dp * me + j) % NE != me)
-        def _():
-            row(j).start()
-
-        @pl.when((dp * me + j) % NE == me)
-        def _():
-            row_kept(j).start()
-    s.first(0)
-    s.first(1)
-    s.second(0)
-    for r in range(1, NE):
-        part_in(r).wait_recv()
-    part_kept().wait()
-    for j in range(dp):
-        @pl.when((dp * me + j) % NE == me)
-        def _():
-            row_kept(j).wait()
-    for d in range(dp):
-        @pl.when((NE * d + me) // dp != me)
-        def _():
-            row_in(d).wait_recv()
-    for i in range(2):
-        for r in range(1, dp):
-            lift(i, r).start()
-    s.first(2)
-    s.second(1)
-    s.first(3)
-    s.second(2)
-    s.second(3)
-    for i in range(2):
-        for r in range(1, dp):
-            lift(i, r).wait_recv()
-            lift(i, r).wait_send()
-    for r in range(1, NE):
-        part(r).wait_send()
-    for j in range(dp):
-        @pl.when((dp * me + j) % NE != me)
-        def _():
-            row(j).wait_send()
+    swap.start()
+    for r in range(1, dp):
+        @pl.when((plane + r) % dp == keeper)
+        def _():
+            row(r).start()
+    s.run()
     s.finish()
+    swap.finish()
+    for r in range(1, dp):
+        @pl.when((plane + r) % dp == keeper)
+        def _():
+            row(r).wait_send()
+
+        @pl.when(plane == keeper)
+        def _():
+            row(r).wait_recv()
 
 
 def returning(dp, p, parts, rows, cid, chunks=2):
     dma = pltpu.SemaphoreType.DMA
     _, n, width = p.shape
     shape = jax.ShapeDtypeStruct
-    out, parts_in, rows_in, parts_far, rows_far = pl.pallas_call(
+    return pl.pallas_call(
         functools.partial(return_kernel, dp, chunks),
         out_shape=(
-            shape((n, width), jnp.float32), shape(parts.shape, parts.dtype), shape(rows.shape, rows.dtype),
-            shape((dp - 1,) + parts.shape[1:], parts.dtype), shape((dp - 1,) + rows.shape[1:], rows.dtype)),
+            shape((n, width), jnp.float32), shape((dp - 1,) + parts.shape[1:], parts.dtype),
+            shape((dp - 1,) + rows.shape, rows.dtype)),
         in_specs=[ANY] * 3,
-        out_specs=[VMEM] + [ANY] * 4,
-        scratch_shapes=Scatter.scratch(n, width, chunks, p.dtype) + [
-            dma((NE,)), dma((NE,)), dma((dp,)), dma((dp,)), dma, dma((dp,)), dma((2, dp)), dma((2, dp))],
+        out_specs=[VMEM, ANY, ANY],
+        scratch_shapes=Scatter.scratch(n, width, chunks, p.dtype) + [dma((dp,))] * 4,
         compiler_params=pltpu.CompilerParams(
             collective_id=cid, has_side_effects=True, vmem_limit_bytes=60 * 1024 * 1024),
         cost_estimate=COST,
         name="returning",
     )(p, parts, rows)
-    plane = lax.axis_index("dp")
-
-    def total(near, far):
-        own = lax.dynamic_index_in_dim(near, plane, 0, False).astype(jnp.float32)
-        return own + jnp.sum(far.astype(jnp.float32), axis=0)
-
-    return out, total(parts_in, parts_far), total(rows_in, rows_far)
-
-
-def closing_kernel(dp, chunks, p_ref, o_ref, far_ref, *scratch):
+
+
+def closing_kernel(dp, p_ref, parts_ref, rows_ref, o_ref, far_ref, query_ref, expand_ref, output_ref,
+                   parts_in, row_in, *scratch):
     ns = Scatter.COUNT
-    s = Scatter(p_ref, o_ref, chunks, scratch[:ns])
-    ys, yr = scratch[ns:]
+    s = Scatter(p_ref, o_ref, 1, scratch[:ns])
+    ys, yr, ps, pr, kept_sem, rs, rr = scratch[ns:]
+    me = s.me
     plane = lax.axis_index("dp")
     rows = o_ref.shape[0] // dp
-    enter(s.me, s.z, s.core, s.side, dp)
+    enter_all(me, plane, dp)
 
     def lift(r):
         to = (plane + r) % dp
@@ -831,33 +802,107 @@
             send_sem=ys.at[r], recv_sem=yr.at[r],
             device_id={"dp": to}, device_id_type=MESH)
 
+    def part(r):
+        e = (me + r) % NE
+        return pltpu.make_async_remote_copy(
+            src_ref=parts_ref.at[e], dst_ref=parts_in.at[me], send_sem=ps.at[r], recv_sem=pr.at[r],
+            device_id={"expert": e}, device_id_type=MESH)
+
+    def part_in(r):
+        h = (me - r + NE) % NE
+        return pltpu.make_async_remote_copy(
+            src_ref=parts_in.at[h], dst_ref=parts_in.at[h], send_sem=ps.at[r], recv_sem=pr.at[r],
+            device_id={"expert": h}, device_id_type=MESH)
+
+    def part_kept():
+        return pltpu.make_async_copy(parts_ref.at[me], parts_in.at[me], kept_sem.at[0])
+
+    keeper = plane == me * dp // NE
+    source = (NE * plane + me) // dp
+
+    def row(j):
+        return pltpu.make_async_remote_copy(
+            src_ref=rows_ref.at[j], dst_ref=row_in, send_sem=rs.at[j], recv_sem=rr,
+            device_id={"expert": (dp * me + j) % NE}, device_id_type=MESH)
+
+    def row_kept(j):
+        return pltpu.make_async_copy(rows_ref.at[j], row_in, kept_sem.at[1])
+
     s.start()
+    for r in range(1, NE):
+        part(r).start()
+    part_kept().start()
+    for j in range(dp):
+        home = (dp * me + j) % NE
+
+        @pl.when(keeper & (home != me))
+        def _():
+            row(j).start()
+
+        @pl.when(keeper & (home == me))
+        def _():
+            row_kept(j).start()
     s.run()
     for r in range(1, dp):
         lift(r).start()
+    for r in range(1, NE):
+        part_in(r).wait_recv()
+    part_kept().wait()
+    rows_l = expand_ref.shape[0]
+    f32 = jnp.float32
+    for h in range(0, NE, 2):
+        pair = [parts_in[h + i].astype(f32) for i in range(2)]
+        query_ref[:, h * 192:(h + 2) * 192] = jnp.concatenate([v[:, :192] for v in pair], axis=1)
+        for i, v in enumerate(pair):
+            expand_ref[:, (h + i) * 256:(h + i + 1) * 256] = jnp.concatenate(
+                [v[c * rows_l:(c + 1) * rows_l, 192:] for c in range(4)], axis=1)
+
+    @pl.when(source != me)
+    def _():
+        row(0).wait_recv()
+
+    for j in range(dp):
+        home = (dp * me + j) % NE
+
+        @pl.when(keeper & (home != me))
+        def _():
+            row(j).wait_send()
+
+        @pl.when(keeper & (home == me))
+        def _():
+            row_kept(j).wait()
+    output_ref[...] = row_in[...].astype(f32)
+    for r in range(1, NE):
+        part(r).wait_send()
     s.finish()
     for r in range(1, dp):
         lift(r).wait_recv()
         lift(r).wait_send()
 
 
-def closing(dp, p, cid):
+def closing(dp, p, parts, rows, rows_l, cid):
     dma = pltpu.SemaphoreType.DMA
     _, n, width = p.shape
     shape = jax.ShapeDtypeStruct
-    near, far = pl.pallas_call(
-        functools.partial(closing_kernel, dp, 1),
-        out_shape=(shape((n, width), p.dtype), shape((dp - 1, n // dp, width), p.dtype)),
-        in_specs=[ANY],
-        out_specs=[VMEM, VMEM],
-        scratch_shapes=Scatter.scratch(n, width, 1, p.dtype) + [dma((dp,)), dma((dp,))],
+    rows_w = parts.shape[1]
+    near, far, query, expand, output = pl.pallas_call(
+        functools.partial(closing_kernel, dp),
+        out_shape=(
+            shape((n, width), p.dtype), shape((dp - 1, n // dp, width), p.dtype),
+            shape((rows_w, NE * 192), jnp.float32), shape((rows_l, NE * 256), jnp.float32),
+            shape(rows.shape[1:], jnp.float32)),
+        in_specs=[ANY] * 3,
+        out_specs=[VMEM] * 5,
+        scratch_shapes=[pltpu.VMEM(parts.shape, parts.dtype), pltpu.VMEM(rows.shape[1:], rows.dtype)]
+        + Scatter.scratch(n, width, 1, p.dtype)
+        + [dma((dp,)), dma((dp,)), dma((NE,)), dma((NE,)), dma((2,)), dma((dp,)), dma],
         compiler_params=pltpu.CompilerParams(
-            collective_id=cid, has_side_effects=True, vmem_limit_bytes=32 * 1024 * 1024),
+            collective_id=cid, has_side_effects=True, vmem_limit_bytes=60 * 1024 * 1024),
         cost_estimate=COST,
         name="closing",
-    )(p)
+    )(p, parts, rows)
     own = lax.dynamic_slice_in_dim(near, lax.axis_index("dp") * (n // dp), n // dp).astype(jnp.float32)
-    return own + jnp.sum(far.astype(jnp.float32), axis=0)
+    return own + jnp.sum(far.astype(jnp.float32), axis=0), query, expand, output
 BF = jnp.bfloat16
 F32 = jnp.float32
 
@@ -1458,8 +1503,8 @@
     )(lengths, q, k, v, wo)
 
 
-def attend_back_kernel(len_ref, dout_ref, q_ref, k_ref, v_ref, lat_ref, att_ref, lse_ref, wo_ref, wq_ref, we_ref,
-                       cos_ref, sin_ref, part_ref, dq_ref, gwo_ref, gwe_ref, dk, dv, datt):
+def attend_back_kernel(len_ref, dout_ref, h_ref, q_ref, k_ref, v_ref, lat_ref, att_ref, lse_ref, wo_ref, wq_ref, we_ref,
+                       cos_ref, sin_ref, part_ref, gwq_ref, gwo_out, gwe_out, dk, dv, datt, gwq, gwo_ref, gwe_ref):
     m = pl.program_id(0)
     length = len_ref[m]
     seq = q_ref.shape[1]
@@ -1470,6 +1515,7 @@
     def _():
         gwo_ref[...] = jnp.zeros_like(gwo_ref)
         gwe_ref[...] = jnp.zeros_like(gwe_ref)
+        gwq[...] = jnp.zeros_like(gwq)
 
     for j in range(4):
         blocks = slice(j * groups // 4, (j + 1) * groups // 4)
@@ -1493,7 +1539,10 @@
         dv[:ext] += mm_lead(p.astype(BF), da)
         rope = turn(dq[:, 128:192], cos_ref[tile], -sin_ref[tile])
         dq = jnp.concatenate([dq[:, :128].astype(BF), rope.astype(BF), jnp.zeros((ROWS, 64), BF)], axis=1)
-        dq_ref[i * per:(i + 1) * per, 0] = dq.reshape(per, here, 256)
+        hidden = h_ref[i * per:(i + 1) * per, 0].reshape(ROWS, width)
+        for j in range(width // 512):
+            cols = slice(j * 512, (j + 1) * 512)
+            gwq[:, cols] += mm_lead(dq, hidden[:, cols])
         for j in range(width // 512):
             cols = slice(j * 512, (j + 1) * 512)
             part_ref[i * per:(i + 1) * per, 0, :, cols] = mm_t(dq, wq_ref[cols]).astype(BF).reshape(per, here, 512)
@@ -1509,8 +1558,16 @@
             tail = jnp.concatenate([tail, jnp.zeros((ROWS, pad), BF)], axis=1)
         part_ref[i * per:(i + 1) * per, 0, :, width:] = tail[:, :part_ref.shape[3] - width].reshape(per, here, -1)
 
-
-def attend_back(lengths, dout, q, k, v, lat, att, lse, wo, wq, we, cosine, sine, tail):
+    @pl.when(m == pl.num_programs(0) - 1)
+    def _():
+        for j in range(width // 256):
+            cols = slice(j * 256, (j + 1) * 256)
+            gwq_ref[cols] = gwq[:, cols].T.astype(BF)
+        gwo_out[...] = gwo_ref[...].astype(BF)
+        gwe_out[...] = gwe_ref[...].astype(BF)
+
+
+def attend_back(lengths, dout, h, q, k, v, lat, att, lse, wo, wq, we, cosine, sine, tail):
     groups, batches, here, width = dout.shape
     seq = groups * here
     shape = jax.ShapeDtypeStruct
@@ -1527,16 +1584,17 @@
     return pl.pallas_call(
         attend_back_kernel,
         grid=(batches,),
-        out_shape=(shape((groups, batches, here, width + tail), BF), shape((groups, batches, here, 256), BF),
-                   shape(wo.shape, F32), shape(we.shape, F32)),
-        in_specs=[pl.BlockSpec(memory_space=pltpu.SMEM), by_dev(width), by_seq(256), by_seq(256), by_seq(128),
+        out_shape=(shape((groups, batches, here, width + tail), BF), shape(wq.shape, BF),
+                   shape(wo.shape, BF), shape(we.shape, BF)),
+        in_specs=[pl.BlockSpec(memory_space=pltpu.SMEM), by_dev(width), by_dev(width), by_seq(256), by_seq(256), by_seq(128),
                   by_seq(512), by_dev(128), by_seq(1), whole(wo), whole(wq), whole(we), whole(cosine), whole(sine)],
-        out_specs=[by_dev(width + tail), by_dev(256), whole(wo), whole(we)],
-        scratch_shapes=[pltpu.VMEM((seq, 256), F32), pltpu.VMEM((seq, 128), F32), pltpu.VMEM((seq, 128), BF)],
+        out_specs=[by_dev(width + tail), whole(wq), whole(wo), whole(we)],
+        scratch_shapes=[pltpu.VMEM((seq, 256), F32), pltpu.VMEM((seq, 128), F32), pltpu.VMEM((seq, 128), BF),
+                        pltpu.VMEM((256, width), F32), pltpu.VMEM(wo.shape, F32), pltpu.VMEM(we.shape, F32)],
         compiler_params=pltpu.CompilerParams(vmem_limit_bytes=56 * 1024 * 1024),
         cost_estimate=pl.CostEstimate(flops=14_000_000_000, bytes_accessed=25_000_000, transcendentals=2_000_000),
         name="attend_back",
-    )(lengths, dout, q, k, v, lat, att, lse, wo, wq, we, cosine, sine)
+    )(lengths, dout, h, q, k, v, lat, att, lse, wo, wq, we, cosine, sine)
 
 
 H = 16
@@ -1659,7 +1717,8 @@
     )
     query_parts = query_weight.reshape(rows_w, H, QK_NOPE + ROPE).transpose(1, 0, 2)
     expand_parts = expand_weight.reshape(rows_l, H, QK_NOPE + V_DIM).transpose(1, 0, 2)
-    parts = jnp.concatenate([query_parts, expand_parts.reshape(H, rows_w, ROPE)], axis=2)
+    expand_parts = expand_parts.reshape(H, rows_l, 4, ROPE).swapaxes(1, 2).reshape(H, rows_w, ROPE)
+    parts = jnp.concatenate([query_parts, expand_parts], axis=2)
     x_all, small, parts_head, output_head = opening(dp, x_own, small, parts, output_weight, 1)
     x_all = x_all.reshape(total, width)
     routes_all = lax.dynamic_index_in_dim(small, plane, 0, False)[..., 595 : 595 + route_columns.shape[1]]
@@ -1671,7 +1730,8 @@
     gain_attn = small[:, 592].astype(F32)
     gain_mixer = small[:, 593].astype(F32)
     gain_latent = small[:, 594].reshape(dp * GROUPS, rows_w)[:, :rows_l].reshape(-1).astype(F32)
-    expand_head = parts_head[:, QK_NOPE + ROPE :].reshape(KV_RANK, QK_NOPE + V_DIM)
+    expand_head = parts_head[:, QK_NOPE + ROPE :].reshape(dp * GROUPS, 4, rows_l, ROPE)
+    expand_head = expand_head.swapaxes(1, 2).reshape(KV_RANK, QK_NOPE + V_DIM)
     output_head = output_head.reshape(V_DIM, width)
 
     ff = gate_weight.shape[2]
@@ -1732,8 +1792,6 @@
     out_down = lax.psum_scatter(grad_down, "dp", scatter_dimension=0, tiled=True)
     out_gate = lax.psum_scatter(grad_gate, "dp", scatter_dimension=0, tiled=True)
     out_up = lax.psum_scatter(grad_up, "dp", scatter_dimension=0, tiled=True)
-    grad_share, out_down, out_gate, out_up = lax.optimization_barrier((grad_share, out_down, out_gate, out_up))
-    out_share = lax.psum_scatter(grad_share, "dp", scatter_dimension=0, tiled=False).astype(F32)
 
     mask_own = selected_experts(routes_own)
     soft_own = masked_softmax(product(hidden_mix, router_full), mask_own)
@@ -1745,19 +1803,22 @@
     grad_middle_norm, grad_gain_mixer = norm_backward(grad_mix, unit_mix, factor_mix, gain_mixer)
     grad_middle = grad_own.astype(F32) + grad_middle_norm
 
-    grad_attn_all = gather16(grad_middle.astype(BF), 6).reshape(GROUPS, batches, here, width)
-    back_part, grad_query, grad_output, grad_expand = attend_back(
-        seq_lengths, grad_attn_all, query, key, values, latent, attended, log_total, output_head, parts_head,
-        expand_head, jnp.asarray(cosine), jnp.asarray(sine_table), 640)
-    grad_query_w = product_lead(hidden_all, grad_query.reshape(total, TILE)).astype(BF)
-    parts_grad = jnp.concatenate(
-        [grad_query_w[:, : QK_NOPE + ROPE], grad_expand.astype(BF).reshape(width, ROPE)], axis=1)
-    back_sum, out_parts, out_output = returning(
-        dp, back_part.reshape(GROUPS, own, back_part.shape[3]),
-        parts_grad.reshape(dp, GROUPS, rows_w, TILE), grad_output.astype(BF).reshape(dp, rows_w, width), 7)
-    out_query = out_parts[..., : QK_NOPE + ROPE].transpose(1, 0, 2).reshape(rows_w, -1)
-    out_expand = out_parts[..., QK_NOPE + ROPE :].reshape(H, rows_l, QK_NOPE + V_DIM)
-    out_expand = out_expand.transpose(1, 0, 2).reshape(rows_l, -1)
+    grad_attn_all, share_far = gather16(grad_middle.astype(BF), 6, dp=dp, side=grad_share)
+    grad_attn_all = grad_attn_all.reshape(GROUPS, batches, here, width)
+    out_share = lax.dynamic_index_in_dim(grad_share, plane, 0, False).astype(F32)
+    out_share = out_share + jnp.sum(share_far.astype(F32), axis=0)
+    back_part, grad_query_w, grad_output, grad_expand = attend_back(
+        seq_lengths, grad_attn_all, hidden_all.reshape(GROUPS, batches, here, width), query, key, values, latent,
+        attended, log_total, output_head, parts_head, expand_head, jnp.asarray(cosine), jnp.asarray(sine_table), 640)
+    grad_expand = grad_expand.reshape(dp * GROUPS, rows_l, 4, ROPE).swapaxes(1, 2).reshape(width, ROPE)
+    parts_grad = grad_query_w + jnp.pad(grad_expand, ((0, 0), (QK_NOPE + ROPE, 0)))
+    parts_grad = parts_grad.reshape(dp, GROUPS, rows_w, TILE)
+    rows_grad = grad_output.reshape(dp, rows_w, width)
+    back_sum, parts_far, rows_far = returning(
+        dp, back_part.reshape(GROUPS, own, back_part.shape[3]), parts_grad, rows_grad, 7)
+    parts_sum = lax.dynamic_index_in_dim(parts_grad, plane, 0, False).astype(F32)
+    parts_sum = (parts_sum + jnp.sum(parts_far.astype(F32), axis=0)).astype(BF)
+    rows_sum = (rows_grad.astype(F32) + jnp.sum(rows_far.astype(F32), axis=0)).astype(BF)
 
     x_normed, unit_attn, factor_attn = norm_forward(x_wide, gain_attn)
     hidden_own = x_normed.astype(BF)
@@ -1784,7 +1845,7 @@
     small_grad = small_grad + jnp.where(lane == 593, grad_gain_mixer[:, None], 0.0)
     small_grad = (small_grad + jnp.where(lane == 594, latent_rows, 0.0)).astype(BF)
     small_grad = small_grad.reshape(dp, GROUPS, rows_w, 640).swapaxes(0, 1).reshape(GROUPS, dp * rows_w, 640)
-    small_sum = closing(dp, small_grad, 9)
+    small_sum, out_query, out_expand, out_output = closing(dp, small_grad, parts_sum, rows_sum, rows_l, 9)
 
     def as_input(v):
         return v.reshape(batches, 1, here, width)

time: 768 us -> 747 us (0.973)
  matrix products: 52.8 us -> 44.5 us
    pallas_call x1, Pallas kernels: 82.7 us -> 65.8 us  [returning(): pl.pallas_call(functools.partial(return_kernel, dp, chunks), out_shape=(s...]
    pallas_call x4, Pallas kernels: 186 us -> 202 us  [the longest x2 104 us: gather16(): pl.pallas_call(functools.partial(gather_kernel, chunks, dp, span, extra),...]
    dot_general x5 -> x4, matrix products: 41.9 us -> 34.7 us  [product_lead(): lax.dot_general(left_side, right_side, (((0,), (0,)), ((), ())), preferre...]
  transfers between devices with their start and end apart: 7 -> 6, of which waited for: 0 -> 0; matrix products, arithmetic and copies ran while one was open for 15% -> 12% of each run, Pallas kernels for 61% -> 63%
where the time goes in v9:
time: 747 us; the launch traced here: 743 us
  Pallas kernels  609 us (82%)
  matrix products  44.5 us (6%)
  other arithmetic  41.3 us (6%)
  local copies, waits for them, and re-layouts  30.9 us (4%)
  between operations  15.1 us (2%)
    pallas_call x2, Pallas kernels, gather16(): pl.pallas_call(functools.partial(gather_kernel, chunks, dp, span, extra),...  104 us
    pallas_call x1, Pallas kernels, opening(): pl.pallas_call(functools.partial(opening_kernel, dp, chunks), out_shape=(...  89.9 us
    pallas_call x1, Pallas kernels, mixture_forward(): pl.pallas_call(functools.partial(forward_kernel, chunks, dp, span, batche...  75.2 us
    pallas_call x1, Pallas kernels, returning(): pl.pallas_call(functools.partial(return_kernel, dp, chunks), out_shape=(s...  65.8 us
    pallas_call x1, Pallas kernels, mixture_backward(): pl.pallas_call(functools.partial(backward_kernel, here, chunks), grid=(NZ...  65.8 us
    pallas_call x1, Pallas kernels, scatter_share(): pl.pallas_call(functools.partial(scatter_share_kernel, chunks), out_shape...  58.6 us
    pallas_call x1, Pallas kernels, scatter16(): pl.pallas_call(functools.partial(scatter_kernel, chunks, dp, span, extra)...  52.6 us
    pallas_call x1, Pallas kernels, closing(): pl.pallas_call(functools.partial(closing_kernel, dp), out_shape=(shape((n...  45.6 us
  transfers between devices with their start and end apart: 6, of which 0 were waited for; matrix products, arithmetic and copies ran while one was open for 12% of the time, Pallas kernels for 63%

profile of v9, /device:TPU:0, one launch (start us, length us, event | category | flops | bytes accessed | tf_op | source)
XLA Modules:
  0.0 742.8 jit_solution(10122973060843174669)
XLA Ops:
  7.2 2.3 pad_maximum_fusion
  14.6 89.9 %opening.1 = (bf16[16,128,2048]{2,1,0:T(8,128)(2,1)}, bf16[2,16,64,640]{3,2,1,0:T(8,128)(2,1)}, bf16[2,16,64,256]{3,2,1,0:T(8,128)(2,1)}, bf16[2,64,2048]{2,1,0:...) custom-call(bf16[128,2048]{1,0:T(8,128)(2,1)} %bitcast.144, ...), custom_call_target="tpu_custom_call" | custom-call | bytes 4000000 | tf_op jit(solution)/shard_map/opening/pallas_call | solution.py:518
  104.5 2.2 slice.123
  115.7 16.8 %project.1 = (bf16[2048,2048]{1,0:T(8,128)(2,1)}, bf16[2,1024,256]{2,1,0:T(8,128)(2,1)S(1)}, bf16[2,1024,256]{2,1,0:T(8,128)(2,1)S(1)}, bf16[2,1024,128]{2,1,0:T(8,128)(2,1)S(1)}, bf16[2,1024,512]{2,1,0:T(8,128)(2,1)}) custom-call(bf16[16,128,2048]{2,1,0:T(8,128)(2,1)} %get-tuple-element.79.x_ref, f32[1,2048]{1,0:T(1,128)S(1)} %bitcast.120, ...), custom_call_target="tpu_custom_call" | custom-call | flops 7000000000 | bytes 20000000 | tf_op jit(solution)/shard_map/project/pallas_call | solution.py:1434
  132.5 9.9 %attend.1 = (bf16[16,2,64,2048]{3,2,1,0:T(8,128)(2,1)}, bf16[16,2,64,128]{3,2,1,0:T(8,128)(2,1)S(1)}, f32[2,1024,1]{2,1,0:T(8,128)S(1)}) custom-call(s32[2]{0:T(128)S(1)} %bitcast.123, bf16[2,1024,256]{2,1,0:T(8,128)(2,1)S(1)} %get-tuple-element.82.q_ref, bf16[2,1024,256]{2,1,0:T(8,128)(2,1)S(1)} %get-tuple-element.83.k_ref, ...), custom_call_target="tpu_custom_call" | custom-call | flops 4000000000 | bytes 15000000 | tf_op jit(solution)/shard_map/attend/pallas_call | solution.py:1492
  144.2 52.6 %scatter16.1 = (f32[128,2048]{1,0:T(8,128)}, bf16[2,208,2048]{2,1,0:T(8,128)(2,1)}) custom-call(bf16[16,128,2048]{2,1,0:T(8,128)(2,1)} %bitcast.143, bf16[704,2048]{1,0:T(8,128)(2,1)} %bitcast.131), custom_call_target="tpu_custom_call" | custom-call | bytes 4000000 | tf_op jit(solution)/shard_map/scatter16/pallas_call | solution.py:721
  196.8 2.3 multiply_reduce_fusion.3
  200.1 52.7 %gather16.2 = (bf16[16,128,2048]{2,1,0:T(8,128)(2,1)}, bf16[2,272,2048]{2,1,0:T(8,128)(2,1)}) custom-call(bf16[128,2048]{1,0:T(8,128)(2,1)} %multiply_convert_fusion.x_ref, bf16[704,2048]{1,0:T(8,128)(2,1)} %bitcast.132), custom_call_target="tpu_custom_call" | custom-call | bytes 4000000 | tf_op jit(solution)/shard_map/gather16/pallas_call | solution.py:370
  259.2 75.2 %mixture_forward.1 = (bf16[2048,2048]{1,0:T(8,128)(2,1)}, bf16[1024,2048]{1,0:T(8,128)(2,1)}, bf16[1024,1408]{1,0:T(8,128)(2,1)}, bf16[1024,1408]{1,0:T(8,128)(2...) custom-call(s32[2]{0:T(128)} %bitcast.121, ...), custom_call_target="tpu_custom_call" | custom-call | bytes 4000000 | tf_op jit(solution)/shard_map/mixture_forward/pallas_call | solution.py:1247
  334.3 65.8 %mixture_backward.1 = (bf16[2048,2176]{1,0:T(8,128)(2,1)}, bf16[1024,2048]{1,0:T(8,128)(2,1)}, bf16[1024,1408]{1,0:T(8,128)(2,1)}, bf16[1024,1408]{1,0:T(8,128)(...) custom-call(f32[1,256]{1,0:T(1,128)} %add_convert_fusion.3.pick_ref, bf16[2048,2048]{1,0:T(8,128)(2,1)} %bitcast.129, ...), custom_call_target="tpu_custom_call" | custom-call | bytes 4000000 | tf_op jit(solution)/shard_map/mixture_backward/pallas_call | solution.py:1279
  400.1 11.4 %convolution_convert_fusion = bf16[2048,1408]{1,0:T(8,128)(2,1)} fusion(bf16[1024,2048]{1,0:T(8,128)(2,1)} %get-tuple-element.104, bf16[1024,1408]{1,0:T(8,128)(2,1)} %get-tuple-element.106), kind=kOutput, calls=%fused_computation | convolution fusion | flops 5908463616 | bytes 12845056 | tf_op jit(solution)/shard_map/dot_general | solution.py:1615
  411.6 11.0 %convolution_convert_fusion.1 = bf16[2048,1408]{1,0:T(8,128)(2,1)} fusion(bf16[1024,2048]{1,0:T(8,128)(2,1)} %get-tuple-element.104, bf16[1024,1408]{1,0:T(8,128)(2,1)} %get-tuple-element.105), kind=kOutput, calls=%fused_computation.1 | convolution fusion | flops 5908463616 | bytes 12845056 | tf_op jit(solution)/shard_map/dot_general | solution.py:1615
  422.7 10.5 %convolution_convert_fusion.2 = bf16[1408,2048]{1,0:T(8,128)(2,1)} fusion(bf16[1024,1408]{1,0:T(8,128)(2,1)} %get-tuple-element.102, bf16[1024,2048]{1,0:T(8,128)(2,1)} %get-tuple-element.103), kind=kOutput, calls=%fused_computation.2 | convolution fusion | flops 5908463616 | bytes 12845056 | tf_op jit(solution)/shard_map/dot_general | solution.py:1615
  436.1 2.1 multiply_reduce_fusion.6
  438.2 58.6 %scatter_share.1 = (f32[128,2176]{1,0:T(8,128)}, bf16[2,528,1024]{2,1,0:T(8,128)(2,1)}) custom-call(bf16[16,128,2176]{2,1,0:T(8,128)(2,1)} %bitcast.140, bf16[2048,512]{1,0:T(8,128)(2,1)} %get-tuple-element.108.ds_ref, bf16[2048,256]{1,0:T(8,128)(2,1)} %get-tuple-element.109.sh_ref, bf16[2048,2048]{1,0:T(8,128)(2,1)} %bitcast.128, bf16[2048,2048]{1,0:T(8,128)(2,1)} %bitcast.130), custom_call_target="tpu_custom_call" | custom-call | bytes 4000000 | tf_op jit(solution)/shard_map/scatter_share/pallas_call | solution.py:1372
  502.3 51.0 %gather16.3 = (bf16[16,128,2048]{2,1,0:T(8,128)(2,1)}, bf16[1,528,1024]{2,1,0:T(8,128)(2,1)}) custom-call(bf16[128,2048]{1,0:T(8,128)(2,1)} %fusion.39.x_ref, bf16[2,528,1024]{2,1,0:T(8,128)(2,1)} %get-tuple-element.111.refs_0_), custom_call_target="tpu_custom_call" | custom-call | bytes 4000000 | tf_op jit(solution)/shard_map/gather16/pallas_call | solution.py:370
  553.3 25.4 %attend_back.1 = (bf16[16,2,64,2688]{3,2,1,0:T(8,128)(2,1)}, bf16[2048,256]{1,0:T(8,128)(2,1)}, bf16[128,2048]{1,0:T(8,128)(2,1)}, bf16[512,256]{1,0:T(8,128)(2,1)}) custom-call(s32[2]{0:T(128)} %bitcast.122, bf16[16,2,64,2048]{3,2,1,0:T(8,128)(2,1)} %bitcast.180, bf16[16,2,64,2048]{3,2,1,0:T(8,128)(2,1)} %bitcast.181, bf16[2,1024,256]{2,1,0:T(8,128)(2,1)} %copy-done.6, ...), custom_call_target="tpu_custom_call" | custom-call | flops 14000000000 | bytes 25000000 | tf_op jit(solution)/shard_map/attend_back/pallas_call | solution.py:1584
  581.9 2.5 pad_add_fusion
  584.3 65.8 %returning.1 = (f32[128,2688]{1,0:T(8,128)}, bf16[1,16,64,256]{3,2,1,0:T(8,128)(2,1)}, bf16[1,2,64,2048]{3,2,1,0:T(8,128)(2,1)}) custom-call(bf16[16,128,2688]{2,1,0:T(8,128)(2,1)} %bitcast.138, bf16[2,16,64,256]{3,2,1,0:T(8,128)(2,1)} %bitcast.146, bf16[2,64,2048]{2,1,0:T(8,128)(2,1)} %bitcast.157), custom_call_target="tpu_custom_call" | custom-call | bytes 4000000 | tf_op jit(solution)/shard_map/returning/pallas_call | solution.py:773
  653.6 4.1 fusion.16
  663.3 45.6 %closing.1 = (bf16[128,640]{1,0:T(8,128)(2,1)}, bf16[1,64,640]{2,1,0:T(8,128)(2,1)}, f32[64,3072]{1,0:T(8,128)}, f32[16,4096]{1,0:T(8,128)}, f32[64,2048]{1,0:T(8,128)}) custom-call(bf16[16,128,640]{2,1,0:T(8,128)(2,1)} %bitcast.139, bf16[16,64,256]{2,1,0:T(8,128)(2,1)} %fusion.23.parts_ref, bf16[2,64,2048]{2,1,0:T(8,128)(2,1)} %fusion.20.rows_ref), custom_call_target="tpu_custom_call" | custom-call | bytes 4000000 | tf_op jit(solution)/shard_map/closing/pallas_call | solution.py:888
  718.5 4.7 bitcast_convert_fusion.1
  723.3 4.7 bitcast_convert_fusion.2
  728.0 5.2 bitcast_convert_fusion
  (178 shorter events, 55.5 us)
Async XLA Ops:
  7.2 252.0 %all-gather.11.cloned.1.call-start = ((), (), s32[]{:S(2)}) async-start(), calls=%async_computation.8 | async-start | bytes 3244032 | tf_op jit(solution)/shard_map/all_gather | solution.py:1742
  9.5 249.6 %all-gather.7.cloned.1.call-start = ((), (), s32[]{:S(2)}) async-start(), calls=%async_computation.6 | async-start | bytes 8650752 | tf_op jit(solution)/shard_map/all_gather | solution.py:1740
  10.4 248.8 %all-gather.9.cloned.1.call-start = ((), (), s32[]{:S(2)}) async-start(), calls=%async_computation.7 | async-start | bytes 8650752 | tf_op jit(solution)/shard_map/all_gather | solution.py:1741
  11.1 707.4 %reduce-scatter.6.cloned.1.call-start = ((), (), s32[]{:S(2)}) async-start(), calls=%async_computation.4 | async-start | bytes 8650752 | tf_op jit(solution)/shard_map/reduce_scatter | solution.py:1794
  14.6 97.5 %copy-start.11 = (bf16[2,1,64,2048]{3,2,1,0:T(8,128)(2,1)S(1)}, bf16[2,1,64,2048]{3,2,1,0:T(8,128)(2,1)}, u32[]{:S(2)}) copy-start(bf16[2,1,64,2048]{3,2,1,0:T(8,128)(2,1)} %param.24) | copy-start | bytes 1572868
  104.5 9.9 %copy-start.1 = (bf16[2,16,64,256]{3,2,1,0:T(8,128)(2,1)S(1)}, bf16[2,16,64,256]{3,2,1,0:T(8,128)(2,1)}, u32[]{:S(2)}) copy-start(bf16[2,16,64,256]{3,2,1,0:T(8,128)(2,1)} %get-tuple-element.81) | copy-start | bytes 3145732
  104.5 9.9 %copy-start.4 = (f32[2048,32]{1,0:T(8,128)S(1)}, f32[2048,32]{1,0:T(8,128)}, u32[]{:S(2)}) copy-start(f32[2048,32]{1,0:T(8,128)} %constant.97.clone.cos_ref) | copy-start | bytes 786436
  112.1 20.4 %copy-start = (bf16[512,256]{1,0:T(8,128)(2,1)}, bf16[512,256]{1,0:T(8,128)(2,1)S(1)}, u32[]{:S(2)}) copy-start(bf16[512,256]{1,0:T(8,128)(2,1)S(1)} %reshape.348.we_ref) | copy-start | bytes 786436
  115.7 16.8 %copy-start.2 = (s32[2,1]{0,1:T(1,128)S(1)}, s32[2,1]{0,1:T(1,128)}, u32[]{:S(2)}) copy-start(s32[2,1]{0,1:T(1,128)} %param.26) | copy-start | bytes 28
  115.7 16.8 %copy-start.3 = (bf16[2,64,2048]{2,1,0:T(8,128)(2,1)S(1)}, bf16[2,64,2048]{2,1,0:T(8,128)(2,1)}, u32[]{:S(2)}) copy-start(bf16[2,64,2048]{2,1,0:T(8,128)(2,1)} %get-tuple-element.85) | copy-start | bytes 1572868
  132.5 9.9 %copy-start.6 = (bf16[2,1024,256]{2,1,0:T(8,128)(2,1)}, bf16[2,1024,256]{2,1,0:T(8,128)(2,1)S(1)}, u32[]{:S(2)}) copy-start(bf16[2,1024,256]{2,1,0:T(8,128)(2,1)S(1)} %get-tuple-element.82.q_ref) | copy-start | bytes 3145732
  132.5 9.9 %copy-start.7 = (bf16[2,1024,256]{2,1,0:T(8,128)(2,1)}, bf16[2,1024,256]{2,1,0:T(8,128)(2,1)S(1)}, u32[]{:S(2)}) copy-start(bf16[2,1024,256]{2,1,0:T(8,128)(2,1)S(1)} %get-tuple-element.83.k_ref) | copy-start | bytes 3145732
  132.5 9.9 %copy-start.9 = (bf16[2,1024,128]{2,1,0:T(8,128)(2,1)}, bf16[2,1024,128]{2,1,0:T(8,128)(2,1)S(1)}, u32[]{:S(2)}) copy-start(bf16[2,1024,128]{2,1,0:T(8,128)(2,1)S(1)} %get-tuple-element.84.v_ref) | copy-start | bytes 1572868
  144.2 52.6 %copy-start.12 = (bf16[2,1,64,2048]{3,2,1,0:T(8,128)(2,1)S(1)}, bf16[2,1,64,2048]{3,2,1,0:T(8,128)(2,1)}, u32[]{:S(2)}) copy-start(bf16[2,1,64,2048]{3,2,1,0:T(8,128)(2,1)} %param.24) | copy-start | bytes 1572868
  252.8 5.4 copy-start.14
  411.5 311.7 %reduce-scatter.4.cloned.1.call-start = ((), (), s32[]{:S(2)}) async-start(), calls=%async_computation.3 | async-start | bytes 8650752 | tf_op jit(solution)/shard_map/reduce_scatter | solution.py:1793
  422.6 305.4 %reduce-scatter.8.cloned.1.call-start = ((), (), s32[]{:S(2)}) async-start(), calls=%async_computation.5 | async-start | bytes 8650752 | tf_op jit(solution)/shard_map/reduce_scatter | solution.py:1792
  496.8 4.3 copy-start.15
  653.6 4.1 copy-start.19
  653.6 4.1 copy-start.27
  709.8 5.5 copy-start.28
  728.0 5.3 copy-start.22
  728.0 6.1 copy-start.30
  728.0 6.8 copy-start.24
  (20 other events, 38.9 us)
Sparse Core Ops, SparseCore 0:
  10.1 55.1 all-gather.10
  66.9 71.1 all-gather.6
  139.6 112.8 all-gather.8
  411.7 69.4 reduce-scatter.5
  484.0 94.5 reduce-scatter.3
  580.7 91.7 reduce-scatter.7

commit v10 on v9

--- a/solution.py
+++ b/solution.py
@@ -350,9 +350,9 @@
         job = side_job(dp, span, src, out, sems[ng:])
     g = Gather(x_ref, o_ref, chunks, sems[:ng])
     enter(g.me, g.z, g.core, g.side, 1 if job is None else dp)
-    g.start()
     if job is not None:
         job.start()
+    g.start()
     for s in range(1, NZ + 1):
         g.round(s)
     g.finish()
@@ -382,7 +382,7 @@
 
 
 def opening_kernel(dp, chunks, x_ref, small_ref, parts_ref, out_ref,
-                   x_all, small_all, parts_head, out_head, small_dp, parts_dp, out_dp, *sems):
+                   x_all, small_all, parts_head, out_head, small_dp, out_dp, *sems):
     ng = Gather.COUNT
     gx = Gather(x_ref, x_all, chunks, sems[:ng])
     gs = Gather(small_dp, small_all, 1, sems[ng:2 * ng], lambda ref, b: ref.at[:, b])
@@ -390,30 +390,49 @@
     me = gx.me
     plane = lax.axis_index("dp")
     enter_all(me, plane, dp)
-    pairs = ((small_ref, small_dp.at[plane]), (parts_ref, parts_dp.at[plane]),
-             (out_ref, out_dp.at[plane]))
+    pairs = ((small_ref, small_dp), (out_ref, out_dp), (parts_head.at[plane], parts_head))
 
     def lift(i, r):
         src, dst = pairs[i]
         return pltpu.make_async_remote_copy(
-            src_ref=src, dst_ref=dst, send_sem=ys.at[i, r], recv_sem=yr.at[i, r],
+            src_ref=src, dst_ref=dst.at[plane], send_sem=ys.at[i, r], recv_sem=yr.at[i, r],
             device_id={"dp": (plane + r) % dp}, device_id_type=MESH)
 
     def landed(i, r):
         p = (plane - r + dp) % dp
-        dst = (small_dp.at[p], parts_dp.at[p], out_dp.at[p])[i]
+        dst = pairs[i][1].at[p]
         return pltpu.make_async_remote_copy(
             src_ref=dst, dst_ref=dst, send_sem=ys.at[i, r], recv_sem=yr.at[i, r],
             device_id={"dp": p}, device_id_type=MESH)
 
     def kept(i):
         src, dst = pairs[i]
-        return pltpu.make_async_copy(src, dst, loc.at[i])
-
-    for i in range(3):
+        return pltpu.make_async_copy(src, dst.at[plane], loc.at[i])
+
+    def part(r):
+        h = (me + r) % NE
+        return pltpu.make_async_remote_copy(
+            src_ref=parts_ref.at[h], dst_ref=parts_head.at[plane, me],
+            send_sem=ps.at[r], recv_sem=pr.at[r],
+            device_id={"expert": h}, device_id_type=MESH)
+
+    def part_in(r):
+        e = (me - r + NE) % NE
+        return pltpu.make_async_remote_copy(
+            src_ref=parts_head.at[plane, e], dst_ref=parts_head.at[plane, e],
+            send_sem=ps.at[r], recv_sem=pr.at[r],
+            device_id={"expert": e}, device_id_type=MESH)
+
+    def part_kept():
+        return pltpu.make_async_copy(parts_ref.at[me], parts_head.at[plane, me], pl_sem)
+
+    for i in range(2):
         for r in range(1, dp):
             lift(i, r).start()
         kept(i).start()
+    for r in range(1, NE):
+        part(r).start()
+    part_kept().start()
     gx.start()
     gx.round(1)
 
@@ -422,29 +441,11 @@
         landed(0, r).wait_recv()
     gs.start()
 
-    def part(r):
-        h = (me + r) % NE
-        return pltpu.make_async_remote_copy(
-            src_ref=parts_dp.at[:, h], dst_ref=parts_head.at[:, me],
-            send_sem=ps.at[r], recv_sem=pr.at[r],
-            device_id={"expert": h}, device_id_type=MESH)
-
-    def part_in(r):
-        e = (me - r + NE) % NE
-        return pltpu.make_async_remote_copy(
-            src_ref=parts_head.at[:, e], dst_ref=parts_head.at[:, e],
-            send_sem=ps.at[r], recv_sem=pr.at[r],
-            device_id={"expert": e}, device_id_type=MESH)
-
-    def part_kept():
-        return pltpu.make_async_copy(parts_dp.at[:, me], parts_head.at[:, me], pl_sem)
-
-    kept(1).wait()
+    for r in range(1, NE):
+        part_in(r).wait_recv()
+    part_kept().wait()
     for r in range(1, dp):
-        landed(1, r).wait_recv()
-    for r in range(1, NE):
-        part(r).start()
-    part_kept().start()
+        lift(2, r).start()
     gx.round(2)
 
     def row(d):
@@ -458,9 +459,9 @@
         b = NE * d + me
         return pltpu.make_async_copy(out_dp.at[d], out_head.at[b % dp], ol_sem.at[d])
 
-    kept(2).wait()
+    kept(1).wait()
     for r in range(1, dp):
-        landed(2, r).wait_recv()
+        landed(1, r).wait_recv()
     for d in range(dp):
         home = (NE * d + me) // dp
 
@@ -485,9 +486,7 @@
             device_id={"expert": gx.core}, device_id_type=MESH)
 
     for r in range(1, NE):
-        part_in(r).wait_recv()
         part(r).wait_send()
-    part_kept().wait()
     for j in range(dp):
         @pl.when((dp * me + j) % NE != me)
         def _():
@@ -502,6 +501,8 @@
         @pl.when(home == me)
         def _():
             row_kept(d).wait()
+    for r in range(1, dp):
+        landed(2, r).wait_recv()
     for i in range(3):
         for r in range(1, dp):
             lift(i, r).wait_send()
@@ -520,12 +521,12 @@
         out_shape=(
             shape((NE,) + x.shape, bf), shape((dp, NE, rows, ws), bf), shape((dp, NE) + parts.shape[1:], bf),
             shape((dp, rows, wo), bf),
-            shape((dp, rows, ws), bf), shape((dp,) + parts.shape, bf), shape((dp, rows, wo), bf),
+            shape((dp, rows, ws), bf), shape((dp, rows, wo), bf),
         ),
         in_specs=[ANY] * 4,
-        out_specs=[ANY] * 7,
+        out_specs=[ANY] * 6,
         scratch_shapes=Gather.scratch(chunks) + Gather.scratch(1) + [
-            dma((3,)), dma((3, dp)), dma((3, dp)), dma((NE,)), dma((NE,)), dma((dp,)), dma((dp,)), dma, dma((dp,))],
+            dma((2,)), dma((3, dp)), dma((3, dp)), dma((NE,)), dma((NE,)), dma((dp,)), dma((dp,)), dma, dma((dp,))],
         compiler_params=pltpu.CompilerParams(collective_id=cid, has_side_effects=True),
         cost_estimate=COST,
         name="opening",
@@ -703,9 +704,9 @@
         job = side_job(dp, span, src, out, scratch[ns:])
     s = Scatter(p_ref, o_ref, chunks, scratch[:ns])
     enter(s.me, s.z, s.core, s.side, 1 if job is None else dp)
-    s.start()
     if job is not None:
         job.start()
+    s.start()
     s.run()
     s.finish()
     if job is not None:
@@ -747,12 +748,12 @@
             src_ref=rows_ref, dst_ref=rows_far.at[r - 1], send_sem=rs.at[r], recv_sem=rr.at[r],
             device_id={"dp": (plane + r) % dp}, device_id_type=MESH)
 
-    s.start()
     swap.start()
     for r in range(1, dp):
         @pl.when((plane + r) % dp == keeper)
         def _():
             row(r).start()
+    s.start()
     s.run()
     s.finish()
     swap.finish()
@@ -955,45 +956,39 @@
     down[SHARE:] = pad
 
 
-def mine_of(routes_ref, pick_ref):
-    tokens = routes_ref.shape[0]
-    lane16 = lax.broadcasted_iota(jnp.int32, (tokens, 16), 1)
-    mask = lane16 < 0
-    for k in range(routes_ref.shape[1]):
-        mask = mask | (lane16 == routes_ref[:, k:k + 1])
-    mine = jnp.sum(jnp.where(mask, pick_ref[:, :16], 0.0), axis=1, keepdims=True)
-    return mask, mine
-
-
 def valid_of(len_ref, first_device, tokens, batches, here):
     n = lax.broadcasted_iota(jnp.int32, (tokens, 1), 0)
-    device = n // (batches * here)
-    batch = (n // here) % batches
-    position = (first_device + device) * here + n % here
+    if here & (here - 1) or batches & (batches - 1):
+        device, batch, place_in = n // (batches * here), (n // here) % batches, n % here
+    else:
+        bits, more = here.bit_length() - 1, (batches * here).bit_length() - 1
+        device, batch, place_in = n >> more, (n >> bits) & (batches - 1), n & (here - 1)
+    position = (first_device + device) * here + place_in
     length = jnp.zeros((tokens, 1), jnp.int32)
     for b in range(batches):
         length = jnp.where(batch == b, len_ref[b], length)
     return (position < length).astype(F32)
 
 
-def one_hots(taken, groups, slots, here):
-    r = lax.broadcasted_iota(jnp.int32, (256, 256), 0)
-    c = lax.broadcasted_iota(jnp.int32, (256, 256), 1)
-    same = r // here == c // here
-    before = (same & (c < r)).astype(BF)
-    after = (same & (r < c)).astype(BF)
-    base_c = (lax.broadcasted_iota(jnp.int32, (256, slots), 0) // here * 32).astype(F32)
-    base_r = (lax.broadcasted_iota(jnp.int32, (slots, 256), 1) // here * 32).astype(F32)
+def slot_tables(here, slots=128):
+    n = np.arange(256)
+    same = n[:, None] // here == n[None, :] // here
+    before = same & (n[None, :] < n[:, None])
+    tables = np.stack([before, before.T, np.eye(256, dtype=bool)]).astype(np.float32)
+    base = np.broadcast_to((n // here * 32)[:, None], (256, slots)).astype(np.float32)
+    return jnp.asarray(tables, BF), jnp.asarray(base), jnp.asarray(base.T)
+
+
+def one_hots(taken, tables, base_c, base_r, groups, slots):
     lane = lax.broadcasted_iota(jnp.int32, (256, slots), 1).astype(F32)
     row = lax.broadcasted_iota(jnp.int32, (slots, 256), 0).astype(F32)
-    ones = jnp.ones((256, slots), BF)
     to_slot, to_token = [], []
     for g in range(groups):
         t = jnp.broadcast_to(taken[g * 256:(g + 1) * 256], (256, slots))
         low = t.astype(BF)
-        place_c = mm(before, low) + base_c
-        place_r = mm_lead(low, after) + base_r
-        taken_r = mm_lead(low, (r == c).astype(BF))
+        place_c = mm(tables[0], low) + base_c[...]
+        place_r = mm_lead(low, tables[1]) + base_r[...]
+        taken_r = mm_lead(low, tables[2])
         to_token.append(jnp.where((place_c == lane) & (t > 0.5), 1.0, 0.0).astype(BF))
         to_slot.append(jnp.where((place_r == row) & (taken_r > 0.5), 1.0, 0.0).astype(BF))
     return to_slot, to_token
@@ -1017,11 +1012,11 @@
         body(total // WIDE * WIDE, total % WIDE)
 
 
-def forward_kernel(chunks, dp, span, batches, here, len_ref, pick_ref, mix_ref, routes_ref, wg_ref, wu_ref, router_ref,
+def forward_kernel(chunks, dp, span, batches, here, len_ref, pick_ref, mix_ref, mask_ref, tab_ref, basec_ref, baser_ref, wg_ref, wu_ref, router_ref,
                    share_ref, wda_ref, wdb_ref, down_ref, dy_ref,
                    out_ref, rows_ref, hid_ref, act_ref, slo_ref, eo_ref, sh_ref, sact_ref, sslo_ref, gate_ref,
-                   dy_all, wdc_ref,
-                   wd_ref, fan_ref, sd_ref, hid_buf, sh_buf, gate_buf, taken_buf, wd_sem, sh_sem, *sems):
+                   slot_ref, token_ref, dy_all, wdc_ref,
+                   wd_ref, fan_ref, sd_ref, hid_buf, sh_buf, gate_buf, token_buf, wd_sem, sh_sem, *sems):
     step = pl.program_id(0)
     tokens, width = mix_ref.shape
     groups, slots = tokens // 256, 128
@@ -1035,8 +1030,8 @@
     @pl.when(step == 0)
     def _():
         enter(g.me, g.z, g.core, g.side, dp)
+        job.start()
         g.start()
-        job.start()
         copies = share_copies(share_ref, fan_ref, sd_ref, sh_sem)
         for copy in copies + down_copies(parts, wd_ref, wd_sem, 0) + down_copies(parts, wd_ref, wd_sem, 1):
             copy.start()
@@ -1058,16 +1053,18 @@
         sact_ref[...] = s_act.astype(BF)
         sslo_ref[...] = (s_up * s_slope).astype(BF)
         logits = fanned[:, SHARE:SHARE + 16]
-        mask, mine = mine_of(routes_ref, pick_ref)
-        taken = mine * valid_of(len_ref, step * (tokens // (batches * here)), tokens, batches, here)
-        held = jnp.where(mask, logits, -1e30)
-        raised = jnp.where(mask, jnp.exp(held - jnp.max(held, axis=1, keepdims=True)), 0.0)
-        soft = raised / jnp.sum(raised, axis=1, keepdims=True)
-        gate = jnp.sum(soft * pick_ref[:, :16], axis=1, keepdims=True) * taken
-        gate_ref[...] = jnp.concatenate([gate, taken], axis=1)
+        mask = mask_ref[...].astype(F32)
+        taken = jnp.sum(mask * pick_ref[:, :16], axis=1, keepdims=True) * valid_of(len_ref, step * (tokens // (batches * here)), tokens, batches, here)
+        held = jnp.where(mask > 0.5, logits, -1e30)
+        raised = jnp.exp(held - jnp.max(held, axis=1, keepdims=True)) * mask
+        gate = jnp.sum(raised * pick_ref[:, :16], axis=1, keepdims=True) / jnp.sum(raised, axis=1, keepdims=True) * taken
+        gate_ref[...] = gate
         gate_buf[at] = gate
-        taken_buf[at] = taken
-        to_slot, _ = one_hots(taken, groups, slots, here)
+        to_slot, to_token = one_hots(taken, tab_ref, basec_ref, baser_ref, groups, slots)
+        for n in range(groups):
+            slot_ref[n * slots:(n + 1) * slots] = to_slot[n]
+            token_ref[n * 256:(n + 1) * 256] = to_token[n]
+            token_buf[pl.ds(pl.multiple_of(step * tokens + n * 256, 256), 256)] = to_token[n]
 
         def dispatch(j, _):
             for n in range(groups):
@@ -1107,7 +1104,7 @@
         rows_at = pl.ds(pl.multiple_of(tile * half, half), half)
         gate = gate_buf[at]
         s_hidden = sh_buf[at]
-        _, to_token = one_hots(taken_buf[at], groups, slots, here)
+        to_token = [token_buf[pl.ds(pl.multiple_of(tile * tokens + n * 256, 256), 256)] for n in range(groups)]
 
         def fan_out(j, _):
             eo = mm(hid_buf[rows_at], wd_ref[:, lanes(j)]).astype(BF)
@@ -1120,7 +1117,7 @@
 
         lax.fori_loop(0, width // WIDE, fan_out, 0)
 
-    for r, s in ((1, 1), (2, 2), (3, 4), (4, 6)):
+    for r, s in ((1, 1), (2, 2), (3, 3), (4, 5)):
         @pl.when(step == s)
         def _():
             g.round(r)
@@ -1130,8 +1127,8 @@
         g.finish()
 
 
-def backward_kernel(here, chunks, pick_ref, dy_ref, wg_ref, wu_ref, share_ref, wda_ref, wdb_ref, wdc_ref,
-                    act_ref, slo_ref, eo_ref, sact_ref, sslo_ref, gate_ref, part_ref,
+def backward_kernel(chunks, pick_ref, dy_ref, wg_ref, wu_ref, share_ref, wda_ref, wdb_ref, wdc_ref,
+                    act_ref, slo_ref, eo_ref, sact_ref, sslo_ref, gate_ref, slot_ref, token_ref, part_ref,
                     dh_ref, deo_ref, dg_ref, du_ref, ds_ref, sum_ref,
                     wd_ref, fan_ref, sd_ref, wd_sem, sh_sem, *scratch):
     step = pl.program_id(0)
@@ -1157,8 +1154,9 @@
     d_s = jnp.concatenate([(d_sh * sslo_ref[...].astype(F32)).astype(BF),
                            (d_sh * sact_ref[...].astype(F32)).astype(BF)], axis=1)
     ds_ref[...] = d_s
-    gate, taken = gate_ref[:, :1], gate_ref[:, 1:]
-    to_slot, to_token = one_hots(taken, groups, slots, here)
+    gate = gate_ref[...]
+    to_slot = [slot_ref[n * slots:(n + 1) * slots] for n in range(groups)]
+    to_token = [token_ref[n * 256:(n + 1) * 256] for n in range(groups)]
 
     @pl.when(step == 0)
     def _():
@@ -1229,11 +1227,12 @@
 SMEM = pl.BlockSpec(memory_space=pltpu.SMEM)
 
 
-def mixture_forward(dp, batches, here, lengths, pick, mix, routes, wg, wu, router, share, wda, wdb, span, down, dy, cid,
+def mixture_forward(dp, batches, here, lengths, pick, mix, mask, wg, wu, router, share, wda, wdb, span, down, dy, cid,
                     chunks=2):
     total, width = mix.shape
     step, half = total // 4, total // 8
     ff = wg.shape[1]
+    tables = slot_tables(here)
     shape = jax.ShapeDtypeStruct
     rows = total // 2
     dma = pltpu.SemaphoreType.DMA
@@ -1250,24 +1249,26 @@
         out_shape=(
             shape((total, width), BF), shape((rows, width), BF), shape((rows, ff), BF), shape((rows, ff), BF),
             shape((rows, ff), BF), shape((rows, width), BF), shape((total, TILE), BF), shape((total, TILE), BF),
-            shape((total, TILE), BF), shape((total, 2), F32), shape((NE,) + dy.shape, BF),
+            shape((total, TILE), BF), shape((total, 1), F32), shape((rows, 256), BF), shape((total, 128), BF),
+            shape((NE,) + dy.shape, BF),
             shape((dp, span[1], width), BF)),
-        in_specs=[SMEM, whole(pick), early(step, width), early(step, routes.shape[1]), whole(wg), whole(wu),
+        in_specs=[SMEM, whole(pick), early(step, width), early(step, mask.shape[1])] + [whole(v) for v in tables] + [whole(wg), whole(wu),
                   whole(router), ANY, ANY, ANY, ANY, ANY],
         out_specs=[late(step, width), early(half, width), early(half, ff), early(half, ff), early(half, ff),
-                   late(half, width), early(step, TILE), early(step, TILE), early(step, TILE), early(step, 2), ANY, ANY],
+                   late(half, width), early(step, TILE), early(step, TILE), early(step, TILE), early(step, 1),
+                   early(half, 256), early(step, 128), ANY, ANY],
         scratch_shapes=[
             pltpu.VMEM((ff, width), BF), pltpu.VMEM((2 * TILE, width), BF), pltpu.VMEM((TILE, width), BF),
             pltpu.VMEM((rows, ff), BF), pltpu.VMEM((total, TILE), BF), pltpu.VMEM((total, 1), F32),
-            pltpu.VMEM((total, 1), F32), dma((3 * dp,)), dma((3 * dp,))] + Gather.scratch(chunks) + Spread.scratch(dp),
+            pltpu.VMEM((total, 128), BF), dma((3 * dp,)), dma((3 * dp,))] + Gather.scratch(chunks) + Spread.scratch(dp),
         compiler_params=pltpu.CompilerParams(
             collective_id=cid, has_side_effects=True, vmem_limit_bytes=60 * 1024 * 1024),
         cost_estimate=COST,
         name="mixture_forward",
-    )(lengths, pick, mix, routes, wg, wu, router, share, wda, wdb, down, dy)
-
-
-def mixture_backward(here, pick, dy, wg, wu, share, wda, wdb, wdc, act, slo, eo, sact, sslo, gate, part, cid, chunks=2):
+    )(lengths, pick, mix, mask, *tables, wg, wu, router, share, wda, wdb, down, dy)
+
+
+def mixture_backward(pick, dy, wg, wu, share, wda, wdb, wdc, act, slo, eo, sact, sslo, gate, slot, token, part, cid, chunks=2):
     total, width = dy.shape
     step, half = total // NZ, total // NZ // 2
     ff = wg.shape[1]
@@ -1277,14 +1278,14 @@
     _, own, _ = part.shape
     dma = pltpu.SemaphoreType.DMA
     return pl.pallas_call(
-        functools.partial(backward_kernel, here, chunks),
+        functools.partial(backward_kernel, chunks),
         grid=(NZ,),
         out_shape=(
             shape((total, width + 128), BF), shape((rows, width), BF), shape((rows, ff), BF), shape((rows, ff), BF),
             shape((total, 2 * TILE), BF), shape((own, width), F32)),
         in_specs=[whole(pick), tiles(step, width), whole(wg), whole(wu), ANY, ANY, ANY, ANY,
                   tiles(half, ff), tiles(half, ff), tiles(half, width), tiles(step, TILE), tiles(step, TILE),
-                  tiles(step, 2), ANY],
+                  tiles(step, 1), tiles(half, 256), tiles(step, 128), ANY],
         out_specs=[tiles(step, width + 128), tiles(half, width), tiles(half, ff), tiles(half, ff),
                    tiles(step, 2 * TILE), pl.BlockSpec((own, width), lambda i: (0, 0))],
         scratch_shapes=[
@@ -1294,7 +1295,7 @@
             collective_id=cid, has_side_effects=True, vmem_limit_bytes=62 * 1024 * 1024),
         cost_estimate=COST,
         name="mixture_backward",
-    )(pick, dy, wg, wu, share, wda, wdb, wdc, act, slo, eo, sact, sslo, gate, part)
+    )(pick, dy, wg, wu, share, wda, wdb, wdc, act, slo, eo, sact, sslo, gate, slot, token, part)
 
 
 class ShareWork:
@@ -1356,30 +1357,110 @@
             self.out[d, 2 * n:] = self.gsd[:n, cols].astype(BF)
 
 
-def scatter_share_kernel(chunks, p_ref, ds_ref, sh_ref, mix_ref, dy_ref, o_ref, g_ref, *scratch):
-    s = Scatter(p_ref, o_ref, chunks, scratch[:Scatter.COUNT])
-    work = ShareWork(ds_ref, sh_ref, mix_ref, dy_ref, g_ref, scratch[Scatter.COUNT:])
-    enter(s.me, s.z, s.core, s.side)
+class WeightWork:
+    COUNT = 6
+    ROWS = 256
+
+    def __init__(self, lhs, rhs, outs, scratch):
+        self.sources, self.outs = (lhs,) + tuple(rhs), outs
+        *self.held, self.buf, self.in_sem, self.out_sem = scratch
+        self.steps = lhs.shape[1] // self.ROWS
+
+    @staticmethod
+    def scratch(lhs, rhs):
+        dma = pltpu.SemaphoreType.DMA
+        return [pltpu.VMEM(v.shape, BF) for v in (lhs,) + tuple(rhs)] + [
+            pltpu.VMEM((2, WeightWork.ROWS, rhs[0].shape[1]), BF), dma((3,)), dma((2,))]
+
+    def loads(self):
+        return [pltpu.make_async_copy(v, held, self.in_sem.at[i])
+                for i, (v, held) in enumerate(zip(self.sources, self.held))]
+
+    def start(self):
+        for copy in self.loads():
+            copy.start()
+
+    def ready(self):
+        for copy in self.loads():
+            copy.wait()
+
+    def store(self, p, n):
+        at = pl.ds(pl.multiple_of(n * self.ROWS, self.ROWS), self.ROWS)
+        return pltpu.make_async_copy(self.buf.at[p], self.outs[p].at[at], self.out_sem.at[p])
+
+    def step(self, begin, end):
+        def body(n, _):
+            left = self.held[0][:, pl.ds(pl.multiple_of(n * self.ROWS, self.ROWS), self.ROWS)]
+            for p in range(2):
+                @pl.when(n > 0)
+                def _():
+                    self.store(p, n - 1).wait()
+
+                rhs = self.held[1 + p]
+                width = rhs.shape[1]
+                for at in range(0, width, WIDE):
+                    size = min(WIDE, width - at)
+                    self.buf[p, :, at:at + size] = mm_lead(left, rhs[:, at:at + size]).astype(BF)
+                self.store(p, n).start()
+            return 0
+
+        lax.fori_loop(begin, end, body, 0)
+
+    def finish(self):
+        for p in range(2):
+            self.store(p, self.steps - 1).wait()
+
+
+def scatter_share_kernel(chunks, dp, p_ref, ds_ref, sh_ref, mix_ref, dy_ref, rows_ref, dg_ref, du_ref, down_ref,
+                         o_ref, g_ref, ggate_ref, gup_ref, far_ref, *scratch):
+    ns, nw = Scatter.COUNT, ShareWork.COUNT
+    s = Scatter(p_ref, o_ref, chunks, scratch[:ns])
+    share = ShareWork(ds_ref, sh_ref, mix_ref, dy_ref, g_ref, scratch[ns:ns + nw])
+    work = WeightWork(rows_ref, (dg_ref, du_ref), (ggate_ref, gup_ref), scratch[ns + nw:-2])
+    swap = Swap(dp, down_ref, far_ref, scratch[-2:])
+    enter(s.me, s.z, s.core, s.side, dp)
+    swap.start()
     s.start()
     work.start()
-    s.run(work.step)
+    share.start()
+    s.first(0)
+    s.first(1)
+    work.ready()
+    third = work.steps // 3
+    work.step(0, third)
+    s.second(0)
+    s.first(2)
+    s.first(3)
+    work.step(third, 2 * third)
+    s.second(1)
+    work.step(2 * third, work.steps)
+    s.second(2)
     work.finish()
+    while share.done < share.steps:
+        share.step()
+    s.second(3)
+    share.finish()
     s.finish()
-
-
-def scatter_share(p, ds, sh, mix, dy, share_shape, cid, chunks=2):
-    _, rows, width = p.shape
+    swap.finish()
+
+
+def scatter_share(p, ds, sh, mix, dy, rows, dg, du, down, share_shape, cid, chunks=2):
+    _, n, width = p.shape
+    shape = jax.ShapeDtypeStruct
+    grad = shape((rows.shape[1], dg.shape[1]), BF)
     return pl.pallas_call(
-        functools.partial(scatter_share_kernel, chunks),
-        out_shape=(jax.ShapeDtypeStruct((rows, width), F32), jax.ShapeDtypeStruct(share_shape, BF)),
-        in_specs=[ANY] * 5,
-        out_specs=(VMEM, VMEM),
-        scratch_shapes=Scatter.scratch(rows, width, chunks, p.dtype) + ShareWork.scratch(mix.shape[1]),
+        functools.partial(scatter_share_kernel, chunks, down.shape[0]),
+        out_shape=(shape((n, width), F32), shape(share_shape, BF), grad, grad,
+                   shape((down.shape[0] - 1,) + down.shape[1:], BF)),
+        in_specs=[ANY] * 9,
+        out_specs=(VMEM, VMEM, ANY, ANY, ANY),
+        scratch_shapes=Scatter.scratch(n, width, chunks, p.dtype) + ShareWork.scratch(mix.shape[1])
+        + WeightWork.scratch(rows, (dg, du)) + Swap.scratch(down.shape[0]),
         compiler_params=pltpu.CompilerParams(
             collective_id=cid, has_side_effects=True, vmem_limit_bytes=60 * 1024 * 1024),
         cost_estimate=COST,
         name="scatter_share",
-    )(p, ds, sh, mix, dy)
+    )(p, ds, sh, mix, dy, rows, dg, du, down)
 
 
 def turn(v, cosine, sine):
@@ -1698,10 +1779,9 @@
     rows_l = expand_weight.shape[0]
 
     x_own = layer_input.reshape(own, width)
-    routes_own = routes.reshape(own, -1)
-    choices = routes_own.shape[1]
-    route_columns = routes_own.astype(BF).reshape(rows_w, -1)
-    small_width = -(-(595 + route_columns.shape[1]) // 128) * 128
+    mask_own = selected_experts(routes.reshape(own, -1))
+    mask_columns = mask_own.astype(BF).reshape(rows_w, -1)
+    small_width = -(-(595 + mask_columns.shape[1]) // 128) * 128
     latent_column = jnp.zeros((rows_w,), BF).at[:rows_l].set(latent_gain)
     small = jnp.concatenate(
         [
@@ -1710,8 +1790,8 @@
             attn_gain[:, None],
             mixer_gain[:, None],
             latent_column[:, None],
-            route_columns,
-            jnp.zeros((rows_w, small_width - 595 - route_columns.shape[1]), BF),
+            mask_columns,
+            jnp.zeros((rows_w, small_width - 595 - mask_columns.shape[1]), BF),
         ],
         axis=1,
     )
@@ -1721,8 +1801,8 @@
     parts = jnp.concatenate([query_parts, expand_parts], axis=2)
     x_all, small, parts_head, output_head = opening(dp, x_own, small, parts, output_weight, 1)
     x_all = x_all.reshape(total, width)
-    routes_all = lax.dynamic_index_in_dim(small, plane, 0, False)[..., 595 : 595 + route_columns.shape[1]]
-    routes_all = routes_all.reshape(total, choices).astype(jnp.int32)
+    mask_all = lax.dynamic_index_in_dim(small, plane, 0, False)[..., 595 : 595 + mask_columns.shape[1]]
+    mask_all = mask_all.reshape(total, GROUPS)
     small = small.reshape(width, small_width)
     parts_head = parts_head.reshape(width, TILE)
     latent_full = small[:, :576]
@@ -1773,27 +1853,26 @@
 
     lane = jnp.arange(128)[None, :]
     pick = jnp.concatenate([lane == me, lane == me + GROUPS], axis=1).astype(F32)
-    (out_part, rows, hidden, act, slope, result, share_hidden, share_act, share_slope, gates, grad_all,
-     down_c) = mixture_forward(
-        dp, batches, here, seq_lengths, pick, mix_all, routes_all, gate_full, up_full, router_full.T, share_full,
+    (out_part, rows, hidden, act, slope, result, share_hidden, share_act, share_slope, gates, to_slot, to_token,
+     grad_all, down_c) = mixture_forward(
+        dp, batches, here, seq_lengths, pick, mix_all, mask_all, gate_full, up_full, router_full.T, share_full,
         down_a, down_b, spans[2], down_own, grad_own, 4)
     grad_all = grad_all.reshape(total, width)
     mix_part, grad_result, grad_gate_in, grad_up_in, grad_share_in, mixed = mixture_backward(
-        here, pick, grad_all, gate_full, up_full, share_full, down_a, down_b, down_c, act, slope, result,
-        share_act, share_slope, gates, out_part.reshape(GROUPS, own, width), 8)
+        pick, grad_all, gate_full, up_full, share_full, down_a, down_b, down_c, act, slope, result,
+        share_act, share_slope, gates, to_slot, to_token, out_part.reshape(GROUPS, own, width), 8)
     grad_down = product_lead(hidden, grad_result).astype(BF)
-    grad_gate = product_lead(rows, grad_gate_in).astype(BF)
-    grad_up = product_lead(rows, grad_up_in).astype(BF)
-    mix_part, _, _, _ = lax.optimization_barrier((mix_part, grad_down, grad_gate, grad_up))
-    mix_sum, grad_share = scatter_share(
-        mix_part.reshape(GROUPS, own, width + 128), grad_share_in, share_hidden, mix_all, grad_all, share_full.shape, 5)
+    grad_down = grad_down.reshape(dp, ff // dp, width)
+    mix_sum, grad_share, grad_gate, grad_up, far_down = scatter_share(
+        mix_part.reshape(GROUPS, own, width + 128), grad_share_in, share_hidden, mix_all, grad_all,
+        rows, grad_gate_in, grad_up_in, grad_down, share_full.shape, 5)
+    out_down = lax.dynamic_index_in_dim(grad_down, plane, 0, False).astype(F32)
+    out_down = out_down + jnp.sum(far_down.astype(F32), axis=0)
     layer_output = valid_own[:, None] * (middle + mixed)
 
-    out_down = lax.psum_scatter(grad_down, "dp", scatter_dimension=0, tiled=True)
     out_gate = lax.psum_scatter(grad_gate, "dp", scatter_dimension=0, tiled=True)
     out_up = lax.psum_scatter(grad_up, "dp", scatter_dimension=0, tiled=True)
 
-    mask_own = selected_experts(routes_own)
     soft_own = masked_softmax(product(hidden_mix, router_full), mask_own)
     grad_masked = (mix_sum[:, width : width + GROUPS] + mix_sum[:, width + GROUPS : width + 2 * GROUPS])
     grad_masked = grad_masked * valid_own[:, None]
@@ -1863,7 +1942,7 @@
         small_sum[:, 576:592],
         out_gate.astype(F32)[None],
         out_up.astype(F32)[None],
-        out_down.astype(F32)[None],
+        out_down[None],
         out_share[:share_width].T,
         out_share[share_width : 2 * share_width].T,
         out_share[2 * share_width :],

time: 747 us -> 719 us (0.963)
  matrix products: 44.5 us -> 22.6 us
    dot_general x4 -> x2, matrix products: 34.7 us -> 12.7 us  [product_lead(): lax.dot_general(left_side, right_side, (((0,), (0,)), ((), ())), preferre...]
    pallas_call x2, Pallas kernels: 124 us -> 135 us  [the longest x1 67.9 us: mixture_backward(): pl.pallas_call(functools.partial(backward_kernel, chunks), grid=(NZ,), ou...]
    pallas_call x1, Pallas kernels: 89.9 us -> 80.6 us  [opening(): pl.pallas_call(functools.partial(opening_kernel, dp, chunks), out_shape=(...]
  transfers between devices with their start and end apart: 6 -> 5, of which waited for: 0 -> 0; matrix products, arithmetic and copies ran while one was open for 12% -> 10% of each run, Pallas kernels for 63% -> 56%
where the time goes in v10:
time: 719 us; the launch traced here: 715 us
  Pallas kernels  605 us (84%)
  other arithmetic  40 us (6%)
  local copies, waits for them, and re-layouts  30 us (4%)
  matrix products  22.6 us (3%)
  between operations  14.7 us (2%)
    pallas_call x2, Pallas kernels, gather16(): pl.pallas_call(functools.partial(gather_kernel, chunks, dp, span, extra),...  104 us
    pallas_call x1, Pallas kernels, opening(): pl.pallas_call(functools.partial(opening_kernel, dp, chunks), out_shape=(...  80.6 us
    pallas_call x1, Pallas kernels, mixture_forward(): pl.pallas_call(functools.partial(forward_kernel, chunks, dp, span, batche...  69.4 us
    pallas_call x1, Pallas kernels, mixture_backward(): pl.pallas_call(functools.partial(backward_kernel, chunks), grid=(NZ,), ou...  67.9 us
    pallas_call x1, Pallas kernels, scatter_share(): pl.pallas_call(functools.partial(scatter_share_kernel, chunks, down.shape...  67.4 us
    pallas_call x1, Pallas kernels, returning(): pl.pallas_call(functools.partial(return_kernel, dp, chunks), out_shape=(s...  65.8 us
    pallas_call x1, Pallas kernels, scatter16(): pl.pallas_call(functools.partial(scatter_kernel, chunks, dp, span, extra)...  53.3 us
    pallas_call x1, Pallas kernels, closing(): pl.pallas_call(functools.partial(closing_kernel, dp), out_shape=(shape((n...  45 us
  transfers between devices with their start and end apart: 5, of which 0 were waited for; matrix products, arithmetic and copies ran while one was open for 10% of the time, Pallas kernels for 56%

profile of v10, /device:TPU:0, one launch (start us, length us, event | category | flops | bytes accessed | tf_op | source)
XLA Modules:
  0.0 715.0 jit_solution(11636591236175365891)
XLA Ops:
  7.2 2.3 pad_maximum_fusion
  14.7 80.6 %opening.1 = (bf16[16,128,2048]{2,1,0:T(8,128)(2,1)}, bf16[2,16,64,640]{3,2,1,0:T(8,128)(2,1)}, bf16[2,16,64,256]{3,2,1,0:T(8,128)(2,1)}, bf16[2,64,2048]{2,1,0:...) custom-call(bf16[128,2048]{1,0:T(8,128)(2,1)} %bitcast.138, ...), custom_call_target="tpu_custom_call" | custom-call | bytes 4000000 | tf_op jit(solution)/shard_map/opening/pallas_call | solution.py:519
  95.3 2.0 slice.123
  106.4 16.7 %project.1 = (bf16[2048,2048]{1,0:T(8,128)(2,1)}, bf16[2,1024,256]{2,1,0:T(8,128)(2,1)S(1)}, bf16[2,1024,256]{2,1,0:T(8,128)(2,1)S(1)}, bf16[2,1024,128]{2,1,0:T(8,128)(2,1)S(1)}, bf16[2,1024,512]{2,1,0:T(8,128)(2,1)}) custom-call(bf16[16,128,2048]{2,1,0:T(8,128)(2,1)} %get-tuple-element.83.x_ref, f32[1,2048]{1,0:T(1,128)S(1)} %bitcast.110, ...), custom_call_target="tpu_custom_call" | custom-call | flops 7000000000 | bytes 20000000 | tf_op jit(solution)/shard_map/project/pallas_call | solution.py:1515
  123.2 9.8 %attend.1 = (bf16[16,2,64,2048]{3,2,1,0:T(8,128)(2,1)}, bf16[16,2,64,128]{3,2,1,0:T(8,128)(2,1)S(1)}, f32[2,1024,1]{2,1,0:T(8,128)S(1)}) custom-call(s32[2]{0:T(128)S(1)} %bitcast.113, bf16[2,1024,256]{2,1,0:T(8,128)(2,1)S(1)} %get-tuple-element.86.q_ref, bf16[2,1024,256]{2,1,0:T(8,128)(2,1)S(1)} %get-tuple-element.87.k_ref, ...), custom_call_target="tpu_custom_call" | custom-call | flops 4000000000 | bytes 15000000 | tf_op jit(solution)/shard_map/attend/pallas_call | solution.py:1573
  134.9 53.3 %scatter16.1 = (f32[128,2048]{1,0:T(8,128)}, bf16[2,208,2048]{2,1,0:T(8,128)(2,1)}) custom-call(bf16[16,128,2048]{2,1,0:T(8,128)(2,1)} %bitcast.137, bf16[704,2048]{1,0:T(8,128)(2,1)} %bitcast.121), custom_call_target="tpu_custom_call" | custom-call | bytes 4000000 | tf_op jit(solution)/shard_map/scatter16/pallas_call | solution.py:722
  188.2 2.3 multiply_reduce_fusion.3
  191.5 53.0 %gather16.2 = (bf16[16,128,2048]{2,1,0:T(8,128)(2,1)}, bf16[2,272,2048]{2,1,0:T(8,128)(2,1)}) custom-call(bf16[128,2048]{1,0:T(8,128)(2,1)} %multiply_convert_fusion.x_ref, bf16[704,2048]{1,0:T(8,128)(2,1)} %bitcast.122), custom_call_target="tpu_custom_call" | custom-call | bytes 4000000 | tf_op jit(solution)/shard_map/gather16/pallas_call | solution.py:370
  249.8 69.4 %mixture_forward.1 = (bf16[2048,2048]{1,0:T(8,128)(2,1)}, bf16[1024,2048]{1,0:T(8,128)(2,1)}, bf16[1024,1408]{1,0:T(8,128)(2,1)}, bf16[1024,1408]{1,0:T(8,128)(2...) custom-call(s32[2]{0:T(128)} %bitcast.111, ...), custom_call_target="tpu_custom_call" | custom-call | bytes 4000000 | tf_op jit(solution)/shard_map/mixture_forward/pallas_call | solution.py:1246
  319.2 67.9 %mixture_backward.1 = (bf16[2048,2176]{1,0:T(8,128)(2,1)}, bf16[1024,2048]{1,0:T(8,128)(2,1)}, bf16[1024,1408]{1,0:T(8,128)(2,1)}, bf16[1024,1408]{1,0:T(8,128)(...) custom-call(f32[1,256]{1,0:T(1,128)} %add_convert_fusion.3.pick_ref, bf16[2048,2048]{1,0:T(8,128)(2,1)} %bitcast.119, ...), custom_call_target="tpu_custom_call" | custom-call | bytes 4000000 | tf_op jit(solution)/shard_map/mixture_backward/pallas_call | solution.py:1280
  387.1 10.8 %convolution_convert_fusion = bf16[1408,2048]{1,0:T(8,128)(2,1)} fusion(bf16[1024,1408]{1,0:T(8,128)(2,1)} %get-tuple-element.113, bf16[1024,2048]{1,0:T(8,128)(2,1)} %get-tuple-element.114), kind=kOutput, calls=%fused_computation | convolution fusion | flops 5908463616 | bytes 12845056 | tf_op jit(solution)/shard_map/dot_general | solution.py:1696
  398.0 67.4 %scatter_share.1 = (f32[128,2176]{1,0:T(8,128)}, bf16[2,528,1024]{2,1,0:T(8,128)(2,1)}, bf16[2048,1408]{1,0:T(8,128)(2,1)}, bf16[2048,1408]{1,0:T(8,128)(2,1)}, bf16[1,704,2048]{2,1,0:T(8,128)(2,1)}) custom-call(bf16[16,128,2176]{2,1,0:T(8,128)(2,1)} %bitcast.134, bf16[2048,512]{1,0:T(8,128)(2,1)} %get-tuple-element.108.ds_ref, ...), custom_call_target="tpu_custom_call" | custom-call | bytes 4000000 | tf_op jit(solution)/shard_map/scatter_share/pallas_call | solution.py:1451
  468.8 2.7 multiply_reduce_fusion.6
  476.6 50.9 %gather16.3 = (bf16[16,128,2048]{2,1,0:T(8,128)(2,1)}, bf16[1,528,1024]{2,1,0:T(8,128)(2,1)}) custom-call(bf16[128,2048]{1,0:T(8,128)(2,1)} %fusion.39.x_ref, bf16[2,528,1024]{2,1,0:T(8,128)(2,1)} %get-tuple-element.116.refs_0_), custom_call_target="tpu_custom_call" | custom-call | bytes 4000000 | tf_op jit(solution)/shard_map/gather16/pallas_call | solution.py:370
  527.5 25.6 %attend_back.1 = (bf16[16,2,64,2688]{3,2,1,0:T(8,128)(2,1)}, bf16[2048,256]{1,0:T(8,128)(2,1)}, bf16[128,2048]{1,0:T(8,128)(2,1)}, bf16[512,256]{1,0:T(8,128)(2,1)}) custom-call(s32[2]{0:T(128)} %bitcast.112, bf16[16,2,64,2048]{3,2,1,0:T(8,128)(2,1)} %bitcast.174, bf16[16,2,64,2048]{3,2,1,0:T(8,128)(2,1)} %bitcast.175, bf16[2,1024,256]{2,1,0:T(8,128)(2,1)} %copy-done.6, ...), custom_call_target="tpu_custom_call" | custom-call | flops 14000000000 | bytes 25000000 | tf_op jit(solution)/shard_map/attend_back/pallas_call | solution.py:1665
  556.3 2.5 pad_add_fusion
  558.7 65.8 %returning.1 = (f32[128,2688]{1,0:T(8,128)}, bf16[1,16,64,256]{3,2,1,0:T(8,128)(2,1)}, bf16[1,2,64,2048]{3,2,1,0:T(8,128)(2,1)}) custom-call(bf16[16,128,2688]{2,1,0:T(8,128)(2,1)} %bitcast.132, bf16[2,16,64,256]{3,2,1,0:T(8,128)(2,1)} %bitcast.140, bf16[2,64,2048]{2,1,0:T(8,128)(2,1)} %bitcast.151), custom_call_target="tpu_custom_call" | custom-call | bytes 4000000 | tf_op jit(solution)/shard_map/returning/pallas_call | solution.py:774
  628.0 4.1 fusion.16
  637.7 45.0 %closing.1 = (bf16[128,640]{1,0:T(8,128)(2,1)}, bf16[1,64,640]{2,1,0:T(8,128)(2,1)}, f32[64,3072]{1,0:T(8,128)}, f32[16,4096]{1,0:T(8,128)}, f32[64,2048]{1,0:T(8,128)}) custom-call(bf16[16,128,640]{2,1,0:T(8,128)(2,1)} %bitcast.133, bf16[16,64,256]{2,1,0:T(8,128)(2,1)} %fusion.23.parts_ref, bf16[2,64,2048]{2,1,0:T(8,128)(2,1)} %fusion.20.rows_ref), custom_call_target="tpu_custom_call" | custom-call | bytes 4000000 | tf_op jit(solution)/shard_map/closing/pallas_call | solution.py:889
  685.8 2.1 convert_add_fusion.1
  690.4 2.1 fusion.15
  692.5 3.7 convert_add_fusion
  696.2 4.7 bitcast_convert_fusion
  701.0 4.8 bitcast_convert_fusion.1
  (184 shorter events, 50.6 us)
Async XLA Ops:
  7.2 242.6 %all-gather.11.cloned.1.call-start = ((), (), s32[]{:S(2)}) async-start(), calls=%async_computation.6 | async-start | bytes 3244032 | tf_op jit(solution)/shard_map/all_gather | solution.py:1822
  9.6 240.2 %all-gather.7.cloned.1.call-start = ((), (), s32[]{:S(2)}) async-start(), calls=%async_computation.4 | async-start | bytes 8650752 | tf_op jit(solution)/shard_map/all_gather | solution.py:1820
  10.4 239.4 %all-gather.9.cloned.1.call-start = ((), (), s32[]{:S(2)}) async-start(), calls=%async_computation.5 | async-start | bytes 8650752 | tf_op jit(solution)/shard_map/all_gather | solution.py:1821
  11.1 685.1 %reduce-scatter.5.cloned.1.call-start = ((), (), s32[]{:S(2)}) async-start(), calls=%async_computation.3 | async-start | bytes 8650752 | tf_op jit(solution)/shard_map/reduce_scatter | solution.py:1874
  14.7 88.2 %copy-start.11 = (bf16[2,1,64,2048]{3,2,1,0:T(8,128)(2,1)S(1)}, bf16[2,1,64,2048]{3,2,1,0:T(8,128)(2,1)}, u32[]{:S(2)}) copy-start(bf16[2,1,64,2048]{3,2,1,0:T(8,128)(2,1)} %param.27) | copy-start | bytes 1572868
  97.3 7.9 %copy-start.1 = (bf16[2,16,64,256]{3,2,1,0:T(8,128)(2,1)S(1)}, bf16[2,16,64,256]{3,2,1,0:T(8,128)(2,1)}, u32[]{:S(2)}) copy-start(bf16[2,16,64,256]{3,2,1,0:T(8,128)(2,1)} %get-tuple-element.85) | copy-start | bytes 3145732
  97.3 7.9 %copy-start.4 = (f32[2048,32]{1,0:T(8,128)S(1)}, f32[2048,32]{1,0:T(8,128)}, u32[]{:S(2)}) copy-start(f32[2048,32]{1,0:T(8,128)} %constant.107.clone.cos_ref) | copy-start | bytes 786436
  102.9 20.3 %copy-start = (bf16[512,256]{1,0:T(8,128)(2,1)}, bf16[512,256]{1,0:T(8,128)(2,1)S(1)}, u32[]{:S(2)}) copy-start(bf16[512,256]{1,0:T(8,128)(2,1)S(1)} %reshape.352.we_ref) | copy-start | bytes 786436
  106.4 16.8 %copy-start.2 = (s32[2,1]{0,1:T(1,128)S(1)}, s32[2,1]{0,1:T(1,128)}, u32[]{:S(2)}) copy-start(s32[2,1]{0,1:T(1,128)} %param.29) | copy-start | bytes 28
  106.4 16.8 %copy-start.3 = (bf16[2,64,2048]{2,1,0:T(8,128)(2,1)S(1)}, bf16[2,64,2048]{2,1,0:T(8,128)(2,1)}, u32[]{:S(2)}) copy-start(bf16[2,64,2048]{2,1,0:T(8,128)(2,1)} %get-tuple-element.89) | copy-start | bytes 1572868
  123.2 9.9 %copy-start.6 = (bf16[2,1024,256]{2,1,0:T(8,128)(2,1)}, bf16[2,1024,256]{2,1,0:T(8,128)(2,1)S(1)}, u32[]{:S(2)}) copy-start(bf16[2,1024,256]{2,1,0:T(8,128)(2,1)S(1)} %get-tuple-element.86.q_ref) | copy-start | bytes 3145732
  123.2 9.9 %copy-start.7 = (bf16[2,1024,256]{2,1,0:T(8,128)(2,1)}, bf16[2,1024,256]{2,1,0:T(8,128)(2,1)S(1)}, u32[]{:S(2)}) copy-start(bf16[2,1024,256]{2,1,0:T(8,128)(2,1)S(1)} %get-tuple-element.87.k_ref) | copy-start | bytes 3145732
  123.2 9.9 %copy-start.9 = (bf16[2,1024,128]{2,1,0:T(8,128)(2,1)}, bf16[2,1024,128]{2,1,0:T(8,128)(2,1)S(1)}, u32[]{:S(2)}) copy-start(bf16[2,1024,128]{2,1,0:T(8,128)(2,1)S(1)} %get-tuple-element.88.v_ref) | copy-start | bytes 1572868
  134.9 53.4 %copy-start.12 = (bf16[2,1,64,2048]{3,2,1,0:T(8,128)(2,1)S(1)}, bf16[2,1,64,2048]{3,2,1,0:T(8,128)(2,1)}, u32[]{:S(2)}) copy-start(bf16[2,1,64,2048]{3,2,1,0:T(8,128)(2,1)} %param.27) | copy-start | bytes 1572868
  244.6 4.3 copy-start.14
  465.4 235.6 %reduce-scatter.3.cloned.1.call-start = ((), (), s32[]{:S(2)}) async-start(), calls=%async_computation.2 | async-start | bytes 8650752 | tf_op jit(solution)/shard_map/reduce_scatter | solution.py:1873
  466.2 7.5 %copy-start.22 = (f32[128,2176]{1,0:T(8,128)S(1)}, f32[128,2176]{1,0:T(8,128)}, u32[]{:S(2)}) copy-start(f32[128,2176]{1,0:T(8,128)} %get-tuple-element.115) | copy-start | bytes 3342340
  628.0 4.1 copy-start.21
  683.6 5.7 copy-start.31
  685.8 6.7 slice-start
  687.9 4.5 slice-start.1
  700.9 4.9 copy-start.25
  700.9 5.7 copy-start.33
  700.9 6.4 copy-start.27
  (24 other events, 53.7 us)
Sparse Core Ops, SparseCore 0:
  10.1 52.5 all-gather.10
  64.3 71.1 all-gather.6
  137.0 106.8 all-gather.8
  465.5 92.8 reduce-scatter.4
  560.7 86.1 reduce-scatter.2

commit v11 on v10

--- a/solution.py
+++ b/solution.py
@@ -146,8 +146,8 @@
     def alt(self, k):
         return k >= (self.chunks + 1) // 2
 
-    def order(self):
-        return range(self.chunks - 1, -1, -1)
+    def order(self, ks=None):
+        return range(self.chunks - 1, -1, -1) if ks is None else ks
 
     def copy(self, block, k, src, send, recv, to):
         src_ref = self.src if src is None else self.view(self.out, src)
@@ -204,11 +204,14 @@
             return self.has(slot)
         return self.z > slot if slot <= 3 else self.z + (slot - 3) < NZ - 1
 
-    def start(self):
+    def kept(self):
+        return pltpu.make_async_copy(self.src, self.view(self.out, self.me), self.own_sem)
+
+    def start(self, ks=None):
         z, me = self.z, self.me
-        self.own = pltpu.make_async_copy(self.src, self.view(self.out, me), self.own_sem)
-        self.own.start()
-        for k in self.order():
+        if ks is None or 0 in ks:
+            self.kept().start()
+        for k in self.order(ks):
             self.across(k, 0, me).start()
 
             @pl.when(z < NZ - 1)
@@ -295,27 +298,36 @@
 
             self.over(k, 7 + slot, b, b).start()
 
-    def round(self, s):
+    def round(self, s, ks=None):
         if s < NZ:
-            for k in self.order():
+            for k in self.order(ks):
                 self.line(k, s)
-        for k in self.order():
+        for k in self.order(ks):
             for slot in ((0,) if s == 1 else (s - 1, s + 2)):
                 self.from_side(k, slot)
         if s > 1:
-            for k in self.order():
+            for k in self.order(ks):
                 if self.alt(k):
                     self.line_b(k, s - 1)
 
-    def finish(self):
+    def landed(self, ks=None):
+        for k in self.order(ks):
+            for slot in range(14):
+                @pl.when(self.has(slot))
+                def _():
+                    b = self.core_block(slot)
+                    self.over(k, slot, b, b).wait_recv()
+
+    def finish(self, landed=True):
         z = self.z
-        self.own.wait()
+        if landed:
+            self.kept().wait()
+            self.landed()
         for k in self.order():
             for slot in range(14):
                 @pl.when(self.has(slot))
                 def _():
                     b = self.core_block(slot)
-                    self.over(k, slot, b, b).wait_recv()
                     self.over(k, slot, b, b).wait_send()
             for slot in range(7):
                 @pl.when(self.crosses(k, slot))
@@ -553,7 +565,7 @@
     def scratch(rows, width, chunks, bf):
         dma = pltpu.SemaphoreType.DMA
         return [pltpu.VMEM((n, rows, width), bf) for n in (8, 8, 4, 4, 4)] + [
-            dma((8,)), dma((8, chunks)), dma((8, chunks))] + [dma((4, chunks))] * 6
+            dma((8, chunks)), dma((8, chunks)), dma((8, chunks))] + [dma((4, chunks))] * 6
 
     def rng(self, k):
         return pl.ds(k * self.rows, self.rows)
@@ -572,9 +584,13 @@
             self.p.at[self.column(i, j) + 1 - self.c, self.rng(k)], self.cbuf.at[n, self.rng(k)],
             self.cs.at[n, k], self.cr.at[n, k], self.core)
 
-    def load(self, i, j):
+    def load(self, i, j, k):
         n = 2 * i + j
-        return pltpu.make_async_copy(self.p.at[self.column(i, j) + self.c], self.own.at[n], self.ld.at[n])
+        return pltpu.make_async_copy(
+            self.p.at[self.column(i, j) + self.c, self.rng(k)], self.own.at[n, self.rng(k)], self.ld.at[n, k])
+
+    def which(self, ks):
+        return range(self.chunks) if ks is None else ks
 
     def across(self, i, k):
         return self.remote(self.own.at[2 * i, self.rng(k)], self.xbuf.at[i, self.rng(k)],
@@ -588,29 +604,29 @@
         return self.remote(self.own.at[2 * i + 1, self.rng(k)], self.dbuf.at[t, self.rng(k)],
                            self.ds.at[t, k], self.dr.at[t, k], self.me - 4)
 
-    def start(self):
+    def start(self, ks=None):
         for i in range(NZ):
             for j in range(2):
-                self.load(i, j).start()
-                for k in range(self.chunks):
+                for k in self.which(ks):
+                    self.load(i, j, k).start()
                     self.over(i, j, k).start()
 
-    def first(self, i):
+    def first(self, i, ks=None):
         f32 = jnp.float32
-        self.load(i, 0).wait()
-        for k in range(self.chunks):
+        for k in self.which(ks):
+            self.load(i, 0, k).wait()
             self.over(i, 0, k).wait_recv()
             s = self.rng(k)
             self.own[2 * i, s] = (
                 self.own[2 * i, s].astype(f32) + self.cbuf[2 * i, s].astype(f32)).astype(self.own.dtype)
             self.across(i, k).start()
 
-    def second(self, i):
+    def second(self, i, ks=None):
         f32 = jnp.float32
         z, own, o = self.z, self.own, self.o
         t = order(z, i)
-        self.load(i, 1).wait()
-        for k in range(self.chunks):
+        for k in self.which(ks):
+            self.load(i, 1, k).wait()
             s = self.rng(k)
             self.over(i, 1, k).wait_recv()
             self.across(i, k).wait_recv()
@@ -1537,10 +1553,23 @@
     return jnp.where((u <= t) & (u < length), s, -1e30)
 
 
-def attend_kernel(len_ref, q_ref, k_ref, v_ref, wo_ref, part_ref, att_ref, lse_ref):
-    length = len_ref[pl.program_id(0)]
+def attend_kernel(dp, span, len_ref, q_ref, k_ref, v_ref, wo_ref, side_ref, sum_ref, att_ref, lse_ref, side_out,
+                  part, *scratch):
+    m = pl.program_id(0)
+    length = len_ref[m]
     seq = q_ref.shape[1]
-    groups, _, here, width = part_ref.shape
+    groups, rows, width = part.shape
+    here = rows // 2
+    per = ROWS // here
+    sc = Scatter(part, sum_ref, 2, scratch[:Scatter.COUNT])
+    job = side_job(dp, span, side_ref, side_out, scratch[Scatter.COUNT:])
+
+    @pl.when(m == 0)
+    def _():
+        enter(sc.me, sc.z, sc.core, sc.side, dp)
+        job.start()
+
+    mine = pl.ds(pl.multiple_of(m * here, here), here)
     for i in range(seq // ROWS):
         tile = slice(i * ROWS, (i + 1) * ROWS)
         ext = (i + 1) * ROWS
@@ -1551,14 +1580,39 @@
         lse_ref[0, tile] = peak + jnp.log(total)
         p = (raised / total).astype(BF)
         att = mm(p, v_ref[0, :ext]).astype(BF)
-        per = ROWS // here
         att_ref[i * per:(i + 1) * per, 0] = att.reshape(per, here, att.shape[1])
         for j in range(width // 512):
             cols = slice(j * 512, (j + 1) * 512)
-            part_ref[i * per:(i + 1) * per, 0, :, cols] = mm(att, wo_ref[:, cols]).astype(BF).reshape(per, here, 512)
-
-
-def attend(lengths, q, k, v, wo, groups):
+            part[i * per:(i + 1) * per, mine, cols] = mm(att, wo_ref[:, cols]).astype(BF).reshape(per, here, 512)
+
+        @pl.when(m == 1)
+        def _():
+            sc.first(i, [0])
+
+    @pl.when(m == 0)
+    def _():
+        sc.start([0])
+
+    @pl.when(m == 1)
+    def _():
+        sc.start([1])
+        sc.first(0, [1])
+        sc.first(1, [1])
+        sc.second(0, [0])
+        sc.first(2, [1])
+        sc.first(3, [1])
+        sc.second(1, [0])
+        sc.second(2, [0])
+        sc.second(0, [1])
+        sc.second(3, [0])
+        sc.second(1, [1])
+        sc.second(2, [1])
+        sc.second(3, [1])
+        sc.finish()
+        job.finish()
+
+
+def attend(lengths, q, k, v, wo, groups, dp, span, side, cid):
     batches, seq, _ = q.shape
     here = seq // groups
     width = wo.shape[1]
@@ -1567,43 +1621,70 @@
     def by_seq(w):
         return pl.BlockSpec((1, seq, w), lambda m: (m, 0, 0))
 
-    def by_dev(w):
-        return pl.BlockSpec((groups, 1, here, w), lambda m: (0, m, 0, 0))
-
     return pl.pallas_call(
-        attend_kernel,
+        functools.partial(attend_kernel, dp, span),
         grid=(batches,),
-        out_shape=(shape((groups, batches, here, width), BF), shape((groups, batches, here, 128), BF),
-                   shape((batches, seq, 1), F32)),
+        out_shape=(shape((batches * here, width), F32), shape((groups, batches, here, 128), BF),
+                   shape((batches, seq, 1), F32), side_shape(dp, span, side)),
         in_specs=[pl.BlockSpec(memory_space=pltpu.SMEM), by_seq(256), by_seq(256), by_seq(128),
-                  pl.BlockSpec(wo.shape, lambda m: (0, 0))],
-        out_specs=[by_dev(width), by_dev(128), by_seq(1)],
-        compiler_params=pltpu.CompilerParams(vmem_limit_bytes=48 * 1024 * 1024),
-        cost_estimate=pl.CostEstimate(flops=4_000_000_000, bytes_accessed=15_000_000, transcendentals=2_000_000),
+                  pl.BlockSpec(wo.shape, lambda m: (0, 0)), ANY],
+        out_specs=[pl.BlockSpec((batches * here, width), lambda m: (0, 0)),
+                   pl.BlockSpec((groups, 1, here, 128), lambda m: (0, m, 0, 0)), by_seq(1), ANY],
+        scratch_shapes=[pltpu.VMEM((groups, batches * here, width), BF)]
+        + Scatter.scratch(batches * here, width, 2, BF) + side_scratch(dp, span),
+        compiler_params=pltpu.CompilerParams(
+            collective_id=cid, has_side_effects=True, vmem_limit_bytes=60 * 1024 * 1024),
+        cost_estimate=COST,
         name="attend",
-    )(lengths, q, k, v, wo)
-
-
-def attend_back_kernel(len_ref, dout_ref, h_ref, q_ref, k_ref, v_ref, lat_ref, att_ref, lse_ref, wo_ref, wq_ref, we_ref,
-                       cos_ref, sin_ref, part_ref, gwq_ref, gwo_out, gwe_out, dk, dv, datt, gwq, gwo_ref, gwe_ref):
+    )(lengths, q, k, v, wo, side)
+
+
+def attend_back_kernel(dp, len_ref, own_ref, side_ref, h_ref, q_ref, k_ref, v_ref, lat_ref, att_ref, lse_ref, wo_ref, wq_ref, we_ref,
+                       cos_ref, sin_ref, part_ref, gwq_ref, gwo_out, gwe_out, side_out,
+                       dout_ref, dk, dv, datt, gwq, gwo_ref, gwe_ref, *scratch):
     m = pl.program_id(0)
     length = len_ref[m]
     seq = q_ref.shape[1]
-    groups, _, here, width = dout_ref.shape
+    groups, _, width = dout_ref.shape
+    here = h_ref.shape[2]
     per = ROWS // here
+    g = Gather(own_ref, dout_ref, 2, scratch[:Gather.COUNT])
+    job = side_job(dp, None, side_ref, side_out, scratch[Gather.COUNT:])
 
     @pl.when(m == 0)
     def _():
+        enter(g.me, g.z, g.core, g.side, dp)
+        job.start()
+        g.start([0])
+        g.start([1])
+        g.round(1, [0])
+        g.round(2, [0])
+        g.round(1, [1])
+        g.round(3, [0])
+        g.round(2, [1])
+        g.round(4, [0])
+        g.kept().wait()
+        g.landed([0])
         gwo_ref[...] = jnp.zeros_like(gwo_ref)
         gwe_ref[...] = jnp.zeros_like(gwe_ref)
         gwq[...] = jnp.zeros_like(gwq)
 
+    @pl.when(m == 1)
+    def _():
+        g.round(4, [1])
+        g.landed([1])
+
+    mine = pl.ds(pl.multiple_of(m * here, here), here)
     for j in range(4):
         blocks = slice(j * groups // 4, (j + 1) * groups // 4)
-        dout = dout_ref[blocks].reshape(seq // 4, width)
+        dout = dout_ref[blocks, mine].reshape(seq // 4, width)
         rows = slice(j * seq // 4, (j + 1) * seq // 4)
         datt[rows] = mm_t(dout, wo_ref[...]).astype(BF)
         gwo_ref[...] += mm_lead(att_ref[blocks].reshape(seq // 4, 128), dout)
+    @pl.when(m == 0)
+    def _():
+        g.round(3, [1])
+
     dk[...] = jnp.zeros_like(dk)
     dv[...] = jnp.zeros_like(dv)
     for i in range(seq // ROWS):
@@ -1646,10 +1727,12 @@
             gwq_ref[cols] = gwq[:, cols].T.astype(BF)
         gwo_out[...] = gwo_ref[...].astype(BF)
         gwe_out[...] = gwe_ref[...].astype(BF)
-
-
-def attend_back(lengths, dout, h, q, k, v, lat, att, lse, wo, wq, we, cosine, sine, tail):
-    groups, batches, here, width = dout.shape
+        g.finish(False)
+        job.finish()
+
+
+def attend_back(dp, lengths, dout, side, h, q, k, v, lat, att, lse, wo, wq, we, cosine, sine, tail, cid):
+    groups, batches, here, width = h.shape
     seq = groups * here
     shape = jax.ShapeDtypeStruct
 
@@ -1663,19 +1746,151 @@
         return pl.BlockSpec(v.shape, lambda m: (0, 0))
 
     return pl.pallas_call(
-        attend_back_kernel,
+        functools.partial(attend_back_kernel, dp),
         grid=(batches,),
         out_shape=(shape((groups, batches, here, width + tail), BF), shape(wq.shape, BF),
-                   shape(wo.shape, BF), shape(we.shape, BF)),
-        in_specs=[pl.BlockSpec(memory_space=pltpu.SMEM), by_dev(width), by_dev(width), by_seq(256), by_seq(256), by_seq(128),
+                   shape(wo.shape, BF), shape(we.shape, BF), side_shape(dp, None, side)),
+        in_specs=[pl.BlockSpec(memory_space=pltpu.SMEM), ANY, ANY, by_dev(width), by_seq(256), by_seq(256), by_seq(128),
                   by_seq(512), by_dev(128), by_seq(1), whole(wo), whole(wq), whole(we), whole(cosine), whole(sine)],
-        out_specs=[by_dev(width + tail), whole(wq), whole(wo), whole(we)],
-        scratch_shapes=[pltpu.VMEM((seq, 256), F32), pltpu.VMEM((seq, 128), F32), pltpu.VMEM((seq, 128), BF),
-                        pltpu.VMEM((256, width), F32), pltpu.VMEM(wo.shape, F32), pltpu.VMEM(we.shape, F32)],
+        out_specs=[by_dev(width + tail), whole(wq), whole(wo), whole(we), ANY],
+        scratch_shapes=[pltpu.VMEM((groups, batches * here, width), BF), pltpu.VMEM((seq, 256), F32), pltpu.VMEM((seq, 128), F32), pltpu.VMEM((seq, 128), BF),
+                        pltpu.VMEM((256, width), F32), pltpu.VMEM(wo.shape, F32), pltpu.VMEM(we.shape, F32)]
+        + Gather.scratch(2) + side_scratch(dp, None),
+        compiler_params=pltpu.CompilerParams(
+            collective_id=cid, has_side_effects=True, vmem_limit_bytes=60 * 1024 * 1024),
+        cost_estimate=COST,
+        name="attend_back",
+    )(lengths, dout, side, h, q, k, v, lat, att, lse, wo, wq, we, cosine, sine)
+
+
+def turn_kernel(v_ref, o_ref):
+    for i in range(v_ref.shape[0] // 128):
+        rows = slice(i * 128, (i + 1) * 128)
+        o_ref[:, rows] = v_ref[rows].astype(F32).T.astype(o_ref.dtype)
+
+
+def turned(v, block):
+    return pl.pallas_call(
+        turn_kernel,
+        grid=(1,),
+        out_shape=jax.ShapeDtypeStruct((128, v.shape[0]), v.dtype),
+        in_specs=[pl.BlockSpec((v.shape[0], 128), lambda i: (0, block))],
+        out_specs=pl.BlockSpec((128, v.shape[0]), lambda i: (0, 0)),
+        compiler_params=pltpu.CompilerParams(vmem_limit_bytes=16 * 1024 * 1024),
+        cost_estimate=COST,
+        name="turned",
+    )(v)
+
+
+def split_rows(v):
+    high = v.astype(BF)
+    return [high, (v - high.astype(F32)).astype(BF)]
+
+
+def own_back_kernel(dp, back_ref, x_ref, mix_ref, logit_ref, gmix_ref, gain_ref, lgain_ref, small_ref, cos_ref, sin_ref,
+                    mid_ref, place_ref, grad_ref, out_ref):
+    width = x_ref.shape[1]
+    rows_w = out_ref.shape[1] // dp
+    lanes_w = out_ref.shape[2]
+    x = x_ref[...].astype(F32)
+    factor = lax.rsqrt(jnp.mean(x * x, axis=1, keepdims=True) + 1e-6)
+    unit = x * factor
+    hidden = (unit * gain_ref[...]).astype(BF)
+    lat = mm(hidden, small_ref[:, :512])
+    factor_l = lax.rsqrt(jnp.mean(lat * lat, axis=1, keepdims=True) + 1e-6)
+    unit_l = lat * factor_l
+    d_lat = back_ref[:, width:width + 512]
+    scaled = d_lat * lgain_ref[...]
+    d_in = factor_l * (scaled - unit_l * jnp.mean(scaled * unit_l, axis=1, keepdims=True))
+    g_lat = jnp.sum(d_lat * unit_l, axis=0, keepdims=True)
+    d_rope = turn(back_ref[:, width + 512:width + 576], cos_ref[...], -sin_ref[...])
+    tokens = x.shape[0]
+    d_raw = jnp.concatenate(
+        [d_in.astype(BF), d_rope.astype(BF), jnp.zeros((tokens, lanes_w - 576), BF)], axis=1)
+    d_hidden = back_ref[:, :width] + mm_t(d_raw, small_ref[...])
+    scaled = d_hidden * gain_ref[...]
+    grad_ref[...] = mid_ref[...] + factor * (scaled - unit * jnp.mean(scaled * unit, axis=1, keepdims=True))
+    g_gain = jnp.sum(d_hidden * unit, axis=0, keepdims=True)
+    spread = [mm(v, place_ref[...]).astype(BF) for v in split_rows(g_lat)]
+    extra = split_rows(g_gain) + split_rows(gmix_ref[...]) + spread + [jnp.zeros((10, width), BF)]
+    left = jnp.concatenate([hidden, mix_ref[...]] + extra, axis=0)
+    logit = jnp.concatenate(
+        [jnp.zeros((tokens, 576), BF), logit_ref[...], jnp.zeros((tokens, lanes_w - 592), BF)], axis=1)
+    n = lax.broadcasted_iota(jnp.int32, (16, lanes_w), 0)
+    at = 592 + (n >> 1)
+    hot = jnp.where((lax.broadcasted_iota(jnp.int32, (16, lanes_w), 1) == at) & (n < 6), 1.0, 0.0).astype(BF)
+    right = jnp.concatenate([d_raw, logit, hot], axis=0)
+    for j in range(width // 256):
+        part = mm_lead(left[:, j * 256:(j + 1) * 256], right).astype(BF)
+        for i in range(256 // rows_w):
+            owner = j * (256 // rows_w) + i
+            d, e = owner // NE, owner % NE
+            out_ref[e, d * rows_w:(d + 1) * rows_w] = part[i * rows_w:(i + 1) * rows_w]
+
+
+def own_back(dp, back, x, mix, logit, gmix, gain, lgain, small, cosine, sine, mid, rows_l):
+    tokens, width = x.shape
+    rows_w = width // (dp * NE)
+    count = np.arange(width)
+    place = (count // rows_w * rows_l + count % rows_w)[None, :] == np.arange(512)[:, None]
+    place = place & (count % rows_w < rows_l)[None, :]
+    shape = jax.ShapeDtypeStruct
+    return pl.pallas_call(
+        functools.partial(own_back_kernel, dp),
+        out_shape=(shape((tokens, width), F32), shape((NE, dp * rows_w, small.shape[1]), BF)),
+        in_specs=[VMEM] * 12,
+        out_specs=(VMEM, VMEM),
+        compiler_params=pltpu.CompilerParams(vmem_limit_bytes=40 * 1024 * 1024),
+        cost_estimate=COST,
+        name="own_back",
+    )(back, x, mix, logit, gmix, gain, lgain, small, cosine, sine, mid, jnp.asarray(place.astype(np.float32), BF))
+
+
+def widen_kernel(gate_ref, up_ref, down_ref, down_far, share_ref, share_far, gate_out, up_out, down_out, sg_out, su_out,
+                 sd_out):
+    gate_out[...] = gate_ref[...].astype(F32)
+    up_out[...] = up_ref[...].astype(F32)
+    down = down_ref[...].astype(F32)
+    for r in range(down_far.shape[0]):
+        down = down + down_far[r].astype(F32)
+    down_out[...] = down
+
+    @pl.when(pl.program_id(0) == 0)
+    def _():
+        n = sg_out.shape[0]
+        for i, out in enumerate((sg_out, su_out, sd_out)):
+            rows = slice(i * n, (i + 1) * n)
+            v = share_ref[rows].astype(F32)
+            for r in range(share_far.shape[0]):
+                v = v + share_far[r, rows].astype(F32)
+            out[...] = v
+
+
+def widen(gate, up, down, down_far, share, share_far):
+    steps = 2 if down.shape[0] % 32 == 0 else 1
+    shape = jax.ShapeDtypeStruct
+
+    def cut(v):
+        return pl.BlockSpec((v.shape[0] // steps, v.shape[1]), lambda i: (i, 0))
+
+    def cut_far(v):
+        return pl.BlockSpec((v.shape[0], v.shape[1] // steps, v.shape[2]), lambda i: (0, i, 0))
+
+    def full(shape_):
+        zeros = (0,) * len(shape_)
+        return pl.BlockSpec(shape_, lambda i: zeros)
+
+    third = (share.shape[0] // 3, share.shape[1])
+    return pl.pallas_call(
+        widen_kernel,
+        grid=(steps,),
+        out_shape=tuple(shape(v.shape, F32) for v in (gate, up, down)) + (shape(third, F32),) * 3,
+        in_specs=[cut(gate), cut(up), cut(down), cut_far(down_far), full(share.shape), full(share_far.shape)],
+        out_specs=[cut(gate), cut(up), cut(down)] + [full(third)] * 3,
         compiler_params=pltpu.CompilerParams(vmem_limit_bytes=56 * 1024 * 1024),
-        cost_estimate=pl.CostEstimate(flops=14_000_000_000, bytes_accessed=25_000_000, transcendentals=2_000_000),
-        name="attend_back",
-    )(lengths, dout, h, q, k, v, lat, att, lse, wo, wq, we, cosine, sine)
+        cost_estimate=COST,
+        name="widen",
+    )(gate, up, down, down_far, share, share_far)
 
 
 H = 16
@@ -1806,10 +2021,11 @@
     small = small.reshape(width, small_width)
     parts_head = parts_head.reshape(width, TILE)
     latent_full = small[:, :576]
-    router_full = small[:, 576:592]
-    gain_attn = small[:, 592].astype(F32)
-    gain_mixer = small[:, 593].astype(F32)
-    gain_latent = small[:, 594].reshape(dp * GROUPS, rows_w)[:, :rows_l].reshape(-1).astype(F32)
+    lines = turned(small, 4)
+    router_lines = lines[64:80]
+    gain_attn = lines[80].astype(F32)
+    gain_mixer = lines[81].astype(F32)
+    gain_latent = lines[82].reshape(dp * GROUPS, rows_w)[:, :rows_l].reshape(-1).astype(F32)
     expand_head = parts_head[:, QK_NOPE + ROPE :].reshape(dp * GROUPS, 4, rows_l, ROPE)
     expand_head = expand_head.swapaxes(1, 2).reshape(KV_RANK, QK_NOPE + V_DIM)
     output_head = output_head.reshape(V_DIM, width)
@@ -1824,8 +2040,6 @@
     own_positions = me * here + jnp.arange(here, dtype=jnp.int32)
     valid_own = (own_positions[None, :] < seq_lengths[:, None]).reshape(own).astype(F32)
     cosine, sine_table = rotary_tables(seq_total)
-    cosine_own = lax.dynamic_slice_in_dim(jnp.asarray(cosine), me * here, here)
-    sine_own = lax.dynamic_slice_in_dim(jnp.asarray(sine_table), me * here, here)
 
     grad_own = out_cotangent.reshape(own, width) * valid_own[:, None].astype(BF)
 
@@ -1836,13 +2050,12 @@
     hidden_all, query, key, values, latent = project(
         x_all.reshape(GROUPS, own, width), gain_attn[None], gain_latent[None], parts_head, small, expand_head,
         by_token(cosine), by_token(sine_table), batches)
-    attn_part, attended, log_total = attend(seq_lengths, query, key, values, output_head, GROUPS)
-    attn_part = attn_part.reshape(GROUPS, own, width)
     down_own = down_weight[0]
     cut = down_own.shape[0] * 3 // 160 * 16
     cuts = (0, cut, 2 * cut + cut // 48 * 16, down_own.shape[0])
     spans = [(first, last - first) for first, last in zip(cuts, cuts[1:])]
-    attn_out, down_a = scatter16(attn_part, 2, dp=dp, span=spans[0], side=down_own)
+    attn_out, attended, log_total, down_a = attend(
+        seq_lengths, query, key, values, output_head, GROUPS, dp, spans[0], down_own, 2)
 
     x_wide = x_own.astype(F32)
     middle = x_wide + attn_out
@@ -1855,7 +2068,7 @@
     pick = jnp.concatenate([lane == me, lane == me + GROUPS], axis=1).astype(F32)
     (out_part, rows, hidden, act, slope, result, share_hidden, share_act, share_slope, gates, to_slot, to_token,
      grad_all, down_c) = mixture_forward(
-        dp, batches, here, seq_lengths, pick, mix_all, mask_all, gate_full, up_full, router_full.T, share_full,
+        dp, batches, here, seq_lengths, pick, mix_all, mask_all, gate_full, up_full, router_lines, share_full,
         down_a, down_b, spans[2], down_own, grad_own, 4)
     grad_all = grad_all.reshape(total, width)
     mix_part, grad_result, grad_gate_in, grad_up_in, grad_share_in, mixed = mixture_backward(
@@ -1866,29 +2079,26 @@
     mix_sum, grad_share, grad_gate, grad_up, far_down = scatter_share(
         mix_part.reshape(GROUPS, own, width + 128), grad_share_in, share_hidden, mix_all, grad_all,
         rows, grad_gate_in, grad_up_in, grad_down, share_full.shape, 5)
-    out_down = lax.dynamic_index_in_dim(grad_down, plane, 0, False).astype(F32)
-    out_down = out_down + jnp.sum(far_down.astype(F32), axis=0)
+    down_own_grad = lax.dynamic_index_in_dim(grad_down, plane, 0, False)
     layer_output = valid_own[:, None] * (middle + mixed)
 
     out_gate = lax.psum_scatter(grad_gate, "dp", scatter_dimension=0, tiled=True)
     out_up = lax.psum_scatter(grad_up, "dp", scatter_dimension=0, tiled=True)
 
-    soft_own = masked_softmax(product(hidden_mix, router_full), mask_own)
+    soft_own = masked_softmax(product_trail(hidden_mix, router_lines), mask_own)
     grad_masked = (mix_sum[:, width : width + GROUPS] + mix_sum[:, width + GROUPS : width + 2 * GROUPS])
     grad_masked = grad_masked * valid_own[:, None]
     grad_logits = soft_own * (grad_masked - jnp.sum(grad_masked * soft_own, axis=1, keepdims=True))
     grad_logits = grad_logits.astype(BF)
-    grad_mix = mix_sum[:, :width] + product_trail(grad_logits, router_full)
+    grad_mix = mix_sum[:, :width] + product(grad_logits, router_lines)
     grad_middle_norm, grad_gain_mixer = norm_backward(grad_mix, unit_mix, factor_mix, gain_mixer)
     grad_middle = grad_own.astype(F32) + grad_middle_norm
 
-    grad_attn_all, share_far = gather16(grad_middle.astype(BF), 6, dp=dp, side=grad_share)
-    grad_attn_all = grad_attn_all.reshape(GROUPS, batches, here, width)
-    out_share = lax.dynamic_index_in_dim(grad_share, plane, 0, False).astype(F32)
-    out_share = out_share + jnp.sum(share_far.astype(F32), axis=0)
-    back_part, grad_query_w, grad_output, grad_expand = attend_back(
-        seq_lengths, grad_attn_all, hidden_all.reshape(GROUPS, batches, here, width), query, key, values, latent,
-        attended, log_total, output_head, parts_head, expand_head, jnp.asarray(cosine), jnp.asarray(sine_table), 640)
+    back_part, grad_query_w, grad_output, grad_expand, share_far = attend_back(
+        dp, seq_lengths, grad_middle.astype(BF), grad_share, hidden_all.reshape(GROUPS, batches, here, width), query, key,
+        values, latent, attended, log_total, output_head, parts_head, expand_head, jnp.asarray(cosine),
+        jnp.asarray(sine_table), 640, 6)
+    share_own_grad = lax.dynamic_index_in_dim(grad_share, plane, 0, False)
     grad_expand = grad_expand.reshape(dp * GROUPS, rows_l, 4, ROPE).swapaxes(1, 2).reshape(width, ROPE)
     parts_grad = grad_query_w + jnp.pad(grad_expand, ((0, 0), (QK_NOPE + ROPE, 0)))
     parts_grad = parts_grad.reshape(dp, GROUPS, rows_w, TILE)
@@ -1899,32 +2109,17 @@
     parts_sum = (parts_sum + jnp.sum(parts_far.astype(F32), axis=0)).astype(BF)
     rows_sum = (rows_grad.astype(F32) + jnp.sum(rows_far.astype(F32), axis=0)).astype(BF)
 
-    x_normed, unit_attn, factor_attn = norm_forward(x_wide, gain_attn)
-    hidden_own = x_normed.astype(BF)
-    latent_own = product(hidden_own, latent_full)
-    _, unit_latent, factor_latent = norm_forward(latent_own[:, :KV_RANK], gain_latent)
-    grad_latent_in, grad_gain_latent = norm_backward(
-        back_sum[:, width : width + KV_RANK], unit_latent, factor_latent, gain_latent
-    )
-    grad_rope = back_sum[:, width + KV_RANK : width + KV_RANK + ROPE].reshape(batches, here, ROPE)
-    grad_rope = rotate(grad_rope, cosine_own, -sine_own).reshape(own, ROPE)
-    grad_latent_raw = jnp.concatenate([grad_latent_in, grad_rope], axis=1).astype(BF)
-    grad_hidden_attn = back_sum[:, :width] + product_trail(grad_latent_raw, latent_full)
-    grad_input_norm, grad_gain_attn = norm_backward(grad_hidden_attn, unit_attn, factor_attn, gain_attn)
-    grad_input = grad_middle + grad_input_norm
-
-    latent_rows = grad_gain_latent.reshape(dp * GROUPS, rows_l)
-    latent_rows = jnp.pad(latent_rows, ((0, 0), (0, rows_w - rows_l))).reshape(width, 1)
-    tokens_side = jnp.concatenate([hidden_own, hidden_mix], axis=0)
-    grads_side = jnp.concatenate(
-        [jnp.pad(grad_latent_raw, ((0, 0), (0, 64))), jnp.pad(grad_logits, ((0, 0), (576, 640 - 592)))], axis=0)
-    lane = jnp.arange(640)[None, :]
-    small_grad = product_lead(tokens_side, grads_side)
-    small_grad = small_grad + jnp.where(lane == 592, grad_gain_attn[:, None], 0.0)
-    small_grad = small_grad + jnp.where(lane == 593, grad_gain_mixer[:, None], 0.0)
-    small_grad = (small_grad + jnp.where(lane == 594, latent_rows, 0.0)).astype(BF)
-    small_grad = small_grad.reshape(dp, GROUPS, rows_w, 640).swapaxes(0, 1).reshape(GROUPS, dp * rows_w, 640)
+    def own_table(table):
+        own_rows = lax.dynamic_slice_in_dim(jnp.asarray(table), me * here, here)
+        return jnp.broadcast_to(own_rows[None], (batches, here, ROPE // 2)).reshape(own, ROPE // 2)
+
+    grad_input, small_grad = own_back(
+        dp, back_sum, x_own, hidden_mix, grad_logits, grad_gain_mixer[None], gain_attn[None], gain_latent[None], small,
+        own_table(cosine), own_table(sine_table), grad_middle, rows_l)
     small_sum, out_query, out_expand, out_output = closing(dp, small_grad, parts_sum, rows_sum, rows_l, 9)
+
+    out_gate, out_up, out_down, out_sgate, out_sup, out_sdown = widen(
+        out_gate, out_up, down_own_grad, far_down, share_own_grad, share_far)
 
     def as_input(v):
         return v.reshape(batches, 1, here, width)
@@ -1940,12 +2135,12 @@
         out_output,
         small_sum[:, 593],
         small_sum[:, 576:592],
-        out_gate.astype(F32)[None],
-        out_up.astype(F32)[None],
+        out_gate[None],
+        out_up[None],
         out_down[None],
-        out_share[:share_width].T,
-        out_share[share_width : 2 * share_width].T,
-        out_share[2 * share_width :],
+        out_sgate.T,
+        out_sup.T,
+        out_sdown,
     )
 
 

time: 719 us -> 702 us (0.976)
  other arithmetic: 40 us -> 18 us
  Pallas kernels: 605 us -> 614 us
  matrix products: 22.6 us -> 13.9 us
    pallas_call x3 -> x5, Pallas kernels: 88.7 us -> 147 us  [the longest x1 68.2 us: attend_back(): pl.pallas_call(functools.partial(attend_back_kernel, dp), grid=(batches,)...]
    pallas_call x2 -> x1, Pallas kernels: 104 us -> 52.8 us  [gather16(): pl.pallas_call(functools.partial(gather_kernel, chunks, dp, span, extra),...]
    broadcast_in_dim x2 -> x0, other arithmetic: 9.55 us -> none  [the longest x1 4.83 us: per_device(): out_gate.astype(F32)[None]]
    add x3 -> x0, other arithmetic: 7.92 us -> none  [the longest x1 3.71 us: per_device(): out_down = out_down + jnp.sum(far_down.astype(F32), axis=0)]
    unnamed x94 -> x84, local copies, waits for them, and re-layouts: 10.3 us -> 14.7 us
  transfers between devices with their start and end apart: 5 -> 5, of which waited for: 0 -> 1; matrix products, arithmetic and copies ran while one was open for 10% -> 5% of each run, Pallas kernels for 56% -> 57%
where the time goes in v11:
time: 702 us; the launch traced here: 696 us
  Pallas kernels  614 us (87%)
  local copies, waits for them, and re-layouts  30.7 us (4%)
  other arithmetic  18 us (3%)
  between operations  14.6 us (2%)
  matrix products  13.9 us (2%)
    pallas_call x1, Pallas kernels, opening(): pl.pallas_call(functools.partial(opening_kernel, dp, chunks), out_shape=(...  80.6 us
    pallas_call x1, Pallas kernels, mixture_forward(): pl.pallas_call(functools.partial(forward_kernel, chunks, dp, span, batche...  70.1 us
    pallas_call x1, Pallas kernels, mixture_backward(): pl.pallas_call(functools.partial(backward_kernel, chunks), grid=(NZ,), ou...  68.4 us
    pallas_call x1, Pallas kernels, attend_back(): pl.pallas_call(functools.partial(attend_back_kernel, dp), grid=(batches,)...  68.2 us
    pallas_call x1, Pallas kernels, scatter_share(): pl.pallas_call(functools.partial(scatter_share_kernel, chunks, down.shape...  66.8 us
    pallas_call x1, Pallas kernels, returning(): pl.pallas_call(functools.partial(return_kernel, dp, chunks), out_shape=(s...  66.1 us
    pallas_call x1, Pallas kernels, attend(): pl.pallas_call(functools.partial(attend_kernel, dp, span), grid=(batches,...  63 us
    pallas_call x1, Pallas kernels, gather16(): pl.pallas_call(functools.partial(gather_kernel, chunks, dp, span, extra),...  52.8 us
  transfers between devices with their start and end apart: 5, of which 1 were waited for; matrix products, arithmetic and copies ran while one was open for 5% of the time, Pallas kernels for 57%

profile of v11, /device:TPU:0, one launch (start us, length us, event | category | flops | bytes accessed | tf_op | source)
XLA Modules:
  0.0 696.2 jit_solution(17889903474455224657)
XLA Ops:
  7.2 2.3 pad_maximum_fusion
  14.7 80.6 %opening.1 = (bf16[16,128,2048]{2,1,0:T(8,128)(2,1)}, bf16[2,16,64,640]{3,2,1,0:T(8,128)(2,1)}, bf16[2,16,64,256]{3,2,1,0:T(8,128)(2,1)}, bf16[2,64,2048]{2,1,0:...) custom-call(bf16[128,2048]{1,0:T(8,128)(2,1)} %bitcast.90, ...), custom_call_target="tpu_custom_call" | custom-call | bytes 4000000 | tf_op jit(solution)/shard_map/opening/pallas_call | solution.py:531
  95.3 1.7 copy-done
  99.7 1.5 reshape.250.we_ref
  101.2 16.9 %project.1 = (bf16[2048,2048]{1,0:T(8,128)(2,1)}, bf16[2,1024,256]{2,1,0:T(8,128)(2,1)S(1)}, bf16[2,1024,256]{2,1,0:T(8,128)(2,1)S(1)}, bf16[2,1024,128]{2,1,0:T(8,128)(2,1)S(1)}, bf16[2,1024,512]{2,1,0:T(8,128)(2,1)}) custom-call(bf16[16,128,2048]{2,1,0:T(8,128)(2,1)} %get-tuple-element.89.x_ref, f32[1,2048]{1,0:T(1,128)S(1)} %get-tuple-element.209.gain_ref, ...), custom_call_target="tpu_custom_call" | custom-call | flops 7000000000 | bytes 20000000 | tf_op jit(solution)/shard_map/project/pallas_call | solution.py:1531
  120.8 63.0 %attend.1 = (f32[128,2048]{1,0:T(8,128)}, bf16[16,2,64,128]{3,2,1,0:T(8,128)(2,1)}, f32[2,1024,1]{2,1,0:T(8,128)}, bf16[2,208,2048]{2,1,0:T(8,128)(2,1)}) custom-call(s32[2]{0:T(128)} %bitcast.139, bf16[2,1024,256]{2,1,0:T(8,128)(2,1)} %copy-done.5, bf16[2,1024,256]{2,1,0:T(8,128)(2,1)} %copy-done.6, bf16[2,1024,128]{2,1,0:T(8,128)(2,1)} %copy-done.11, ...), custom_call_target="tpu_custom_call" | custom-call | bytes 4000000 | tf_op jit(solution)/shard_map/attend/pallas_call | solution.py:1624
  187.2 52.8 %gather16.1 = (bf16[16,128,2048]{2,1,0:T(8,128)(2,1)}, bf16[2,272,2048]{2,1,0:T(8,128)(2,1)}) custom-call(bf16[128,2048]{1,0:T(8,128)(2,1)} %multiply_convert_fusion.x_ref.mix_ref, bf16[704,2048]{1,0:T(8,128)(2,1)} %bitcast.103), custom_call_target="tpu_custom_call" | custom-call | bytes 4000000 | tf_op jit(solution)/shard_map/gather16/pallas_call | solution.py:382
  242.1 1.9 bitcast_multiply_fusion.dy_ref
  244.0 2.9 all-gather.9.cloned.1.call-done
  246.9 70.1 %mixture_forward.1 = (bf16[2048,2048]{1,0:T(8,128)(2,1)}, bf16[1024,2048]{1,0:T(8,128)(2,1)}, bf16[1024,1408]{1,0:T(8,128)(2,1)}, bf16[1024,1408]{1,0:T(8,128)(2...) custom-call(s32[2]{0:T(128)} %bitcast.140, ...), custom_call_target="tpu_custom_call" | custom-call | bytes 4000000 | tf_op jit(solution)/shard_map/mixture_forward/pallas_call | solution.py:1262
  317.1 68.4 %mixture_backward.1 = (bf16[2048,2176]{1,0:T(8,128)(2,1)}, bf16[1024,2048]{1,0:T(8,128)(2,1)}, bf16[1024,1408]{1,0:T(8,128)(2,1)}, bf16[1024,1408]{1,0:T(8,128)(...) custom-call(f32[1,256]{1,0:T(1,128)} %add_convert_fusion.1.pick_ref, bf16[2048,2048]{1,0:T(8,128)(2,1)} %bitcast.100, ...), custom_call_target="tpu_custom_call" | custom-call | bytes 4000000 | tf_op jit(solution)/shard_map/mixture_backward/pallas_call | solution.py:1296
  385.5 10.6 %convolution_convert_fusion = bf16[1408,2048]{1,0:T(8,128)(2,1)} fusion(bf16[1024,1408]{1,0:T(8,128)(2,1)} %get-tuple-element.118, bf16[1024,2048]{1,0:T(8,128)(2,1)} %get-tuple-element.119), kind=kOutput, calls=%fused_computation | convolution fusion | flops 5908463616 | bytes 12845056 | tf_op jit(solution)/shard_map/dot_general | solution.py:1911
  396.1 66.8 %scatter_share.1 = (f32[128,2176]{1,0:T(8,128)}, bf16[2,528,1024]{2,1,0:T(8,128)(2,1)}, bf16[2048,1408]{1,0:T(8,128)(2,1)}, bf16[2048,1408]{1,0:T(8,128)(2,1)}, bf16[1,704,2048]{2,1,0:T(8,128)(2,1)}) custom-call(bf16[16,128,2176]{2,1,0:T(8,128)(2,1)} %bitcast.112, bf16[2048,512]{1,0:T(8,128)(2,1)} %get-tuple-element.113.ds_ref, ...), custom_call_target="tpu_custom_call" | custom-call | bytes 4000000 | tf_op jit(solution)/shard_map/scatter_share/pallas_call | solution.py:1467
  468.1 2.1 multiply_reduce_fusion
  470.3 2.0 fusion.7
  472.2 68.2 %attend_back.1 = (bf16[16,2,64,2688]{3,2,1,0:T(8,128)(2,1)}, bf16[2048,256]{1,0:T(8,128)(2,1)}, bf16[128,2048]{1,0:T(8,128)(2,1)}, bf16[512,256]{1,0:T(8,128)(2,1)}, bf16[1,528,1024]{2,1,0:T(8,128)(2,1)}) custom-call(s32[2]{0:T(128)} %bitcast.141, bf16[128,2048]{1,0:T(8,128)(2,1)} %get-tuple-element.202.own_ref, ...), custom_call_target="tpu_custom_call" | custom-call | bytes 4000000 | tf_op jit(solution)/shard_map/attend_back/pallas_call | solution.py:1748
  541.7 2.5 pad_add_fusion
  544.2 66.1 %returning.1 = (f32[128,2688]{1,0:T(8,128)}, bf16[1,16,64,256]{3,2,1,0:T(8,128)(2,1)}, bf16[1,2,64,2048]{3,2,1,0:T(8,128)(2,1)}) custom-call(bf16[16,128,2688]{2,1,0:T(8,128)(2,1)} %bitcast.111, bf16[2,16,64,256]{3,2,1,0:T(8,128)(2,1)} %bitcast.117, bf16[2,64,2048]{2,1,0:T(8,128)(2,1)} %bitcast.121), custom_call_target="tpu_custom_call" | custom-call | bytes 4000000 | tf_op jit(solution)/shard_map/returning/pallas_call | solution.py:790
  611.7 1.6 copy-done.10
  614.7 4.0 own_back.1
  618.7 1.5 copy-done.8
  622.1 45.6 %closing.1 = (bf16[128,640]{1,0:T(8,128)(2,1)}, bf16[1,64,640]{2,1,0:T(8,128)(2,1)}, f32[64,3072]{1,0:T(8,128)}, f32[16,4096]{1,0:T(8,128)}, f32[64,2048]{1,0:T(8,128)}) custom-call(bf16[16,128,640]{2,1,0:T(8,128)(2,1)} %copy-done.8, bf16[16,64,256]{2,1,0:T(8,128)(2,1)} %fusion.1.parts_ref, bf16[2,64,2048]{2,1,0:T(8,128)(2,1)} %fusion.rows_ref), custom_call_target="tpu_custom_call" | custom-call | bytes 4000000 | tf_op jit(solution)/shard_map/closing/pallas_call | solution.py:905
  671.9 3.8 dynamic-slice_bitcast_fusion.down_ref
  675.8 11.3 %widen.1 = (f32[1024,1408]{1,0:T(8,128)}, f32[1024,1408]{1,0:T(8,128)}, f32[704,2048]{1,0:T(8,128)}, f32[176,1024]{1,0:T(8,128)}, f32[176,1024]{1,0:T(8,128)}, /*index=5*/f32[176,1024]{1,0:T(8,128)}) custom-call(bf16[1024,1408]{1,0:T(8,128)(2,1)} %reduce-scatter.3.cloned.1.call-done.gate_ref, bf16[1024,1408]{1,0:T(8,128)(2,1)} %reduce-scatter.5.cloned.1.call-done.up_ref, ...), custom_call_target="tpu_custom_call" | custom-call | bytes 4000000 | tf_op jit(solution)/shard_map/widen/pallas_call | solution.py:1884
  (150 shorter events, 33.5 us)
Async XLA Ops:
  7.2 236.9 %all-gather.11.cloned.1.call-start = ((), (), s32[]{:S(2)}) async-start(), calls=%async_computation.6 | async-start | bytes 3244032 | tf_op jit(solution)/shard_map/all_gather | solution.py:2038
  9.6 234.5 %all-gather.7.cloned.1.call-start = ((), (), s32[]{:S(2)}) async-start(), calls=%async_computation.4 | async-start | bytes 8650752 | tf_op jit(solution)/shard_map/all_gather | solution.py:2036
  10.4 236.6 %all-gather.9.cloned.1.call-start = ((), (), s32[]{:S(2)}) async-start(), calls=%async_computation.5 | async-start | bytes 8650752 | tf_op jit(solution)/shard_map/all_gather | solution.py:2037
  11.1 664.6 %reduce-scatter.3.cloned.1.call-start = ((), (), s32[]{:S(2)}) async-start(), calls=%async_computation.2 | async-start | bytes 8650752 | tf_op jit(solution)/shard_map/reduce_scatter | solution.py:2085
  97.1 4.1 copy-start.15
  97.1 4.1 copy-start.16
  101.1 17.0 %copy-start.13 = (bf16[512,256]{1,0:T(8,128)(2,1)}, bf16[512,256]{1,0:T(8,128)(2,1)S(1)}, u32[]{:S(2)}) copy-start(bf16[512,256]{1,0:T(8,128)(2,1)S(1)} %reshape.250.we_ref) | copy-start | bytes 786436
  120.8 63.0 %copy-start.3 = (bf16[2,1,64,2048]{3,2,1,0:T(8,128)(2,1)S(1)}, bf16[2,1,64,2048]{3,2,1,0:T(8,128)(2,1)}, u32[]{:S(2)}) copy-start(bf16[2,1,64,2048]{3,2,1,0:T(8,128)(2,1)} %param.28) | copy-start | bytes 1572868
  185.3 54.7 %copy-start.1 = (bf16[2,16,64,640]{3,2,1,0:T(8,128)(2,1)S(1)}, bf16[2,16,64,640]{3,2,1,0:T(8,128)(2,1)}, u32[]{:S(2)}) copy-start(bf16[2,16,64,640]{3,2,1,0:T(8,128)(2,1)} %get-tuple-element.90) | copy-start | bytes 7864324
  187.2 54.1 %copy-start.33 = (s32[2,1]{0,1:T(1,128)S(1)}, s32[2,1]{0,1:T(1,128)}, u32[]{:S(2)}) copy-start(s32[2,1]{0,1:T(1,128)} %param.30) | copy-start | bytes 28
  462.9 212.8 %reduce-scatter.5.cloned.1.call-start = ((), (), s32[]{:S(2)}) async-start(), calls=%async_computation.3 | async-start | bytes 8650752 | tf_op jit(solution)/shard_map/reduce_scatter | solution.py:2086
  463.0 5.1 copy-start.18
  463.5 6.7 copy-start.22
  463.6 6.6 copy-start.23
  544.2 66.1 %copy-start.2 = (bf16[2,16,64,640]{3,2,1,0:T(8,128)(2,1)S(1)}, bf16[2,16,64,640]{3,2,1,0:T(8,128)(2,1)}, u32[]{:S(2)}) copy-start(bf16[2,16,64,640]{3,2,1,0:T(8,128)(2,1)} %get-tuple-element.90) | copy-start | bytes 7864324
  614.7 5.5 copy-start.19
  614.7 5.5 copy-start.27
  614.7 6.5 copy-start.21
  614.7 6.5 copy-start.25
  621.2 49.7 %copy-start.20 = (bf16[2,528,1024]{2,1,0:T(8,128)(2,1)S(1)}, bf16[2,528,1024]{2,1,0:T(8,128)(2,1)}, u32[]{:S(2)}) copy-start(bf16[2,528,1024]{2,1,0:T(8,128)(2,1)} %get-tuple-element.121.side_ref) | copy-start | bytes 6488068
  668.7 7.1 %copy-start.28 = (f32[64,640]{1,0:T(8,128)}, f32[64,640]{1,0:T(8,128)S(1)}, u32[]{:S(2)}) copy-start(f32[64,640]{1,0:T(8,128)S(1)} %convert_add_fusion.2) | copy-start | bytes 491524
  675.7 11.4 %copy-start.24 = (f32[64,3072]{1,0:T(8,128)S(1)}, f32[64,3072]{1,0:T(8,128)}, u32[]{:S(2)}) copy-start(f32[64,3072]{1,0:T(8,128)} %get-tuple-element.236) | copy-start | bytes 2359300
  675.7 12.2 %copy-start.30 = (f32[16,4096]{1,0:T(8,128)S(1)}, f32[16,4096]{1,0:T(8,128)}, u32[]{:S(2)}) copy-start(f32[16,4096]{1,0:T(8,128)} %get-tuple-element.239) | copy-start | bytes 786436
  675.8 12.9 %copy-start.26 = (f32[64,2048]{1,0:T(8,128)S(1)}, f32[64,2048]{1,0:T(8,128)}, u32[]{:S(2)}) copy-start(f32[64,2048]{1,0:T(8,128)} %get-tuple-element.240) | copy-start | bytes 1572868
  (20 other events, 32.5 us)
Sparse Core Ops, SparseCore 0:
  10.1 52.5 all-gather.10
  64.3 78.5 all-gather.6
  144.4 102.4 all-gather.8
  463.1 102.9 reduce-scatter.2
  568.3 73.4 reduce-scatter.4

commit v12 on v11

--- a/solution.py
+++ b/solution.py
@@ -846,6 +846,8 @@
         return pltpu.make_async_copy(rows_ref.at[j], row_in, kept_sem.at[1])
 
     s.start()
+    for i in range(NZ):
+        s.first(i)
     for r in range(1, NE):
         part(r).start()
     part_kept().start()
@@ -859,7 +861,8 @@
         @pl.when(keeper & (home == me))
         def _():
             row_kept(j).start()
-    s.run()
+    for i in range(NZ):
+        s.second(i)
     for r in range(1, dp):
         lift(r).start()
     for r in range(1, NE):
@@ -1133,7 +1136,7 @@
 
         lax.fori_loop(0, width // WIDE, fan_out, 0)
 
-    for r, s in ((1, 1), (2, 2), (3, 3), (4, 5)):
+    for r, s in ((1, 1), (2, 3), (3, 5), (4, 7)):
         @pl.when(step == s)
         def _():
             g.round(r)
@@ -1828,6 +1831,10 @@
             out_ref[e, d * rows_w:(d + 1) * rows_w] = part[i * rows_w:(i + 1) * rows_w]
 
 
+def one_step(*arrays):
+    return [pl.BlockSpec(v.shape, lambda i, n=v.ndim if hasattr(v, "ndim") else len(v.shape): (0,) * n) for v in arrays]
+
+
 def own_back(dp, back, x, mix, logit, gmix, gain, lgain, small, cosine, sine, mid, rows_l):
     tokens, width = x.shape
     rows_w = width // (dp * NE)
@@ -1835,22 +1842,62 @@
     place = (count // rows_w * rows_l + count % rows_w)[None, :] == np.arange(512)[:, None]
     place = place & (count % rows_w < rows_l)[None, :]
     shape = jax.ShapeDtypeStruct
+    args = (back, x, mix, logit, gmix, gain, lgain, small, cosine, sine, mid, jnp.asarray(place.astype(np.float32), BF))
+    outs = (shape((tokens, width), F32), shape((NE, dp * rows_w, small.shape[1]), BF))
     return pl.pallas_call(
         functools.partial(own_back_kernel, dp),
-        out_shape=(shape((tokens, width), F32), shape((NE, dp * rows_w, small.shape[1]), BF)),
-        in_specs=[VMEM] * 12,
-        out_specs=(VMEM, VMEM),
-        compiler_params=pltpu.CompilerParams(vmem_limit_bytes=40 * 1024 * 1024),
+        grid=(1,),
+        out_shape=outs,
+        in_specs=one_step(*args),
+        out_specs=tuple(one_step(*outs)),
+        compiler_params=pltpu.CompilerParams(vmem_limit_bytes=60 * 1024 * 1024),
         cost_estimate=COST,
         name="own_back",
-    )(back, x, mix, logit, gmix, gain, lgain, small, cosine, sine, mid, jnp.asarray(place.astype(np.float32), BF))
-
-
-def widen_kernel(gate_ref, up_ref, down_ref, down_far, share_ref, share_far, gate_out, up_out, down_out, sg_out, su_out,
-                 sd_out):
+    )(*args)
+
+
+def own_middle_kernel(sum_ref, mix_ref, mask_ref, router_ref, middle_ref, gain_ref, dy_ref, valid_ref,
+                      grad_ref, low_ref, logit_ref, gmix_ref):
+    width = mix_ref.shape[1]
+    middle = middle_ref[...]
+    factor = lax.rsqrt(jnp.mean(middle * middle, axis=1, keepdims=True) + 1e-6)
+    unit = middle * factor
+    mask = mask_ref[...].astype(F32)
+    held = jnp.where(mask > 0.5, mm_t(mix_ref[...], router_ref[...]), -1e30)
+    raised = jnp.exp(held - jnp.max(held, axis=1, keepdims=True)) * mask
+    soft = raised / jnp.sum(raised, axis=1, keepdims=True)
+    d_gates = (sum_ref[:, width:width + 16] + sum_ref[:, width + 16:width + 32]) * valid_ref[...]
+    d_logits = (soft * (d_gates - jnp.sum(d_gates * soft, axis=1, keepdims=True))).astype(BF)
+    logit_ref[...] = d_logits
+    d_mix = sum_ref[:, :width] + mm(d_logits, router_ref[...])
+    gmix_ref[...] = jnp.sum(d_mix * unit, axis=0, keepdims=True)
+    scaled = d_mix * gain_ref[...]
+    grad = dy_ref[...].astype(F32) + factor * (scaled - unit * jnp.mean(scaled * unit, axis=1, keepdims=True))
+    grad_ref[...] = grad
+    low_ref[...] = grad.astype(BF)
+
+
+def own_middle(total, mix, mask, router, middle, gain, dy, valid):
+    shape = jax.ShapeDtypeStruct
+    args = (total, mix, mask, router, middle, gain, dy, valid)
+    outs = (shape(middle.shape, F32), shape(middle.shape, BF), shape(mask.shape, BF), shape(gain.shape, F32))
+    return pl.pallas_call(
+        own_middle_kernel,
+        grid=(1,),
+        out_shape=outs,
+        in_specs=one_step(*args),
+        out_specs=tuple(one_step(*outs)),
+        compiler_params=pltpu.CompilerParams(vmem_limit_bytes=60 * 1024 * 1024),
+        cost_estimate=COST,
+        name="own_middle",
+    )(*args)
+
+
+def widen_kernel(plane_ref, gate_ref, up_ref, down_ref, down_far, share_ref, share_far, gate_out, up_out, down_out, sg_out,
+                 su_out, sd_out):
     gate_out[...] = gate_ref[...].astype(F32)
     up_out[...] = up_ref[...].astype(F32)
-    down = down_ref[...].astype(F32)
+    down = down_ref[0].astype(F32)
     for r in range(down_far.shape[0]):
         down = down + down_far[r].astype(F32)
     down_out[...] = down
@@ -1860,37 +1907,41 @@
         n = sg_out.shape[0]
         for i, out in enumerate((sg_out, su_out, sd_out)):
             rows = slice(i * n, (i + 1) * n)
-            v = share_ref[rows].astype(F32)
+            v = share_ref[0, rows].astype(F32)
             for r in range(share_far.shape[0]):
                 v = v + share_far[r, rows].astype(F32)
             out[...] = v
 
 
-def widen(gate, up, down, down_far, share, share_far):
-    steps = 2 if down.shape[0] % 32 == 0 else 1
+def widen(plane, gate, up, down, down_far, share, share_far):
+    steps = 2 if down.shape[1] % 32 == 0 else 1
     shape = jax.ShapeDtypeStruct
 
-    def cut(v):
-        return pl.BlockSpec((v.shape[0] // steps, v.shape[1]), lambda i: (i, 0))
-
-    def cut_far(v):
-        return pl.BlockSpec((v.shape[0], v.shape[1] // steps, v.shape[2]), lambda i: (0, i, 0))
+    def cut(rows, w):
+        return pl.BlockSpec((rows // steps, w), lambda i, p: (i, 0))
 
     def full(shape_):
         zeros = (0,) * len(shape_)
-        return pl.BlockSpec(shape_, lambda i: zeros)
-
-    third = (share.shape[0] // 3, share.shape[1])
+        return pl.BlockSpec(shape_, lambda i, p: zeros)
+
+    _, rows, w = down.shape
+    third = (share.shape[1] // 3, share.shape[2])
     return pl.pallas_call(
         widen_kernel,
-        grid=(steps,),
-        out_shape=tuple(shape(v.shape, F32) for v in (gate, up, down)) + (shape(third, F32),) * 3,
-        in_specs=[cut(gate), cut(up), cut(down), cut_far(down_far), full(share.shape), full(share_far.shape)],
-        out_specs=[cut(gate), cut(up), cut(down)] + [full(third)] * 3,
+        grid_spec=pltpu.PrefetchScalarGridSpec(
+            num_scalar_prefetch=1,
+            grid=(steps,),
+            in_specs=[cut(*gate.shape), cut(*up.shape),
+                      pl.BlockSpec((1, rows // steps, w), lambda i, p: (p[0], i, 0)),
+                      pl.BlockSpec((down_far.shape[0], rows // steps, w), lambda i, p: (0, i, 0)),
+                      pl.BlockSpec((1,) + share.shape[1:], lambda i, p: (p[0], 0, 0)), full(share_far.shape)],
+            out_specs=[cut(*gate.shape), cut(*up.shape), cut(rows, w)] + [full(third)] * 3,
+        ),
+        out_shape=tuple(shape(v, F32) for v in (gate.shape, up.shape, (rows, w))) + (shape(third, F32),) * 3,
         compiler_params=pltpu.CompilerParams(vmem_limit_bytes=56 * 1024 * 1024),
         cost_estimate=COST,
         name="widen",
-    )(gate, up, down, down_far, share, share_far)
+    )(plane, gate, up, down, down_far, share, share_far)
 
 
 H = 16
@@ -2079,26 +2130,18 @@
     mix_sum, grad_share, grad_gate, grad_up, far_down = scatter_share(
         mix_part.reshape(GROUPS, own, width + 128), grad_share_in, share_hidden, mix_all, grad_all,
         rows, grad_gate_in, grad_up_in, grad_down, share_full.shape, 5)
-    down_own_grad = lax.dynamic_index_in_dim(grad_down, plane, 0, False)
     layer_output = valid_own[:, None] * (middle + mixed)
 
     out_gate = lax.psum_scatter(grad_gate, "dp", scatter_dimension=0, tiled=True)
     out_up = lax.psum_scatter(grad_up, "dp", scatter_dimension=0, tiled=True)
 
-    soft_own = masked_softmax(product_trail(hidden_mix, router_lines), mask_own)
-    grad_masked = (mix_sum[:, width : width + GROUPS] + mix_sum[:, width + GROUPS : width + 2 * GROUPS])
-    grad_masked = grad_masked * valid_own[:, None]
-    grad_logits = soft_own * (grad_masked - jnp.sum(grad_masked * soft_own, axis=1, keepdims=True))
-    grad_logits = grad_logits.astype(BF)
-    grad_mix = mix_sum[:, :width] + product(grad_logits, router_lines)
-    grad_middle_norm, grad_gain_mixer = norm_backward(grad_mix, unit_mix, factor_mix, gain_mixer)
-    grad_middle = grad_own.astype(F32) + grad_middle_norm
+    grad_middle, grad_middle_low, grad_logits, grad_gain_mixer = own_middle(
+        mix_sum, hidden_mix, mask_own.astype(BF), router_lines, middle, gain_mixer[None], grad_own, valid_own[:, None])
 
     back_part, grad_query_w, grad_output, grad_expand, share_far = attend_back(
-        dp, seq_lengths, grad_middle.astype(BF), grad_share, hidden_all.reshape(GROUPS, batches, here, width), query, key,
+        dp, seq_lengths, grad_middle_low, grad_share, hidden_all.reshape(GROUPS, batches, here, width), query, key,
         values, latent, attended, log_total, output_head, parts_head, expand_head, jnp.asarray(cosine),
         jnp.asarray(sine_table), 640, 6)
-    share_own_grad = lax.dynamic_index_in_dim(grad_share, plane, 0, False)
     grad_expand = grad_expand.reshape(dp * GROUPS, rows_l, 4, ROPE).swapaxes(1, 2).reshape(width, ROPE)
     parts_grad = grad_query_w + jnp.pad(grad_expand, ((0, 0), (QK_NOPE + ROPE, 0)))
     parts_grad = parts_grad.reshape(dp, GROUPS, rows_w, TILE)
@@ -2114,12 +2157,12 @@
         return jnp.broadcast_to(own_rows[None], (batches, here, ROPE // 2)).reshape(own, ROPE // 2)
 
     grad_input, small_grad = own_back(
-        dp, back_sum, x_own, hidden_mix, grad_logits, grad_gain_mixer[None], gain_attn[None], gain_latent[None], small,
+        dp, back_sum, x_own, hidden_mix, grad_logits, grad_gain_mixer, gain_attn[None], gain_latent[None], small,
         own_table(cosine), own_table(sine_table), grad_middle, rows_l)
     small_sum, out_query, out_expand, out_output = closing(dp, small_grad, parts_sum, rows_sum, rows_l, 9)
 
     out_gate, out_up, out_down, out_sgate, out_sup, out_sdown = widen(
-        out_gate, out_up, down_own_grad, far_down, share_own_grad, share_far)
+        plane.reshape(1).astype(jnp.int32), out_gate, out_up, grad_down, far_down, grad_share, share_far)
 
     def as_input(v):
         return v.reshape(batches, 1, here, width)

time: 702 us -> 691 us (0.984)
  local copies, waits for them, and re-layouts: 30.7 us -> 21.1 us
    pallas_call x2 -> x3, Pallas kernels: 15.3 us -> 25 us  [the longest x1 11.3 us: widen(): pl.pallas_call(widen_kernel, grid_spec=pltpu.PrefetchScalarGridSpec(num_s...]
    unnamed x84 -> x76, local copies, waits for them, and re-layouts: 14.7 us -> 10.1 us
  transfers between devices with their start and end apart: 5 -> 5, of which waited for: 1 -> 1; matrix products, arithmetic and copies ran while one was open for 5% -> 3% of each run, Pallas kernels for 57% -> 60%
where the time goes in v12:
time: 691 us; the launch traced here: 686 us
  Pallas kernels  619 us (90%)
  local copies, waits for them, and re-layouts  21.1 us (3%)
  between operations  14.5 us (2%)
  other arithmetic  13.7 us (2%)
  matrix products  10.7 us (2%)
    pallas_call x1, Pallas kernels, opening(): pl.pallas_call(functools.partial(opening_kernel, dp, chunks), out_shape=(...  80.6 us
    pallas_call x1, Pallas kernels, attend_back(): pl.pallas_call(functools.partial(attend_back_kernel, dp), grid=(batches,)...  69.5 us
    pallas_call x1, Pallas kernels, scatter_share(): pl.pallas_call(functools.partial(scatter_share_kernel, chunks, down.shape...  66.7 us
    pallas_call x1, Pallas kernels, returning(): pl.pallas_call(functools.partial(return_kernel, dp, chunks), out_shape=(s...  66.5 us
    pallas_call x1, Pallas kernels, mixture_backward(): pl.pallas_call(functools.partial(backward_kernel, chunks), grid=(NZ,), ou...  65.6 us
    pallas_call x1, Pallas kernels, mixture_forward(): pl.pallas_call(functools.partial(forward_kernel, chunks, dp, span, batche...  65.6 us
    pallas_call x1, Pallas kernels, attend(): pl.pallas_call(functools.partial(attend_kernel, dp, span), grid=(batches,...  63 us
    pallas_call x1, Pallas kernels, gather16(): pl.pallas_call(functools.partial(gather_kernel, chunks, dp, span, extra),...  52.8 us
  transfers between devices with their start and end apart: 5, of which 1 were waited for; matrix products, arithmetic and copies ran while one was open for 3% of the time, Pallas kernels for 60%

profile of v12, /device:TPU:0, one launch (start us, length us, event | category | flops | bytes accessed | tf_op | source)
XLA Modules:
  0.0 685.8 jit_solution(15190670661155421718)
XLA Ops:
  7.2 2.3 pad_maximum_fusion
  14.7 80.6 %opening.1 = (bf16[16,128,2048]{2,1,0:T(8,128)(2,1)}, bf16[2,16,64,640]{3,2,1,0:T(8,128)(2,1)}, bf16[2,16,64,256]{3,2,1,0:T(8,128)(2,1)}, bf16[2,64,2048]{2,1,0:...) custom-call(bf16[128,2048]{1,0:T(8,128)(2,1)} %bitcast.106, ...), custom_call_target="tpu_custom_call" | custom-call | bytes 4000000 | tf_op jit(solution)/shard_map/opening/pallas_call | solution.py:531
  95.4 1.7 copy-done
  99.2 1.3 copy-done.10
  100.5 17.2 %project.1 = (bf16[2048,2048]{1,0:T(8,128)(2,1)}, bf16[2,1024,256]{2,1,0:T(8,128)(2,1)S(1)}, bf16[2,1024,256]{2,1,0:T(8,128)(2,1)S(1)}, bf16[2,1024,128]{2,1,0:T(8,128)(2,1)S(1)}, bf16[2,1024,512]{2,1,0:T(8,128)(2,1)}) custom-call(bf16[16,128,2048]{2,1,0:T(8,128)(2,1)} %get-tuple-element.93.x_ref, f32[1,2048]{1,0:T(1,128)S(1)} %get-tuple-element.212.gain_ref, ...), custom_call_target="tpu_custom_call" | custom-call | flops 7000000000 | bytes 20000000 | tf_op jit(solution)/shard_map/project/pallas_call | solution.py:1534
  118.7 1.0 copy-done.3
  120.4 63.0 %attend.1 = (f32[128,2048]{1,0:T(8,128)}, bf16[16,2,64,128]{3,2,1,0:T(8,128)(2,1)}, f32[2,1024,1]{2,1,0:T(8,128)}, bf16[2,208,2048]{2,1,0:T(8,128)(2,1)}) custom-call(s32[2]{0:T(128)} %bitcast.128, bf16[2,1024,256]{2,1,0:T(8,128)(2,1)} %copy-done.2, bf16[2,1024,256]{2,1,0:T(8,128)(2,1)} %copy-done.3, bf16[2,1024,128]{2,1,0:T(8,128)(2,1)} %copy-done.5, ...), custom_call_target="tpu_custom_call" | custom-call | bytes 4000000 | tf_op jit(solution)/shard_map/attend/pallas_call | solution.py:1627
  183.5 1.4 multiply_reduce_fusion
  186.8 52.8 %gather16.1 = (bf16[16,128,2048]{2,1,0:T(8,128)(2,1)}, bf16[2,272,2048]{2,1,0:T(8,128)(2,1)}) custom-call(bf16[128,2048]{1,0:T(8,128)(2,1)} %multiply_convert_fusion.x_ref.mix_ref, bf16[704,2048]{1,0:T(8,128)(2,1)} %bitcast.90), custom_call_target="tpu_custom_call" | custom-call | bytes 4000000 | tf_op jit(solution)/shard_map/gather16/pallas_call | solution.py:382
  239.9 1.1 reshape.264.mask_ref
  242.6 4.8 all-gather.9.cloned.1.call-done
  247.4 65.6 %mixture_forward.1 = (bf16[2048,2048]{1,0:T(8,128)(2,1)}, bf16[1024,2048]{1,0:T(8,128)(2,1)}, bf16[1024,1408]{1,0:T(8,128)(2,1)}, bf16[1024,1408]{1,0:T(8,128)(2...) custom-call(s32[2]{0:T(128)} %bitcast.129, ...), custom_call_target="tpu_custom_call" | custom-call | bytes 4000000 | tf_op jit(solution)/shard_map/mixture_forward/pallas_call | solution.py:1265
  313.0 65.6 %mixture_backward.1 = (bf16[2048,2176]{1,0:T(8,128)(2,1)}, bf16[1024,2048]{1,0:T(8,128)(2,1)}, bf16[1024,1408]{1,0:T(8,128)(2,1)}, bf16[1024,1408]{1,0:T(8,128)(...) custom-call(f32[1,256]{1,0:T(1,128)} %add_convert_fusion.1.pick_ref, bf16[2048,2048]{1,0:T(8,128)(2,1)} %bitcast.87, ...), custom_call_target="tpu_custom_call" | custom-call | bytes 4000000 | tf_op jit(solution)/shard_map/mixture_backward/pallas_call | solution.py:1299
  378.6 10.7 %convolution_convert_fusion = bf16[1408,2048]{1,0:T(8,128)(2,1)} fusion(bf16[1024,1408]{1,0:T(8,128)(2,1)} %get-tuple-element.122, bf16[1024,2048]{1,0:T(8,128)(2,1)} %get-tuple-element.123), kind=kOutput, calls=%fused_computation | convolution fusion | flops 5908463616 | bytes 12845056 | tf_op jit(solution)/shard_map/dot_general | solution.py:1962
  389.3 66.7 %scatter_share.1 = (f32[128,2176]{1,0:T(8,128)}, bf16[2,528,1024]{2,1,0:T(8,128)(2,1)}, bf16[2048,1408]{1,0:T(8,128)(2,1)}, bf16[2048,1408]{1,0:T(8,128)(2,1)}, bf16[1,704,2048]{2,1,0:T(8,128)(2,1)}) custom-call(bf16[16,128,2176]{2,1,0:T(8,128)(2,1)} %bitcast.99, bf16[2048,512]{1,0:T(8,128)(2,1)} %get-tuple-element.117.ds_ref, ...), custom_call_target="tpu_custom_call" | custom-call | bytes 4000000 | tf_op jit(solution)/shard_map/scatter_share/pallas_call | solution.py:1470
  458.2 4.3 own_middle.1
  462.5 69.5 %attend_back.1 = (bf16[16,2,64,2688]{3,2,1,0:T(8,128)(2,1)}, bf16[2048,256]{1,0:T(8,128)(2,1)}, bf16[128,2048]{1,0:T(8,128)(2,1)}, bf16[512,256]{1,0:T(8,128)(2,1)}, bf16[1,528,1024]{2,1,0:T(8,128)(2,1)}) custom-call(s32[2]{0:T(128)} %bitcast.130, bf16[128,2048]{1,0:T(8,128)(2,1)} %get-tuple-element.125.own_ref, ...), custom_call_target="tpu_custom_call" | custom-call | bytes 4000000 | tf_op jit(solution)/shard_map/attend_back/pallas_call | solution.py:1751
  532.1 1.2 reshape.273
  533.4 2.5 pad_add_fusion
  535.9 66.5 %returning.1 = (f32[128,2688]{1,0:T(8,128)}, bf16[1,16,64,256]{3,2,1,0:T(8,128)(2,1)}, bf16[1,2,64,2048]{3,2,1,0:T(8,128)(2,1)}) custom-call(bf16[16,128,2688]{2,1,0:T(8,128)(2,1)} %bitcast.98, bf16[2,16,64,256]{3,2,1,0:T(8,128)(2,1)} %bitcast.104, bf16[2,64,2048]{2,1,0:T(8,128)(2,1)} %bitcast.110), custom_call_target="tpu_custom_call" | custom-call | bytes 4000000 | tf_op jit(solution)/shard_map/returning/pallas_call | solution.py:790
  603.7 9.3 %own_back.1 = (f32[128,2048]{1,0:T(8,128)}, bf16[16,128,640]{2,1,0:T(8,128)(2,1)}) custom-call(f32[128,2688]{1,0:T(8,128)} %get-tuple-element.135.back_ref, bf16[128,2048]{1,0:T(8,128)(2,1)} %bitcast.107, bf16[128,2048]{1,0:T(8,128)(2,1)} %multiply_convert_fusion.x_ref.mix_ref, bf16[128,16]{1,0:T(8,128)(2,1)} %get-tuple-element.136.logit_ref, ...), custom_call_target="tpu_custom_call" | custom-call | bytes 4000000 | tf_op jit(solution)/shard_map/own_back/pallas_call | solution.py:1847
  614.9 46.1 %closing.1 = (bf16[128,640]{1,0:T(8,128)(2,1)}, bf16[1,64,640]{2,1,0:T(8,128)(2,1)}, f32[64,3072]{1,0:T(8,128)}, f32[16,4096]{1,0:T(8,128)}, f32[64,2048]{1,0:T(8,128)}) custom-call(bf16[16,128,640]{2,1,0:T(8,128)(2,1)} %get-tuple-element.140.p_ref, bf16[16,64,256]{2,1,0:T(8,128)(2,1)} %fusion.1.parts_ref, bf16[2,64,2048]{2,1,0:T(8,128)(2,1)} %fusion.rows_ref), custom_call_target="tpu_custom_call" | custom-call | bytes 4000000 | tf_op jit(solution)/shard_map/closing/pallas_call | solution.py:908
  664.1 1.2 add_multiply_fusion
  665.3 11.3 %widen.1 = (f32[1024,1408]{1,0:T(8,128)}, f32[1024,1408]{1,0:T(8,128)}, f32[704,2048]{1,0:T(8,128)}, f32[176,1024]{1,0:T(8,128)}, f32[176,1024]{1,0:T(8,128)}, /*index=5*/f32[176,1024]{1,0:T(8,128)}) custom-call(s32[1]{0:T(128)} %bitcast.45.plane_ref, bf16[1024,1408]{1,0:T(8,128)(2,1)} %reduce-scatter.3.cloned.1.call-done.gate_ref, ...), custom_call_target="tpu_custom_call" | custom-call | bytes 4000000 | tf_op jit(solution)/shard_map/widen/pallas_call | solution.py:1929
  (135 shorter events, 23.6 us)
Async XLA Ops:
  7.2 235.4 %all-gather.11.cloned.1.call-start = ((), (), s32[]{:S(2)}) async-start(), calls=%async_computation.6 | async-start | bytes 3244032 | tf_op jit(solution)/shard_map/all_gather | solution.py:2089
  9.6 233.0 %all-gather.7.cloned.1.call-start = ((), (), s32[]{:S(2)}) async-start(), calls=%async_computation.4 | async-start | bytes 8650752 | tf_op jit(solution)/shard_map/all_gather | solution.py:2087
  10.4 237.0 %all-gather.9.cloned.1.call-start = ((), (), s32[]{:S(2)}) async-start(), calls=%async_computation.5 | async-start | bytes 8650752 | tf_op jit(solution)/shard_map/all_gather | solution.py:2088
  11.1 654.2 %reduce-scatter.3.cloned.1.call-start = ((), (), s32[]{:S(2)}) async-start(), calls=%async_computation.2 | async-start | bytes 8650752 | tf_op jit(solution)/shard_map/reduce_scatter | solution.py:2135
  11.4 83.9 %copy-start.24 = (bf16[128,16]{1,0:T(8,128)(2,1)}, bf16[128,16]{1,0:T(8,128)(2,1)S(1)}, u32[]{:S(2)}) copy-start(bf16[128,16]{1,0:T(8,128)(2,1)S(1)} %convert_element_type.120.mask_ref) | copy-start | bytes 12292
  98.0 19.7 %copy-start.7 = (f32[1,2048]{1,0:T(1,128)}, f32[1,2048]{1,0:T(1,128)S(1)}, u32[]{:S(2)}) copy-start(f32[1,2048]{1,0:T(1,128)S(1)} %get-tuple-element.212.gain_ref) | copy-start | bytes 24580
  98.0 86.9 %copy-start.28 = (f32[1,2048]{1,0:T(1,128)}, f32[1,2048]{1,0:T(1,128)S(1)}, u32[]{:S(2)}) copy-start(f32[1,2048]{1,0:T(1,128)S(1)} %get-tuple-element.210.gain_ref) | copy-start | bytes 24580
  98.2 19.5 %copy-start.8 = (f32[1,512]{1,0:T(1,128)}, f32[1,512]{1,0:T(1,128)S(1)}, u32[]{:S(2)}) copy-start(f32[1,512]{1,0:T(1,128)S(1)} %reshape.283.lgain_ref) | copy-start | bytes 6148
  99.2 18.5 %copy-start.6 = (bf16[512,256]{1,0:T(8,128)(2,1)}, bf16[512,256]{1,0:T(8,128)(2,1)S(1)}, u32[]{:S(2)}) copy-start(bf16[512,256]{1,0:T(8,128)(2,1)S(1)} %reshape.261.we_ref) | copy-start | bytes 786436
  120.4 63.0 %copy-start.14 = (bf16[2,1,64,2048]{3,2,1,0:T(8,128)(2,1)S(1)}, bf16[2,1,64,2048]{3,2,1,0:T(8,128)(2,1)}, u32[]{:S(2)}) copy-start(bf16[2,1,64,2048]{3,2,1,0:T(8,128)(2,1)} %param.28) | copy-start | bytes 1572868
  184.9 54.7 %copy-start.1 = (bf16[2,16,64,640]{3,2,1,0:T(8,128)(2,1)S(1)}, bf16[2,16,64,640]{3,2,1,0:T(8,128)(2,1)}, u32[]{:S(2)}) copy-start(bf16[2,16,64,640]{3,2,1,0:T(8,128)(2,1)} %get-tuple-element.94) | copy-start | bytes 7864324
  186.8 54.1 %copy-start.29 = (s32[2,1]{0,1:T(1,128)S(1)}, s32[2,1]{0,1:T(1,128)}, u32[]{:S(2)}) copy-start(s32[2,1]{0,1:T(1,128)} %param.30) | copy-start | bytes 28
  186.8 54.9 %copy-start.21 = (bf16[2,1,64,2048]{3,2,1,0:T(8,128)(2,1)S(1)}, bf16[2,1,64,2048]{3,2,1,0:T(8,128)(2,1)}, u32[]{:S(2)}) copy-start(bf16[2,1,64,2048]{3,2,1,0:T(8,128)(2,1)} %param.29) | copy-start | bytes 1572868
  456.1 209.2 %reduce-scatter.5.cloned.1.call-start = ((), (), s32[]{:S(2)}) async-start(), calls=%async_computation.3 | async-start | bytes 8650752 | tf_op jit(solution)/shard_map/reduce_scatter | solution.py:2136
  603.7 9.3 %copy-start.13 = (bf16[2048,256]{1,0:T(8,128)(2,1)S(1)}, bf16[2048,256]{1,0:T(8,128)(2,1)}, u32[]{:S(2)}) copy-start(bf16[2048,256]{1,0:T(8,128)(2,1)} %pad_add_fusion) | copy-start | bytes 3145732
  603.7 9.3 %copy-start.20 = (bf16[1,16,64,256]{3,2,1,0:T(8,128)(2,1)S(1)}, bf16[1,16,64,256]{3,2,1,0:T(8,128)(2,1)}, u32[]{:S(2)}) copy-start(bf16[1,16,64,256]{3,2,1,0:T(8,128)(2,1)} %get-tuple-element.141) | copy-start | bytes 1572868
  603.7 10.3 %copy-start.15 = (bf16[128,2048]{1,0:T(8,128)(2,1)S(1)}, bf16[128,2048]{1,0:T(8,128)(2,1)}, u32[]{:S(2)}) copy-start(bf16[128,2048]{1,0:T(8,128)(2,1)} %get-tuple-element.134) | copy-start | bytes 1572868
  603.7 10.3 %copy-start.18 = (bf16[1,2,64,2048]{3,2,1,0:T(8,128)(2,1)S(1)}, bf16[1,2,64,2048]{3,2,1,0:T(8,128)(2,1)}, u32[]{:S(2)}) copy-start(bf16[1,2,64,2048]{3,2,1,0:T(8,128)(2,1)} %get-tuple-element.142) | copy-start | bytes 1572868
  613.9 50.1 %copy-start.12 = (f32[128,2048]{1,0:T(8,128)S(1)}, f32[128,2048]{1,0:T(8,128)}, u32[]{:S(2)}) copy-start(f32[128,2048]{1,0:T(8,128)} %copy-done.11) | copy-start | bytes 3145732
  613.9 50.1 %copy-start.16 = (f32[128,2048]{1,0:T(8,128)S(1)}, f32[128,2048]{1,0:T(8,128)}, u32[]{:S(2)}) copy-start(f32[128,2048]{1,0:T(8,128)} %get-tuple-element.115) | copy-start | bytes 3145732
  661.9 14.7 %copy-start.22 = (f32[64,640]{1,0:T(8,128)}, f32[64,640]{1,0:T(8,128)S(1)}, u32[]{:S(2)}) copy-start(f32[64,640]{1,0:T(8,128)S(1)} %convert_add_fusion.2) | copy-start | bytes 491524
  665.3 11.4 %copy-start.17 = (f32[64,3072]{1,0:T(8,128)S(1)}, f32[64,3072]{1,0:T(8,128)}, u32[]{:S(2)}) copy-start(f32[64,3072]{1,0:T(8,128)} %get-tuple-element.236) | copy-start | bytes 2359300
  665.3 12.3 %copy-start.25 = (f32[16,4096]{1,0:T(8,128)S(1)}, f32[16,4096]{1,0:T(8,128)}, u32[]{:S(2)}) copy-start(f32[16,4096]{1,0:T(8,128)} %get-tuple-element.239) | copy-start | bytes 786436
  665.3 13.0 %copy-start.19 = (f32[64,2048]{1,0:T(8,128)S(1)}, f32[64,2048]{1,0:T(8,128)}, u32[]{:S(2)}) copy-start(f32[64,2048]{1,0:T(8,128)} %get-tuple-element.240) | copy-start | bytes 1572868
  (16 other events, 27.7 us)
Sparse Core Ops, SparseCore 0:
  10.1 52.5 all-gather.10
  64.3 78.9 all-gather.6
  144.9 102.4 all-gather.8
  456.2 103.7 reduce-scatter.2
  562.3 72.7 reduce-scatter.4

commit v13 on v12

--- a/solution.py
+++ b/solution.py
@@ -442,10 +442,10 @@
         for r in range(1, dp):
             lift(i, r).start()
         kept(i).start()
+    gx.start()
     for r in range(1, NE):
         part(r).start()
     part_kept().start()
-    gx.start()
     gx.round(1)
 
     kept(0).wait()

time: 691 us -> 684 us (0.990)
  transfers between devices with their start and end apart: 5 -> 5, of which waited for: 1 -> 0; matrix products, arithmetic and copies ran while one was open for 3% -> 3% of each run, Pallas kernels for 60% -> 60%
where the time goes in v13:
time: 684 us; the launch traced here: 679 us
  Pallas kernels  617 us (90%)
  local copies, waits for them, and re-layouts  21.1 us (3%)
  between operations  14.5 us (2%)
  other arithmetic  13.7 us (2%)
  matrix products  10.7 us (2%)
    pallas_call x1, Pallas kernels, opening(): pl.pallas_call(functools.partial(opening_kernel, dp, chunks), out_shape=(...  79.9 us
    pallas_call x1, Pallas kernels, attend_back(): pl.pallas_call(functools.partial(attend_back_kernel, dp), grid=(batches,)...  69.3 us
    pallas_call x1, Pallas kernels, scatter_share(): pl.pallas_call(functools.partial(scatter_share_kernel, chunks, down.shape...  66.7 us
    pallas_call x1, Pallas kernels, mixture_backward(): pl.pallas_call(functools.partial(backward_kernel, chunks), grid=(NZ,), ou...  66.2 us
    pallas_call x1, Pallas kernels, returning(): pl.pallas_call(functools.partial(return_kernel, dp, chunks), out_shape=(s...  66 us
    pallas_call x1, Pallas kernels, mixture_forward(): pl.pallas_call(functools.partial(forward_kernel, chunks, dp, span, batche...  65.1 us
    pallas_call x1, Pallas kernels, attend(): pl.pallas_call(functools.partial(attend_kernel, dp, span), grid=(batches,...  62.8 us
    pallas_call x1, Pallas kernels, gather16(): pl.pallas_call(functools.partial(gather_kernel, chunks, dp, span, extra),...  52.8 us
  transfers between devices with their start and end apart: 5, of which 0 were waited for; matrix products, arithmetic and copies ran while one was open for 3% of the time, Pallas kernels for 60%

profile of v13, /device:TPU:0, one launch (start us, length us, event | category | flops | bytes accessed | tf_op | source)
XLA Modules:
  0.0 679.4 jit_solution(1995257990148957875)
XLA Ops:
  7.2 2.3 pad_maximum_fusion
  14.7 79.9 %opening.1 = (bf16[16,128,2048]{2,1,0:T(8,128)(2,1)}, bf16[2,16,64,640]{3,2,1,0:T(8,128)(2,1)}, bf16[2,16,64,256]{3,2,1,0:T(8,128)(2,1)}, bf16[2,64,2048]{2,1,0:...) custom-call(bf16[128,2048]{1,0:T(8,128)(2,1)} %bitcast.106, ...), custom_call_target="tpu_custom_call" | custom-call | bytes 4000000 | tf_op jit(solution)/shard_map/opening/pallas_call | solution.py:531
  94.6 1.7 copy-done
  98.4 1.3 copy-done.10
  99.7 17.2 %project.1 = (bf16[2048,2048]{1,0:T(8,128)(2,1)}, bf16[2,1024,256]{2,1,0:T(8,128)(2,1)S(1)}, bf16[2,1024,256]{2,1,0:T(8,128)(2,1)S(1)}, bf16[2,1024,128]{2,1,0:T(8,128)(2,1)S(1)}, bf16[2,1024,512]{2,1,0:T(8,128)(2,1)}) custom-call(bf16[16,128,2048]{2,1,0:T(8,128)(2,1)} %get-tuple-element.93.x_ref, f32[1,2048]{1,0:T(1,128)S(1)} %get-tuple-element.212.gain_ref, ...), custom_call_target="tpu_custom_call" | custom-call | flops 7000000000 | bytes 20000000 | tf_op jit(solution)/shard_map/project/pallas_call | solution.py:1534
  117.0 1.0 copy-done.2
  117.9 1.0 copy-done.3
  119.7 62.8 %attend.1 = (f32[128,2048]{1,0:T(8,128)}, bf16[16,2,64,128]{3,2,1,0:T(8,128)(2,1)}, f32[2,1024,1]{2,1,0:T(8,128)}, bf16[2,208,2048]{2,1,0:T(8,128)(2,1)}) custom-call(s32[2]{0:T(128)} %bitcast.128, bf16[2,1024,256]{2,1,0:T(8,128)(2,1)} %copy-done.2, bf16[2,1024,256]{2,1,0:T(8,128)(2,1)} %copy-done.3, bf16[2,1024,128]{2,1,0:T(8,128)(2,1)} %copy-done.5, ...), custom_call_target="tpu_custom_call" | custom-call | bytes 4000000 | tf_op jit(solution)/shard_map/attend/pallas_call | solution.py:1627
  182.5 1.4 multiply_reduce_fusion
  185.9 52.8 %gather16.1 = (bf16[16,128,2048]{2,1,0:T(8,128)(2,1)}, bf16[2,272,2048]{2,1,0:T(8,128)(2,1)}) custom-call(bf16[128,2048]{1,0:T(8,128)(2,1)} %multiply_convert_fusion.x_ref.mix_ref, bf16[704,2048]{1,0:T(8,128)(2,1)} %bitcast.90), custom_call_target="tpu_custom_call" | custom-call | bytes 4000000 | tf_op jit(solution)/shard_map/gather16/pallas_call | solution.py:382
  238.9 1.1 reshape.264.mask_ref
  241.6 65.1 %mixture_forward.1 = (bf16[2048,2048]{1,0:T(8,128)(2,1)}, bf16[1024,2048]{1,0:T(8,128)(2,1)}, bf16[1024,1408]{1,0:T(8,128)(2,1)}, bf16[1024,1408]{1,0:T(8,128)(2...) custom-call(s32[2]{0:T(128)} %bitcast.129, ...), custom_call_target="tpu_custom_call" | custom-call | bytes 4000000 | tf_op jit(solution)/shard_map/mixture_forward/pallas_call | solution.py:1265
  306.7 66.2 %mixture_backward.1 = (bf16[2048,2176]{1,0:T(8,128)(2,1)}, bf16[1024,2048]{1,0:T(8,128)(2,1)}, bf16[1024,1408]{1,0:T(8,128)(2,1)}, bf16[1024,1408]{1,0:T(8,128)(...) custom-call(f32[1,256]{1,0:T(1,128)} %add_convert_fusion.1.pick_ref, bf16[2048,2048]{1,0:T(8,128)(2,1)} %bitcast.87, ...), custom_call_target="tpu_custom_call" | custom-call | bytes 4000000 | tf_op jit(solution)/shard_map/mixture_backward/pallas_call | solution.py:1299
  372.9 10.7 %convolution_convert_fusion = bf16[1408,2048]{1,0:T(8,128)(2,1)} fusion(bf16[1024,1408]{1,0:T(8,128)(2,1)} %get-tuple-element.122, bf16[1024,2048]{1,0:T(8,128)(2,1)} %get-tuple-element.123), kind=kOutput, calls=%fused_computation | convolution fusion | flops 5908463616 | bytes 12845056 | tf_op jit(solution)/shard_map/dot_general | solution.py:1962
  383.6 66.7 %scatter_share.1 = (f32[128,2176]{1,0:T(8,128)}, bf16[2,528,1024]{2,1,0:T(8,128)(2,1)}, bf16[2048,1408]{1,0:T(8,128)(2,1)}, bf16[2048,1408]{1,0:T(8,128)(2,1)}, bf16[1,704,2048]{2,1,0:T(8,128)(2,1)}) custom-call(bf16[16,128,2176]{2,1,0:T(8,128)(2,1)} %bitcast.99, bf16[2048,512]{1,0:T(8,128)(2,1)} %get-tuple-element.117.ds_ref, ...), custom_call_target="tpu_custom_call" | custom-call | bytes 4000000 | tf_op jit(solution)/shard_map/scatter_share/pallas_call | solution.py:1470
  452.4 4.3 own_middle.1
  456.8 69.3 %attend_back.1 = (bf16[16,2,64,2688]{3,2,1,0:T(8,128)(2,1)}, bf16[2048,256]{1,0:T(8,128)(2,1)}, bf16[128,2048]{1,0:T(8,128)(2,1)}, bf16[512,256]{1,0:T(8,128)(2,1)}, bf16[1,528,1024]{2,1,0:T(8,128)(2,1)}) custom-call(s32[2]{0:T(128)} %bitcast.130, bf16[128,2048]{1,0:T(8,128)(2,1)} %get-tuple-element.125.own_ref, ...), custom_call_target="tpu_custom_call" | custom-call | bytes 4000000 | tf_op jit(solution)/shard_map/attend_back/pallas_call | solution.py:1751
  526.1 1.2 reshape.273
  527.4 2.5 pad_add_fusion
  529.9 66.0 %returning.1 = (f32[128,2688]{1,0:T(8,128)}, bf16[1,16,64,256]{3,2,1,0:T(8,128)(2,1)}, bf16[1,2,64,2048]{3,2,1,0:T(8,128)(2,1)}) custom-call(bf16[16,128,2688]{2,1,0:T(8,128)(2,1)} %bitcast.98, bf16[2,16,64,256]{3,2,1,0:T(8,128)(2,1)} %bitcast.104, bf16[2,64,2048]{2,1,0:T(8,128)(2,1)} %bitcast.110), custom_call_target="tpu_custom_call" | custom-call | bytes 4000000 | tf_op jit(solution)/shard_map/returning/pallas_call | solution.py:790
  597.2 9.4 %own_back.1 = (f32[128,2048]{1,0:T(8,128)}, bf16[16,128,640]{2,1,0:T(8,128)(2,1)}) custom-call(f32[128,2688]{1,0:T(8,128)} %get-tuple-element.135.back_ref, bf16[128,2048]{1,0:T(8,128)(2,1)} %bitcast.107, bf16[128,2048]{1,0:T(8,128)(2,1)} %multiply_convert_fusion.x_ref.mix_ref, bf16[128,16]{1,0:T(8,128)(2,1)} %get-tuple-element.136.logit_ref, ...), custom_call_target="tpu_custom_call" | custom-call | bytes 4000000 | tf_op jit(solution)/shard_map/own_back/pallas_call | solution.py:1847
  608.5 46.1 %closing.1 = (bf16[128,640]{1,0:T(8,128)(2,1)}, bf16[1,64,640]{2,1,0:T(8,128)(2,1)}, f32[64,3072]{1,0:T(8,128)}, f32[16,4096]{1,0:T(8,128)}, f32[64,2048]{1,0:T(8,128)}) custom-call(bf16[16,128,640]{2,1,0:T(8,128)(2,1)} %get-tuple-element.140.p_ref, bf16[16,64,256]{2,1,0:T(8,128)(2,1)} %fusion.1.parts_ref, bf16[2,64,2048]{2,1,0:T(8,128)(2,1)} %fusion.rows_ref), custom_call_target="tpu_custom_call" | custom-call | bytes 4000000 | tf_op jit(solution)/shard_map/closing/pallas_call | solution.py:908
  657.7 1.2 add_multiply_fusion
  658.9 11.3 %widen.1 = (f32[1024,1408]{1,0:T(8,128)}, f32[1024,1408]{1,0:T(8,128)}, f32[704,2048]{1,0:T(8,128)}, f32[176,1024]{1,0:T(8,128)}, f32[176,1024]{1,0:T(8,128)}, /*index=5*/f32[176,1024]{1,0:T(8,128)}) custom-call(s32[1]{0:T(128)} %bitcast.45.plane_ref, bf16[1024,1408]{1,0:T(8,128)(2,1)} %reduce-scatter.3.cloned.1.call-done.gate_ref, ...), custom_call_target="tpu_custom_call" | custom-call | bytes 4000000 | tf_op jit(solution)/shard_map/widen/pallas_call | solution.py:1929
  (135 shorter events, 22.6 us)
Async XLA Ops:
  7.2 234.4 %all-gather.11.cloned.1.call-start = ((), (), s32[]{:S(2)}) async-start(), calls=%async_computation.6 | async-start | bytes 3244032 | tf_op jit(solution)/shard_map/all_gather | solution.py:2089
  9.6 232.0 %all-gather.7.cloned.1.call-start = ((), (), s32[]{:S(2)}) async-start(), calls=%async_computation.4 | async-start | bytes 8650752 | tf_op jit(solution)/shard_map/all_gather | solution.py:2087
  10.4 231.3 %all-gather.9.cloned.1.call-start = ((), (), s32[]{:S(2)}) async-start(), calls=%async_computation.5 | async-start | bytes 8650752 | tf_op jit(solution)/shard_map/all_gather | solution.py:2088
  11.1 647.8 %reduce-scatter.3.cloned.1.call-start = ((), (), s32[]{:S(2)}) async-start(), calls=%async_computation.2 | async-start | bytes 8650752 | tf_op jit(solution)/shard_map/reduce_scatter | solution.py:2135
  11.4 83.2 %copy-start.24 = (bf16[128,16]{1,0:T(8,128)(2,1)}, bf16[128,16]{1,0:T(8,128)(2,1)S(1)}, u32[]{:S(2)}) copy-start(bf16[128,16]{1,0:T(8,128)(2,1)S(1)} %convert_element_type.120.mask_ref) | copy-start | bytes 12292
  97.3 19.7 %copy-start.7 = (f32[1,2048]{1,0:T(1,128)}, f32[1,2048]{1,0:T(1,128)S(1)}, u32[]{:S(2)}) copy-start(f32[1,2048]{1,0:T(1,128)S(1)} %get-tuple-element.212.gain_ref) | copy-start | bytes 24580
  97.3 86.7 %copy-start.28 = (f32[1,2048]{1,0:T(1,128)}, f32[1,2048]{1,0:T(1,128)S(1)}, u32[]{:S(2)}) copy-start(f32[1,2048]{1,0:T(1,128)S(1)} %get-tuple-element.210.gain_ref) | copy-start | bytes 24580
  97.5 19.5 %copy-start.8 = (f32[1,512]{1,0:T(1,128)}, f32[1,512]{1,0:T(1,128)S(1)}, u32[]{:S(2)}) copy-start(f32[1,512]{1,0:T(1,128)S(1)} %reshape.283.lgain_ref) | copy-start | bytes 6148
  98.4 18.5 %copy-start.6 = (bf16[512,256]{1,0:T(8,128)(2,1)}, bf16[512,256]{1,0:T(8,128)(2,1)S(1)}, u32[]{:S(2)}) copy-start(bf16[512,256]{1,0:T(8,128)(2,1)S(1)} %reshape.261.we_ref) | copy-start | bytes 786436
  119.7 62.8 %copy-start.14 = (bf16[2,1,64,2048]{3,2,1,0:T(8,128)(2,1)S(1)}, bf16[2,1,64,2048]{3,2,1,0:T(8,128)(2,1)}, u32[]{:S(2)}) copy-start(bf16[2,1,64,2048]{3,2,1,0:T(8,128)(2,1)} %param.28) | copy-start | bytes 1572868
  183.9 54.7 %copy-start.1 = (bf16[2,16,64,640]{3,2,1,0:T(8,128)(2,1)S(1)}, bf16[2,16,64,640]{3,2,1,0:T(8,128)(2,1)}, u32[]{:S(2)}) copy-start(bf16[2,16,64,640]{3,2,1,0:T(8,128)(2,1)} %get-tuple-element.94) | copy-start | bytes 7864324
  185.8 54.1 %copy-start.29 = (s32[2,1]{0,1:T(1,128)S(1)}, s32[2,1]{0,1:T(1,128)}, u32[]{:S(2)}) copy-start(s32[2,1]{0,1:T(1,128)} %param.30) | copy-start | bytes 28
  185.8 54.9 %copy-start.21 = (bf16[2,1,64,2048]{3,2,1,0:T(8,128)(2,1)S(1)}, bf16[2,1,64,2048]{3,2,1,0:T(8,128)(2,1)}, u32[]{:S(2)}) copy-start(bf16[2,1,64,2048]{3,2,1,0:T(8,128)(2,1)} %param.29) | copy-start | bytes 1572868
  450.3 208.6 %reduce-scatter.5.cloned.1.call-start = ((), (), s32[]{:S(2)}) async-start(), calls=%async_computation.3 | async-start | bytes 8650752 | tf_op jit(solution)/shard_map/reduce_scatter | solution.py:2136
  597.2 9.4 %copy-start.13 = (bf16[2048,256]{1,0:T(8,128)(2,1)S(1)}, bf16[2048,256]{1,0:T(8,128)(2,1)}, u32[]{:S(2)}) copy-start(bf16[2048,256]{1,0:T(8,128)(2,1)} %pad_add_fusion) | copy-start | bytes 3145732
  597.2 9.4 %copy-start.20 = (bf16[1,16,64,256]{3,2,1,0:T(8,128)(2,1)S(1)}, bf16[1,16,64,256]{3,2,1,0:T(8,128)(2,1)}, u32[]{:S(2)}) copy-start(bf16[1,16,64,256]{3,2,1,0:T(8,128)(2,1)} %get-tuple-element.141) | copy-start | bytes 1572868
  597.2 10.3 %copy-start.15 = (bf16[128,2048]{1,0:T(8,128)(2,1)S(1)}, bf16[128,2048]{1,0:T(8,128)(2,1)}, u32[]{:S(2)}) copy-start(bf16[128,2048]{1,0:T(8,128)(2,1)} %get-tuple-element.134) | copy-start | bytes 1572868
  597.2 10.3 %copy-start.18 = (bf16[1,2,64,2048]{3,2,1,0:T(8,128)(2,1)S(1)}, bf16[1,2,64,2048]{3,2,1,0:T(8,128)(2,1)}, u32[]{:S(2)}) copy-start(bf16[1,2,64,2048]{3,2,1,0:T(8,128)(2,1)} %get-tuple-element.142) | copy-start | bytes 1572868
  607.6 50.1 %copy-start.12 = (f32[128,2048]{1,0:T(8,128)S(1)}, f32[128,2048]{1,0:T(8,128)}, u32[]{:S(2)}) copy-start(f32[128,2048]{1,0:T(8,128)} %copy-done.11) | copy-start | bytes 3145732
  607.6 50.1 %copy-start.16 = (f32[128,2048]{1,0:T(8,128)S(1)}, f32[128,2048]{1,0:T(8,128)}, u32[]{:S(2)}) copy-start(f32[128,2048]{1,0:T(8,128)} %get-tuple-element.115) | copy-start | bytes 3145732
  655.5 14.7 %copy-start.22 = (f32[64,640]{1,0:T(8,128)}, f32[64,640]{1,0:T(8,128)S(1)}, u32[]{:S(2)}) copy-start(f32[64,640]{1,0:T(8,128)S(1)} %convert_add_fusion.2) | copy-start | bytes 491524
  658.9 11.4 %copy-start.17 = (f32[64,3072]{1,0:T(8,128)S(1)}, f32[64,3072]{1,0:T(8,128)}, u32[]{:S(2)}) copy-start(f32[64,3072]{1,0:T(8,128)} %get-tuple-element.236) | copy-start | bytes 2359300
  658.9 12.3 %copy-start.25 = (f32[16,4096]{1,0:T(8,128)S(1)}, f32[16,4096]{1,0:T(8,128)}, u32[]{:S(2)}) copy-start(f32[16,4096]{1,0:T(8,128)} %get-tuple-element.239) | copy-start | bytes 786436
  658.9 13.0 %copy-start.19 = (f32[64,2048]{1,0:T(8,128)S(1)}, f32[64,2048]{1,0:T(8,128)}, u32[]{:S(2)}) copy-start(f32[64,2048]{1,0:T(8,128)} %get-tuple-element.240) | copy-start | bytes 1572868
  (16 other events, 27.7 us)
Sparse Core Ops, SparseCore 0:
  10.1 45.8 all-gather.10
  57.5 73.2 all-gather.6
  132.3 98.6 all-gather.8
  450.4 102.9 reduce-scatter.2
  555.7 73.1 reduce-scatter.4

commit v14 on v13

--- a/solution.py
+++ b/solution.py
@@ -764,12 +764,12 @@
             src_ref=rows_ref, dst_ref=rows_far.at[r - 1], send_sem=rs.at[r], recv_sem=rr.at[r],
             device_id={"dp": (plane + r) % dp}, device_id_type=MESH)
 
+    s.start()
     swap.start()
     for r in range(1, dp):
         @pl.when((plane + r) % dp == keeper)
         def _():
             row(r).start()
-    s.start()
     s.run()
     s.finish()
     swap.finish()

time: 684 us -> 684 us (level)
  no operation moved by 1% of the time
where the time goes in v14:
time: 684 us; the launch traced here: 679 us
  Pallas kernels  617 us (90%)
  local copies, waits for them, and re-layouts  21.1 us (3%)
  between operations  14.5 us (2%)
  other arithmetic  13.7 us (2%)
  matrix products  10.7 us (2%)
    pallas_call x1, Pallas kernels, opening(): pl.pallas_call(functools.partial(opening_kernel, dp, chunks), out_shape=(...  79.9 us
    pallas_call x1, Pallas kernels, attend_back(): pl.pallas_call(functools.partial(attend_back_kernel, dp), grid=(batches,)...  69.3 us
    pallas_call x1, Pallas kernels, scatter_share(): pl.pallas_call(functools.partial(scatter_share_kernel, chunks, down.shape...  66.7 us
    pallas_call x1, Pallas kernels, mixture_backward(): pl.pallas_call(functools.partial(backward_kernel, chunks), grid=(NZ,), ou...  66.2 us
    pallas_call x1, Pallas kernels, returning(): pl.pallas_call(functools.partial(return_kernel, dp, chunks), out_shape=(s...  66 us
    pallas_call x1, Pallas kernels, mixture_forward(): pl.pallas_call(functools.partial(forward_kernel, chunks, dp, span, batche...  65.1 us
    pallas_call x1, Pallas kernels, attend(): pl.pallas_call(functools.partial(attend_kernel, dp, span), grid=(batches,...  62.8 us
    pallas_call x1, Pallas kernels, gather16(): pl.pallas_call(functools.partial(gather_kernel, chunks, dp, span, extra),...  52.8 us
  transfers between devices with their start and end apart: 5, of which 0 were waited for; matrix products, arithmetic and copies ran while one was open for 3% of the time, Pallas kernels for 60%

profile of v14, /device:TPU:0, one launch (start us, length us, event | category | flops | bytes accessed | tf_op | source)
XLA Modules:
  0.0 679.4 jit_solution(16415869236100122954)
XLA Ops:
  7.2 2.3 pad_maximum_fusion
  14.7 79.9 %opening.1 = (bf16[16,128,2048]{2,1,0:T(8,128)(2,1)}, bf16[2,16,64,640]{3,2,1,0:T(8,128)(2,1)}, bf16[2,16,64,256]{3,2,1,0:T(8,128)(2,1)}, bf16[2,64,2048]{2,1,0:...) custom-call(bf16[128,2048]{1,0:T(8,128)(2,1)} %bitcast.106, ...), custom_call_target="tpu_custom_call" | custom-call | bytes 4000000 | tf_op jit(solution)/shard_map/opening/pallas_call | solution.py:531
  94.6 1.7 copy-done
  98.4 1.3 copy-done.10
  99.7 17.2 %project.1 = (bf16[2048,2048]{1,0:T(8,128)(2,1)}, bf16[2,1024,256]{2,1,0:T(8,128)(2,1)S(1)}, bf16[2,1024,256]{2,1,0:T(8,128)(2,1)S(1)}, bf16[2,1024,128]{2,1,0:T(8,128)(2,1)S(1)}, bf16[2,1024,512]{2,1,0:T(8,128)(2,1)}) custom-call(bf16[16,128,2048]{2,1,0:T(8,128)(2,1)} %get-tuple-element.93.x_ref, f32[1,2048]{1,0:T(1,128)S(1)} %get-tuple-element.212.gain_ref, ...), custom_call_target="tpu_custom_call" | custom-call | flops 7000000000 | bytes 20000000 | tf_op jit(solution)/shard_map/project/pallas_call | solution.py:1534
  117.0 1.0 copy-done.2
  117.9 1.0 copy-done.3
  119.7 62.8 %attend.1 = (f32[128,2048]{1,0:T(8,128)}, bf16[16,2,64,128]{3,2,1,0:T(8,128)(2,1)}, f32[2,1024,1]{2,1,0:T(8,128)}, bf16[2,208,2048]{2,1,0:T(8,128)(2,1)}) custom-call(s32[2]{0:T(128)} %bitcast.128, bf16[2,1024,256]{2,1,0:T(8,128)(2,1)} %copy-done.2, bf16[2,1024,256]{2,1,0:T(8,128)(2,1)} %copy-done.3, bf16[2,1024,128]{2,1,0:T(8,128)(2,1)} %copy-done.5, ...), custom_call_target="tpu_custom_call" | custom-call | bytes 4000000 | tf_op jit(solution)/shard_map/attend/pallas_call | solution.py:1627
  182.5 1.4 multiply_reduce_fusion
  185.9 52.8 %gather16.1 = (bf16[16,128,2048]{2,1,0:T(8,128)(2,1)}, bf16[2,272,2048]{2,1,0:T(8,128)(2,1)}) custom-call(bf16[128,2048]{1,0:T(8,128)(2,1)} %multiply_convert_fusion.x_ref.mix_ref, bf16[704,2048]{1,0:T(8,128)(2,1)} %bitcast.90), custom_call_target="tpu_custom_call" | custom-call | bytes 4000000 | tf_op jit(solution)/shard_map/gather16/pallas_call | solution.py:382
  238.9 1.1 reshape.264.mask_ref
  241.6 65.1 %mixture_forward.1 = (bf16[2048,2048]{1,0:T(8,128)(2,1)}, bf16[1024,2048]{1,0:T(8,128)(2,1)}, bf16[1024,1408]{1,0:T(8,128)(2,1)}, bf16[1024,1408]{1,0:T(8,128)(2...) custom-call(s32[2]{0:T(128)} %bitcast.129, ...), custom_call_target="tpu_custom_call" | custom-call | bytes 4000000 | tf_op jit(solution)/shard_map/mixture_forward/pallas_call | solution.py:1265
  306.7 66.2 %mixture_backward.1 = (bf16[2048,2176]{1,0:T(8,128)(2,1)}, bf16[1024,2048]{1,0:T(8,128)(2,1)}, bf16[1024,1408]{1,0:T(8,128)(2,1)}, bf16[1024,1408]{1,0:T(8,128)(...) custom-call(f32[1,256]{1,0:T(1,128)} %add_convert_fusion.1.pick_ref, bf16[2048,2048]{1,0:T(8,128)(2,1)} %bitcast.87, ...), custom_call_target="tpu_custom_call" | custom-call | bytes 4000000 | tf_op jit(solution)/shard_map/mixture_backward/pallas_call | solution.py:1299
  372.9 10.7 %convolution_convert_fusion = bf16[1408,2048]{1,0:T(8,128)(2,1)} fusion(bf16[1024,1408]{1,0:T(8,128)(2,1)} %get-tuple-element.122, bf16[1024,2048]{1,0:T(8,128)(2,1)} %get-tuple-element.123), kind=kOutput, calls=%fused_computation | convolution fusion | flops 5908463616 | bytes 12845056 | tf_op jit(solution)/shard_map/dot_general | solution.py:1962
  383.6 66.7 %scatter_share.1 = (f32[128,2176]{1,0:T(8,128)}, bf16[2,528,1024]{2,1,0:T(8,128)(2,1)}, bf16[2048,1408]{1,0:T(8,128)(2,1)}, bf16[2048,1408]{1,0:T(8,128)(2,1)}, bf16[1,704,2048]{2,1,0:T(8,128)(2,1)}) custom-call(bf16[16,128,2176]{2,1,0:T(8,128)(2,1)} %bitcast.99, bf16[2048,512]{1,0:T(8,128)(2,1)} %get-tuple-element.117.ds_ref, ...), custom_call_target="tpu_custom_call" | custom-call | bytes 4000000 | tf_op jit(solution)/shard_map/scatter_share/pallas_call | solution.py:1470
  452.4 4.3 own_middle.1
  456.8 69.3 %attend_back.1 = (bf16[16,2,64,2688]{3,2,1,0:T(8,128)(2,1)}, bf16[2048,256]{1,0:T(8,128)(2,1)}, bf16[128,2048]{1,0:T(8,128)(2,1)}, bf16[512,256]{1,0:T(8,128)(2,1)}, bf16[1,528,1024]{2,1,0:T(8,128)(2,1)}) custom-call(s32[2]{0:T(128)} %bitcast.130, bf16[128,2048]{1,0:T(8,128)(2,1)} %get-tuple-element.125.own_ref, ...), custom_call_target="tpu_custom_call" | custom-call | bytes 4000000 | tf_op jit(solution)/shard_map/attend_back/pallas_call | solution.py:1751
  526.1 1.2 reshape.273
  527.4 2.5 pad_add_fusion
  529.9 66.0 %returning.1 = (f32[128,2688]{1,0:T(8,128)}, bf16[1,16,64,256]{3,2,1,0:T(8,128)(2,1)}, bf16[1,2,64,2048]{3,2,1,0:T(8,128)(2,1)}) custom-call(bf16[16,128,2688]{2,1,0:T(8,128)(2,1)} %bitcast.98, bf16[2,16,64,256]{3,2,1,0:T(8,128)(2,1)} %bitcast.104, bf16[2,64,2048]{2,1,0:T(8,128)(2,1)} %bitcast.110), custom_call_target="tpu_custom_call" | custom-call | bytes 4000000 | tf_op jit(solution)/shard_map/returning/pallas_call | solution.py:790
  597.2 9.4 %own_back.1 = (f32[128,2048]{1,0:T(8,128)}, bf16[16,128,640]{2,1,0:T(8,128)(2,1)}) custom-call(f32[128,2688]{1,0:T(8,128)} %get-tuple-element.135.back_ref, bf16[128,2048]{1,0:T(8,128)(2,1)} %bitcast.107, bf16[128,2048]{1,0:T(8,128)(2,1)} %multiply_convert_fusion.x_ref.mix_ref, bf16[128,16]{1,0:T(8,128)(2,1)} %get-tuple-element.136.logit_ref, ...), custom_call_target="tpu_custom_call" | custom-call | bytes 4000000 | tf_op jit(solution)/shard_map/own_back/pallas_call | solution.py:1847
  608.5 46.1 %closing.1 = (bf16[128,640]{1,0:T(8,128)(2,1)}, bf16[1,64,640]{2,1,0:T(8,128)(2,1)}, f32[64,3072]{1,0:T(8,128)}, f32[16,4096]{1,0:T(8,128)}, f32[64,2048]{1,0:T(8,128)}) custom-call(bf16[16,128,640]{2,1,0:T(8,128)(2,1)} %get-tuple-element.140.p_ref, bf16[16,64,256]{2,1,0:T(8,128)(2,1)} %fusion.1.parts_ref, bf16[2,64,2048]{2,1,0:T(8,128)(2,1)} %fusion.rows_ref), custom_call_target="tpu_custom_call" | custom-call | bytes 4000000 | tf_op jit(solution)/shard_map/closing/pallas_call | solution.py:908
  657.7 1.2 add_multiply_fusion
  658.9 11.3 %widen.1 = (f32[1024,1408]{1,0:T(8,128)}, f32[1024,1408]{1,0:T(8,128)}, f32[704,2048]{1,0:T(8,128)}, f32[176,1024]{1,0:T(8,128)}, f32[176,1024]{1,0:T(8,128)}, /*index=5*/f32[176,1024]{1,0:T(8,128)}) custom-call(s32[1]{0:T(128)} %bitcast.45.plane_ref, bf16[1024,1408]{1,0:T(8,128)(2,1)} %reduce-scatter.3.cloned.1.call-done.gate_ref, ...), custom_call_target="tpu_custom_call" | custom-call | bytes 4000000 | tf_op jit(solution)/shard_map/widen/pallas_call | solution.py:1929
  (135 shorter events, 22.6 us)
Async XLA Ops:
  7.2 234.4 %all-gather.11.cloned.1.call-start = ((), (), s32[]{:S(2)}) async-start(), calls=%async_computation.6 | async-start | bytes 3244032 | tf_op jit(solution)/shard_map/all_gather | solution.py:2089
  9.6 232.0 %all-gather.7.cloned.1.call-start = ((), (), s32[]{:S(2)}) async-start(), calls=%async_computation.4 | async-start | bytes 8650752 | tf_op jit(solution)/shard_map/all_gather | solution.py:2087
  10.4 231.3 %all-gather.9.cloned.1.call-start = ((), (), s32[]{:S(2)}) async-start(), calls=%async_computation.5 | async-start | bytes 8650752 | tf_op jit(solution)/shard_map/all_gather | solution.py:2088
  11.1 647.8 %reduce-scatter.3.cloned.1.call-start = ((), (), s32[]{:S(2)}) async-start(), calls=%async_computation.2 | async-start | bytes 8650752 | tf_op jit(solution)/shard_map/reduce_scatter | solution.py:2135
  11.4 83.2 %copy-start.24 = (bf16[128,16]{1,0:T(8,128)(2,1)}, bf16[128,16]{1,0:T(8,128)(2,1)S(1)}, u32[]{:S(2)}) copy-start(bf16[128,16]{1,0:T(8,128)(2,1)S(1)} %convert_element_type.120.mask_ref) | copy-start | bytes 12292
  97.3 19.7 %copy-start.7 = (f32[1,2048]{1,0:T(1,128)}, f32[1,2048]{1,0:T(1,128)S(1)}, u32[]{:S(2)}) copy-start(f32[1,2048]{1,0:T(1,128)S(1)} %get-tuple-element.212.gain_ref) | copy-start | bytes 24580
  97.3 86.7 %copy-start.28 = (f32[1,2048]{1,0:T(1,128)}, f32[1,2048]{1,0:T(1,128)S(1)}, u32[]{:S(2)}) copy-start(f32[1,2048]{1,0:T(1,128)S(1)} %get-tuple-element.210.gain_ref) | copy-start | bytes 24580
  97.5 19.5 %copy-start.8 = (f32[1,512]{1,0:T(1,128)}, f32[1,512]{1,0:T(1,128)S(1)}, u32[]{:S(2)}) copy-start(f32[1,512]{1,0:T(1,128)S(1)} %reshape.283.lgain_ref) | copy-start | bytes 6148
  98.4 18.5 %copy-start.6 = (bf16[512,256]{1,0:T(8,128)(2,1)}, bf16[512,256]{1,0:T(8,128)(2,1)S(1)}, u32[]{:S(2)}) copy-start(bf16[512,256]{1,0:T(8,128)(2,1)S(1)} %reshape.261.we_ref) | copy-start | bytes 786436
  119.7 62.8 %copy-start.14 = (bf16[2,1,64,2048]{3,2,1,0:T(8,128)(2,1)S(1)}, bf16[2,1,64,2048]{3,2,1,0:T(8,128)(2,1)}, u32[]{:S(2)}) copy-start(bf16[2,1,64,2048]{3,2,1,0:T(8,128)(2,1)} %param.28) | copy-start | bytes 1572868
  183.9 54.7 %copy-start.1 = (bf16[2,16,64,640]{3,2,1,0:T(8,128)(2,1)S(1)}, bf16[2,16,64,640]{3,2,1,0:T(8,128)(2,1)}, u32[]{:S(2)}) copy-start(bf16[2,16,64,640]{3,2,1,0:T(8,128)(2,1)} %get-tuple-element.94) | copy-start | bytes 7864324
  185.8 54.1 %copy-start.29 = (s32[2,1]{0,1:T(1,128)S(1)}, s32[2,1]{0,1:T(1,128)}, u32[]{:S(2)}) copy-start(s32[2,1]{0,1:T(1,128)} %param.30) | copy-start | bytes 28
  185.8 54.9 %copy-start.21 = (bf16[2,1,64,2048]{3,2,1,0:T(8,128)(2,1)S(1)}, bf16[2,1,64,2048]{3,2,1,0:T(8,128)(2,1)}, u32[]{:S(2)}) copy-start(bf16[2,1,64,2048]{3,2,1,0:T(8,128)(2,1)} %param.29) | copy-start | bytes 1572868
  450.3 208.6 %reduce-scatter.5.cloned.1.call-start = ((), (), s32[]{:S(2)}) async-start(), calls=%async_computation.3 | async-start | bytes 8650752 | tf_op jit(solution)/shard_map/reduce_scatter | solution.py:2136
  597.2 9.4 %copy-start.13 = (bf16[2048,256]{1,0:T(8,128)(2,1)S(1)}, bf16[2048,256]{1,0:T(8,128)(2,1)}, u32[]{:S(2)}) copy-start(bf16[2048,256]{1,0:T(8,128)(2,1)} %pad_add_fusion) | copy-start | bytes 3145732
  597.2 9.4 %copy-start.20 = (bf16[1,16,64,256]{3,2,1,0:T(8,128)(2,1)S(1)}, bf16[1,16,64,256]{3,2,1,0:T(8,128)(2,1)}, u32[]{:S(2)}) copy-start(bf16[1,16,64,256]{3,2,1,0:T(8,128)(2,1)} %get-tuple-element.141) | copy-start | bytes 1572868
  597.2 10.3 %copy-start.15 = (bf16[128,2048]{1,0:T(8,128)(2,1)S(1)}, bf16[128,2048]{1,0:T(8,128)(2,1)}, u32[]{:S(2)}) copy-start(bf16[128,2048]{1,0:T(8,128)(2,1)} %get-tuple-element.134) | copy-start | bytes 1572868
  597.2 10.3 %copy-start.18 = (bf16[1,2,64,2048]{3,2,1,0:T(8,128)(2,1)S(1)}, bf16[1,2,64,2048]{3,2,1,0:T(8,128)(2,1)}, u32[]{:S(2)}) copy-start(bf16[1,2,64,2048]{3,2,1,0:T(8,128)(2,1)} %get-tuple-element.142) | copy-start | bytes 1572868
  607.6 50.1 %copy-start.12 = (f32[128,2048]{1,0:T(8,128)S(1)}, f32[128,2048]{1,0:T(8,128)}, u32[]{:S(2)}) copy-start(f32[128,2048]{1,0:T(8,128)} %copy-done.11) | copy-start | bytes 3145732
  607.6 50.1 %copy-start.16 = (f32[128,2048]{1,0:T(8,128)S(1)}, f32[128,2048]{1,0:T(8,128)}, u32[]{:S(2)}) copy-start(f32[128,2048]{1,0:T(8,128)} %get-tuple-element.115) | copy-start | bytes 3145732
  655.5 14.7 %copy-start.22 = (f32[64,640]{1,0:T(8,128)}, f32[64,640]{1,0:T(8,128)S(1)}, u32[]{:S(2)}) copy-start(f32[64,640]{1,0:T(8,128)S(1)} %convert_add_fusion.2) | copy-start | bytes 491524
  658.9 11.4 %copy-start.17 = (f32[64,3072]{1,0:T(8,128)S(1)}, f32[64,3072]{1,0:T(8,128)}, u32[]{:S(2)}) copy-start(f32[64,3072]{1,0:T(8,128)} %get-tuple-element.236) | copy-start | bytes 2359300
  658.9 12.3 %copy-start.25 = (f32[16,4096]{1,0:T(8,128)S(1)}, f32[16,4096]{1,0:T(8,128)}, u32[]{:S(2)}) copy-start(f32[16,4096]{1,0:T(8,128)} %get-tuple-element.239) | copy-start | bytes 786436
  658.9 13.0 %copy-start.19 = (f32[64,2048]{1,0:T(8,128)S(1)}, f32[64,2048]{1,0:T(8,128)}, u32[]{:S(2)}) copy-start(f32[64,2048]{1,0:T(8,128)} %get-tuple-element.240) | copy-start | bytes 1572868
  (16 other events, 27.7 us)
Sparse Core Ops, SparseCore 0:
  10.1 45.8 all-gather.10
  57.5 73.2 all-gather.6
  132.3 98.6 all-gather.8
  450.4 102.8 reduce-scatter.2
  555.6 73.1 reduce-scatter.4
